TPU v7x, 32 devices: a whole 2x2x4 slice. The times are simulated.
32 devices in a mesh: table: 16 (over z, y, x), group: 2 (over core).
Axes of the slice: x: 2, y: 2, z: 4, core: 2. Of those that a mesh axis runs over, the one named last changes fastest.
Arguments:
- item_owner: int32 [16384, 1], P(('table', 'group')), may hold values from 0 to 15; in each aligned block of 512 rows (0 to 511, 512 to 1023, ...) at most 48 rows name the same one
- item_row: int32 [16384], P(('table', 'group')), may hold values from 0 to 2047
- lengths: int32 [32, 8], P(('table', 'group')), may hold values from 1 to 256, 512 in all within a row
- table: bfloat16 [32768, 512], P('table'), may hold values from -6 to 6
- w_in: bfloat16 [512, 2048], replicated, may hold values from -0.25 to 0.25
- w_out: bfloat16 [512, 512], replicated, may hold values from -0.25 to 0.25
- gain: float32 [512], replicated, may hold values from 0.1 to 1.9
- cotangent: bfloat16 [16384, 512], P(('table', 'group')), may hold values from -6 to 6
Outputs:
- result: bfloat16 [16384, 512], P(('table', 'group'))
- table_grad: float32 [32768, 512], P(('table', 'group'))
- w_in_grad: float32 [512, 2048], P('table', 'group')
- w_out_grad: float32 [512, 512], P('table')
- gain_grad: float32 [512], P('table')
Inputs may be any that keep to these rules, and one draw needn't show every extreme that they name: `item_owner`: among the 512 items of one device, no index of table owns more than 48 items' rows, a bound that some block reaches.
All inputs are finite; a program needn't handle non-finite values.
Results may differ from a plain program's by a relative error of at most 0.008.
Values may be sent and summed in bfloat16 or wider, within the bound.
No kernel may reach another device: no remote copies, remote signals or barrier semaphores. Data moves between devices by JAX's collectives and lax.ppermute only.
A program may use at most 128 MiB of HBM per device.

v0:
```python
import math

import jax
import jax.numpy as jnp
from jax import lax
from jax.sharding import PartitionSpec as P

D = 512
HEADS = 8
HEAD_DIM = 64


def rounded(value):
    return lax.optimization_barrier(value.astype(jnp.bfloat16))


def silu_slope(value):
    sig_val = jax.nn.sigmoid(value)
    return sig_val * (1.0 + value * (1.0 - sig_val))


def layer_block(embedded, lengths_row, w_in, w_out, gain, grad_out):
    count = embedded.shape[0]
    scale = 1.0 / math.sqrt(HEAD_DIM)
    position = jnp.arange(count, dtype=jnp.int32)
    ends = jnp.cumsum(lengths_row)
    segment = jnp.sum((position[:, None] >= ends[None, :]).astype(jnp.int32), 1)
    allowed = (segment[:, None] == segment[None, :]) & (position[None, :] <= position[:, None])
    pre_act = jnp.dot(embedded, w_in, preferred_element_type=jnp.float32)
    projected = jax.nn.silu(pre_act).astype(jnp.bfloat16)
    upd_part = projected[:, :D].astype(jnp.float32)
    val_heads = projected[:, D : 2 * D].reshape(count, HEADS, HEAD_DIM)
    qry_heads = projected[:, 2 * D : 3 * D].reshape(count, HEADS, HEAD_DIM)
    key_heads = projected[:, 3 * D :].reshape(count, HEADS, HEAD_DIM)
    scores = (
        jnp.einsum("thd,shd->hts", qry_heads, key_heads, preferred_element_type=jnp.float32) * scale
    )
    weights = jnp.where(allowed[None], jax.nn.silu(scores), 0.0).astype(jnp.bfloat16)
    attended = jnp.einsum(
        "hts,shd->thd", weights, val_heads, preferred_element_type=jnp.float32
    ).reshape(count, D)
    centered = attended - jnp.mean(attended, 1, keepdims=True)
    inv_std = lax.rsqrt(jnp.mean(centered * centered, 1, keepdims=True) + 1e-05)
    normed = centered * inv_std
    mixed = (normed * gain * upd_part).astype(jnp.bfloat16)
    result = (
        embedded.astype(jnp.float32) + jnp.dot(mixed, w_out, preferred_element_type=jnp.float32)
    ).astype(jnp.bfloat16)
    grad_w_out = lax.dot_general(
        mixed, grad_out, (((0,), (0,)), ((), ())), preferred_element_type=jnp.float32
    )
    grad_mixed = rounded(
        lax.dot_general(
            grad_out, w_out, (((1,), (1,)), ((), ())), preferred_element_type=jnp.float32
        )
    ).astype(jnp.float32)
    grad_upd = grad_mixed * normed * gain
    grad_normed = grad_mixed * gain * upd_part
    grad_gain = jnp.sum(grad_mixed * normed * upd_part, 0)
    grad_att = (
        (
            grad_normed
            - jnp.mean(grad_normed, 1, keepdims=True)
            - normed * jnp.mean(grad_normed * normed, 1, keepdims=True)
        )
        * inv_std
    ).astype(jnp.bfloat16)
    att_heads = grad_att.reshape(count, HEADS, HEAD_DIM)
    grad_weights = jnp.einsum(
        "thd,shd->hts", att_heads, val_heads, preferred_element_type=jnp.float32
    )
    grad_val = jnp.einsum(
        "hts,thd->shd", weights, att_heads, preferred_element_type=jnp.float32
    ).reshape(count, D)
    grad_score = (jnp.where(allowed[None], grad_weights * silu_slope(scores), 0.0) * scale).astype(
        jnp.bfloat16
    )
    grad_qry = jnp.einsum(
        "hts,shd->thd", grad_score, key_heads, preferred_element_type=jnp.float32
    ).reshape(count, D)
    grad_key = jnp.einsum(
        "hts,thd->shd", grad_score, qry_heads, preferred_element_type=jnp.float32
    ).reshape(count, D)
    grad_proj = jnp.concatenate([grad_upd, grad_val, grad_qry, grad_key], 1)
    grad_pre = (grad_proj * silu_slope(pre_act)).astype(jnp.bfloat16)
    grad_w_in = lax.dot_general(
        embedded, grad_pre, (((0,), (0,)), ((), ())), preferred_element_type=jnp.float32
    )
    grad_emb = (
        grad_out.astype(jnp.float32)
        + lax.dot_general(
            grad_pre, w_in, (((1,), (1,)), ((), ())), preferred_element_type=jnp.float32
        )
    ).astype(jnp.bfloat16)
    return (result, grad_emb, grad_w_in, grad_w_out, grad_gain)


def on_device(item_owner, item_row, lengths, table, w_in, w_out, gain, cotangent):
    owners = lax.axis_size("table")
    groups = lax.axis_size("group")
    count = item_row.shape[0]
    capacity = max(2, 3 * count // (2 * owners))
    owner = item_owner[:, 0]
    onehot = (owner[:, None] == jnp.arange(owners, dtype=jnp.int32)[None, :]).astype(jnp.int32)
    earlier = jnp.cumsum(onehot, 0) - onehot
    slot_pos = jnp.sum(earlier * onehot, 1)
    requested = jnp.zeros((owners, capacity), jnp.int32).at[owner, slot_pos].set(item_row)
    wanted = lax.all_to_all(requested, "table", split_axis=0, concat_axis=0, tiled=True)
    found = table[wanted]
    returned = lax.all_to_all(found, "table", split_axis=0, concat_axis=0, tiled=True)
    flat_slot = owner * capacity + slot_pos
    embedded = returned.reshape(owners * capacity, D)[flat_slot]
    result, grad_emb, grad_w_in, grad_w_out, grad_gain = layer_block(
        embedded, lengths[0], w_in, w_out, gain, cotangent
    )
    outgoing = (
        jnp.zeros((owners * capacity, D), jnp.bfloat16)
        .at[flat_slot]
        .set(grad_emb)
        .reshape(owners, capacity, D)
    )
    incoming = lax.all_to_all(outgoing, "table", split_axis=0, concat_axis=0, tiled=True)
    flat_rows = incoming.reshape(owners * capacity, D)
    flat_ids = wanted.reshape(owners * capacity)
    local_grad = (
        jnp.zeros((table.shape[0], D), jnp.float32).at[flat_ids].add(flat_rows.astype(jnp.float32))
    )
    table_grad = lax.psum_scatter(
        local_grad.astype(jnp.bfloat16), "group", scatter_dimension=0, tiled=True
    ).astype(jnp.float32)
    rows_per = D // owners
    cols_per = 4 * D // groups
    sum_in, sum_out, sum_gain = lax.psum((grad_w_in, grad_w_out, grad_gain), ("table", "group"))
    row_start = lax.axis_index("table") * rows_per
    col_start = lax.axis_index("group") * cols_per
    w_in_grad = lax.dynamic_slice(sum_in, (row_start, col_start), (rows_per, cols_per))
    w_out_grad = lax.dynamic_slice_in_dim(sum_out, row_start, rows_per, 0)
    gain_grad = lax.dynamic_slice_in_dim(sum_gain, row_start, rows_per, 0)
    return (result, table_grad, w_in_grad, w_out_grad, gain_grad)


def solution(mesh):
    return jax.shard_map(
        on_device,
        mesh=mesh,
        in_specs=(
            P(("table", "group"), None),
            P(("table", "group")),
            P(("table", "group"), None),
            P("table", None),
            P(),
            P(),
            P(),
            P(("table", "group"), None),
        ),
        out_specs=(
            P(("table", "group"), None),
            P(("table", "group"), None),
            P("table", "group"),
            P("table", None),
            P("table"),
        ),
        check_vma=False,
    )
```

profile of v0, /device:TPU:0, one launch (start us, length us, event | category | flops | bytes accessed | tf_op | source)
XLA Modules:
  0.0 337.7 jit_solution(13936023580540699034)
XLA Ops:
  8.0 0.0 copy-start
  8.0 0.8 fusion.18
  8.9 1.1 reduce-window.18
  10.0 0.2 slice_reduce_fusion
  10.2 0.8 fusion.17
  11.0 0.7 compare_select_fusion.2
  11.7 43.2 %scatter_fusion = s32[16,48]{1,0:T(8,128)S(1)} fusion(s32[16,48]{1,0:T(8,128)S(1)} %broadcast.145, s32[512]{0:T(512)S(1)} %bitcast.83, s32[512]{0:T(512)} %param.9), kind=kCustom, calls=%fused_computation.2 | custom fusion | bytes 10240 | tf_op jit(solution)/shard_map/scatter | solution.py:107
  55.0 15.4 %all_to_all.22 = s32[16,1,48]{2,1,0:T(1,128)S(1)} all-to-all(s32[16,1,48]{2,1,0:T(1,128)S(1)} %bitcast.82), channel_id=1, replica_groups=mesh['table'=16,'group'=2] {'table'}, dimensions={0} | all-to-all | bytes 6144 | tf_op jit(solution)/shard_map/all_to_all | solution.py:108
  70.4 0.1 reshape.242
  70.5 0.0 copy-start.16
  70.5 5.3 %gather_fusion = bf16[768,512]{1,0:T(8,128)(2,1)} fusion(bf16[2048,512]{1,0:T(8,128)(2,1)} %param.11, s32[1024]{0:T(1024)S(1)} %pad_clamp_fusion.1), kind=kCustom, calls=%fused_computation | custom fusion | bytes 1575936 | tf_op jit(solution)/shard_map/gather | solution.py:109
  75.8 3.6 %all-to-all-start.1 = ((bf16[16,48,512]{2,1,0:T(8,128)(2,1)}), bf16[16,48,512]{2,1,0:T(8,128)(2,1)S(1)}, u32[]{:S(2)}, u32[]{:S(2)}) async-start(bf16[16,48,512]{2,1,0:T(8,128)(2,1)} %bitcast.90), calls=%async_computation.1 | async-start | bytes 1572864 | tf_op jit(solution)/shard_map/all_to_all | solution.py:110
  79.4 0.2 all-reduce.3.cloned.1.call-start
  79.6 0.2 reduce-window.20
  79.8 2.3 convolution_convert_fusion
  82.1 0.1 convert_reduce_fusion
  82.2 0.9 fusion.10
  83.1 14.8 %all-to-all-done.1 = bf16[16,48,512]{2,1,0:T(8,128)(2,1)S(1)} async-done(((bf16[16,48,512]{2,1,0:T(8,128)(2,1)}), bf16[16,48,512]{2,1,0:T(8,128)(2,1)S(1)}, u32[]{:S(2)}, u32[]{:S(2)}) %all-to-all-start.1) | async-done | bytes 786464 | tf_op jit(solution)/shard_map/all_to_all | solution.py:110
  98.0 2.0 gather_fusion.1
  99.9 3.6 %multiply_convert_fusion.1 = (bf16[512,2048]{1,0:T(8,128)(2,1)S(1)}, f32[512,2048]{1,0:T(8,128)}) fusion(bf16[512,512]{1,0:T(8,128)(2,1)S(1)} %gather_fusion.1, bf16[512,2048]{1,0:T(8,128)(2,1)S(1)} %copy-done), kind=kOutput, calls=%fused_computation.10 | convolution fusion | flops 1078984704 | bytes 8912896 | tf_op jit(solution)/shard_map/dot_general | solution.py:29
  103.5 1.3 copy-done.7
  104.8 1.0 fusion.21
  105.8 2.0 copy.47
  107.8 1.0 copy.48
  108.9 0.2 copy.46
  109.1 7.4 %select_convert_fusion = (bf16[8,512,512]{2,1,0:T(8,128)(2,1)S(1)}, f32[8,512,512]{2,1,0:T(8,128)}) fusion(pred[512,512]{1,0:T(8,128)(4,1)S(1)} %copy-done.14, bf16[512,8,64]{0,2,1:T(8,128)(2,1)} %bitcast.91, bf16[512,8,64]{0,2,1:T(8,128)(2,1)} %bitcast.93), kind=kOutput, calls=%fused_computation.6 | convolution fusion | flops 283115520 | bytes 13893632 | tf_op jit(solution)/shard_map/thd,shd->hts/dot_general | solution.py:36
  116.6 2.0 copy-done.1
  118.5 1.4 fusion.22
  119.9 0.2 fusion.9
  120.1 0.8 copy-done.2
  120.9 1.6 copy.49
  122.5 2.9 fusion.7
  125.3 2.7 multiply_convert_fusion.2
  128.0 2.0 copy.50
  130.0 3.2 fusion.23
  133.3 7.0 %multiply_convert_fusion = bf16[8,512,512]{2,1,0:T(8,128)(2,1)S(1)} fusion(f32[8,512,512]{2,1,0:T(8,128)} %get-tuple-element.21, pred[512,512]{1,0:T(8,128)(4,1)S(1)} %copy-done.14, bf16[512,8,64]{0,2,1:T(8,128)(2,1)S(1)} %bitcast.98, bf16[512,8,64]{0,2,1:T(8,128)(2,1)} %bitcast.96), kind=kOutput, calls=%fused_computation.5 | convolution fusion | flops 293601280 | bytes 13893632 | tf_op jit(solution)/shard_map/thd,shd->hts/dot_general | solution.py:69
  140.4 2.4 fusion.24
  142.7 1.8 fusion.25
  144.5 1.3 copy.51
  145.8 2.6 copy.52
  148.5 2.5 copy.53
  151.0 4.3 %fusion = bf16[512,2048]{1,0:T(8,128)(2,1)S(1)} fusion(f32[512,512]{1,0:T(8,128)} %copy.53, f32[512,512]{1,0:T(8,128)} %copy.52, f32[512,512]{1,0:T(8,128)} %copy.51, f32[512,512]{1,0:T(8,128)} %get-tuple-element.15, f32[512,2048]{1,0:T(8,128)} %get-tuple-element.19), kind=kLoop, calls=%fused_computation.9 | loop fusion | flops 12582912 | bytes 10485760 | tf_op jit(solution)/shard_map/convert_element_type | solution.py:85
  155.3 1.3 copy-done.3
  156.6 3.2 fusion.26
  159.8 1.4 fusion.27
  161.3 0.0 all-reduce.3.cloned.1.call-update
  161.3 3.8 %fusion.4 = bf16[512,512]{1,0:T(8,128)(2,1)} fusion(bf16[512,2048]{1,0:T(8,128)(2,1)} %copy-done.3, bf16[512,2048]{1,0:T(8,128)(2,1)S(1)} %copy-done, bf16[512,512]{1,0:T(8,128)(2,1)} %param.15), kind=kOutput, calls=%fused_computation.23 | convolution fusion | flops 1074528256 | bytes 5242880 | tf_op jit(solution)/shard_map/dot_general | solution.py:91
  165.1 3.9 %scatter_custom_fusion.1 = bf16[768,512]{1,0:T(8,128)(2,1)} fusion(s32[512]{0:T(512)S(1)} %bitcast.103, bf16[512,512]{1,0:T(8,128)(2,1)} %fusion.4, bf16[]{:T(256)} %constant.26.clone.1), kind=kCustom, calls=%fused_computation.37 | custom fusion | bytes 786944 | tf_op jit(solution)/shard_map/scatter | solution.py:119
  169.0 4.8 %all-to-all-start.2 = ((bf16[16,48,512]{2,1,0:T(8,128)(2,1)}), bf16[16,48,512]{2,1,0:T(8,128)(2,1)}, u32[]{:S(2)}, u32[]{:S(2)}) async-start(bf16[16,48,512]{2,1,0:T(8,128)(2,1)} %bitcast.89), calls=%async_computation.2 | async-start | bytes 1572864 | tf_op jit(solution)/shard_map/all_to_all | solution.py:122
  173.7 0.0 reduce-scatter.2.cloned.1.call-start
  173.8 0.5 broadcast.201
  174.3 0.7 reduce.10
  175.0 0.1 reshape.233
  175.1 28.4 %all-to-all-done.2 = bf16[16,48,512]{2,1,0:T(8,128)(2,1)} async-done(((bf16[16,48,512]{2,1,0:T(8,128)(2,1)}), bf16[16,48,512]{2,1,0:T(8,128)(2,1)}, u32[]{:S(2)}, u32[]{:S(2)}) %all-to-all-start.2) | async-done | bytes 786464 | tf_op jit(solution)/shard_map/all_to_all | solution.py:122
  203.5 9.4 %scatter_custom_fusion.2 = f32[2048,512]{1,0:T(8,128)} fusion(s32[768]{0:T(1024)S(1)} %fusion.19, f32[]{:T(128)} %constant.23.clone.1, bf16[768,512]{1,0:T(8,128)(2,1)} %bitcast.32), kind=kCustom, calls=%fused_computation.12 | custom fusion | flops 786432 | bytes 4980740 | tf_op jit(solution)/shard_map/scatter-add | solution.py:126
  212.9 3.8 %convert_element_type.79 = bf16[2048,512]{1,0:T(8,128)(2,1)} convert(f32[2048,512]{1,0:T(8,128)} %scatter_custom_fusion.2) | non-fusion elementwise | flops 1048576 | bytes 6291456 | tf_op jit(solution)/shard_map/convert_element_type | solution.py:129
  216.7 0.0 reduce-scatter.2.cloned.1.call-update
  216.7 38.5 %psum.23 = f32[512]{0:T(512)S(1)} all-reduce(f32[512]{0:T(512)S(1)} %get-tuple-element.5), channel_id=1, replica_groups=mesh['table'=16,'group'=2] {'table','group'}, use_global_device_ids=true, to_apply=%region_16.17 | all-reduce | flops 512 | bytes 4096 | tf_op jit(solution)/shard_map/psum | solution.py:133
  255.3 0.6 dynamic_slice.11
  255.8 2.3 fusion.5
  258.1 66.3 %all-reduce.3.cloned.1.call-done = (f32[512,2048]{1,0:T(8,128)}, f32[512,512]{1,0:T(8,128)}) async-done(((f32[512,2048]{1,0:T(8,128)}, f32[512,512]{1,0:T(8,128)}), (f32[512,2048]{1,0:T(8,128)}, f32[512,512]{1,0:T(8,128)})) %all-reduce.3.cloned.1.call-update) | async-done | bytes 5242896 | tf_op jit(solution)/shard_map/psum | solution.py:133
  324.4 1.6 dynamic_slice.9
  326.0 1.5 constant_dynamic-slice_fusion
  327.5 2.8 convert_element_type.80
  (39 shorter events, 0.2 us)
Async XLA Ops:
  8.0 91.9 %copy-start = (bf16[512,2048]{1,0:T(8,128)(2,1)S(1)}, bf16[512,2048]{1,0:T(8,128)(2,1)}, u32[]{:S(2)}) copy-start(bf16[512,2048]{1,0:T(8,128)(2,1)} %param.12) | copy-start | bytes 6291460
  70.5 9.2 %copy-start.16 = (s32[1,8]{1,0:T(1,128)S(1)}, s32[1,8]{1,0:T(1,128)}, u32[]{:S(2)}) copy-start(s32[1,8]{1,0:T(1,128)} %param.10) | copy-start | bytes 100
  70.5 9.3 %copy-start.8 = (bf16[512,512]{1,0:T(8,128)(2,1)S(1)}, bf16[512,512]{1,0:T(8,128)(2,1)}, u32[]{:S(2)}) copy-start(bf16[512,512]{1,0:T(8,128)(2,1)} %param.15) | copy-start | bytes 1572868
  75.8 22.2 %all-to-all-start.1 = ((bf16[16,48,512]{2,1,0:T(8,128)(2,1)}), bf16[16,48,512]{2,1,0:T(8,128)(2,1)S(1)}, u32[]{:S(2)}, u32[]{:S(2)}) async-start(bf16[16,48,512]{2,1,0:T(8,128)(2,1)} %bitcast.90), calls=%async_computation.1 | async-start | bytes 1572864 | tf_op jit(solution)/shard_map/all_to_all | solution.py:110
  79.4 245.0 %all-reduce.3.cloned.1.call-start = ((), (), s32[]{:S(2)}) async-start(), calls=%async_computation.5 | async-start | bytes 10485760 | tf_op jit(solution)/shard_map/psum | solution.py:133
  99.9 3.6 %copy-start.4 = (bf16[512,512]{1,0:T(8,128)(2,1)}, bf16[512,512]{1,0:T(8,128)(2,1)S(1)}, u32[]{:S(2)}) copy-start(bf16[512,512]{1,0:T(8,128)(2,1)S(1)} %gather_fusion.1) | copy-start | bytes 1572868
  103.5 1.3 copy-start.7
  104.8 4.3 %copy-start.14 = (pred[512,512]{1,0:T(8,128)(4,1)S(1)}, pred[512,512]{1,0:T(8,128)(4,1)}, u32[]{:S(2)}) copy-start(pred[512,512]{1,0:T(8,128)(4,1)} %fusion.10) | copy-start | bytes 786436
  109.1 7.5 %copy-start.12 = (bf16[512,512]{0,1:T(8,128)(2,1)}, bf16[512,512]{0,1:T(8,128)(2,1)S(1)}, u32[]{:S(2)}) copy-start(bf16[512,512]{0,1:T(8,128)(2,1)S(1)} %copy.46) | copy-start | bytes 1572868
  116.5 2.0 copy-start.1
  118.5 4.0 %copy-start.15 = (f32[512]{0:T(512)S(1)}, f32[512]{0:T(512)}, u32[]{:S(2)}) copy-start(f32[512]{0:T(512)} %param.14) | copy-start | bytes 6148
  119.9 1.0 copy-start.2
  130.0 3.2 copy-start.13
  133.3 7.0 %copy-start.11 = (bf16[512,512]{0,1:T(8,128)(2,1)S(1)}, bf16[512,512]{0,1:T(8,128)(2,1)}, u32[]{:S(2)}) copy-start(bf16[512,512]{0,1:T(8,128)(2,1)} %copy.48) | copy-start | bytes 1572868
  140.3 2.4 copy-start.10
  151.0 5.6 %copy-start.5 = (bf16[512,512]{1,0:T(8,128)(2,1)S(1)}, bf16[512,512]{1,0:T(8,128)(2,1)}, u32[]{:S(2)}) copy-start(bf16[512,512]{1,0:T(8,128)(2,1)} %copy-done.4) | copy-start | bytes 1572868
  155.3 1.3 copy-start.3
  156.6 3.2 copy-start.6
  156.6 3.2 copy-start.9
  169.0 34.6 %all-to-all-start.2 = ((bf16[16,48,512]{2,1,0:T(8,128)(2,1)}), bf16[16,48,512]{2,1,0:T(8,128)(2,1)}, u32[]{:S(2)}, u32[]{:S(2)}) async-start(bf16[16,48,512]{2,1,0:T(8,128)(2,1)} %bitcast.89), calls=%async_computation.2 | async-start | bytes 1572864 | tf_op jit(solution)/shard_map/all_to_all | solution.py:122
  173.7 153.7 %reduce-scatter.2.cloned.1.call-start = ((), (), s32[]{:S(2)}) async-start(), calls=%async_computation.4 | async-start | bytes 3145728 | tf_op jit(solution)/shard_map/reduce_scatter | solution.py:128
Sparse Core Ops, SparseCore 0:
  161.4 162.9 all-reduce.2
Sparse Core Ops, SparseCore 1:
  216.8 8.2 reduce-scatter.1
where the time goes:
time: 340 us; the launch traced here: 338 us
  waiting for transfers between devices  110 us (32%)
  local copies, waits for them, and re-layouts  78.6 us (23%)
  blocking collectives  53.9 us (16%)
  matrix products  39.8 us (12%)
  other arithmetic  31.4 us (9%)
  between operations  15.7 us (5%)
  starting transfers between devices  8.66 us (3%)
    psum x1, waiting for transfers between devices, on_device(): lax.psum((grad_w_in, grad_w_out, grad_gain), ('table', 'group'))  66.3 us
    scatter x1, local copies, waits for them, and re-layouts, on_device(): jnp.zeros((owners, capacity), jnp.int32).at[owner, slot_pos].set(item_row)  43.2 us
    psum x1, blocking collectives, on_device(): lax.psum((grad_w_in, grad_w_out, grad_gain), ('table', 'group'))  38.5 us
    all_to_all x1, waiting for transfers between devices, on_device(): lax.all_to_all(outgoing, 'table', split_axis=0, concat_axis=0, tiled=True)  28.4 us
    all_to_all x1, blocking collectives, on_device(): lax.all_to_all(requested, 'table', split_axis=0, concat_axis=0, tiled=True)  15.4 us
    all_to_all x1, waiting for transfers between devices, on_device(): lax.all_to_all(found, 'table', split_axis=0, concat_axis=0, tiled=True)  14.8 us
    scatter-add x1, other arithmetic, on_device(): jnp.zeros((table.shape[0], D), jnp.float32).at[flat_ids]  9.39 us
    dot_general x1, matrix products, layer_block(): jnp.einsum('thd,shd->hts', qry_heads, key_heads, preferred_element_type=j...  7.44 us
  transfers between devices with their start and end apart: 4, of which 3 were waited for; matrix products, arithmetic and copies ran while one was open for 9% of the time, Pallas kernels for 0%

commit v1 on v0

v1 whole, which is shorter than its diff:
```python
import functools
import math

import jax
import jax.numpy as jnp
from jax import lax
from jax.experimental import pallas as pl
from jax.experimental.pallas import tpu as pltpu
from jax.sharding import PartitionSpec as P

HEADS = 8
HEAD_DIM = 64
LANES = 128
QUERY_ROWS = 256
VMEM_LIMIT = 56 * 1024 * 1024

F32 = jnp.float32
BF16 = jnp.bfloat16


def iota(shape, dim):
    return lax.broadcasted_iota(jnp.int32, shape, dim)


def hot(cond):
    return jnp.where(cond, 1.0, 0.0).astype(BF16)


def dot_nn(a, b):
    return lax.dot_general(a, b, (((1,), (0,)), ((), ())), preferred_element_type=F32)


def dot_nt(a, b):
    return lax.dot_general(a, b, (((1,), (1,)), ((), ())), preferred_element_type=F32)


def dot_tn(a, b):
    return lax.dot_general(a, b, (((0,), (0,)), ((), ())), preferred_element_type=F32)


def call(kernel, out_shape, flops, nbytes, operands, smem=(), scratch=()):
    specs = [
        pl.BlockSpec(memory_space=pltpu.SMEM if i in smem else pltpu.VMEM)
        for i in range(len(operands))
    ]
    return pl.pallas_call(
        kernel,
        out_shape=out_shape,
        in_specs=specs,
        out_specs=jax.tree.map(lambda _: pl.BlockSpec(memory_space=pltpu.VMEM), out_shape),
        scratch_shapes=scratch,
        compiler_params=pltpu.CompilerParams(vmem_limit_bytes=VMEM_LIMIT),
        cost_estimate=pl.CostEstimate(flops=flops, bytes_accessed=nbytes, transcendentals=0),
    )(*operands)


def request_kernel(cap, owner_ref, row_ref, req_ref, slot_ref):
    owners, width = req_ref.shape
    count = owner_ref.shape[1]
    owner = owner_ref[...]
    row = row_ref[...]
    mine = iota((owners, count), 0) == owner
    mine_b = hot(mine)
    before = hot(iota((count, count), 0) < iota((count, count), 1))
    earlier = dot_nn(mine_b, before)
    place = jnp.sum(jnp.where(mine, earlier, 0.0), axis=0, keepdims=True)
    slot_ref[...] = owner.astype(F32) * float(cap) + place
    at_place = hot(iota((width, count), 0).astype(F32) == place)
    high = jnp.where(mine, (row >> 8).astype(F32), 0.0).astype(BF16)
    low = jnp.where(mine, (row & 255).astype(F32), 0.0).astype(BF16)
    found = dot_nt(high, at_place) * 256.0 + dot_nt(low, at_place)
    req_ref[...] = found.astype(jnp.int32)


def lookup_kernel(cap, wanted_ref, table_ref, found_ref, ids_ref):
    owners, width = wanted_ref.shape
    slots = found_ref.shape[0]
    rows = table_ref.shape[0]
    wanted = wanted_ref[...]
    high = (wanted >> 8).astype(F32).astype(BF16)
    low = (wanted & 255).astype(F32).astype(BF16)
    slot = iota((slots, owners), 0).astype(F32)
    holder = jnp.floor((slot + 0.5) * (1.0 / cap))
    spread = hot(holder == iota((slots, owners), 1).astype(F32))
    ids = dot_nn(spread, high) * 256.0 + dot_nn(spread, low)
    slot = iota((slots, width), 0).astype(F32)
    place = slot - jnp.floor((slot + 0.5) * (1.0 / cap)) * float(cap)
    ids = jnp.sum(
        jnp.where(iota((slots, width), 1).astype(F32) == place, ids, 0.0), axis=1, keepdims=True
    )
    wide = jnp.broadcast_to(ids, (slots, LANES))
    ids_ref[...] = wide.T[0:1, :]
    step = 256 if slots % 256 == 0 else slots
    for start in range(0, slots, step):
        part = ids[start : start + step]
        pick = hot(iota((step, rows), 1).astype(F32) == part)
        found_ref[start : start + step, :] = dot_nn(pick, table_ref[...]).astype(BF16)


def collect_kernel(groups, *refs):
    ids_refs, in_refs, out_ref = refs[:groups], refs[groups : 2 * groups], refs[-1]
    rows = out_ref.shape[0]
    slots = in_refs[0].shape[0]
    base = lax.axis_index("group") * rows
    step = 256 if rows % 256 == 0 else rows

    def chunk(i, _):
        start = pl.multiple_of(i * step, step)
        own = (iota((step, slots), 0) + (base + start)).astype(F32)
        total = None
        for ids_ref, in_ref in zip(ids_refs, in_refs):
            part = dot_nn(hot(own == ids_ref[...]), in_ref[...])
            total = part if total is None else total + part
        out_ref[pl.ds(start, step), :] = total
        return 0

    lax.fori_loop(0, rows // step, chunk, 0)


def layer_kernel(
    groups,
    wparts,
    len_ref,
    slot_ref,
    ret_ref,
    w_in_ref,
    w_out_ref,
    gain_ref,
    cot_ref,
    result_ref,
    outgoing_ref,
    grads_ref,
    emb_ref,
    proj_ref,
    slope_ref,
    bias_ref,
    weight_ref,
    wslope_ref,
    att_ref,
    mixed_ref,
    gatt_ref,
    gpre_ref,
    gval_ref,
    gkey_ref,
    gwo_ref,
):
    count, width = cot_ref.shape
    slots = ret_ref.shape[0]
    per = LANES // HEAD_DIM
    slabs = width // LANES
    qrows = QUERY_ROWS if count % QUERY_ROWS == 0 else count
    half_scale = 0.5 / math.sqrt(HEAD_DIM)

    slot = jnp.broadcast_to(slot_ref[...], (LANES, count)).T
    emb = None
    for start in range(0, slots, LANES):
        pick = hot(slot == (iota((count, LANES), 1) + start).astype(F32))
        part = dot_nn(pick, ret_ref[start : start + LANES, :])
        emb = part if emb is None else emb + part
    emb_ref[...] = emb.astype(BF16)

    def project(i, _):
        cols = pl.ds(pl.multiple_of(i * width, width), width)
        pre = dot_nn(emb_ref[...], w_in_ref[:, cols])
        sig = 0.5 * jnp.tanh(0.5 * pre) + 0.5
        act = pre * sig
        proj_ref[i] = act.astype(BF16)
        slope_ref[i] = sig + act * (1.0 - sig)
        return 0

    lax.fori_loop(0, 4, project, 0)

    pos = iota((count, 1), 0)
    begin = jnp.zeros((count, 1), jnp.int32)
    end = jnp.int32(0)
    for s in range(len_ref.shape[1]):
        end = end + len_ref[0, s]
        begin = jnp.where(pos >= end, end, begin)
    key = iota((count, count), 1)
    allowed = (key >= begin) & (key <= iota((count, count), 0))
    bias_ref[...] = jnp.where(allowed, 3.0e38, -30.0)

    lane = iota((count, LANES), 1)

    def only(value, head, factor=1.0):
        inside = (lane >= head * HEAD_DIM) & (lane < (head + 1) * HEAD_DIM)
        return jnp.where(inside, value.astype(F32) * factor, 0.0).astype(BF16)

    def forward(p, _):
        cols = pl.ds(pl.multiple_of(p * LANES, LANES), LANES)
        val, qry, key_all = proj_ref[1, :, cols], proj_ref[2, :, cols], proj_ref[3, :, cols]
        qrys = [only(qry, a, half_scale) for a in range(per)]
        vals = [only(val, a) for a in range(per)]
        for r0 in range(0, count, qrows):
            r1 = r0 + qrows
            total = None
            for a in range(per):
                half = dot_nt(qrys[a][r0:r1], key_all[:r1])
                half = jnp.minimum(half, bias_ref[r0:r1, :r1])
                th = jnp.tanh(half)
                weight = half + half * th
                weight_b = weight.astype(BF16)
                weight_ref[p * per + a, r0:r1, :r1] = weight_b
                wslope_ref[p * per + a, r0:r1, :r1] = (1.0 + th) + weight * (1.0 - th)
                part = dot_nn(weight_b, vals[a][:r1])
                total = part if total is None else total + part
            att_ref[r0:r1, cols] = total
        return 0

    lax.fori_loop(0, slabs, forward, 0)

    gain = gain_ref[...]
    gain_sum = jnp.zeros((1, width), F32)
    for r0 in range(0, count, qrows):
        rows = slice(r0, r0 + qrows)
        att = att_ref[rows, :]
        centered = att - jnp.mean(att, 1, keepdims=True)
        inv = lax.rsqrt(jnp.mean(centered * centered, 1, keepdims=True) + 1e-05)
        normed = centered * inv
        upd = proj_ref[0, rows, :].astype(F32)
        scaled = normed * gain
        mixed = (scaled * upd).astype(BF16)
        mixed_ref[rows, :] = mixed
        result_ref[rows, :] = (
            emb_ref[rows, :].astype(F32) + dot_nn(mixed, w_out_ref[...])
        ).astype(BF16)
        gmix = dot_nt(cot_ref[rows, :], w_out_ref[...]).astype(BF16).astype(F32)
        gpre_ref[rows, 0:width] = (gmix * scaled * slope_ref[0, rows, :]).astype(BF16)
        gnorm = gmix * gain * upd
        gain_sum = gain_sum + jnp.sum(gmix * normed * upd, 0, keepdims=True)
        mean1 = jnp.mean(gnorm, 1, keepdims=True)
        mean2 = jnp.mean(gnorm * normed, 1, keepdims=True)
        gatt_ref[rows, :] = ((gnorm - mean1 - normed * mean2) * inv).astype(BF16)
    gwo_ref[...] = dot_tn(mixed_ref[...], cot_ref[...]).astype(BF16)

    def backward(p, _):
        start = pl.multiple_of(p * LANES, LANES)
        cols = pl.ds(start, LANES)
        val, qry, key_all = proj_ref[1, :, cols], proj_ref[2, :, cols], proj_ref[3, :, cols]
        gatt = gatt_ref[:, cols]
        qrys = [only(qry, a, half_scale) for a in range(per)]
        keys = [only(key_all, a) for a in range(per)]
        gatts = [only(gatt, a) for a in range(per)]
        gval_ref[...] = jnp.zeros_like(gval_ref)
        gkey_ref[...] = jnp.zeros_like(gkey_ref)
        for r0 in range(0, count, qrows):
            r1 = r0 + qrows
            gqry = None
            for a in range(per):
                gweight = dot_nt(gatts[a][r0:r1], val[:r1])
                gscore = (gweight * wslope_ref[p * per + a, r0:r1, :r1]).astype(BF16)
                part = dot_nn(gscore, keys[a][:r1])
                gqry = part if gqry is None else gqry + part
                gval_ref[:r1, :] += dot_tn(weight_ref[p * per + a, r0:r1, :r1], gatts[a][r0:r1])
                gkey_ref[:r1, :] += dot_tn(gscore, qrys[a][r0:r1])
            gpre_ref[r0:r1, pl.ds(2 * width + start, LANES)] = (
                gqry * half_scale * slope_ref[2, r0:r1, cols]
            ).astype(BF16)
        gpre_ref[:, pl.ds(width + start, LANES)] = (gval_ref[...] * slope_ref[1, :, cols]).astype(BF16)
        gpre_ref[:, pl.ds(3 * width + start, LANES)] = (gkey_ref[...] * slope_ref[3, :, cols]).astype(BF16)
        return 0

    lax.fori_loop(0, slabs, backward, 0)

    gemb = (cot_ref[...].astype(F32) + dot_nt(gpre_ref[...], w_in_ref[...])).astype(BF16)
    for start in range(0, slots, 256):
        stop = min(start + 256, slots)
        put = hot((iota((stop - start, count), 0) + start).astype(F32) == slot_ref[...])
        outgoing_ref[start:stop, :] = dot_nn(put, gemb).astype(BF16)

    me = lax.axis_index("group")
    emb_t = emb_ref[...].T
    cols_in = 4 * width // groups
    cols_out = width // wparts
    chunk = min(cols_in, 512)
    gain_col = jnp.broadcast_to(gain_sum, (LANES, width)).T.astype(BF16)
    for k in range(groups):
        part = lax.rem(me + k, groups)
        for c in range(0, cols_in, chunk):
            cols = pl.ds(pl.multiple_of(part * cols_in + c, LANES), chunk)
            grads_ref[k, :, c : c + chunk] = dot_nn(emb_t, gpre_ref[:, cols]).astype(BF16)
        cols = pl.ds(pl.multiple_of(lax.rem(part, wparts) * cols_out, LANES), cols_out)
        grads_ref[k, :, cols_in : cols_in + cols_out] = gwo_ref[:, cols]
        grads_ref[k, :, cols_in + cols_out :] = gain_col


def shift(value, axis, size, amount):
    return lax.ppermute(value, axis, [(i, (i + amount) % size) for i in range(size)])


def sum_scatter(value, owners):
    inner = 4 if owners % 4 == 0 else 1
    outer = owners // inner
    me = lax.axis_index("table")
    high, low = me // inner, me % inner
    rows, cols = value.shape[1:]
    value = value.reshape(outer, inner, rows, cols)

    def pick_low(k):
        return lax.dynamic_index_in_dim(value, low ^ k, 1, keepdims=False)

    total = pick_low(0).astype(F32)
    for k in range(1, inner):
        perm = [(i, i // inner * inner + ((i % inner) ^ k)) for i in range(owners)]
        total = total + lax.ppermute(pick_low(k), "table", perm).astype(F32)
    part = total.astype(BF16)
    final = lax.dynamic_index_in_dim(total, high, 0, keepdims=False)
    for k in range(1, outer):
        perm = [(i, ((i // inner + k) % outer) * inner + i % inner) for i in range(owners)]
        sent = lax.dynamic_index_in_dim(part, (high + k) % outer, 0, keepdims=False)
        final = final + lax.ppermute(sent, "table", perm).astype(F32)
    return final


def on_device(item_owner, item_row, lengths, table, w_in, w_out, gain, cotangent):
    owners = lax.axis_size("table")
    groups = lax.axis_size("group")
    count = item_row.shape[0]
    width = table.shape[1]
    capacity = max(2, 3 * count // (2 * owners))
    slots = owners * capacity
    padded = -(-capacity // LANES) * LANES
    me = lax.axis_index("group")

    requested, slot = call(
        functools.partial(request_kernel, capacity),
        (
            jax.ShapeDtypeStruct((owners, padded), jnp.int32),
            jax.ShapeDtypeStruct((1, count), F32),
        ),
        4 * count * count * owners,
        8 * count,
        (item_owner.reshape(1, count), item_row.reshape(1, count)),
    )
    wanted = lax.all_to_all(requested, "table", split_axis=0, concat_axis=0, tiled=True)
    found, ids = call(
        functools.partial(lookup_kernel, capacity),
        (
            jax.ShapeDtypeStruct((slots, width), BF16),
            jax.ShapeDtypeStruct((1, slots), F32),
        ),
        2 * slots * table.shape[0] * width,
        2 * (slots + table.shape[0]) * width,
        (wanted, table),
    )
    returned = lax.all_to_all(found, "table", split_axis=0, concat_axis=0, tiled=True)
    all_ids = [ids] + [shift(ids, "group", groups, k) for k in range(1, groups)]

    wparts = min(groups, width // LANES)
    cols_in = 4 * width // groups
    cols_out = width // wparts
    cols_all = cols_in + cols_out + LANES
    square = pltpu.VMEM((count, width), BF16)
    result, outgoing, grads = call(
        functools.partial(layer_kernel, groups, wparts),
        (
            jax.ShapeDtypeStruct((count, width), BF16),
            jax.ShapeDtypeStruct((slots, width), BF16),
            jax.ShapeDtypeStruct((groups, width, cols_all), BF16),
        ),
        32 * count * width * width + 14 * count * count * width,
        24 * count * width,
        (lengths, slot, returned, w_in, w_out, gain.reshape(1, width), cotangent),
        smem=(0,),
        scratch=[
            square,
            pltpu.VMEM((4, count, width), BF16),
            pltpu.VMEM((4, count, width), F32),
            pltpu.VMEM((count, count), F32),
            pltpu.VMEM((HEADS, count, count), BF16),
            pltpu.VMEM((HEADS, count, count), F32),
            pltpu.VMEM((count, width), F32),
            square,
            square,
            pltpu.VMEM((count, 4 * width), BF16),
            pltpu.VMEM((count, LANES), F32),
            pltpu.VMEM((count, LANES), F32),
            pltpu.VMEM((width, width), BF16),
        ],
    )

    incoming = lax.all_to_all(outgoing, "table", split_axis=0, concat_axis=0, tiled=True)
    all_incoming = [incoming] + [shift(incoming, "group", groups, k) for k in range(1, groups)]
    table_grad = call(
        functools.partial(collect_kernel, groups),
        jax.ShapeDtypeStruct((table.shape[0] // groups, width), F32),
        2 * slots * table.shape[0] * width,
        2 * groups * slots * width + 4 * table.shape[0] // groups * width,
        (*all_ids, *all_incoming),
    )

    chip = grads[0].astype(F32)
    for k in range(1, groups):
        chip = chip + shift(grads[k], "group", groups, k).astype(F32)
    rows = width // owners
    summed = sum_scatter(chip.astype(BF16).reshape(owners, rows, cols_all), owners)
    w_in_grad = summed[:, :cols_in]
    mine = summed[:, cols_in : cols_in + cols_out]
    pieces = jnp.stack([mine] + [shift(mine, "group", groups, k) for k in range(1, groups)])
    w_out_grad = jnp.concatenate(
        [
            lax.dynamic_index_in_dim(pieces, (me - p) % groups, 0, keepdims=False)
            for p in range(wparts)
        ],
        1,
    )
    gain_grad = summed[:, cols_in + cols_out]
    return (result, table_grad, w_in_grad, w_out_grad, gain_grad)


def solution(mesh):
    return jax.shard_map(
        on_device,
        mesh=mesh,
        in_specs=(
            P(("table", "group"), None),
            P(("table", "group")),
            P(("table", "group"), None),
            P("table", None),
            P(),
            P(),
            P(),
            P(("table", "group"), None),
        ),
        out_specs=(
            P(("table", "group"), None),
            P(("table", "group"), None),
            P("table", "group"),
            P("table", None),
            P("table"),
        ),
        check_vma=False,
    )
```

time: 340 us -> 122 us (0.36)
  waiting for transfers between devices: 110 us -> 26.6 us
  local copies, waits for them, and re-layouts: 78.6 us -> 4.41 us
  matrix products: 39.8 us -> 0 us
  Pallas kernels: 0 us -> 32.6 us
  other arithmetic: 31.4 us -> 3.56 us
  between operations: 15.7 us -> 0.75 us
  blocking collectives: 53.9 us -> 39.9 us
  starting transfers between devices: 8.66 us -> 13.9 us
    psum x1 -> x0, waiting for transfers between devices: 66.3 us -> none  [on_device(): lax.psum((grad_w_in, grad_w_out, grad_gain), ('table', 'group'))]
    scatter x2 -> x0, local copies, waits for them, and re-layouts: 47.1 us -> none  [the longest x1 43.2 us: on_device(): jnp.zeros((owners, capacity), jnp.int32).at[owner, slot_pos].set(item_row)]
    dot_general x12 -> x0, matrix products: 39.8 us -> none  [the longest x1 7.44 us: layer_block(): jnp.einsum('thd,shd->hts', qry_heads, key_heads, preferred_element_type=j...]
    psum x1 -> x0, blocking collectives: 38.5 us -> none  [on_device(): lax.psum((grad_w_in, grad_w_out, grad_gain), ('table', 'group'))]
    pallas_call x0 -> x4, Pallas kernels: none -> 32.6 us  [call(): pl.pallas_call(kernel, out_shape=out_shape, in_specs=specs, out_specs=jax...]
    all_to_all x1, waiting for transfers between devices: 28.4 us -> 0.01 us  [on_device(): lax.all_to_all(outgoing, 'table', split_axis=0, concat_axis=0, tiled=True)]
    ppermute x0 -> x10, waiting for transfers between devices: none -> 26.6 us  [the longest x3 22.5 us: sum_scatter(): total = total + lax.ppermute(pick_low(k), 'table', perm).astype(F32)]
    all_to_all x0 -> x1, blocking collectives: none -> 24.3 us  [on_device(): lax.all_to_all(found, 'table', split_axis=0, concat_axis=0, tiled=True)]
  transfers between devices with their start and end apart: 4 -> 11, of which waited for: 3 -> 6; matrix products, arithmetic and copies ran while one was open for 9% -> 4% of each run, Pallas kernels for 0% -> 0%
where the time goes in v1:
time: 122 us
  blocking collectives  39.9 us (33%)
  Pallas kernels  32.6 us (27%)
  waiting for transfers between devices  26.6 us (22%)
  starting transfers between devices  13.9 us (11%)
  local copies, waits for them, and re-layouts  4.41 us (4%)
  other arithmetic  3.56 us (3%)
    pallas_call x4, Pallas kernels, call(): pl.pallas_call(kernel, out_shape=out_shape, in_specs=specs, out_specs=jax...  32.6 us
    all_to_all x1, blocking collectives, on_device(): lax.all_to_all(found, 'table', split_axis=0, concat_axis=0, tiled=True)  24.3 us
    ppermute x3, waiting for transfers between devices, sum_scatter(): total = total + lax.ppermute(pick_low(k), 'table', perm).astype(F32)  22.5 us
    all_to_all x1, blocking collectives, on_device(): lax.all_to_all(requested, 'table', split_axis=0, concat_axis=0, tiled=True)  15.6 us
    ppermute x3, starting transfers between devices, sum_scatter(): final = final + lax.ppermute(sent, 'table', perm).astype(F32)  5.44 us
    all_to_all x1, starting transfers between devices, on_device(): lax.all_to_all(outgoing, 'table', split_axis=0, concat_axis=0, tiled=True)  4.3 us
    ppermute x3, waiting for transfers between devices, sum_scatter(): final = final + lax.ppermute(sent, 'table', perm).astype(F32)  4.13 us
    ppermute x3, starting transfers between devices, sum_scatter(): total = total + lax.ppermute(pick_low(k), 'table', perm).astype(F32)  3.55 us
  transfers between devices with their start and end apart: 11, of which 6 were waited for; matrix products, arithmetic and copies ran while one was open for 4% of the time, Pallas kernels for 0%

profile of v1, /device:TPU:0, one launch (start us, length us, event | category | flops | bytes accessed | tf_op | source)
XLA Modules:
  0.0 121.7 jit_solution(15407383219384621286)
XLA Ops:
  0.6 1.7 %shard_map.119 = (s32[16,128]{1,0:T(8,128)}, f32[1,512]{1,0:T(1,128)}) custom-call(s32[1,512]{1,0:T(1,128)} %bitcast.54, s32[1,512]{1,0:T(1,128)} %bitcast.55), custom_call_target="tpu_custom_call" | custom-call | flops 16777216 | bytes 4096 | tf_op jit(solution)/shard_map/pallas_call | solution.py:46
  2.3 15.6 %all_to_all.33 = s32[16,1,128]{2,1,0:T(1,128)} all-to-all(s32[16,1,128]{2,1,0:T(1,128)} %bitcast.53), channel_id=1, replica_groups=mesh['table'=16,'group'=2] {'table'}, dimensions={0} | all-to-all | bytes 16384 | tf_op jit(solution)/shard_map/all_to_all | solution.py:335
  17.9 4.5 %shard_map.120 = (bf16[768,512]{1,0:T(8,128)(2,1)}, f32[1,768]{1,0:T(1,128)}) custom-call(s32[16,128]{1,0:T(8,128)} %bitcast.52, bf16[2048,512]{1,0:T(8,128)(2,1)} %table_ref.1), custom_call_target="tpu_custom_call" | custom-call | flops 1610612736 | bytes 2883584 | tf_op jit(solution)/shard_map/pallas_call | solution.py:46
  22.4 24.3 %all_to_all.34 = bf16[16,48,512]{2,1,0:T(8,128)(2,1)} all-to-all(bf16[16,48,512]{2,1,0:T(8,128)(2,1)} %bitcast.50), channel_id=1, replica_groups=mesh['table'=16,'group'=2] {'table'}, dimensions={0} | all-to-all | bytes 1572864 | tf_op jit(solution)/shard_map/all_to_all | solution.py:346
  46.7 21.4 %shard_map.121 = (bf16[512,512]{1,0:T(8,128)(2,1)}, bf16[768,512]{1,0:T(8,128)(2,1)}, bf16[2,512,1408]{2,1,0:T(8,128)(2,1)}) custom-call(s32[1,8]{1,0:T(1,128)} %len_ref.1, f32[1,512]{1,0:T(1,128)} %get-tuple-element.12.slot_ref, bf16[768,512]{1,0:T(8,128)(2,1)} %bitcast.49, bf16[512,2048]{1,0:T(8,128)(2,1)} %w_in_ref.1, bf16[512,512]{1,0:T(8,128)(2,1)} %w_out_ref.1, ...), custom_call_target="tpu_custom_call" | custom-call | flops 6174015488 | bytes 6291456 | tf_op jit(solution)/shard_map/pallas_call | solution.py:46
  68.1 1.5 %slice_bitcast_fusion = bf16[512,1408]{1,0:T(8,128)(2,1)S(1)} fusion(bf16[2,512,1408]{2,1,0:T(8,128)(2,1)} %get-tuple-element.18), kind=kLoop, calls=%fused_computation.2 | loop fusion | bytes 2883584 | tf_op jit(solution)/shard_map/squeeze | solution.py:394
  69.6 0.1 collective-permute-start.2
  69.7 4.3 %all-to-all-start.2 = ((bf16[16,48,512]{2,1,0:T(8,128)(2,1)}), bf16[16,48,512]{2,1,0:T(8,128)(2,1)}, u32[]{:S(2)}, u32[]{:S(2)}) async-start(bf16[16,48,512]{2,1,0:T(8,128)(2,1)} %bitcast.48), calls=%async_computation.2 | async-start | bytes 1572864 | tf_op jit(solution)/shard_map/all_to_all | solution.py:382
  74.0 0.0 collective-permute-done.2
  74.0 1.7 %fusion = bf16[512,1408]{1,0:T(8,128)(2,1)S(1)} fusion(bf16[512,1408]{1,0:T(8,128)(2,1)S(1)} %collective-permute-done.2, bf16[2,512,1408]{2,1,0:T(8,128)(2,1)} %get-tuple-element.18), kind=kLoop, calls=%fused_computation.1 | loop fusion | flops 2883584 | bytes 4325376 | tf_op jit(solution)/shard_map/convert_element_type | solution.py:396
  75.7 0.1 dynamic-slice_bitcast_fusion.2
  75.9 0.0 copy-start.1
  75.9 1.8 %collective-permute-start.3 = (bf16[4,32,1408]{2,1,0:T(8,128)(2,1)S(1)}, bf16[4,32,1408]{2,1,0:T(8,128)(2,1)S(1)}, u32[]{:S(2)}, u32[]{:S(2)}) collective-permute-start(bf16[4,32,1408]{2,1,0:T(8,128)(2,1)S(1)} %get-tuple-element.21), channel_id=1, source_target_pairs={{0,2},{2,0},{4,6},{6,4},{8,10},{10,8},{12,14},{14,12},{16,18},{18,... | collective-permute-start | bytes 1081352 | tf_op jit(solution)/shard_map/ppermute | solution.py:305
  77.7 1.5 %collective-permute-start.4 = (bf16[4,32,1408]{2,1,0:T(8,128)(2,1)S(1)}, bf16[4,32,1408]{2,1,0:T(8,128)(2,1)S(1)}, u32[]{:S(2)}, u32[]{:S(2)}) collective-permute-start(bf16[4,32,1408]{2,1,0:T(8,128)(2,1)S(1)} %get-tuple-element.23), channel_id=1, source_target_pairs={{0,4},{2,6},{4,0},{6,2},{8,12},{10,14},{12,8},{14,10},{16,20},{18,... | collective-permute-start | bytes 1081352 | tf_op jit(solution)/shard_map/ppermute | solution.py:305
  79.2 0.3 collective-permute-start.5
  79.4 13.2 %collective-permute-done.3 = bf16[4,32,1408]{2,1,0:T(8,128)(2,1)S(1)} collective-permute-done((bf16[4,32,1408]{2,1,0:T(8,128)(2,1)S(1)}, bf16[4,32,1408]{2,1,0:T(8,128)(2,1)S(1)}, u32[]{:S(2)}, u32[]{:S(2)}) %collective-permute-start.3) | collective-permute-done | bytes 360480 | tf_op jit(solution)/shard_map/ppermute | solution.py:305
  92.6 7.7 %collective-permute-done.4 = bf16[4,32,1408]{2,1,0:T(8,128)(2,1)S(1)} collective-permute-done((bf16[4,32,1408]{2,1,0:T(8,128)(2,1)S(1)}, bf16[4,32,1408]{2,1,0:T(8,128)(2,1)S(1)}, u32[]{:S(2)}, u32[]{:S(2)}) %collective-permute-start.4) | collective-permute-done | bytes 360480 | tf_op jit(solution)/shard_map/ppermute | solution.py:305
  100.3 1.6 %collective-permute-done.5 = bf16[4,32,1408]{2,1,0:T(8,128)(2,1)} collective-permute-done((bf16[4,32,1408]{2,1,0:T(8,128)(2,1)S(1)}, bf16[4,32,1408]{2,1,0:T(8,128)(2,1)}, u32[]{:S(2)}, u32[]{:S(2)}) %collective-permute-start.5) | collective-permute-done | bytes 360480 | tf_op jit(solution)/shard_map/ppermute | solution.py:305
  101.9 1.2 fusion.9
  103.1 1.6 %collective-permute-start.6 = (bf16[32,1408]{1,0:T(8,128)(2,1)S(1)}, bf16[32,1408]{1,0:T(8,128)(2,1)S(1)}, u32[]{:S(2)}, u32[]{:S(2)}) collective-permute-start(bf16[32,1408]{1,0:T(8,128)(2,1)S(1)} %get-tuple-element.24), channel_id=1, source_target_pairs={{0,8},{2,10},{4,12},{6,14},{8,16},{10,18},{12,20},{14,22},{16,24},... | collective-permute-start | bytes 270344 | tf_op jit(solution)/shard_map/ppermute | solution.py:311
  104.7 2.4 %collective-permute-start.7 = (bf16[32,1408]{1,0:T(8,128)(2,1)S(1)}, bf16[32,1408]{1,0:T(8,128)(2,1)S(1)}, u32[]{:S(2)}, u32[]{:S(2)}) collective-permute-start(bf16[32,1408]{1,0:T(8,128)(2,1)S(1)} %get-tuple-element.26), channel_id=1, source_target_pairs={{0,16},{2,18},{4,20},{6,22},{8,24},{10,26},{12,28},{14,30},{16,0},... | collective-permute-start | bytes 270344 | tf_op jit(solution)/shard_map/ppermute | solution.py:311
  107.0 1.5 %collective-permute-start.8 = (bf16[32,1408]{1,0:T(8,128)(2,1)S(1)}, bf16[32,1408]{1,0:T(8,128)(2,1)S(1)}, u32[]{:S(2)}, u32[]{:S(2)}) collective-permute-start(bf16[32,1408]{1,0:T(8,128)(2,1)S(1)} %get-tuple-element.25), channel_id=1, source_target_pairs={{0,24},{2,26},{4,28},{6,30},{8,0},{10,2},{12,4},{14,6},{16,8},{18,... | collective-permute-start | bytes 270344 | tf_op jit(solution)/shard_map/ppermute | solution.py:311
  108.5 0.0 copy-done.1
  108.5 0.0 collective-permute-start
  108.5 0.0 all-to-all-done.2
  108.5 0.5 collective-permute-start.1
  109.0 1.5 %collective-permute-done.6 = bf16[32,1408]{1,0:T(8,128)(2,1)S(1)} collective-permute-done((bf16[32,1408]{1,0:T(8,128)(2,1)S(1)}, bf16[32,1408]{1,0:T(8,128)(2,1)S(1)}, u32[]{:S(2)}, u32[]{:S(2)}) %collective-permute-start.6) | collective-permute-done | bytes 90144 | tf_op jit(solution)/shard_map/ppermute | solution.py:311
  110.5 2.5 %collective-permute-done.7 = bf16[32,1408]{1,0:T(8,128)(2,1)S(1)} collective-permute-done((bf16[32,1408]{1,0:T(8,128)(2,1)S(1)}, bf16[32,1408]{1,0:T(8,128)(2,1)S(1)}, u32[]{:S(2)}, u32[]{:S(2)}) %collective-permute-start.7) | collective-permute-done | bytes 90144 | tf_op jit(solution)/shard_map/ppermute | solution.py:311
  113.1 0.1 collective-permute-done.8
  113.2 0.1 collective-permute-start.9
  113.3 0.6 slice_reduce_fusion
  113.9 0.7 slice.20
  114.6 0.0 collective-permute-done.9
  114.6 0.6 pad_maximum_fusion
  115.3 0.0 collective-permute-done.refs_1_
  115.3 0.0 copy-start.2
  115.3 0.0 collective-permute-done.1.refs_3_
  115.3 0.6 copy-done.2
  115.9 0.0 copy-start
  115.9 0.9 copy-done
  116.8 5.0 %shard_map.122 = f32[1024,512]{1,0:T(8,128)} custom-call(f32[1,768]{1,0:T(1,128)} %get-tuple-element.16.refs_0_, f32[1,768]{1,0:T(1,128)} %copy-done.2, bf16[768,512]{1,0:T(8,128)(2,1)} %bitcast.9.refs_2_, bf16[768,512]{1,0:T(8,128)(2,1)} %copy-done), custom_call_target="tpu_custom_call" | custom-call | flops 1610612736 | bytes 3670016 | tf_op jit(solution)/shard_map/pallas_call | solution.py:46
  (4 shorter events, 0.1 us)
Async XLA Ops:
  69.6 4.4 %collective-permute-start.2 = (bf16[512,1408]{1,0:T(8,128)(2,1)S(1)}, bf16[512,1408]{1,0:T(8,128)(2,1)S(1)}, u32[]{:S(2)}, u32[]{:S(2)}) collective-permute-start(bf16[512,1408]{1,0:T(8,128)(2,1)S(1)} %slice_bitcast_fusion), channel_id=1, source_target_pairs={{0,1},{1,0},{2,3},{3,2},{4,5},{5,4},{6,7},{7,6},{8,9},{9,8},{10,11... | collective-permute-start | bytes 4325384 | tf_op jit(solution)/shard_map/ppermute | solution.py:288
  69.7 38.8 %all-to-all-start.2 = ((bf16[16,48,512]{2,1,0:T(8,128)(2,1)}), bf16[16,48,512]{2,1,0:T(8,128)(2,1)}, u32[]{:S(2)}, u32[]{:S(2)}) async-start(bf16[16,48,512]{2,1,0:T(8,128)(2,1)} %bitcast.48), calls=%async_computation.2 | async-start | bytes 1572864 | tf_op jit(solution)/shard_map/all_to_all | solution.py:382
  75.9 32.7 %copy-start.1 = (f32[1,768]{1,0:T(1,128)S(1)}, f32[1,768]{1,0:T(1,128)}, u32[]{:S(2)}) copy-start(f32[1,768]{1,0:T(1,128)} %get-tuple-element.16.refs_0_) | copy-start | bytes 9220
  75.9 16.8 %collective-permute-start.3 = (bf16[4,32,1408]{2,1,0:T(8,128)(2,1)S(1)}, bf16[4,32,1408]{2,1,0:T(8,128)(2,1)S(1)}, u32[]{:S(2)}, u32[]{:S(2)}) collective-permute-start(bf16[4,32,1408]{2,1,0:T(8,128)(2,1)S(1)} %get-tuple-element.21), channel_id=1, source_target_pairs={{0,2},{2,0},{4,6},{6,4},{8,10},{10,8},{12,14},{14,12},{16,18},{18,... | collective-permute-start | bytes 1081352 | tf_op jit(solution)/shard_map/ppermute | solution.py:305
  77.7 22.6 %collective-permute-start.4 = (bf16[4,32,1408]{2,1,0:T(8,128)(2,1)S(1)}, bf16[4,32,1408]{2,1,0:T(8,128)(2,1)S(1)}, u32[]{:S(2)}, u32[]{:S(2)}) collective-permute-start(bf16[4,32,1408]{2,1,0:T(8,128)(2,1)S(1)} %get-tuple-element.23), channel_id=1, source_target_pairs={{0,4},{2,6},{4,0},{6,2},{8,12},{10,14},{12,8},{14,10},{16,20},{18,... | collective-permute-start | bytes 1081352 | tf_op jit(solution)/shard_map/ppermute | solution.py:305
  79.2 22.7 %collective-permute-start.5 = (bf16[4,32,1408]{2,1,0:T(8,128)(2,1)S(1)}, bf16[4,32,1408]{2,1,0:T(8,128)(2,1)}, u32[]{:S(2)}, u32[]{:S(2)}) collective-permute-start(bf16[4,32,1408]{2,1,0:T(8,128)(2,1)S(1)} %get-tuple-element.22), channel_id=1, source_target_pairs={{0,6},{2,4},{4,2},{6,0},{8,14},{10,12},{12,10},{14,8},{16,22},{18,... | collective-permute-start | bytes 1081352 | tf_op jit(solution)/shard_map/ppermute | solution.py:305
  103.1 7.4 %collective-permute-start.6 = (bf16[32,1408]{1,0:T(8,128)(2,1)S(1)}, bf16[32,1408]{1,0:T(8,128)(2,1)S(1)}, u32[]{:S(2)}, u32[]{:S(2)}) collective-permute-start(bf16[32,1408]{1,0:T(8,128)(2,1)S(1)} %get-tuple-element.24), channel_id=1, source_target_pairs={{0,8},{2,10},{4,12},{6,14},{8,16},{10,18},{12,20},{14,22},{16,24},... | collective-permute-start | bytes 270344 | tf_op jit(solution)/shard_map/ppermute | solution.py:311
  104.7 8.4 %collective-permute-start.7 = (bf16[32,1408]{1,0:T(8,128)(2,1)S(1)}, bf16[32,1408]{1,0:T(8,128)(2,1)S(1)}, u32[]{:S(2)}, u32[]{:S(2)}) collective-permute-start(bf16[32,1408]{1,0:T(8,128)(2,1)S(1)} %get-tuple-element.26), channel_id=1, source_target_pairs={{0,16},{2,18},{4,20},{6,22},{8,24},{10,26},{12,28},{14,30},{16,0},... | collective-permute-start | bytes 270344 | tf_op jit(solution)/shard_map/ppermute | solution.py:311
  107.0 6.1 %collective-permute-start.8 = (bf16[32,1408]{1,0:T(8,128)(2,1)S(1)}, bf16[32,1408]{1,0:T(8,128)(2,1)S(1)}, u32[]{:S(2)}, u32[]{:S(2)}) collective-permute-start(bf16[32,1408]{1,0:T(8,128)(2,1)S(1)} %get-tuple-element.25), channel_id=1, source_target_pairs={{0,24},{2,26},{4,28},{6,30},{8,0},{10,2},{12,4},{14,6},{16,8},{18,... | collective-permute-start | bytes 270344 | tf_op jit(solution)/shard_map/ppermute | solution.py:311
  108.5 6.7 %collective-permute-start = (f32[1,768]{1,0:T(1,128)S(1)}, f32[1,768]{1,0:T(1,128)S(1)}, u32[]{:S(2)}, u32[]{:S(2)}) collective-permute-start(f32[1,768]{1,0:T(1,128)S(1)} %copy-done.1), channel_id=1, source_target_pairs={{0,1},{1,0},{2,3},{3,2},{4,5},{5,4},{6,7},{7,6},{8,9},{9,8},{10,11... | collective-permute-start | bytes 9224 | tf_op jit(solution)/shard_map/ppermute | solution.py:288
  108.5 6.7 %collective-permute-start.1 = (bf16[768,512]{1,0:T(8,128)(2,1)}, bf16[768,512]{1,0:T(8,128)(2,1)S(1)}, u32[]{:S(2)}, u32[]{:S(2)}) collective-permute-start(bf16[768,512]{1,0:T(8,128)(2,1)} %bitcast.9.refs_2_), channel_id=1, source_target_pairs={{0,1},{1,0},{2,3},{3,2},{4,5},{5,4},{6,7},{7,6},{8,9},{9,8},{10,11... | collective-permute-start | bytes 2359304 | tf_op jit(solution)/shard_map/ppermute | solution.py:288
  113.2 1.4 %collective-permute-start.9 = (f32[32,256]{1,0:T(8,128)S(1)}, f32[32,256]{1,0:T(8,128)S(1)}, u32[]{:S(2)}, u32[]{:S(2)}) collective-permute-start(f32[32,256]{1,0:T(8,128)S(1)} %get-tuple-element.27), channel_id=1, source_target_pairs={{0,1},{1,0},{2,3},{3,2},{4,5},{5,4},{6,7},{7,6},{8,9},{9,8},{10,11... | collective-permute-start | bytes 98312 | tf_op jit(solution)/shard_map/ppermute | solution.py:288
  115.3 0.6 copy-start.2
  115.9 0.9 copy-start

commit v2 on v1

--- a/solution.py
+++ b/solution.py
@@ -12,7 +12,6 @@
 HEAD_DIM = 64
 LANES = 128
 QUERY_ROWS = 256
-VMEM_LIMIT = 56 * 1024 * 1024
 
 F32 = jnp.float32
 BF16 = jnp.bfloat16
@@ -38,18 +37,23 @@
     return lax.dot_general(a, b, (((0,), (0,)), ((), ())), preferred_element_type=F32)
 
 
-def call(kernel, out_shape, flops, nbytes, operands, smem=(), scratch=()):
-    specs = [
-        pl.BlockSpec(memory_space=pltpu.SMEM if i in smem else pltpu.VMEM)
+def row_step(rows):
+    return 256 if rows % 256 == 0 else rows
+
+
+def call(kernel, out_shape, flops, nbytes, operands, smem=(), far=(), far_out=(), limit=20, scratch=()):
+    spaces = [
+        pltpu.SMEM if i in smem else pl.ANY if i in far else pltpu.VMEM
         for i in range(len(operands))
     ]
+    out_spaces = [pl.ANY if i in far_out else pltpu.VMEM for i in range(len(out_shape))]
     return pl.pallas_call(
         kernel,
         out_shape=out_shape,
-        in_specs=specs,
-        out_specs=jax.tree.map(lambda _: pl.BlockSpec(memory_space=pltpu.VMEM), out_shape),
+        in_specs=[pl.BlockSpec(memory_space=space) for space in spaces],
+        out_specs=[pl.BlockSpec(memory_space=space) for space in out_spaces],
         scratch_shapes=scratch,
-        compiler_params=pltpu.CompilerParams(vmem_limit_bytes=VMEM_LIMIT),
+        compiler_params=pltpu.CompilerParams(vmem_limit_bytes=limit * 1024 * 1024),
         cost_estimate=pl.CostEstimate(flops=flops, bytes_accessed=nbytes, transcendentals=0),
     )(*operands)
 
@@ -72,10 +76,12 @@
     req_ref[...] = found.astype(jnp.int32)
 
 
-def lookup_kernel(cap, wanted_ref, table_ref, found_ref, ids_ref):
+def lookup_kernel(cap, wanted_ref, table_hbm, found_hbm, ids_ref, table_ref, found_ref, sems):
     owners, width = wanted_ref.shape
     slots = found_ref.shape[0]
     rows = table_ref.shape[0]
+    fetch = pltpu.make_async_copy(table_hbm, table_ref, sems.at[0])
+    fetch.start()
     wanted = wanted_ref[...]
     high = (wanted >> 8).astype(F32).astype(BF16)
     low = (wanted & 255).astype(F32).astype(BF16)
@@ -90,31 +96,52 @@
     )
     wide = jnp.broadcast_to(ids, (slots, LANES))
     ids_ref[...] = wide.T[0:1, :]
-    step = 256 if slots % 256 == 0 else slots
-    for start in range(0, slots, step):
+    step = row_step(slots)
+    fetch.wait()
+    stores = []
+    for n, start in enumerate(range(0, slots, step)):
         part = ids[start : start + step]
         pick = hot(iota((step, rows), 1).astype(F32) == part)
         found_ref[start : start + step, :] = dot_nn(pick, table_ref[...]).astype(BF16)
+        here = pl.ds(start, step)
+        stores.append(
+            pltpu.make_async_copy(found_ref.at[here], found_hbm.at[here], sems.at[1 + n])
+        )
+        stores[-1].start()
+    for store in stores:
+        store.wait()
 
 
 def collect_kernel(groups, *refs):
-    ids_refs, in_refs, out_ref = refs[:groups], refs[groups : 2 * groups], refs[-1]
+    ids_refs, in_hbms, out_hbm = refs[:groups], refs[groups : 2 * groups], refs[2 * groups]
+    in_refs, out_ref, sems = refs[2 * groups + 1 : 3 * groups + 1], refs[-2], refs[-1]
     rows = out_ref.shape[0]
     slots = in_refs[0].shape[0]
+    fetches = [
+        pltpu.make_async_copy(hbm, ref, sems.at[n])
+        for n, (hbm, ref) in enumerate(zip(in_hbms, in_refs))
+    ]
+    for fetch in fetches:
+        fetch.start()
     base = lax.axis_index("group") * rows
-    step = 256 if rows % 256 == 0 else rows
-
-    def chunk(i, _):
-        start = pl.multiple_of(i * step, step)
+    step = row_step(rows)
+    for fetch in fetches:
+        fetch.wait()
+    stores = []
+    for n, start in enumerate(range(0, rows, step)):
         own = (iota((step, slots), 0) + (base + start)).astype(F32)
         total = None
         for ids_ref, in_ref in zip(ids_refs, in_refs):
             part = dot_nn(hot(own == ids_ref[...]), in_ref[...])
             total = part if total is None else total + part
-        out_ref[pl.ds(start, step), :] = total
-        return 0
-
-    lax.fori_loop(0, rows // step, chunk, 0)
+        out_ref[start : start + step, :] = total
+        here = pl.ds(start, step)
+        stores.append(
+            pltpu.make_async_copy(out_ref.at[here], out_hbm.at[here], sems.at[groups + n])
+        )
+        stores[-1].start()
+    for store in stores:
+        store.wait()
 
 
 def layer_kernel(
@@ -123,13 +150,21 @@
     len_ref,
     slot_ref,
     ret_ref,
+    w_in_hbm,
+    w_out_hbm,
+    gain_ref,
+    cot_hbm,
+    *rest,
+):
+    result_hbm, gpre_hbm = rest[:2]
+    grads_hbms = rest[2 : 2 + groups]
+    (
     w_in_ref,
     w_out_ref,
-    gain_ref,
     cot_ref,
     result_ref,
-    outgoing_ref,
     grads_ref,
+    pick_ref,
     emb_ref,
     proj_ref,
     slope_ref,
@@ -143,7 +178,8 @@
     gval_ref,
     gkey_ref,
     gwo_ref,
-):
+    sems,
+    ) = rest[2 + groups :]
     count, width = cot_ref.shape
     slots = ret_ref.shape[0]
     per = LANES // HEAD_DIM
@@ -151,13 +187,19 @@
     qrows = QUERY_ROWS if count % QUERY_ROWS == 0 else count
     half_scale = 0.5 / math.sqrt(HEAD_DIM)
 
+    get_in = pltpu.make_async_copy(w_in_hbm, w_in_ref, sems.at[0])
+    get_cot = pltpu.make_async_copy(cot_hbm, cot_ref, sems.at[1])
+    get_out = pltpu.make_async_copy(w_out_hbm, w_out_ref, sems.at[2])
+    for fetch in (get_in, get_cot, get_out):
+        fetch.start()
+
     slot = jnp.broadcast_to(slot_ref[...], (LANES, count)).T
-    emb = None
     for start in range(0, slots, LANES):
-        pick = hot(slot == (iota((count, LANES), 1) + start).astype(F32))
-        part = dot_nn(pick, ret_ref[start : start + LANES, :])
-        emb = part if emb is None else emb + part
-    emb_ref[...] = emb.astype(BF16)
+        pick_ref[:, start : start + LANES] = hot(
+            slot == (iota((count, LANES), 1) + start).astype(F32)
+        )
+    emb_ref[...] = dot_nn(pick_ref[...], ret_ref[...]).astype(BF16)
+    get_in.wait()
 
     def project(i, _):
         cols = pl.ds(pl.multiple_of(i * width, width), width)
@@ -209,6 +251,8 @@
 
     lax.fori_loop(0, slabs, forward, 0)
 
+    get_cot.wait()
+    get_out.wait()
     gain = gain_ref[...]
     gain_sum = jnp.zeros((1, width), F32)
     for r0 in range(0, count, qrows):
@@ -231,6 +275,8 @@
         mean1 = jnp.mean(gnorm, 1, keepdims=True)
         mean2 = jnp.mean(gnorm * normed, 1, keepdims=True)
         gatt_ref[rows, :] = ((gnorm - mean1 - normed * mean2) * inv).astype(BF16)
+    put_result = pltpu.make_async_copy(result_ref, result_hbm, sems.at[3])
+    put_result.start()
     gwo_ref[...] = dot_tn(mixed_ref[...], cot_ref[...]).astype(BF16)
 
     def backward(p, _):
@@ -262,11 +308,8 @@
 
     lax.fori_loop(0, slabs, backward, 0)
 
-    gemb = (cot_ref[...].astype(F32) + dot_nt(gpre_ref[...], w_in_ref[...])).astype(BF16)
-    for start in range(0, slots, 256):
-        stop = min(start + 256, slots)
-        put = hot((iota((stop - start, count), 0) + start).astype(F32) == slot_ref[...])
-        outgoing_ref[start:stop, :] = dot_nn(put, gemb).astype(BF16)
+    put_gpre = pltpu.make_async_copy(gpre_ref, gpre_hbm, sems.at[4])
+    put_gpre.start()
 
     me = lax.axis_index("group")
     emb_t = emb_ref[...].T
@@ -274,7 +317,8 @@
     cols_out = width // wparts
     chunk = min(cols_in, 512)
     gain_col = jnp.broadcast_to(gain_sum, (LANES, width)).T.astype(BF16)
-    for k in range(groups):
+    puts = [put_result, put_gpre]
+    for k in [*range(1, groups), 0]:
         part = lax.rem(me + k, groups)
         for c in range(0, cols_in, chunk):
             cols = pl.ds(pl.multiple_of(part * cols_in + c, LANES), chunk)
@@ -282,34 +326,47 @@
         cols = pl.ds(pl.multiple_of(lax.rem(part, wparts) * cols_out, LANES), cols_out)
         grads_ref[k, :, cols_in : cols_in + cols_out] = gwo_ref[:, cols]
         grads_ref[k, :, cols_in + cols_out :] = gain_col
+        put = pltpu.make_async_copy(grads_ref.at[k], grads_hbms[k], sems.at[5 + k])
+        put.start()
+        puts.append(put)
+    for put in puts:
+        put.wait()
+
+
+def rows_kernel(slot_ref, gpre_hbm, w_in_hbm, cot_ref, out_hbm, gpre_ref, w_in_ref, out_ref, sems):
+    count, width = cot_ref.shape
+    slots = out_ref.shape[0]
+    fetches = []
+    for i in range(4):
+        cols = pl.ds(i * width, width)
+        pair = (
+            pltpu.make_async_copy(gpre_hbm.at[:, cols], gpre_ref.at[:, cols], sems.at[2 * i]),
+            pltpu.make_async_copy(w_in_hbm.at[:, cols], w_in_ref.at[:, cols], sems.at[2 * i + 1]),
+        )
+        for fetch in pair:
+            fetch.start()
+        fetches.append(pair)
+    total = cot_ref[...].astype(F32)
+    for i in range(4):
+        for fetch in fetches[i]:
+            fetch.wait()
+        cols = slice(i * width, (i + 1) * width)
+        total = total + dot_nt(gpre_ref[:, cols], w_in_ref[:, cols])
+    gemb = total.astype(BF16)
+    step = row_step(slots)
+    stores = []
+    for n, start in enumerate(range(0, slots, step)):
+        put = hot((iota((step, count), 0) + start).astype(F32) == slot_ref[...])
+        out_ref[start : start + step, :] = dot_nn(put, gemb).astype(BF16)
+        here = pl.ds(start, step)
+        stores.append(pltpu.make_async_copy(out_ref.at[here], out_hbm.at[here], sems.at[8 + n]))
+        stores[-1].start()
+    for store in stores:
+        store.wait()
 
 
 def shift(value, axis, size, amount):
     return lax.ppermute(value, axis, [(i, (i + amount) % size) for i in range(size)])
-
-
-def sum_scatter(value, owners):
-    inner = 4 if owners % 4 == 0 else 1
-    outer = owners // inner
-    me = lax.axis_index("table")
-    high, low = me // inner, me % inner
-    rows, cols = value.shape[1:]
-    value = value.reshape(outer, inner, rows, cols)
-
-    def pick_low(k):
-        return lax.dynamic_index_in_dim(value, low ^ k, 1, keepdims=False)
-
-    total = pick_low(0).astype(F32)
-    for k in range(1, inner):
-        perm = [(i, i // inner * inner + ((i % inner) ^ k)) for i in range(owners)]
-        total = total + lax.ppermute(pick_low(k), "table", perm).astype(F32)
-    part = total.astype(BF16)
-    final = lax.dynamic_index_in_dim(total, high, 0, keepdims=False)
-    for k in range(1, outer):
-        perm = [(i, ((i // inner + k) % outer) * inner + i % inner) for i in range(owners)]
-        sent = lax.dynamic_index_in_dim(part, (high + k) % outer, 0, keepdims=False)
-        final = final + lax.ppermute(sent, "table", perm).astype(F32)
-    return final
 
 
 def on_device(item_owner, item_row, lengths, table, w_in, w_out, gain, cotangent):
@@ -324,10 +381,10 @@
 
     requested, slot = call(
         functools.partial(request_kernel, capacity),
-        (
+        [
             jax.ShapeDtypeStruct((owners, padded), jnp.int32),
             jax.ShapeDtypeStruct((1, count), F32),
-        ),
+        ],
         4 * count * count * owners,
         8 * count,
         (item_owner.reshape(1, count), item_row.reshape(1, count)),
@@ -335,34 +392,51 @@
     wanted = lax.all_to_all(requested, "table", split_axis=0, concat_axis=0, tiled=True)
     found, ids = call(
         functools.partial(lookup_kernel, capacity),
-        (
+        [
             jax.ShapeDtypeStruct((slots, width), BF16),
             jax.ShapeDtypeStruct((1, slots), F32),
-        ),
+        ],
         2 * slots * table.shape[0] * width,
         2 * (slots + table.shape[0]) * width,
         (wanted, table),
+        far=(1,),
+        far_out=(0,),
+        scratch=[
+            pltpu.VMEM(table.shape, BF16),
+            pltpu.VMEM((slots, width), BF16),
+            pltpu.SemaphoreType.DMA((1 + slots // row_step(slots),)),
+        ],
     )
     returned = lax.all_to_all(found, "table", split_axis=0, concat_axis=0, tiled=True)
     all_ids = [ids] + [shift(ids, "group", groups, k) for k in range(1, groups)]
+    returned, *all_ids = lax.optimization_barrier((returned, *all_ids))
 
     wparts = min(groups, width // LANES)
     cols_in = 4 * width // groups
     cols_out = width // wparts
     cols_all = cols_in + cols_out + LANES
     square = pltpu.VMEM((count, width), BF16)
-    result, outgoing, grads = call(
+    result, gpre, *grads = call(
         functools.partial(layer_kernel, groups, wparts),
-        (
+        [
             jax.ShapeDtypeStruct((count, width), BF16),
-            jax.ShapeDtypeStruct((slots, width), BF16),
-            jax.ShapeDtypeStruct((groups, width, cols_all), BF16),
-        ),
-        32 * count * width * width + 14 * count * count * width,
+            jax.ShapeDtypeStruct((count, 4 * width), BF16),
+            *[jax.ShapeDtypeStruct((width, cols_all), BF16) for _ in range(groups)],
+        ],
+        24 * count * width * width + 14 * count * count * width,
         24 * count * width,
         (lengths, slot, returned, w_in, w_out, gain.reshape(1, width), cotangent),
         smem=(0,),
+        far=(3, 4, 6),
+        far_out=range(2 + groups),
+        limit=44,
         scratch=[
+            pltpu.VMEM(w_in.shape, BF16),
+            pltpu.VMEM(w_out.shape, BF16),
+            square,
+            square,
+            pltpu.VMEM((groups, width, cols_all), BF16),
+            pltpu.VMEM((count, slots), BF16),
             square,
             pltpu.VMEM((4, count, width), BF16),
             pltpu.VMEM((4, count, width), F32),
@@ -376,24 +450,67 @@
             pltpu.VMEM((count, LANES), F32),
             pltpu.VMEM((count, LANES), F32),
             pltpu.VMEM((width, width), BF16),
-        ],
-    )
-
-    incoming = lax.all_to_all(outgoing, "table", split_axis=0, concat_axis=0, tiled=True)
-    all_incoming = [incoming] + [shift(incoming, "group", groups, k) for k in range(1, groups)]
-    table_grad = call(
-        functools.partial(collect_kernel, groups),
-        jax.ShapeDtypeStruct((table.shape[0] // groups, width), F32),
-        2 * slots * table.shape[0] * width,
-        2 * groups * slots * width + 4 * table.shape[0] // groups * width,
-        (*all_ids, *all_incoming),
-    )
-
+            pltpu.SemaphoreType.DMA((5 + groups,)),
+        ],
+    )
+    (outgoing,) = call(
+        rows_kernel,
+        [jax.ShapeDtypeStruct((slots, width), BF16)],
+        8 * count * width * width + 2 * slots * count * width,
+        20 * count * width,
+        (slot, gpre, w_in, cotangent),
+        far=(1, 2),
+        far_out=(0,),
+        scratch=[
+            pltpu.VMEM((count, 4 * width), BF16),
+            pltpu.VMEM(w_in.shape, BF16),
+            pltpu.VMEM((slots, width), BF16),
+            pltpu.SemaphoreType.DMA((8 + slots // row_step(slots),)),
+        ],
+    )
+
+    rows = width // owners
+    inner = 4 if owners % 4 == 0 else 1
+    outer = owners // inner
+    here = lax.axis_index("table")
+    high, low = here // inner, here % inner
     chip = grads[0].astype(F32)
     for k in range(1, groups):
         chip = chip + shift(grads[k], "group", groups, k).astype(F32)
-    rows = width // owners
-    summed = sum_scatter(chip.astype(BF16).reshape(owners, rows, cols_all), owners)
+    chip = chip.astype(BF16).reshape(outer, inner, rows, cols_all)
+    planes = [
+        lax.dynamic_index_in_dim(chip, low ^ k, 1, keepdims=False) for k in range(inner)
+    ]
+    outgoing, *planes = lax.optimization_barrier((outgoing, *planes))
+    total = planes[0].astype(F32)
+    for k in range(1, inner):
+        perm = [(i, i // inner * inner + ((i % inner) ^ k)) for i in range(owners)]
+        total = total + lax.ppermute(planes[k], "table", perm).astype(F32)
+    part = total.astype(BF16)
+    summed = lax.dynamic_index_in_dim(part, high, 0, keepdims=False).astype(F32)
+    for k in range(1, outer):
+        perm = [(i, ((i // inner + k) % outer) * inner + i % inner) for i in range(owners)]
+        sent = lax.dynamic_index_in_dim(part, (high + k) % outer, 0, keepdims=False)
+        summed = summed + lax.ppermute(sent, "table", perm).astype(F32)
+
+    incoming = lax.all_to_all(outgoing, "table", split_axis=0, concat_axis=0, tiled=True)
+    all_incoming = [incoming] + [shift(incoming, "group", groups, k) for k in range(1, groups)]
+    grad_rows = table.shape[0] // groups
+    (table_grad,) = call(
+        functools.partial(collect_kernel, groups),
+        [jax.ShapeDtypeStruct((grad_rows, width), F32)],
+        2 * slots * table.shape[0] * width,
+        2 * groups * slots * width + 4 * grad_rows * width,
+        (*all_ids, *all_incoming),
+        far=range(groups, 2 * groups),
+        far_out=(0,),
+        scratch=[
+            *[pltpu.VMEM((slots, width), BF16) for _ in range(groups)],
+            pltpu.VMEM((grad_rows, width), F32),
+            pltpu.SemaphoreType.DMA((groups + grad_rows // row_step(grad_rows),)),
+        ],
+    )
+
     w_in_grad = summed[:, :cols_in]
     mine = summed[:, cols_in : cols_in + cols_out]
     pieces = jnp.stack([mine] + [shift(mine, "group", groups, k) for k in range(1, groups)])

time: 122 us -> 126 us (1.033)
  blocking collectives: 39.9 us -> 15.4 us
  waiting for transfers between devices: 26.6 us -> 49.2 us
  local copies, waits for them, and re-layouts: 4.41 us -> 14 us
  Pallas kernels: 32.6 us -> 26.7 us
  starting transfers between devices: 13.9 us -> 17 us
    all_to_all x1 -> x0, blocking collectives: 24.3 us -> none  [on_device(): lax.all_to_all(found, 'table', split_axis=0, concat_axis=0, tiled=True)]
    all_to_all x0 -> x1, waiting for transfers between devices: none -> 17.3 us  [on_device(): lax.all_to_all(found, 'table', split_axis=0, concat_axis=0, tiled=True)]
    unnamed x6 -> x28, local copies, waits for them, and re-layouts: 1.48 us -> 12.5 us
    pallas_call x4 -> x5, Pallas kernels: 32.6 us -> 26.7 us  [call(): pl.pallas_call(kernel, out_shape=out_shape, in_specs=[pl.BlockSpec(memory...]
    ppermute x6, waiting for transfers between devices: 26.6 us -> 30.6 us  [the longest x3 24.3 us: on_device(): total = total + lax.ppermute(planes[k], 'table', perm).astype(F32)]
    all_to_all x0 -> x1, starting transfers between devices: none -> 3.61 us  [on_device(): lax.all_to_all(found, 'table', split_axis=0, concat_axis=0, tiled=True)]
    squeeze x3 -> x2, local copies, waits for them, and re-layouts: 1.64 us -> 0.23 us  [the longest x1 0.19 us: on_device(): lax.dynamic_index_in_dim(chip, low ^ k, 1, keepdims=False)]
  transfers between devices with their start and end apart: 11 -> 12, of which waited for: 6 -> 7; matrix products, arithmetic and copies ran while one was open for 4% -> 2% of each run, Pallas kernels for 0% -> 3%
where the time goes in v2:
time: 126 us
  waiting for transfers between devices  49.2 us (39%)
  Pallas kernels  26.7 us (21%)
  starting transfers between devices  17 us (13%)
  blocking collectives  15.4 us (12%)
  local copies, waits for them, and re-layouts  14 us (11%)
  other arithmetic  2.58 us (2%)
    pallas_call x5, Pallas kernels, call(): pl.pallas_call(kernel, out_shape=out_shape, in_specs=[pl.BlockSpec(memory...  26.7 us
    ppermute x3, waiting for transfers between devices, on_device(): total = total + lax.ppermute(planes[k], 'table', perm).astype(F32)  24.3 us
    all_to_all x1, waiting for transfers between devices, on_device(): lax.all_to_all(found, 'table', split_axis=0, concat_axis=0, tiled=True)  17.3 us
    all_to_all x1, blocking collectives, on_device(): lax.all_to_all(requested, 'table', split_axis=0, concat_axis=0, tiled=True)  15.4 us
    unnamed x28, local copies, waits for them, and re-layouts  12.5 us
    ppermute x3, waiting for transfers between devices, on_device(): summed = summed + lax.ppermute(sent, 'table', perm).astype(F32)  6.36 us
    all_to_all x1, starting transfers between devices, on_device(): lax.all_to_all(outgoing, 'table', split_axis=0, concat_axis=0, tiled=True)  4.84 us
    ppermute x3, starting transfers between devices, on_device(): summed = summed + lax.ppermute(sent, 'table', perm).astype(F32)  4.81 us
  transfers between devices with their start and end apart: 12, of which 7 were waited for; matrix products, arithmetic and copies ran while one was open for 2% of the time, Pallas kernels for 3%

profile of v2, /device:TPU:0, one launch (start us, length us, event | category | flops | bytes accessed | tf_op | source)
XLA Modules:
  0.0 125.7 jit_solution(4455957703169569113)
XLA Ops:
  0.6 0.0 copy-start.10
  0.6 0.7 copy-done.10
  1.3 0.0 copy-start.11
  1.3 0.7 copy-done.11
  2.0 0.3 shard_map.119
  2.3 15.4 %all_to_all.34 = s32[16,1,128]{2,1,0:T(1,128)S(1)} all-to-all(s32[16,1,128]{2,1,0:T(1,128)S(1)} %bitcast.41), channel_id=1, replica_groups=mesh['table'=16,'group'=2] {'table'}, dimensions={0} | all-to-all | bytes 16384 | tf_op jit(solution)/shard_map/all_to_all | solution.py:392
  17.7 0.0 copy-start.8
  17.7 1.6 %copy-done.8 = bf16[2048,512]{1,0:T(8,128)(2,1)S(1)} copy-done((bf16[2048,512]{1,0:T(8,128)(2,1)S(1)}, bf16[2048,512]{1,0:T(8,128)(2,1)}, u32[]{:S(2)}) %copy-start.8) | copy-done | bytes 2097176
  19.3 0.0 copy-start
  19.3 2.8 %shard_map.120 = (bf16[768,512]{1,0:T(8,128)(2,1)S(1)}, f32[1,768]{1,0:T(1,128)S(1)}) custom-call(s32[16,128]{1,0:T(8,128)S(1)} %bitcast.40, bf16[2048,512]{1,0:T(8,128)(2,1)S(1)} %copy-done.8), custom_call_target="tpu_custom_call" | custom-call | flops 1610612736 | bytes 2883584 | tf_op jit(solution)/shard_map/pallas_call | solution.py:50
  22.1 0.0 copy-start.5
  22.1 0.0 copy-start.12
  22.1 0.9 copy-done.5
  23.0 3.6 %all-to-all-start.1 = ((bf16[16,48,512]{2,1,0:T(8,128)(2,1)}), bf16[16,48,512]{2,1,0:T(8,128)(2,1)S(1)}, u32[]{:S(2)}, u32[]{:S(2)}) async-start(bf16[16,48,512]{2,1,0:T(8,128)(2,1)} %bitcast.39), calls=%async_computation.1 | async-start | bytes 1572864 | tf_op jit(solution)/shard_map/all_to_all | solution.py:410
  26.6 0.1 collective-permute-start
  26.7 1.1 collective-permute-done.refs_1_
  27.8 17.3 %all-to-all-done.1 = bf16[16,48,512]{2,1,0:T(8,128)(2,1)S(1)} async-done(((bf16[16,48,512]{2,1,0:T(8,128)(2,1)}), bf16[16,48,512]{2,1,0:T(8,128)(2,1)S(1)}, u32[]{:S(2)}, u32[]{:S(2)}) %all-to-all-start.1) | async-done | bytes 786464 | tf_op jit(solution)/shard_map/all_to_all | solution.py:410
  45.2 0.0 copy-start.3
  45.2 0.9 copy-done.3
  46.1 0.0 copy-done
  46.1 0.0 copy-done.12
  46.1 0.0 copy-start.4
  46.1 1.1 copy-done.4
  47.2 0.0 copy-start.6
  47.2 1.0 copy-done.6
  48.2 0.0 copy-start.9
  48.3 1.0 copy-done.9
  49.3 0.0 copy-start.13
  49.3 0.7 copy-done.13
  49.9 17.5 %shard_map.121 = (bf16[512,512]{1,0:T(8,128)(2,1)}, bf16[512,2048]{1,0:T(8,128)(2,1)S(1)}, bf16[512,1408]{1,0:T(8,128)(2,1)S(1)}, bf16[512,1408]{1,0:T(8,128)(2,1)}) custom-call(s32[1,8]{1,0:T(1,128)S(1)} %copy-done.13, f32[1,512]{1,0:T(1,128)S(1)} %get-tuple-element.21.slot_ref, bf16[768,512]{1,0:T(8,128)(2,1)S(1)} %bitcast.38, ...), custom_call_target="tpu_custom_call" | custom-call | flops 5100273664 | bytes 6291456 | tf_op jit(solution)/shard_map/pallas_call | solution.py:50
  67.5 0.0 copy-start.1
  67.5 1.3 %copy-done.1 = bf16[512,2048]{1,0:T(8,128)(2,1)} copy-done((bf16[512,2048]{1,0:T(8,128)(2,1)}, bf16[512,2048]{1,0:T(8,128)(2,1)S(1)}, u32[]{:S(2)}) %copy-start.1) | copy-done | bytes 2097176
  68.8 0.0 collective-permute-start.1
  68.8 0.0 copy-start.2
  68.8 1.6 %copy-done.2 = bf16[512,2048]{1,0:T(8,128)(2,1)S(1)} copy-done((bf16[512,2048]{1,0:T(8,128)(2,1)S(1)}, bf16[512,2048]{1,0:T(8,128)(2,1)}, u32[]{:S(2)}) %copy-start.2) | copy-done | bytes 2097176
  70.4 0.0 copy-start.7
  70.4 1.0 copy-done.7
  71.4 3.4 %shard_map.122 = bf16[768,512]{1,0:T(8,128)(2,1)} custom-call(f32[1,512]{1,0:T(1,128)S(1)} %get-tuple-element.21.slot_ref, bf16[512,2048]{1,0:T(8,128)(2,1)S(1)} %copy-done.2, bf16[512,2048]{1,0:T(8,128)(2,1)S(1)} %copy-done, bf16[512,512]{1,0:T(8,128)(2,1)S(1)} %copy-done.7), custom_call_target="tpu_custom_call" | custom-call | flops 1476395008 | bytes 5242880 | tf_op jit(solution)/shard_map/pallas_call | solution.py:50
  74.9 0.0 collective-permute-done.1
  74.9 1.7 %add_convert_fusion = bf16[512,1408]{1,0:T(8,128)(2,1)S(1)} fusion(bf16[512,1408]{1,0:T(8,128)(2,1)} %collective-permute-done.1, bf16[512,1408]{1,0:T(8,128)(2,1)S(1)} %get-tuple-element.30), kind=kLoop, calls=%fused_computation | loop fusion | flops 2883584 | bytes 4325376 | tf_op jit(solution)/shard_map/convert_element_type | solution.py:480
  76.6 0.2 dynamic-slice_bitcast_fusion
  76.8 4.8 %all-to-all-start.2 = ((bf16[16,48,512]{2,1,0:T(8,128)(2,1)}), bf16[16,48,512]{2,1,0:T(8,128)(2,1)S(1)}, u32[]{:S(2)}, u32[]{:S(2)}) async-start(bf16[16,48,512]{2,1,0:T(8,128)(2,1)} %bitcast.13), calls=%async_computation.2 | async-start | bytes 1572864 | tf_op jit(solution)/shard_map/all_to_all | solution.py:496
  81.6 2.9 %collective-permute-start.5 = (bf16[4,32,1408]{2,1,0:T(8,128)(2,1)S(1)}, bf16[4,32,1408]{2,1,0:T(8,128)(2,1)S(1)}, u32[]{:S(2)}, u32[]{:S(2)}) collective-permute-start(bf16[4,32,1408]{2,1,0:T(8,128)(2,1)S(1)} %get-tuple-element.36), channel_id=1, source_target_pairs={{0,6},{2,4},{4,2},{6,0},{8,14},{10,12},{12,10},{14,8},{16,22},{18,... | collective-permute-start | bytes 1081352 | tf_op jit(solution)/shard_map/ppermute | solution.py:488
  84.5 0.5 collective-permute-start.4
  85.0 0.2 collective-permute-start.3
  85.2 18.2 %collective-permute-done.5 = bf16[4,32,1408]{2,1,0:T(8,128)(2,1)S(1)} collective-permute-done((bf16[4,32,1408]{2,1,0:T(8,128)(2,1)S(1)}, bf16[4,32,1408]{2,1,0:T(8,128)(2,1)S(1)}, u32[]{:S(2)}, u32[]{:S(2)}) %collective-permute-start.5) | collective-permute-done | bytes 360480 | tf_op jit(solution)/shard_map/ppermute | solution.py:488
  103.3 5.3 %collective-permute-done.4 = bf16[4,32,1408]{2,1,0:T(8,128)(2,1)S(1)} collective-permute-done((bf16[4,32,1408]{2,1,0:T(8,128)(2,1)S(1)}, bf16[4,32,1408]{2,1,0:T(8,128)(2,1)S(1)}, u32[]{:S(2)}, u32[]{:S(2)}) %collective-permute-start.4) | collective-permute-done | bytes 360480 | tf_op jit(solution)/shard_map/ppermute | solution.py:488
  108.6 0.8 collective-permute-done.3
  109.5 0.2 add_convert_fusion.1
  109.7 3.6 %collective-permute-start.8 = (bf16[32,1408]{1,0:T(8,128)(2,1)S(1)}, bf16[32,1408]{1,0:T(8,128)(2,1)S(1)}, u32[]{:S(2)}, u32[]{:S(2)}) collective-permute-start(bf16[32,1408]{1,0:T(8,128)(2,1)S(1)} %get-tuple-element.42), channel_id=1, source_target_pairs={{0,24},{2,26},{4,28},{6,30},{8,0},{10,2},{12,4},{14,6},{16,8},{18,... | collective-permute-start | bytes 270344 | tf_op jit(solution)/shard_map/ppermute | solution.py:494
  113.3 0.0 collective-permute-start.7
  113.3 1.2 collective-permute-start.6
  114.5 0.0 all-to-all-done.2
  114.5 0.0 collective-permute-start.2
  114.5 1.9 %collective-permute-done.8 = bf16[32,1408]{1,0:T(8,128)(2,1)S(1)} collective-permute-done((bf16[32,1408]{1,0:T(8,128)(2,1)S(1)}, bf16[32,1408]{1,0:T(8,128)(2,1)S(1)}, u32[]{:S(2)}, u32[]{:S(2)}) %collective-permute-start.8) | collective-permute-done | bytes 90144 | tf_op jit(solution)/shard_map/ppermute | solution.py:494
  116.4 4.5 %collective-permute-done.7 = bf16[32,1408]{1,0:T(8,128)(2,1)S(1)} collective-permute-done((bf16[32,1408]{1,0:T(8,128)(2,1)S(1)}, bf16[32,1408]{1,0:T(8,128)(2,1)S(1)}, u32[]{:S(2)}, u32[]{:S(2)}) %collective-permute-start.7) | collective-permute-done | bytes 90144 | tf_op jit(solution)/shard_map/ppermute | solution.py:494
  120.9 0.0 collective-permute-done.6
  120.9 0.1 collective-permute-start.9
  121.0 0.6 slice_reduce_fusion
  121.6 0.7 slice.12
  122.3 0.0 collective-permute-done.9
  122.3 0.6 pad_maximum_fusion
  123.0 0.0 collective-permute-done.2.refs_3_
  123.0 2.7 %shard_map.123 = f32[1024,512]{1,0:T(8,128)} custom-call(f32[1,768]{1,0:T(1,128)S(1)} %get-tuple-element.27.refs_0_, f32[1,768]{1,0:T(1,128)S(1)} %collective-permute-done.refs_1_, bf16[768,512]{1,0:T(8,128)(2,1)S(1)} %bitcast.37, bf16[768,512]{1,0:T(8,128)(2,1)S(1)} %collective-permute-done.2.refs_3_), custom_call_target="tpu_custom_call" | custom-call | flops 1610612736 | bytes 3670016 | tf_op jit(solution)/shard_map/pallas_call | solution.py:50
  (4 shorter events, 0.1 us)
Async XLA Ops:
  0.6 0.7 copy-start.10
  1.3 0.7 copy-start.11
  17.7 1.6 %copy-start.8 = (bf16[2048,512]{1,0:T(8,128)(2,1)S(1)}, bf16[2048,512]{1,0:T(8,128)(2,1)}, u32[]{:S(2)}) copy-start(bf16[2048,512]{1,0:T(8,128)(2,1)} %table_hbm.1) | copy-start | bytes 6291460
  19.3 26.8 %copy-start = (bf16[512,2048]{1,0:T(8,128)(2,1)S(1)}, bf16[512,2048]{1,0:T(8,128)(2,1)}, u32[]{:S(2)}) copy-start(bf16[512,2048]{1,0:T(8,128)(2,1)} %w_in_hbm.3) | copy-start | bytes 6291460
  22.1 0.9 copy-start.5
  22.1 24.0 %copy-start.12 = (f32[512]{0:T(512)S(1)}, f32[512]{0:T(512)}, u32[]{:S(2)}) copy-start(f32[512]{0:T(512)} %param.14) | copy-start | bytes 6148
  23.0 22.2 %all-to-all-start.1 = ((bf16[16,48,512]{2,1,0:T(8,128)(2,1)}), bf16[16,48,512]{2,1,0:T(8,128)(2,1)S(1)}, u32[]{:S(2)}, u32[]{:S(2)}) async-start(bf16[16,48,512]{2,1,0:T(8,128)(2,1)} %bitcast.39), calls=%async_computation.1 | async-start | bytes 1572864 | tf_op jit(solution)/shard_map/all_to_all | solution.py:410
  26.6 1.2 collective-permute-start
  45.2 0.9 copy-start.3
  46.1 1.1 copy-start.4
  47.2 1.0 copy-start.6
  48.2 1.0 copy-start.9
  49.3 0.7 copy-start.13
  67.5 1.3 %copy-start.1 = (bf16[512,2048]{1,0:T(8,128)(2,1)}, bf16[512,2048]{1,0:T(8,128)(2,1)S(1)}, u32[]{:S(2)}) copy-start(bf16[512,2048]{1,0:T(8,128)(2,1)S(1)} %get-tuple-element.29.gpre_hbm) | copy-start | bytes 6291460
  68.8 6.1 %collective-permute-start.1 = (bf16[512,1408]{1,0:T(8,128)(2,1)}, bf16[512,1408]{1,0:T(8,128)(2,1)}, u32[]{:S(2)}, u32[]{:S(2)}) collective-permute-start(bf16[512,1408]{1,0:T(8,128)(2,1)} %get-tuple-element.31), channel_id=1, source_target_pairs={{0,1},{1,0},{2,3},{3,2},{4,5},{5,4},{6,7},{7,6},{8,9},{9,8},{10,11... | collective-permute-start | bytes 4325384 | tf_op jit(solution)/shard_map/ppermute | solution.py:369
  68.8 1.6 %copy-start.2 = (bf16[512,2048]{1,0:T(8,128)(2,1)S(1)}, bf16[512,2048]{1,0:T(8,128)(2,1)}, u32[]{:S(2)}) copy-start(bf16[512,2048]{1,0:T(8,128)(2,1)} %copy-done.1) | copy-start | bytes 6291460
  70.4 1.0 copy-start.7
  76.8 37.7 %all-to-all-start.2 = ((bf16[16,48,512]{2,1,0:T(8,128)(2,1)}), bf16[16,48,512]{2,1,0:T(8,128)(2,1)S(1)}, u32[]{:S(2)}, u32[]{:S(2)}) async-start(bf16[16,48,512]{2,1,0:T(8,128)(2,1)} %bitcast.13), calls=%async_computation.2 | async-start | bytes 1572864 | tf_op jit(solution)/shard_map/all_to_all | solution.py:496
  81.6 21.7 %collective-permute-start.5 = (bf16[4,32,1408]{2,1,0:T(8,128)(2,1)S(1)}, bf16[4,32,1408]{2,1,0:T(8,128)(2,1)S(1)}, u32[]{:S(2)}, u32[]{:S(2)}) collective-permute-start(bf16[4,32,1408]{2,1,0:T(8,128)(2,1)S(1)} %get-tuple-element.36), channel_id=1, source_target_pairs={{0,6},{2,4},{4,2},{6,0},{8,14},{10,12},{12,10},{14,8},{16,22},{18,... | collective-permute-start | bytes 1081352 | tf_op jit(solution)/shard_map/ppermute | solution.py:488
  84.5 24.2 %collective-permute-start.4 = (bf16[4,32,1408]{2,1,0:T(8,128)(2,1)S(1)}, bf16[4,32,1408]{2,1,0:T(8,128)(2,1)S(1)}, u32[]{:S(2)}, u32[]{:S(2)}) collective-permute-start(bf16[4,32,1408]{2,1,0:T(8,128)(2,1)S(1)} %get-tuple-element.35), channel_id=1, source_target_pairs={{0,4},{2,6},{4,0},{6,2},{8,12},{10,14},{12,8},{14,10},{16,20},{18,... | collective-permute-start | bytes 1081352 | tf_op jit(solution)/shard_map/ppermute | solution.py:488
  85.0 24.5 %collective-permute-start.3 = (bf16[4,32,1408]{2,1,0:T(8,128)(2,1)S(1)}, bf16[4,32,1408]{2,1,0:T(8,128)(2,1)S(1)}, u32[]{:S(2)}, u32[]{:S(2)}) collective-permute-start(bf16[4,32,1408]{2,1,0:T(8,128)(2,1)S(1)} %get-tuple-element.34), channel_id=1, source_target_pairs={{0,2},{2,0},{4,6},{6,4},{8,10},{10,8},{12,14},{14,12},{16,18},{18,... | collective-permute-start | bytes 1081352 | tf_op jit(solution)/shard_map/ppermute | solution.py:488
  109.7 6.7 %collective-permute-start.8 = (bf16[32,1408]{1,0:T(8,128)(2,1)S(1)}, bf16[32,1408]{1,0:T(8,128)(2,1)S(1)}, u32[]{:S(2)}, u32[]{:S(2)}) collective-permute-start(bf16[32,1408]{1,0:T(8,128)(2,1)S(1)} %get-tuple-element.42), channel_id=1, source_target_pairs={{0,24},{2,26},{4,28},{6,30},{8,0},{10,2},{12,4},{14,6},{16,8},{18,... | collective-permute-start | bytes 270344 | tf_op jit(solution)/shard_map/ppermute | solution.py:494
  113.3 7.5 %collective-permute-start.7 = (bf16[32,1408]{1,0:T(8,128)(2,1)S(1)}, bf16[32,1408]{1,0:T(8,128)(2,1)S(1)}, u32[]{:S(2)}, u32[]{:S(2)}) collective-permute-start(bf16[32,1408]{1,0:T(8,128)(2,1)S(1)} %get-tuple-element.43), channel_id=1, source_target_pairs={{0,16},{2,18},{4,20},{6,22},{8,24},{10,26},{12,28},{14,30},{16,0},... | collective-permute-start | bytes 270344 | tf_op jit(solution)/shard_map/ppermute | solution.py:494
  113.3 7.5 %collective-permute-start.6 = (bf16[32,1408]{1,0:T(8,128)(2,1)S(1)}, bf16[32,1408]{1,0:T(8,128)(2,1)S(1)}, u32[]{:S(2)}, u32[]{:S(2)}) collective-permute-start(bf16[32,1408]{1,0:T(8,128)(2,1)S(1)} %get-tuple-element.41), channel_id=1, source_target_pairs={{0,8},{2,10},{4,12},{6,14},{8,16},{10,18},{12,20},{14,22},{16,24},... | collective-permute-start | bytes 270344 | tf_op jit(solution)/shard_map/ppermute | solution.py:494
  114.5 8.5 %collective-permute-start.2 = (bf16[768,512]{1,0:T(8,128)(2,1)S(1)}, bf16[768,512]{1,0:T(8,128)(2,1)S(1)}, u32[]{:S(2)}, u32[]{:S(2)}) collective-permute-start(bf16[768,512]{1,0:T(8,128)(2,1)S(1)} %bitcast.36), channel_id=1, source_target_pairs={{0,1},{1,0},{2,3},{3,2},{4,5},{5,4},{6,7},{7,6},{8,9},{9,8},{10,11... | collective-permute-start | bytes 2359304 | tf_op jit(solution)/shard_map/ppermute | solution.py:369
  120.9 1.4 %collective-permute-start.9 = (f32[32,256]{1,0:T(8,128)S(1)}, f32[32,256]{1,0:T(8,128)S(1)}, u32[]{:S(2)}, u32[]{:S(2)}) collective-permute-start(f32[32,256]{1,0:T(8,128)S(1)} %get-tuple-element.44), channel_id=1, source_target_pairs={{0,1},{1,0},{2,3},{3,2},{4,5},{5,4},{6,7},{7,6},{8,9},{9,8},{10,11... | collective-permute-start | bytes 98312 | tf_op jit(solution)/shard_map/ppermute | solution.py:369

commit v3 on v2

--- a/solution.py
+++ b/solution.py
@@ -41,7 +41,7 @@
     return 256 if rows % 256 == 0 else rows
 
 
-def call(kernel, out_shape, flops, nbytes, operands, smem=(), far=(), far_out=(), limit=20, scratch=()):
+def call(kernel, out_shape, flops, nbytes, operands, smem=(), far=(), far_out=(), limit=56, scratch=()):
     spaces = [
         pltpu.SMEM if i in smem else pl.ANY if i in far else pltpu.VMEM
         for i in range(len(operands))
@@ -145,6 +145,7 @@
 
 
 def layer_kernel(
+    owners,
     groups,
     wparts,
     len_ref,
@@ -156,14 +157,14 @@
     cot_hbm,
     *rest,
 ):
-    result_hbm, gpre_hbm = rest[:2]
-    grads_hbms = rest[2 : 2 + groups]
+    result_hbm, gpre_hbm, gin_hbm, gout_hbm = rest[:4]
     (
     w_in_ref,
     w_out_ref,
     cot_ref,
     result_ref,
-    grads_ref,
+    gin_ref,
+    gout_ref,
     pick_ref,
     emb_ref,
     proj_ref,
@@ -177,9 +178,8 @@
     gpre_ref,
     gval_ref,
     gkey_ref,
-    gwo_ref,
     sems,
-    ) = rest[2 + groups :]
+    ) = rest[4:]
     count, width = cot_ref.shape
     slots = ret_ref.shape[0]
     per = LANES // HEAD_DIM
@@ -277,7 +277,6 @@
         gatt_ref[rows, :] = ((gnorm - mean1 - normed * mean2) * inv).astype(BF16)
     put_result = pltpu.make_async_copy(result_ref, result_hbm, sems.at[3])
     put_result.start()
-    gwo_ref[...] = dot_tn(mixed_ref[...], cot_ref[...]).astype(BF16)
 
     def backward(p, _):
         start = pl.multiple_of(p * LANES, LANES)
@@ -311,24 +310,25 @@
     put_gpre = pltpu.make_async_copy(gpre_ref, gpre_hbm, sems.at[4])
     put_gpre.start()
 
-    me = lax.axis_index("group")
     emb_t = emb_ref[...].T
+    rows = width // owners
     cols_in = 4 * width // groups
     cols_out = width // wparts
-    chunk = min(cols_in, 512)
+    puts = [put_result, put_gpre]
+    for g in range(groups):
+        part = dot_nn(emb_t, gpre_ref[:, g * cols_in : (g + 1) * cols_in]).astype(BF16)
+        gin_ref[:, g] = part.reshape(owners, rows, cols_in)
+    puts.append(pltpu.make_async_copy(gin_ref, gin_hbm, sems.at[5]))
+    puts[-1].start()
+    gwo = dot_tn(mixed_ref[...], cot_ref[...]).astype(BF16)
     gain_col = jnp.broadcast_to(gain_sum, (LANES, width)).T.astype(BF16)
-    puts = [put_result, put_gpre]
-    for k in [*range(1, groups), 0]:
-        part = lax.rem(me + k, groups)
-        for c in range(0, cols_in, chunk):
-            cols = pl.ds(pl.multiple_of(part * cols_in + c, LANES), chunk)
-            grads_ref[k, :, c : c + chunk] = dot_nn(emb_t, gpre_ref[:, cols]).astype(BF16)
-        cols = pl.ds(pl.multiple_of(lax.rem(part, wparts) * cols_out, LANES), cols_out)
-        grads_ref[k, :, cols_in : cols_in + cols_out] = gwo_ref[:, cols]
-        grads_ref[k, :, cols_in + cols_out :] = gain_col
-        put = pltpu.make_async_copy(grads_ref.at[k], grads_hbms[k], sems.at[5 + k])
-        put.start()
-        puts.append(put)
+    for g in range(groups):
+        p = g % wparts
+        part = gwo[:, p * cols_out : (p + 1) * cols_out]
+        gout_ref[:, g, :, 0:cols_out] = part.reshape(owners, rows, cols_out)
+        gout_ref[:, g, :, cols_out:] = gain_col.reshape(owners, rows, LANES)
+    puts.append(pltpu.make_async_copy(gout_ref, gout_hbm, sems.at[6]))
+    puts[-1].start()
     for put in puts:
         put.wait()
 
@@ -414,28 +414,29 @@
     wparts = min(groups, width // LANES)
     cols_in = 4 * width // groups
     cols_out = width // wparts
-    cols_all = cols_in + cols_out + LANES
+    rows = width // owners
     square = pltpu.VMEM((count, width), BF16)
-    result, gpre, *grads = call(
-        functools.partial(layer_kernel, groups, wparts),
+    result, gpre, grad_in, grad_out = call(
+        functools.partial(layer_kernel, owners, groups, wparts),
         [
             jax.ShapeDtypeStruct((count, width), BF16),
             jax.ShapeDtypeStruct((count, 4 * width), BF16),
-            *[jax.ShapeDtypeStruct((width, cols_all), BF16) for _ in range(groups)],
+            jax.ShapeDtypeStruct((owners, groups, rows, cols_in), BF16),
+            jax.ShapeDtypeStruct((owners, groups, rows, cols_out + LANES), BF16),
         ],
         24 * count * width * width + 14 * count * count * width,
         24 * count * width,
         (lengths, slot, returned, w_in, w_out, gain.reshape(1, width), cotangent),
         smem=(0,),
         far=(3, 4, 6),
-        far_out=range(2 + groups),
-        limit=44,
+        far_out=range(4),
         scratch=[
             pltpu.VMEM(w_in.shape, BF16),
             pltpu.VMEM(w_out.shape, BF16),
             square,
             square,
-            pltpu.VMEM((groups, width, cols_all), BF16),
+            pltpu.VMEM((owners, groups, rows, cols_in), BF16),
+            pltpu.VMEM((owners, groups, rows, cols_out + LANES), BF16),
             pltpu.VMEM((count, slots), BF16),
             square,
             pltpu.VMEM((4, count, width), BF16),
@@ -449,8 +450,7 @@
             pltpu.VMEM((count, 4 * width), BF16),
             pltpu.VMEM((count, LANES), F32),
             pltpu.VMEM((count, LANES), F32),
-            pltpu.VMEM((width, width), BF16),
-            pltpu.SemaphoreType.DMA((5 + groups,)),
+            pltpu.SemaphoreType.DMA((7,)),
         ],
     )
     (outgoing,) = call(
@@ -469,29 +469,16 @@
         ],
     )
 
-    rows = width // owners
-    inner = 4 if owners % 4 == 0 else 1
-    outer = owners // inner
-    here = lax.axis_index("table")
-    high, low = here // inner, here % inner
-    chip = grads[0].astype(F32)
-    for k in range(1, groups):
-        chip = chip + shift(grads[k], "group", groups, k).astype(F32)
-    chip = chip.astype(BF16).reshape(outer, inner, rows, cols_all)
-    planes = [
-        lax.dynamic_index_in_dim(chip, low ^ k, 1, keepdims=False) for k in range(inner)
-    ]
-    outgoing, *planes = lax.optimization_barrier((outgoing, *planes))
-    total = planes[0].astype(F32)
-    for k in range(1, inner):
-        perm = [(i, i // inner * inner + ((i % inner) ^ k)) for i in range(owners)]
-        total = total + lax.ppermute(planes[k], "table", perm).astype(F32)
-    part = total.astype(BF16)
-    summed = lax.dynamic_index_in_dim(part, high, 0, keepdims=False).astype(F32)
-    for k in range(1, outer):
-        perm = [(i, ((i // inner + k) % outer) * inner + i % inner) for i in range(owners)]
-        sent = lax.dynamic_index_in_dim(part, (high + k) % outer, 0, keepdims=False)
-        summed = summed + lax.ppermute(sent, "table", perm).astype(F32)
+    everyone = ("table", "group")
+    sum_in = lax.psum_scatter(
+        grad_in.reshape(owners * groups * rows, cols_in), everyone, scatter_dimension=0, tiled=True
+    )
+    sum_out = lax.psum_scatter(
+        grad_out.reshape(owners * groups * rows, cols_out + LANES),
+        everyone,
+        scatter_dimension=0,
+        tiled=True,
+    )
 
     incoming = lax.all_to_all(outgoing, "table", split_axis=0, concat_axis=0, tiled=True)
     all_incoming = [incoming] + [shift(incoming, "group", groups, k) for k in range(1, groups)]
@@ -504,6 +491,7 @@
         (*all_ids, *all_incoming),
         far=range(groups, 2 * groups),
         far_out=(0,),
+        limit=24,
         scratch=[
             *[pltpu.VMEM((slots, width), BF16) for _ in range(groups)],
             pltpu.VMEM((grad_rows, width), F32),
@@ -511,8 +499,8 @@
         ],
     )
 
-    w_in_grad = summed[:, :cols_in]
-    mine = summed[:, cols_in : cols_in + cols_out]
+    w_in_grad = sum_in.astype(F32)
+    mine = sum_out[:, :cols_out].astype(F32)
     pieces = jnp.stack([mine] + [shift(mine, "group", groups, k) for k in range(1, groups)])
     w_out_grad = jnp.concatenate(
         [
@@ -521,7 +509,7 @@
         ],
         1,
     )
-    gain_grad = summed[:, cols_in + cols_out]
+    gain_grad = sum_out[:, cols_out].astype(F32)
     return (result, table_grad, w_in_grad, w_out_grad, gain_grad)
 
 

time: 126 us -> 315 us (2.50)
  waiting for transfers between devices: 49.2 us -> 216 us
  blocking collectives: 15.4 us -> 40.5 us
  between operations: 0.78 us -> 14.1 us
  starting transfers between devices: 17 us -> 3.85 us
  local copies, waits for them, and re-layouts: 14 us -> 2.66 us
  Pallas kernels: 26.7 us -> 34.3 us
    reduce_scatter x0 -> x1, waiting for transfers between devices: none -> 131 us  [on_device(): lax.psum_scatter(grad_in.reshape(owners * groups * rows, cols_in), everyo...]
    unnamed x0 -> x3, waiting for transfers between devices: none -> 65.3 us
    ppermute x6 -> x0, waiting for transfers between devices: 30.6 us -> none  [the longest x3 24.3 us: on_device(): total = total + lax.ppermute(planes[k], 'table', perm).astype(F32)]
    all_to_all x0 -> x1, blocking collectives: none -> 24.9 us  [on_device(): lax.all_to_all(outgoing, 'table', split_axis=0, concat_axis=0, tiled=True)]
    unnamed x28 -> x6, local copies, waits for them, and re-layouts: 12.5 us -> 1.12 us
    ppermute x6 -> x0, starting transfers between devices: 8.36 us -> none  [the longest x3 4.81 us: on_device(): summed = summed + lax.ppermute(sent, 'table', perm).astype(F32)]
    pallas_call x5, Pallas kernels: 26.7 us -> 34.3 us  [call(): pl.pallas_call(kernel, out_shape=out_shape, in_specs=[pl.BlockSpec(memory...]
    all_to_all x1 -> x0, starting transfers between devices: 4.84 us -> none  [on_device(): lax.all_to_all(outgoing, 'table', split_axis=0, concat_axis=0, tiled=True)]
  transfers between devices with their start and end apart: 12 -> 6, of which waited for: 7 -> 5; matrix products, arithmetic and copies ran while one was open for 2% -> 1% of each run, Pallas kernels for 3% -> 2%
where the time goes in v3:
time: 315 us; the launch traced here: 314 us
  waiting for transfers between devices  216 us (69%)
  blocking collectives  40.5 us (13%)
  Pallas kernels  34.3 us (11%)
  between operations  14.1 us (4%)
  starting transfers between devices  3.85 us (1%)
    reduce_scatter x1, waiting for transfers between devices, on_device(): lax.psum_scatter(grad_in.reshape(owners * groups * rows, cols_in), everyo...  131 us
    unnamed x3, waiting for transfers between devices  65.3 us
    pallas_call x5, Pallas kernels, call(): pl.pallas_call(kernel, out_shape=out_shape, in_specs=[pl.BlockSpec(memory...  34.3 us
    all_to_all x1, blocking collectives, on_device(): lax.all_to_all(outgoing, 'table', split_axis=0, concat_axis=0, tiled=True)  24.9 us
    all_to_all x1, waiting for transfers between devices, on_device(): lax.all_to_all(found, 'table', split_axis=0, concat_axis=0, tiled=True)  17 us
    all_to_all x1, blocking collectives, on_device(): lax.all_to_all(requested, 'table', split_axis=0, concat_axis=0, tiled=True)  15.6 us
  transfers between devices with their start and end apart: 6, of which 5 were waited for; matrix products, arithmetic and copies ran while one was open for 1% of the time, Pallas kernels for 2%

profile of v3, /device:TPU:0, one launch (start us, length us, event | category | flops | bytes accessed | tf_op | source)
XLA Modules:
  0.0 314.0 jit_solution(2121670896503725328)
XLA Ops:
  7.2 1.7 shard_map.119
  8.8 15.6 %all_to_all.34 = s32[16,1,128]{2,1,0:T(1,128)} all-to-all(s32[16,1,128]{2,1,0:T(1,128)} %bitcast.33), channel_id=1, replica_groups=mesh['table'=16,'group'=2] {'table'}, dimensions={0} | all-to-all | bytes 16384 | tf_op jit(solution)/shard_map/all_to_all | solution.py:392
  24.4 5.4 %shard_map.120 = (bf16[768,512]{1,0:T(8,128)(2,1)}, f32[1,768]{1,0:T(1,128)}) custom-call(s32[16,128]{1,0:T(8,128)} %bitcast.32, bf16[2048,512]{1,0:T(8,128)(2,1)} %table_hbm.1), custom_call_target="tpu_custom_call" | custom-call | flops 1610612736 | bytes 2883584 | tf_op jit(solution)/shard_map/pallas_call | solution.py:50
  29.8 3.6 %all-to-all-start.1 = ((bf16[16,48,512]{2,1,0:T(8,128)(2,1)}), bf16[16,48,512]{2,1,0:T(8,128)(2,1)S(1)}, u32[]{:S(2)}, u32[]{:S(2)}) async-start(bf16[16,48,512]{2,1,0:T(8,128)(2,1)} %bitcast.30), calls=%async_computation.1 | async-start | bytes 1572864 | tf_op jit(solution)/shard_map/all_to_all | solution.py:410
  33.5 0.0 reduce-scatter.7.cloned.1.call-start
  33.5 0.1 collective-permute-start
  33.6 1.4 collective-permute-done.refs_1_
  35.0 17.0 %all-to-all-done.1 = bf16[16,48,512]{2,1,0:T(8,128)(2,1)S(1)} async-done(((bf16[16,48,512]{2,1,0:T(8,128)(2,1)}), bf16[16,48,512]{2,1,0:T(8,128)(2,1)S(1)}, u32[]{:S(2)}, u32[]{:S(2)}) %all-to-all-start.1) | async-done | bytes 786464 | tf_op jit(solution)/shard_map/all_to_all | solution.py:410
  52.0 0.0 copy-start.1
  52.0 0.9 copy-done.1
  52.9 19.4 %shard_map.121 = (bf16[512,512]{1,0:T(8,128)(2,1)}, bf16[512,2048]{1,0:T(8,128)(2,1)}, bf16[16,2,32,1024]{3,2,1,0:T(8,128)(2,1)}, bf16[16,2,32,384]{3,2,1,0:T(8,128)(2,1)}) custom-call(s32[1,8]{1,0:T(1,128)} %len_ref.1, f32[1,512]{1,0:T(1,128)} %get-tuple-element.16.slot_ref, bf16[768,512]{1,0:T(8,128)(2,1)} %bitcast.29, bf16[512,2048]{1,0:T(8,128)(2,1)} %w_in_hbm.3, ...), custom_call_target="tpu_custom_call" | custom-call | flops 5100273664 | bytes 6291456 | tf_op jit(solution)/shard_map/pallas_call | solution.py:50
  72.3 0.0 reduce-scatter.7.cloned.1.call-update
  72.3 0.0 reduce-scatter.5.cloned.1.call-start
  72.3 0.7 reduce-scatter.5.cloned.1.call-update
  73.1 5.1 %shard_map.122 = bf16[768,512]{1,0:T(8,128)(2,1)} custom-call(f32[1,512]{1,0:T(1,128)} %get-tuple-element.16.slot_ref, bf16[512,2048]{1,0:T(8,128)(2,1)} %get-tuple-element.24.gpre_hbm, bf16[512,2048]{1,0:T(8,128)(2,1)} %w_in_hbm.3, bf16[512,512]{1,0:T(8,128)(2,1)} %cot_ref.1), custom_call_target="tpu_custom_call" | custom-call | flops 1476395008 | bytes 5242880 | tf_op jit(solution)/shard_map/pallas_call | solution.py:50
  78.1 0.0 copy-start
  78.2 24.9 %all_to_all.35 = bf16[16,48,512]{2,1,0:T(8,128)(2,1)S(1)} all-to-all(bf16[16,48,512]{2,1,0:T(8,128)(2,1)} %bitcast.26), channel_id=1, replica_groups=mesh['table'=16,'group'=2] {'table'}, dimensions={0} | all-to-all | bytes 1572864 | tf_op jit(solution)/shard_map/all_to_all | solution.py:483
  103.1 0.0 collective-permute-start.1
  103.1 64.6 %reduce-scatter.7.cloned.1.call-done = bf16[32,384]{1,0:T(8,128)(2,1)} async-done(((bf16[1024,384]{1,0:T(8,128)(2,1)}), bf16[32,384]{1,0:T(8,128)(2,1)}) %reduce-scatter.7.cloned.1.call-update) | async-done | bytes 24592
  167.6 0.7 slice.9
  168.3 0.1 copy.23
  168.4 0.7 slice.8
  169.2 0.1 copy.22
  169.3 0.1 collective-permute-start.2
  169.4 0.5 bitcast_convert_fusion
  169.9 0.1 copy.18
  170.0 0.8 collective-permute-done.2
  170.7 0.1 copy.19
  170.8 0.6 pad_maximum_fusion
  171.5 0.0 collective-permute-done.1.refs_3_
  171.5 0.0 copy-done
  171.5 2.7 shard_map.123
  174.2 131.4 %reduce-scatter.5.cloned.1.call-done = bf16[32,1024]{1,0:T(8,128)(2,1)} async-done(((bf16[1024,1024]{1,0:T(8,128)(2,1)}), bf16[32,1024]{1,0:T(8,128)(2,1)}) %reduce-scatter.5.cloned.1.call-update) | async-done | bytes 65552 | tf_op jit(solution)/shard_map/reduce_scatter | solution.py:473
  305.6 1.5 convert_element_type.12
  (2 shorter events, 0.0 us)
Async XLA Ops:
  29.8 22.1 %all-to-all-start.1 = ((bf16[16,48,512]{2,1,0:T(8,128)(2,1)}), bf16[16,48,512]{2,1,0:T(8,128)(2,1)S(1)}, u32[]{:S(2)}, u32[]{:S(2)}) async-start(bf16[16,48,512]{2,1,0:T(8,128)(2,1)} %bitcast.30), calls=%async_computation.1 | async-start | bytes 1572864 | tf_op jit(solution)/shard_map/all_to_all | solution.py:410
  33.5 134.2 %reduce-scatter.7.cloned.1.call-start = ((), (), s32[]{:S(2)}) async-start(), calls=%async_computation.6 | async-start | bytes 811008
  33.5 1.4 collective-permute-start
  52.0 0.9 copy-start.1
  72.3 233.3 %reduce-scatter.5.cloned.1.call-start = ((), (), s32[]{:S(2)}) async-start(), calls=%async_computation.5 | async-start | bytes 2162688 | tf_op jit(solution)/shard_map/reduce_scatter | solution.py:473
  78.1 93.3 %copy-start = (f32[1,768]{1,0:T(1,128)S(1)}, f32[1,768]{1,0:T(1,128)}, u32[]{:S(2)}) copy-start(f32[1,768]{1,0:T(1,128)} %get-tuple-element.22.refs_0_) | copy-start | bytes 9220
  103.1 68.4 %collective-permute-start.1 = (bf16[768,512]{1,0:T(8,128)(2,1)S(1)}, bf16[768,512]{1,0:T(8,128)(2,1)S(1)}, u32[]{:S(2)}, u32[]{:S(2)}) collective-permute-start(bf16[768,512]{1,0:T(8,128)(2,1)S(1)} %bitcast.24), channel_id=1, source_target_pairs={{0,1},{1,0},{2,3},{3,2},{4,5},{5,4},{6,7},{7,6},{8,9},{9,8},{10,11... | collective-permute-start | bytes 2359304 | tf_op jit(solution)/shard_map/ppermute | solution.py:369
  169.3 1.4 collective-permute-start.2
Sparse Core Ops, SparseCore 0:
  72.4 95.1 reduce-scatter.6
  169.9 135.6 reduce-scatter.4

commit v4 on v2

--- a/solution.py
+++ b/solution.py
@@ -41,7 +41,7 @@
     return 256 if rows % 256 == 0 else rows
 
 
-def call(kernel, out_shape, flops, nbytes, operands, smem=(), far=(), far_out=(), limit=20, scratch=()):
+def call(kernel, out_shape, flops, nbytes, operands, smem=(), far=(), far_out=(), limit=56, scratch=()):
     spaces = [
         pltpu.SMEM if i in smem else pl.ANY if i in far else pltpu.VMEM
         for i in range(len(operands))
@@ -76,12 +76,20 @@
     req_ref[...] = found.astype(jnp.int32)
 
 
-def lookup_kernel(cap, wanted_ref, table_hbm, found_hbm, ids_ref, table_ref, found_ref, sems):
+def lookup_kernel(cap, wanted_ref, table_hbm, found_hbm, ids_ref, table_ref, found_ref, pick_ref, sems):
     owners, width = wanted_ref.shape
     slots = found_ref.shape[0]
     rows = table_ref.shape[0]
-    fetch = pltpu.make_async_copy(table_hbm, table_ref, sems.at[0])
-    fetch.start()
+    half_width = table_ref.shape[1] // 2
+    halves = [pl.ds(i * half_width, half_width) for i in range(2)]
+    fetches = []
+    for i, half in enumerate(halves):
+        for j in range(2):
+            at = (pl.ds(j * (rows // 2), rows // 2), half)
+            fetches.append(
+                pltpu.make_async_copy(table_hbm.at[at], table_ref.at[at], sems.at[2 * i + j])
+            )
+            fetches[-1].start()
     wanted = wanted_ref[...]
     high = (wanted >> 8).astype(F32).astype(BF16)
     low = (wanted & 255).astype(F32).astype(BF16)
@@ -97,15 +105,16 @@
     wide = jnp.broadcast_to(ids, (slots, LANES))
     ids_ref[...] = wide.T[0:1, :]
     step = row_step(slots)
-    fetch.wait()
+    for start in range(0, slots, step):
+        part = ids[start : start + step]
+        pick_ref[start : start + step, :] = hot(iota((step, rows), 1).astype(F32) == part)
     stores = []
-    for n, start in enumerate(range(0, slots, step)):
-        part = ids[start : start + step]
-        pick = hot(iota((step, rows), 1).astype(F32) == part)
-        found_ref[start : start + step, :] = dot_nn(pick, table_ref[...]).astype(BF16)
-        here = pl.ds(start, step)
+    for i, half in enumerate(halves):
+        for fetch in fetches[2 * i : 2 * i + 2]:
+            fetch.wait()
+        found_ref[:, half] = dot_nn(pick_ref[...], table_ref[:, half]).astype(BF16)
         stores.append(
-            pltpu.make_async_copy(found_ref.at[here], found_hbm.at[here], sems.at[1 + n])
+            pltpu.make_async_copy(found_ref.at[:, half], found_hbm.at[:, half], sems.at[4 + i])
         )
         stores[-1].start()
     for store in stores:
@@ -157,7 +166,7 @@
     *rest,
 ):
     result_hbm, gpre_hbm = rest[:2]
-    grads_hbms = rest[2 : 2 + groups]
+    grads_hbms = rest[2 : 2 + 2 * groups]
     (
     w_in_ref,
     w_out_ref,
@@ -179,7 +188,7 @@
     gkey_ref,
     gwo_ref,
     sems,
-    ) = rest[2 + groups :]
+    ) = rest[2 + 2 * groups :]
     count, width = cot_ref.shape
     slots = ret_ref.shape[0]
     per = LANES // HEAD_DIM
@@ -187,10 +196,14 @@
     qrows = QUERY_ROWS if count % QUERY_ROWS == 0 else count
     half_scale = 0.5 / math.sqrt(HEAD_DIM)
 
-    get_in = pltpu.make_async_copy(w_in_hbm, w_in_ref, sems.at[0])
-    get_cot = pltpu.make_async_copy(cot_hbm, cot_ref, sems.at[1])
-    get_out = pltpu.make_async_copy(w_out_hbm, w_out_ref, sems.at[2])
-    for fetch in (get_in, get_cot, get_out):
+    parts = [pl.ds(i * width, width) for i in range(4)]
+    get_ins = [
+        pltpu.make_async_copy(w_in_hbm.at[:, part], w_in_ref.at[:, part], sems.at[i])
+        for i, part in enumerate(parts)
+    ]
+    get_cot = pltpu.make_async_copy(cot_hbm, cot_ref, sems.at[4])
+    get_out = pltpu.make_async_copy(w_out_hbm, w_out_ref, sems.at[5])
+    for fetch in (*get_ins, get_cot, get_out):
         fetch.start()
 
     slot = jnp.broadcast_to(slot_ref[...], (LANES, count)).T
@@ -199,18 +212,14 @@
             slot == (iota((count, LANES), 1) + start).astype(F32)
         )
     emb_ref[...] = dot_nn(pick_ref[...], ret_ref[...]).astype(BF16)
-    get_in.wait()
-
-    def project(i, _):
-        cols = pl.ds(pl.multiple_of(i * width, width), width)
-        pre = dot_nn(emb_ref[...], w_in_ref[:, cols])
+
+    for i in range(4):
+        get_ins[i].wait()
+        pre = dot_nn(emb_ref[...], w_in_ref[:, parts[i]])
         sig = 0.5 * jnp.tanh(0.5 * pre) + 0.5
         act = pre * sig
         proj_ref[i] = act.astype(BF16)
         slope_ref[i] = sig + act * (1.0 - sig)
-        return 0
-
-    lax.fori_loop(0, 4, project, 0)
 
     pos = iota((count, 1), 0)
     begin = jnp.zeros((count, 1), jnp.int32)
@@ -275,7 +284,7 @@
         mean1 = jnp.mean(gnorm, 1, keepdims=True)
         mean2 = jnp.mean(gnorm * normed, 1, keepdims=True)
         gatt_ref[rows, :] = ((gnorm - mean1 - normed * mean2) * inv).astype(BF16)
-    put_result = pltpu.make_async_copy(result_ref, result_hbm, sems.at[3])
+    put_result = pltpu.make_async_copy(result_ref, result_hbm, sems.at[6])
     put_result.start()
     gwo_ref[...] = dot_tn(mixed_ref[...], cot_ref[...]).astype(BF16)
 
@@ -308,8 +317,12 @@
 
     lax.fori_loop(0, slabs, backward, 0)
 
-    put_gpre = pltpu.make_async_copy(gpre_ref, gpre_hbm, sems.at[4])
-    put_gpre.start()
+    puts = [put_result]
+    for i, part in enumerate(parts):
+        puts.append(
+            pltpu.make_async_copy(gpre_ref.at[:, part], gpre_hbm.at[:, part], sems.at[7 + i])
+        )
+        puts[-1].start()
 
     me = lax.axis_index("group")
     emb_t = emb_ref[...].T
@@ -317,7 +330,6 @@
     cols_out = width // wparts
     chunk = min(cols_in, 512)
     gain_col = jnp.broadcast_to(gain_sum, (LANES, width)).T.astype(BF16)
-    puts = [put_result, put_gpre]
     for k in [*range(1, groups), 0]:
         part = lax.rem(me + k, groups)
         for c in range(0, cols_in, chunk):
@@ -326,16 +338,19 @@
         cols = pl.ds(pl.multiple_of(lax.rem(part, wparts) * cols_out, LANES), cols_out)
         grads_ref[k, :, cols_in : cols_in + cols_out] = gwo_ref[:, cols]
         grads_ref[k, :, cols_in + cols_out :] = gain_col
-        put = pltpu.make_async_copy(grads_ref.at[k], grads_hbms[k], sems.at[5 + k])
-        put.start()
-        puts.append(put)
+        cut = grads_hbms[2 * k].shape[1]
+        for i, cols in enumerate((pl.ds(0, cut), pl.ds(cut, grads_ref.shape[2] - cut))):
+            put = pltpu.make_async_copy(
+                grads_ref.at[k, :, cols], grads_hbms[2 * k + i], sems.at[11 + 2 * k + i]
+            )
+            put.start()
+            puts.append(put)
     for put in puts:
         put.wait()
 
 
-def rows_kernel(slot_ref, gpre_hbm, w_in_hbm, cot_ref, out_hbm, gpre_ref, w_in_ref, out_ref, sems):
-    count, width = cot_ref.shape
-    slots = out_ref.shape[0]
+def row_grad_kernel(gpre_hbm, w_in_hbm, cot_ref, out_ref, gpre_ref, w_in_ref, sems):
+    width = cot_ref.shape[1]
     fetches = []
     for i in range(4):
         cols = pl.ds(i * width, width)
@@ -352,14 +367,19 @@
             fetch.wait()
         cols = slice(i * width, (i + 1) * width)
         total = total + dot_nt(gpre_ref[:, cols], w_in_ref[:, cols])
-    gemb = total.astype(BF16)
+    out_ref[...] = total.astype(BF16)
+
+
+def slots_kernel(slot_ref, grad_ref, out_hbm, out_ref, sems):
+    count = grad_ref.shape[0]
+    slots = out_ref.shape[0]
     step = row_step(slots)
     stores = []
     for n, start in enumerate(range(0, slots, step)):
         put = hot((iota((step, count), 0) + start).astype(F32) == slot_ref[...])
-        out_ref[start : start + step, :] = dot_nn(put, gemb).astype(BF16)
+        out_ref[start : start + step, :] = dot_nn(put, grad_ref[...]).astype(BF16)
         here = pl.ds(start, step)
-        stores.append(pltpu.make_async_copy(out_ref.at[here], out_hbm.at[here], sems.at[8 + n]))
+        stores.append(pltpu.make_async_copy(out_ref.at[here], out_hbm.at[here], sems.at[n]))
         stores[-1].start()
     for store in stores:
         store.wait()
@@ -404,7 +424,8 @@
         scratch=[
             pltpu.VMEM(table.shape, BF16),
             pltpu.VMEM((slots, width), BF16),
-            pltpu.SemaphoreType.DMA((1 + slots // row_step(slots),)),
+            pltpu.VMEM((slots, table.shape[0]), BF16),
+            pltpu.SemaphoreType.DMA((6,)),
         ],
     )
     returned = lax.all_to_all(found, "table", split_axis=0, concat_axis=0, tiled=True)
@@ -415,21 +436,25 @@
     cols_in = 4 * width // groups
     cols_out = width // wparts
     cols_all = cols_in + cols_out + LANES
+    cut = cols_all // LANES // 2 * LANES
     square = pltpu.VMEM((count, width), BF16)
     result, gpre, *grads = call(
         functools.partial(layer_kernel, groups, wparts),
         [
             jax.ShapeDtypeStruct((count, width), BF16),
             jax.ShapeDtypeStruct((count, 4 * width), BF16),
-            *[jax.ShapeDtypeStruct((width, cols_all), BF16) for _ in range(groups)],
+            *[
+                jax.ShapeDtypeStruct((width, cols), BF16)
+                for _ in range(groups)
+                for cols in (cut, cols_all - cut)
+            ],
         ],
         24 * count * width * width + 14 * count * count * width,
         24 * count * width,
         (lengths, slot, returned, w_in, w_out, gain.reshape(1, width), cotangent),
         smem=(0,),
         far=(3, 4, 6),
-        far_out=range(2 + groups),
-        limit=44,
+        far_out=range(2 + 2 * groups),
         scratch=[
             pltpu.VMEM(w_in.shape, BF16),
             pltpu.VMEM(w_out.shape, BF16),
@@ -450,49 +475,75 @@
             pltpu.VMEM((count, LANES), F32),
             pltpu.VMEM((count, LANES), F32),
             pltpu.VMEM((width, width), BF16),
-            pltpu.SemaphoreType.DMA((5 + groups,)),
-        ],
-    )
-    (outgoing,) = call(
-        rows_kernel,
-        [jax.ShapeDtypeStruct((slots, width), BF16)],
-        8 * count * width * width + 2 * slots * count * width,
+            pltpu.SemaphoreType.DMA((11 + 2 * groups,)),
+        ],
+    )
+    (row_grad,) = call(
+        row_grad_kernel,
+        [jax.ShapeDtypeStruct((count, width), BF16)],
+        8 * count * width * width,
         20 * count * width,
-        (slot, gpre, w_in, cotangent),
-        far=(1, 2),
-        far_out=(0,),
+        (gpre, w_in, cotangent),
+        far=(0, 1),
         scratch=[
             pltpu.VMEM((count, 4 * width), BF16),
             pltpu.VMEM(w_in.shape, BF16),
+            pltpu.SemaphoreType.DMA((8,)),
+        ],
+    )
+
+    rows = width // owners
+    side = 2 if owners % 4 == 0 else 1
+    plane = side * side
+    outer = owners // plane
+    here = lax.axis_index("table")
+    high, middle, low = here // plane, here // side % side, here % side
+    sides = []
+    for i in range(2):
+        terms = [grads[i]] + [shift(grads[2 * k + i], "group", groups, k) for k in range(1, groups)]
+        sides.append([term.reshape(outer, side, side, rows, term.shape[1]) for term in terms])
+
+    def entry(value, index, axis):
+        return lax.dynamic_index_in_dim(value, index, axis, keepdims=False)
+
+    def add(terms):
+        return sum(term.astype(F32) for term in terms)
+
+    def halve(terms, index, axis, bit, tie=None):
+        send = add([entry(term, 1 - index, axis) for term in terms]).astype(BF16)
+        if tie is not None:
+            tie, send = lax.optimization_barrier((tie, send))
+        got = lax.ppermute(send, "table", [(i, i ^ bit) for i in range(owners)])
+        return [entry(term, index, axis) for term in terms] + [got], tie
+
+    if side == 2:
+        left, row_grad = halve(sides[0], low, 2, 1, row_grad)
+        right, row_grad = halve(sides[1], middle, 1, 2, row_grad)
+        left, _ = halve(left, middle, 1, 2)
+        right, _ = halve(right, low, 1, 1)
+    else:
+        left, right = [[term[:, 0, 0] for term in terms] for terms in sides]
+    sums = [[add([entry(term, high, 0) for term in terms])] for terms in (left, right)]
+    for k in range(1, outer):
+        perm = [(i, ((i // plane + k) % outer) * plane + i % plane) for i in range(owners)]
+        send = [add([entry(term, (high + k) % outer, 0) for term in terms]) for terms in (left, right)]
+        got = lax.ppermute(jnp.concatenate(send, 1).astype(BF16), "table", perm)
+        sums[0].append(got[:, :cut])
+        sums[1].append(got[:, cut:])
+    summed = jnp.concatenate([add(terms) for terms in sums], 1)
+
+    (outgoing,) = call(
+        slots_kernel,
+        [jax.ShapeDtypeStruct((slots, width), BF16)],
+        2 * slots * count * width,
+        4 * count * width,
+        (slot, row_grad),
+        far_out=(0,),
+        scratch=[
             pltpu.VMEM((slots, width), BF16),
-            pltpu.SemaphoreType.DMA((8 + slots // row_step(slots),)),
-        ],
-    )
-
-    rows = width // owners
-    inner = 4 if owners % 4 == 0 else 1
-    outer = owners // inner
-    here = lax.axis_index("table")
-    high, low = here // inner, here % inner
-    chip = grads[0].astype(F32)
-    for k in range(1, groups):
-        chip = chip + shift(grads[k], "group", groups, k).astype(F32)
-    chip = chip.astype(BF16).reshape(outer, inner, rows, cols_all)
-    planes = [
-        lax.dynamic_index_in_dim(chip, low ^ k, 1, keepdims=False) for k in range(inner)
-    ]
-    outgoing, *planes = lax.optimization_barrier((outgoing, *planes))
-    total = planes[0].astype(F32)
-    for k in range(1, inner):
-        perm = [(i, i // inner * inner + ((i % inner) ^ k)) for i in range(owners)]
-        total = total + lax.ppermute(planes[k], "table", perm).astype(F32)
-    part = total.astype(BF16)
-    summed = lax.dynamic_index_in_dim(part, high, 0, keepdims=False).astype(F32)
-    for k in range(1, outer):
-        perm = [(i, ((i // inner + k) % outer) * inner + i % inner) for i in range(owners)]
-        sent = lax.dynamic_index_in_dim(part, (high + k) % outer, 0, keepdims=False)
-        summed = summed + lax.ppermute(sent, "table", perm).astype(F32)
-
+            pltpu.SemaphoreType.DMA((slots // row_step(slots),)),
+        ],
+    )
     incoming = lax.all_to_all(outgoing, "table", split_axis=0, concat_axis=0, tiled=True)
     all_incoming = [incoming] + [shift(incoming, "group", groups, k) for k in range(1, groups)]
     grad_rows = table.shape[0] // groups
@@ -504,6 +555,7 @@
         (*all_ids, *all_incoming),
         far=range(groups, 2 * groups),
         far_out=(0,),
+        limit=24,
         scratch=[
             *[pltpu.VMEM((slots, width), BF16) for _ in range(groups)],
             pltpu.VMEM((grad_rows, width), F32),

time: 126 us -> 119 us (0.944)
  waiting for transfers between devices: 49.2 us -> 32.3 us
  local copies, waits for them, and re-layouts: 14 us -> 1.53 us
  Pallas kernels: 26.7 us -> 37.5 us
  other arithmetic: 2.58 us -> 10.7 us
  starting transfers between devices: 17 us -> 19.3 us
    ppermute x6 -> x7, waiting for transfers between devices: 30.6 us -> 13.9 us  [the longest x4 8.13 us: halve(): got = lax.ppermute(send, 'table', [(i, i ^ bit) for i in range(owners)])]
    unnamed x28 -> x10, local copies, waits for them, and re-layouts: 12.5 us -> 0.9 us
    pallas_call x5 -> x6, Pallas kernels: 26.7 us -> 37.5 us  [call(): pl.pallas_call(kernel, out_shape=out_shape, in_specs=[pl.BlockSpec(memory...]
    convert_element_type x2 -> x4, other arithmetic: 1.88 us -> 4.27 us  [halve(): send = add([entry(term, 1 - index, axis) for term in terms]).astype(BF16)]
    concatenate x0 -> x4, other arithmetic: none -> 1.96 us  [the longest x3 1.29 us: on_device(): got = lax.ppermute(jnp.concatenate(send, 1).astype(BF16), 'table', perm)]
    another operation x0 -> x2, other arithmetic: none -> 1.94 us
    add x1 -> x2, other arithmetic: 0.05 us -> 1.84 us  [add(): return sum((term.astype(F32) for term in terms))]
    ppermute x6 -> x7, starting transfers between devices: 8.36 us -> 9.52 us  [the longest x4 5.78 us: halve(): got = lax.ppermute(send, 'table', [(i, i ^ bit) for i in range(owners)])]
  transfers between devices with their start and end apart: 12 -> 14, of which waited for: 7 -> 7; matrix products, arithmetic and copies ran while one was open for 2% -> 10% of each run, Pallas kernels for 3% -> 6%
where the time goes in v4:
time: 119 us; the launch traced here: 118 us
  Pallas kernels  37.5 us (32%)
  waiting for transfers between devices  32.3 us (27%)
  starting transfers between devices  19.3 us (16%)
  blocking collectives  15.5 us (13%)
  other arithmetic  10.7 us (9%)
  local copies, waits for them, and re-layouts  1.53 us (1%)
    pallas_call x6, Pallas kernels, call(): pl.pallas_call(kernel, out_shape=out_shape, in_specs=[pl.BlockSpec(memory...  37.5 us
    all_to_all x1, waiting for transfers between devices, on_device(): lax.all_to_all(found, 'table', split_axis=0, concat_axis=0, tiled=True)  17.1 us
    all_to_all x1, blocking collectives, on_device(): lax.all_to_all(requested, 'table', split_axis=0, concat_axis=0, tiled=True)  15.5 us
    ppermute x4, waiting for transfers between devices, halve(): got = lax.ppermute(send, 'table', [(i, i ^ bit) for i in range(owners)])  8.13 us
    ppermute x4, starting transfers between devices, halve(): got = lax.ppermute(send, 'table', [(i, i ^ bit) for i in range(owners)])  5.78 us
    ppermute x3, waiting for transfers between devices, on_device(): got = lax.ppermute(jnp.concatenate(send, 1).astype(BF16), 'table', perm)  5.73 us
    all_to_all x1, starting transfers between devices, on_device(): lax.all_to_all(outgoing, 'table', split_axis=0, concat_axis=0, tiled=True)  4.73 us
    convert_element_type x4, other arithmetic, halve(): send = add([entry(term, 1 - index, axis) for term in terms]).astype(BF16)  4.27 us
  transfers between devices with their start and end apart: 14, of which 7 were waited for; matrix products, arithmetic and copies ran while one was open for 10% of the time, Pallas kernels for 6%

profile of v4, /device:TPU:0, one launch (start us, length us, event | category | flops | bytes accessed | tf_op | source)
XLA Modules:
  0.0 117.7 jit_solution(10548258454599853025)
XLA Ops:
  0.6 1.7 %shard_map.119 = (s32[16,128]{1,0:T(8,128)}, f32[1,512]{1,0:T(1,128)}) custom-call(s32[1,512]{1,0:T(1,128)} %bitcast.128, s32[1,512]{1,0:T(1,128)} %bitcast.129), custom_call_target="tpu_custom_call" | custom-call | flops 16777216 | bytes 4096 | tf_op jit(solution)/shard_map/pallas_call | solution.py:50
  2.3 15.5 %all_to_all.34 = s32[16,1,128]{2,1,0:T(1,128)} all-to-all(s32[16,1,128]{2,1,0:T(1,128)} %bitcast.127), channel_id=1, replica_groups=mesh['table'=16,'group'=2] {'table'}, dimensions={0} | all-to-all | bytes 16384 | tf_op jit(solution)/shard_map/all_to_all | solution.py:412
  17.7 6.8 %shard_map.120 = (bf16[768,512]{1,0:T(8,128)(2,1)}, f32[1,768]{1,0:T(1,128)}) custom-call(s32[16,128]{1,0:T(8,128)} %bitcast.126, bf16[2048,512]{1,0:T(8,128)(2,1)} %table_hbm.1), custom_call_target="tpu_custom_call" | custom-call | flops 1610612736 | bytes 2883584 | tf_op jit(solution)/shard_map/pallas_call | solution.py:50
  24.6 3.8 %all-to-all-start.1 = ((bf16[16,48,512]{2,1,0:T(8,128)(2,1)}), bf16[16,48,512]{2,1,0:T(8,128)(2,1)S(1)}, u32[]{:S(2)}, u32[]{:S(2)}) async-start(bf16[16,48,512]{2,1,0:T(8,128)(2,1)} %bitcast.108), calls=%async_computation.1 | async-start | bytes 1572864 | tf_op jit(solution)/shard_map/all_to_all | solution.py:431
  28.4 0.1 collective-permute-start
  28.5 1.4 %collective-permute-done.refs_1_ = f32[1,768]{1,0:T(1,128)S(1)} collective-permute-done((f32[1,768]{1,0:T(1,128)}, f32[1,768]{1,0:T(1,128)S(1)}, u32[]{:S(2)}, u32[]{:S(2)}) %collective-permute-start) | collective-permute-done | bytes 3104 | tf_op jit(solution)/shard_map/ppermute | solution.py:389
  29.8 17.1 %all-to-all-done.1 = bf16[16,48,512]{2,1,0:T(8,128)(2,1)S(1)} async-done(((bf16[16,48,512]{2,1,0:T(8,128)(2,1)}), bf16[16,48,512]{2,1,0:T(8,128)(2,1)S(1)}, u32[]{:S(2)}, u32[]{:S(2)}) %all-to-all-start.1) | async-done | bytes 786464 | tf_op jit(solution)/shard_map/all_to_all | solution.py:431
  46.9 0.0 copy-start.1
  46.9 0.9 copy-done.1
  47.8 19.2 %shard_map.121 = (bf16[512,512]{1,0:T(8,128)(2,1)}, bf16[512,2048]{1,0:T(8,128)(2,1)}, bf16[512,640]{1,0:T(8,128)(2,1)}, bf16[512,768]{1,0:T(8,128)(2,1)}, bf16[...) custom-call(s32[1,8]{1,0:T(1,128)} %len_ref.1, f32[1,512]{1,0:T(1,128)} %get-tuple-element.22.slot_ref, ...), custom_call_target="tpu_custom_call" | custom-call | flops 5100273664 | bytes 6291456 | tf_op jit(solution)/shard_map/pallas_call | solution.py:50
  67.0 0.1 collective-permute-start.2
  67.1 0.5 collective-permute-start.1
  67.6 0.0 copy-start.3
  67.6 0.0 copy-start.2
  67.6 4.8 %shard_map.122.grad_ref = bf16[512,512]{1,0:T(8,128)(2,1)} custom-call(bf16[512,2048]{1,0:T(8,128)(2,1)} %get-tuple-element.30.gpre_hbm, bf16[512,2048]{1,0:T(8,128)(2,1)} %w_in_hbm.3, bf16[512,512]{1,0:T(8,128)(2,1)} %cot_ref.1), custom_call_target="tpu_custom_call" | custom-call | flops 1073741824 | bytes 5242880 | tf_op jit(solution)/shard_map/pallas_call | solution.py:50
  72.4 0.0 collective-permute-done.1
  72.4 0.0 copy-start.4
  72.4 0.0 copy-done.3
  72.4 0.9 fusion.2
  73.3 0.6 collective-permute-start.4
  73.9 0.0 collective-permute-done.2
  73.9 0.0 copy-done.2
  73.9 0.9 fusion
  74.8 1.6 %collective-permute-start.6 = (bf16[4,2,32,768]{3,2,1,0:T(8,128)(2,1)}, bf16[4,2,32,768]{3,2,1,0:T(8,128)(2,1)S(1)}, u32[]{:S(2)}, u32[]{:S(2)}) collective-permute-start(bf16[4,2,32,768]{3,2,1,0:T(8,128)(2,1)} %fusion), channel_id=1, source_target_pairs={{0,4},{2,6},{4,0},{6,2},{8,12},{10,14},{12,8},{14,10},{16,20},{18,... | collective-permute-start | bytes 1179656 | tf_op jit(solution)/shard_map/ppermute | solution.py:516
  76.3 2.4 %shard_map.123 = bf16[768,512]{1,0:T(8,128)(2,1)} custom-call(f32[1,512]{1,0:T(1,128)} %get-tuple-element.22.slot_ref, bf16[512,512]{1,0:T(8,128)(2,1)} %shard_map.122.grad_ref), custom_call_target="tpu_custom_call" | custom-call | flops 402653184 | bytes 1048576 | tf_op jit(solution)/shard_map/pallas_call | solution.py:50
  78.7 0.0 copy-done.4
  78.7 4.7 %all-to-all-start.2 = ((bf16[16,48,512]{2,1,0:T(8,128)(2,1)}), bf16[16,48,512]{2,1,0:T(8,128)(2,1)S(1)}, u32[]{:S(2)}, u32[]{:S(2)}) async-start(bf16[16,48,512]{2,1,0:T(8,128)(2,1)} %bitcast.106), calls=%async_computation.2 | async-start | bytes 1572864 | tf_op jit(solution)/shard_map/all_to_all | solution.py:547
  83.5 0.0 collective-permute-done.4
  83.5 1.7 %fusion.3 = bf16[4,32,640]{2,1,0:T(8,128)(2,1)} fusion(bf16[4,2,32,640]{3,2,1,0:T(8,128)(2,1)} %collective-permute-done.4, s32[]{:T(128)S(6)} %select_n.181, bf16[4,2,2,32,640]{4,3,2,1,0:T(8,128)(2,1)} %bitcast.122, s32[]{:T(128)S(6)} %select_n.189, s32[]{:T(128)S(6)} %select_n.188, bf16[4,2,2,32,640]{4,3,2,1,0:T(8,128)(2,1)S(1)} %bitcast.118), kind=kLoop, calls=%fused_computation.7 | loop fusion | flops 491520 | bytes 655372 | tf_op jit(solution)/shard_map/convert_element_type | solution.py:513
  85.2 0.0 copy-start
  85.2 1.9 %collective-permute-start.5 = (bf16[4,32,640]{2,1,0:T(8,128)(2,1)}, bf16[4,32,640]{2,1,0:T(8,128)(2,1)}, u32[]{:S(2)}, u32[]{:S(2)}) collective-permute-start(bf16[4,32,640]{2,1,0:T(8,128)(2,1)} %fusion.3), channel_id=1, source_target_pairs={{0,4},{2,6},{4,0},{6,2},{8,12},{10,14},{12,8},{14,10},{16,20},{18,... | collective-permute-start | bytes 491528 | tf_op jit(solution)/shard_map/ppermute | solution.py:516
  87.1 1.4 %collective-permute-done.6 = bf16[4,2,32,768]{3,2,1,0:T(8,128)(2,1)S(1)} collective-permute-done((bf16[4,2,32,768]{3,2,1,0:T(8,128)(2,1)}, bf16[4,2,32,768]{3,2,1,0:T(8,128)(2,1)S(1)}, u32[]{:S(2)}, u32[]{:S(2)}) %collective-permute-start.6) | collective-permute-done | bytes 393248 | tf_op jit(solution)/shard_map/ppermute | solution.py:516
  88.5 0.8 fusion.1
  89.3 1.7 %collective-permute-start.7 = (bf16[4,32,768]{2,1,0:T(8,128)(2,1)}, bf16[4,32,768]{2,1,0:T(8,128)(2,1)}, u32[]{:S(2)}, u32[]{:S(2)}) collective-permute-start(bf16[4,32,768]{2,1,0:T(8,128)(2,1)} %fusion.1), channel_id=1, source_target_pairs={{0,2},{2,0},{4,6},{6,4},{8,10},{10,8},{12,14},{14,12},{16,18},{18,... | collective-permute-start | bytes 589832 | tf_op jit(solution)/shard_map/ppermute | solution.py:516
  91.0 4.4 %collective-permute-done.5 = bf16[4,32,640]{2,1,0:T(8,128)(2,1)} collective-permute-done((bf16[4,32,640]{2,1,0:T(8,128)(2,1)}, bf16[4,32,640]{2,1,0:T(8,128)(2,1)}, u32[]{:S(2)}, u32[]{:S(2)}) %collective-permute-start.5) | collective-permute-done | bytes 163872 | tf_op jit(solution)/shard_map/ppermute | solution.py:516
  95.4 1.0 fusion.12
  96.4 2.3 %collective-permute-done.7 = bf16[4,32,768]{2,1,0:T(8,128)(2,1)} collective-permute-done((bf16[4,32,768]{2,1,0:T(8,128)(2,1)}, bf16[4,32,768]{2,1,0:T(8,128)(2,1)}, u32[]{:S(2)}, u32[]{:S(2)}) %collective-permute-start.7) | collective-permute-done | bytes 196640 | tf_op jit(solution)/shard_map/ppermute | solution.py:516
  98.7 0.9 fusion.9
  99.7 1.7 %collective-permute-start.9 = (bf16[32,1408]{1,0:T(8,128)(2,1)S(1)}, bf16[32,1408]{1,0:T(8,128)(2,1)}, u32[]{:S(2)}, u32[]{:S(2)}) collective-permute-start(bf16[32,1408]{1,0:T(8,128)(2,1)S(1)} %pad_maximum_fusion.2), channel_id=1, source_target_pairs={{0,16},{2,18},{4,20},{6,22},{8,24},{10,26},{12,28},{14,30},{16,0},... | collective-permute-start | bytes 270344 | tf_op jit(solution)/shard_map/ppermute | solution.py:530
  101.4 0.6 pad_maximum_fusion.3
  102.0 1.0 collective-permute-start.10
  103.1 0.6 pad_maximum_fusion.1
  103.7 1.0 collective-permute-start.8
  104.7 4.4 %collective-permute-done.9 = bf16[32,1408]{1,0:T(8,128)(2,1)} collective-permute-done((bf16[32,1408]{1,0:T(8,128)(2,1)S(1)}, bf16[32,1408]{1,0:T(8,128)(2,1)}, u32[]{:S(2)}, u32[]{:S(2)}) %collective-permute-start.9) | collective-permute-done | bytes 90144 | tf_op jit(solution)/shard_map/ppermute | solution.py:530
  109.1 0.0 collective-permute-done.10
  109.1 1.3 %collective-permute-done.8 = bf16[32,1408]{1,0:T(8,128)(2,1)} collective-permute-done((bf16[32,1408]{1,0:T(8,128)(2,1)}, bf16[32,1408]{1,0:T(8,128)(2,1)}, u32[]{:S(2)}, u32[]{:S(2)}) %collective-permute-start.8) | collective-permute-done | bytes 90144 | tf_op jit(solution)/shard_map/ppermute | solution.py:530
  110.4 0.9 fusion.6
  111.4 0.0 all-to-all-done.2
  111.4 0.1 collective-permute-start.3
  111.5 0.5 collective-permute-start.11
  112.0 0.9 fusion.15
  112.9 0.7 pad_maximum_fusion
  113.5 0.6 slice_reduce_fusion
  114.2 0.0 collective-permute-done.11
  114.2 0.6 pad_maximum_fusion.4
  114.8 0.0 collective-permute-done.3.refs_3_
  114.8 0.0 copy-done
  114.8 2.7 %shard_map.124 = f32[1024,512]{1,0:T(8,128)} custom-call(f32[1,768]{1,0:T(1,128)S(1)} %copy-done, f32[1,768]{1,0:T(1,128)S(1)} %collective-permute-done.refs_1_, bf16[768,512]{1,0:T(8,128)(2,1)S(1)} %bitcast.105, bf16[768,512]{1,0:T(8,128)(2,1)S(1)} %collective-permute-done.3.refs_3_), custom_call_target="tpu_custom_call" | custom-call | flops 1610612736 | bytes 3670016 | tf_op jit(solution)/shard_map/pallas_call | solution.py:50
  (3 shorter events, 0.0 us)
Async XLA Ops:
  24.6 22.4 %all-to-all-start.1 = ((bf16[16,48,512]{2,1,0:T(8,128)(2,1)}), bf16[16,48,512]{2,1,0:T(8,128)(2,1)S(1)}, u32[]{:S(2)}, u32[]{:S(2)}) async-start(bf16[16,48,512]{2,1,0:T(8,128)(2,1)} %bitcast.108), calls=%async_computation.1 | async-start | bytes 1572864 | tf_op jit(solution)/shard_map/all_to_all | solution.py:431
  28.4 1.4 %collective-permute-start = (f32[1,768]{1,0:T(1,128)}, f32[1,768]{1,0:T(1,128)S(1)}, u32[]{:S(2)}, u32[]{:S(2)}) collective-permute-start(f32[1,768]{1,0:T(1,128)} %get-tuple-element.28.refs_0_), channel_id=1, source_target_pairs={{0,1},{1,0},{2,3},{3,2},{4,5},{5,4},{6,7},{7,6},{8,9},{9,8},{10,11... | collective-permute-start | bytes 9224 | tf_op jit(solution)/shard_map/ppermute | solution.py:389
  46.9 0.9 copy-start.1
  67.0 6.9 %collective-permute-start.2 = (bf16[512,768]{1,0:T(8,128)(2,1)}, bf16[512,768]{1,0:T(8,128)(2,1)S(1)}, u32[]{:S(2)}, u32[]{:S(2)}) collective-permute-start(bf16[512,768]{1,0:T(8,128)(2,1)} %get-tuple-element.35), channel_id=1, source_target_pairs={{0,1},{1,0},{2,3},{3,2},{4,5},{5,4},{6,7},{7,6},{8,9},{9,8},{10,11... | collective-permute-start | bytes 2359304 | tf_op jit(solution)/shard_map/ppermute | solution.py:389
  67.1 5.3 %collective-permute-start.1 = (bf16[512,640]{1,0:T(8,128)(2,1)}, bf16[512,640]{1,0:T(8,128)(2,1)S(1)}, u32[]{:S(2)}, u32[]{:S(2)}) collective-permute-start(bf16[512,640]{1,0:T(8,128)(2,1)} %get-tuple-element.32), channel_id=1, source_target_pairs={{0,1},{1,0},{2,3},{3,2},{4,5},{5,4},{6,7},{7,6},{8,9},{9,8},{10,11... | collective-permute-start | bytes 1966088 | tf_op jit(solution)/shard_map/ppermute | solution.py:389
  67.6 4.8 %copy-start.3 = (bf16[512,640]{1,0:T(8,128)(2,1)S(1)}, bf16[512,640]{1,0:T(8,128)(2,1)}, u32[]{:S(2)}) copy-start(bf16[512,640]{1,0:T(8,128)(2,1)} %get-tuple-element.31) | copy-start | bytes 1966084
  67.6 6.3 %copy-start.2 = (bf16[512,768]{1,0:T(8,128)(2,1)S(1)}, bf16[512,768]{1,0:T(8,128)(2,1)}, u32[]{:S(2)}) copy-start(bf16[512,768]{1,0:T(8,128)(2,1)} %get-tuple-element.34) | copy-start | bytes 2359300
  72.4 6.3 %copy-start.4 = (bf16[512,640]{1,0:T(8,128)(2,1)}, bf16[512,640]{1,0:T(8,128)(2,1)S(1)}, u32[]{:S(2)}) copy-start(bf16[512,640]{1,0:T(8,128)(2,1)S(1)} %collective-permute-done.1) | copy-start | bytes 1966084
  73.3 10.1 %collective-permute-start.4 = (bf16[4,2,32,640]{3,2,1,0:T(8,128)(2,1)}, bf16[4,2,32,640]{3,2,1,0:T(8,128)(2,1)}, u32[]{:S(2)}, u32[]{:S(2)}) collective-permute-start(bf16[4,2,32,640]{3,2,1,0:T(8,128)(2,1)} %fusion.2), channel_id=1, source_target_pairs={{0,2},{2,0},{4,6},{6,4},{8,10},{10,8},{12,14},{14,12},{16,18},{18,... | collective-permute-start | bytes 983048 | tf_op jit(solution)/shard_map/ppermute | solution.py:516
  74.8 13.8 %collective-permute-start.6 = (bf16[4,2,32,768]{3,2,1,0:T(8,128)(2,1)}, bf16[4,2,32,768]{3,2,1,0:T(8,128)(2,1)S(1)}, u32[]{:S(2)}, u32[]{:S(2)}) collective-permute-start(bf16[4,2,32,768]{3,2,1,0:T(8,128)(2,1)} %fusion), channel_id=1, source_target_pairs={{0,4},{2,6},{4,0},{6,2},{8,12},{10,14},{12,8},{14,10},{16,20},{18,... | collective-permute-start | bytes 1179656 | tf_op jit(solution)/shard_map/ppermute | solution.py:516
  78.7 32.6 %all-to-all-start.2 = ((bf16[16,48,512]{2,1,0:T(8,128)(2,1)}), bf16[16,48,512]{2,1,0:T(8,128)(2,1)S(1)}, u32[]{:S(2)}, u32[]{:S(2)}) async-start(bf16[16,48,512]{2,1,0:T(8,128)(2,1)} %bitcast.106), calls=%async_computation.2 | async-start | bytes 1572864 | tf_op jit(solution)/shard_map/all_to_all | solution.py:547
  85.2 29.6 %copy-start = (f32[1,768]{1,0:T(1,128)S(1)}, f32[1,768]{1,0:T(1,128)}, u32[]{:S(2)}) copy-start(f32[1,768]{1,0:T(1,128)} %get-tuple-element.28.refs_0_) | copy-start | bytes 9220
  85.2 10.2 %collective-permute-start.5 = (bf16[4,32,640]{2,1,0:T(8,128)(2,1)}, bf16[4,32,640]{2,1,0:T(8,128)(2,1)}, u32[]{:S(2)}, u32[]{:S(2)}) collective-permute-start(bf16[4,32,640]{2,1,0:T(8,128)(2,1)} %fusion.3), channel_id=1, source_target_pairs={{0,4},{2,6},{4,0},{6,2},{8,12},{10,14},{12,8},{14,10},{16,20},{18,... | collective-permute-start | bytes 491528 | tf_op jit(solution)/shard_map/ppermute | solution.py:516
  89.3 9.4 %collective-permute-start.7 = (bf16[4,32,768]{2,1,0:T(8,128)(2,1)}, bf16[4,32,768]{2,1,0:T(8,128)(2,1)}, u32[]{:S(2)}, u32[]{:S(2)}) collective-permute-start(bf16[4,32,768]{2,1,0:T(8,128)(2,1)} %fusion.1), channel_id=1, source_target_pairs={{0,2},{2,0},{4,6},{6,4},{8,10},{10,8},{12,14},{14,12},{16,18},{18,... | collective-permute-start | bytes 589832 | tf_op jit(solution)/shard_map/ppermute | solution.py:516
  99.7 9.4 %collective-permute-start.9 = (bf16[32,1408]{1,0:T(8,128)(2,1)S(1)}, bf16[32,1408]{1,0:T(8,128)(2,1)}, u32[]{:S(2)}, u32[]{:S(2)}) collective-permute-start(bf16[32,1408]{1,0:T(8,128)(2,1)S(1)} %pad_maximum_fusion.2), channel_id=1, source_target_pairs={{0,16},{2,18},{4,20},{6,22},{8,24},{10,26},{12,28},{14,30},{16,0},... | collective-permute-start | bytes 270344 | tf_op jit(solution)/shard_map/ppermute | solution.py:530
  102.0 7.1 %collective-permute-start.10 = (bf16[32,1408]{1,0:T(8,128)(2,1)}, bf16[32,1408]{1,0:T(8,128)(2,1)}, u32[]{:S(2)}, u32[]{:S(2)}) collective-permute-start(bf16[32,1408]{1,0:T(8,128)(2,1)} %pad_maximum_fusion.3), channel_id=1, source_target_pairs={{0,24},{2,26},{4,28},{6,30},{8,0},{10,2},{12,4},{14,6},{16,8},{18,... | collective-permute-start | bytes 270344 | tf_op jit(solution)/shard_map/ppermute | solution.py:530
  103.7 6.8 %collective-permute-start.8 = (bf16[32,1408]{1,0:T(8,128)(2,1)}, bf16[32,1408]{1,0:T(8,128)(2,1)}, u32[]{:S(2)}, u32[]{:S(2)}) collective-permute-start(bf16[32,1408]{1,0:T(8,128)(2,1)} %pad_maximum_fusion.1), channel_id=1, source_target_pairs={{0,8},{2,10},{4,12},{6,14},{8,16},{10,18},{12,20},{14,22},{16,24},... | collective-permute-start | bytes 270344 | tf_op jit(solution)/shard_map/ppermute | solution.py:530
  111.4 3.5 %collective-permute-start.3 = (bf16[768,512]{1,0:T(8,128)(2,1)S(1)}, bf16[768,512]{1,0:T(8,128)(2,1)S(1)}, u32[]{:S(2)}, u32[]{:S(2)}) collective-permute-start(bf16[768,512]{1,0:T(8,128)(2,1)S(1)} %bitcast.104), channel_id=1, source_target_pairs={{0,1},{1,0},{2,3},{3,2},{4,5},{5,4},{6,7},{7,6},{8,9},{9,8},{10,11... | collective-permute-start | bytes 2359304 | tf_op jit(solution)/shard_map/ppermute | solution.py:389
  111.5 2.7 %collective-permute-start.11 = (f32[32,256]{1,0:T(8,128)S(1)}, f32[32,256]{1,0:T(8,128)S(1)}, u32[]{:S(2)}, u32[]{:S(2)}) collective-permute-start(f32[32,256]{1,0:T(8,128)S(1)} %get-tuple-element.45), channel_id=1, source_target_pairs={{0,1},{1,0},{2,3},{3,2},{4,5},{5,4},{6,7},{7,6},{8,9},{9,8},{10,11... | collective-permute-start | bytes 98312 | tf_op jit(solution)/shard_map/ppermute | solution.py:389

commit v5 on v4

--- a/solution.py
+++ b/solution.py
@@ -76,20 +76,10 @@
     req_ref[...] = found.astype(jnp.int32)
 
 
-def lookup_kernel(cap, wanted_ref, table_hbm, found_hbm, ids_ref, table_ref, found_ref, pick_ref, sems):
+def lookup_kernel(cap, wanted_ref, table_ref, found_ref, ids_ref):
     owners, width = wanted_ref.shape
     slots = found_ref.shape[0]
     rows = table_ref.shape[0]
-    half_width = table_ref.shape[1] // 2
-    halves = [pl.ds(i * half_width, half_width) for i in range(2)]
-    fetches = []
-    for i, half in enumerate(halves):
-        for j in range(2):
-            at = (pl.ds(j * (rows // 2), rows // 2), half)
-            fetches.append(
-                pltpu.make_async_copy(table_hbm.at[at], table_ref.at[at], sems.at[2 * i + j])
-            )
-            fetches[-1].start()
     wanted = wanted_ref[...]
     high = (wanted >> 8).astype(F32).astype(BF16)
     low = (wanted & 255).astype(F32).astype(BF16)
@@ -104,21 +94,11 @@
     )
     wide = jnp.broadcast_to(ids, (slots, LANES))
     ids_ref[...] = wide.T[0:1, :]
-    step = row_step(slots)
+    step = 256 if slots % 256 == 0 else slots
     for start in range(0, slots, step):
         part = ids[start : start + step]
-        pick_ref[start : start + step, :] = hot(iota((step, rows), 1).astype(F32) == part)
-    stores = []
-    for i, half in enumerate(halves):
-        for fetch in fetches[2 * i : 2 * i + 2]:
-            fetch.wait()
-        found_ref[:, half] = dot_nn(pick_ref[...], table_ref[:, half]).astype(BF16)
-        stores.append(
-            pltpu.make_async_copy(found_ref.at[:, half], found_hbm.at[:, half], sems.at[4 + i])
-        )
-        stores[-1].start()
-    for store in stores:
-        store.wait()
+        pick = hot(iota((step, rows), 1).astype(F32) == part)
+        found_ref[start : start + step, :] = dot_nn(pick, table_ref[...]).astype(BF16)
 
 
 def collect_kernel(groups, *refs):
@@ -165,13 +145,14 @@
     cot_hbm,
     *rest,
 ):
-    result_hbm, gpre_hbm = rest[:2]
+    result_hbm, row_hbm = rest[:2]
     grads_hbms = rest[2 : 2 + 2 * groups]
     (
     w_in_ref,
     w_out_ref,
     cot_ref,
     result_ref,
+    row_ref,
     grads_ref,
     pick_ref,
     emb_ref,
@@ -318,12 +299,6 @@
     lax.fori_loop(0, slabs, backward, 0)
 
     puts = [put_result]
-    for i, part in enumerate(parts):
-        puts.append(
-            pltpu.make_async_copy(gpre_ref.at[:, part], gpre_hbm.at[:, part], sems.at[7 + i])
-        )
-        puts[-1].start()
-
     me = lax.axis_index("group")
     emb_t = emb_ref[...].T
     cols_in = 4 * width // groups
@@ -341,33 +316,17 @@
         cut = grads_hbms[2 * k].shape[1]
         for i, cols in enumerate((pl.ds(0, cut), pl.ds(cut, grads_ref.shape[2] - cut))):
             put = pltpu.make_async_copy(
-                grads_ref.at[k, :, cols], grads_hbms[2 * k + i], sems.at[11 + 2 * k + i]
+                grads_ref.at[k, :, cols], grads_hbms[2 * k + i], sems.at[8 + 2 * k + i]
             )
             put.start()
             puts.append(put)
+    row_ref[...] = (
+        cot_ref[...].astype(F32) + dot_nt(gpre_ref[...], w_in_ref[...])
+    ).astype(BF16)
+    puts.append(pltpu.make_async_copy(row_ref, row_hbm, sems.at[7]))
+    puts[-1].start()
     for put in puts:
         put.wait()
-
-
-def row_grad_kernel(gpre_hbm, w_in_hbm, cot_ref, out_ref, gpre_ref, w_in_ref, sems):
-    width = cot_ref.shape[1]
-    fetches = []
-    for i in range(4):
-        cols = pl.ds(i * width, width)
-        pair = (
-            pltpu.make_async_copy(gpre_hbm.at[:, cols], gpre_ref.at[:, cols], sems.at[2 * i]),
-            pltpu.make_async_copy(w_in_hbm.at[:, cols], w_in_ref.at[:, cols], sems.at[2 * i + 1]),
-        )
-        for fetch in pair:
-            fetch.start()
-        fetches.append(pair)
-    total = cot_ref[...].astype(F32)
-    for i in range(4):
-        for fetch in fetches[i]:
-            fetch.wait()
-        cols = slice(i * width, (i + 1) * width)
-        total = total + dot_nt(gpre_ref[:, cols], w_in_ref[:, cols])
-    out_ref[...] = total.astype(BF16)
 
 
 def slots_kernel(slot_ref, grad_ref, out_hbm, out_ref, sems):
@@ -385,6 +344,30 @@
         store.wait()
 
 
+def plane_kernel(outer, terms, *refs):
+    left, right, outs = refs[:terms], refs[terms : 2 * terms], refs[2 * terms :]
+    cut = left[0].shape[2]
+    high = lax.div(lax.axis_index("table"), lax.axis_size("table") // outer)
+    for k in range(outer):
+        at = lax.rem(high + k, outer)
+        for parts, cols in ((left, slice(0, cut)), (right, slice(cut, None))):
+            total = parts[0][at].astype(F32)
+            for part in parts[1:]:
+                total = total + part[at].astype(F32)
+            outs[k][:, cols] = total.astype(outs[k].dtype)
+
+
+def finish_kernel(kept_ref, *refs):
+    got_refs, (in_ref, out_ref, gain_ref) = refs[:-3], refs[-3:]
+    total = kept_ref[...]
+    for got_ref in got_refs:
+        total = total + got_ref[...].astype(F32)
+    cols_in, cols_out = in_ref.shape[1], out_ref.shape[1]
+    in_ref[...] = total[:, :cols_in]
+    out_ref[...] = total[:, cols_in : cols_in + cols_out]
+    gain_ref[...] = total[:, cols_in + cols_out :].T[0:1, :]
+
+
 def shift(value, axis, size, amount):
     return lax.ppermute(value, axis, [(i, (i + amount) % size) for i in range(size)])
 
@@ -419,14 +402,6 @@
         2 * slots * table.shape[0] * width,
         2 * (slots + table.shape[0]) * width,
         (wanted, table),
-        far=(1,),
-        far_out=(0,),
-        scratch=[
-            pltpu.VMEM(table.shape, BF16),
-            pltpu.VMEM((slots, width), BF16),
-            pltpu.VMEM((slots, table.shape[0]), BF16),
-            pltpu.SemaphoreType.DMA((6,)),
-        ],
     )
     returned = lax.all_to_all(found, "table", split_axis=0, concat_axis=0, tiled=True)
     all_ids = [ids] + [shift(ids, "group", groups, k) for k in range(1, groups)]
@@ -438,18 +413,18 @@
     cols_all = cols_in + cols_out + LANES
     cut = cols_all // LANES // 2 * LANES
     square = pltpu.VMEM((count, width), BF16)
-    result, gpre, *grads = call(
+    result, row_grad, *grads = call(
         functools.partial(layer_kernel, groups, wparts),
         [
             jax.ShapeDtypeStruct((count, width), BF16),
-            jax.ShapeDtypeStruct((count, 4 * width), BF16),
+            jax.ShapeDtypeStruct((count, width), BF16),
             *[
                 jax.ShapeDtypeStruct((width, cols), BF16)
                 for _ in range(groups)
                 for cols in (cut, cols_all - cut)
             ],
         ],
-        24 * count * width * width + 14 * count * count * width,
+        32 * count * width * width + 14 * count * count * width,
         24 * count * width,
         (lengths, slot, returned, w_in, w_out, gain.reshape(1, width), cotangent),
         smem=(0,),
@@ -458,6 +433,7 @@
         scratch=[
             pltpu.VMEM(w_in.shape, BF16),
             pltpu.VMEM(w_out.shape, BF16),
+            square,
             square,
             square,
             pltpu.VMEM((groups, width, cols_all), BF16),
@@ -475,23 +451,9 @@
             pltpu.VMEM((count, LANES), F32),
             pltpu.VMEM((count, LANES), F32),
             pltpu.VMEM((width, width), BF16),
-            pltpu.SemaphoreType.DMA((11 + 2 * groups,)),
-        ],
-    )
-    (row_grad,) = call(
-        row_grad_kernel,
-        [jax.ShapeDtypeStruct((count, width), BF16)],
-        8 * count * width * width,
-        20 * count * width,
-        (gpre, w_in, cotangent),
-        far=(0, 1),
-        scratch=[
-            pltpu.VMEM((count, 4 * width), BF16),
-            pltpu.VMEM(w_in.shape, BF16),
-            pltpu.SemaphoreType.DMA((8,)),
-        ],
-    )
-
+            pltpu.SemaphoreType.DMA((8 + 2 * groups,)),
+        ],
+    )
     rows = width // owners
     side = 2 if owners % 4 == 0 else 1
     plane = side * side
@@ -514,7 +476,7 @@
         if tie is not None:
             tie, send = lax.optimization_barrier((tie, send))
         got = lax.ppermute(send, "table", [(i, i ^ bit) for i in range(owners)])
-        return [entry(term, index, axis) for term in terms] + [got], tie
+        return [add([entry(term, index, axis) for term in terms]), got], tie
 
     if side == 2:
         left, row_grad = halve(sides[0], low, 2, 1, row_grad)
@@ -523,14 +485,26 @@
         right, _ = halve(right, low, 1, 1)
     else:
         left, right = [[term[:, 0, 0] for term in terms] for terms in sides]
-    sums = [[add([entry(term, high, 0) for term in terms])] for terms in (left, right)]
-    for k in range(1, outer):
-        perm = [(i, ((i // plane + k) % outer) * plane + i % plane) for i in range(owners)]
-        send = [add([entry(term, (high + k) % outer, 0) for term in terms]) for terms in (left, right)]
-        got = lax.ppermute(jnp.concatenate(send, 1).astype(BF16), "table", perm)
-        sums[0].append(got[:, :cut])
-        sums[1].append(got[:, cut:])
-    summed = jnp.concatenate([add(terms) for terms in sums], 1)
+    cols = cols_all
+    kept, *sends = call(
+        functools.partial(plane_kernel, outer, len(left)),
+        [
+            jax.ShapeDtypeStruct((rows, cols), F32),
+            *[jax.ShapeDtypeStruct((rows, cols), BF16) for _ in range(1, outer)],
+        ],
+        12 * outer * rows * cols,
+        8 * outer * rows * cols,
+        (*left, *right),
+        limit=24,
+    )
+    got = [
+        lax.ppermute(
+            sends[k - 1],
+            "table",
+            [(i, ((i // plane + k) % outer) * plane + i % plane) for i in range(owners)],
+        )
+        for k in range(1, outer)
+    ]
 
     (outgoing,) = call(
         slots_kernel,
@@ -563,8 +537,19 @@
         ],
     )
 
-    w_in_grad = summed[:, :cols_in]
-    mine = summed[:, cols_in : cols_in + cols_out]
+    kept, table_grad = lax.optimization_barrier((kept, table_grad))
+    w_in_grad, mine, gain_grad = call(
+        finish_kernel,
+        [
+            jax.ShapeDtypeStruct((rows, cols_in), F32),
+            jax.ShapeDtypeStruct((rows, cols_out), F32),
+            jax.ShapeDtypeStruct((1, rows), F32),
+        ],
+        4 * rows * cols_all,
+        14 * rows * cols_all,
+        (kept, *got),
+        limit=24,
+    )
     pieces = jnp.stack([mine] + [shift(mine, "group", groups, k) for k in range(1, groups)])
     w_out_grad = jnp.concatenate(
         [
@@ -573,8 +558,7 @@
         ],
         1,
     )
-    gain_grad = summed[:, cols_in + cols_out]
-    return (result, table_grad, w_in_grad, w_out_grad, gain_grad)
+    return (result, table_grad, w_in_grad, w_out_grad, gain_grad.reshape(rows))
 
 
 def solution(mesh):

time: 119 us -> 128 us (1.076)
  waiting for transfers between devices: 32.3 us -> 52.8 us
  Pallas kernels: 37.5 us -> 31.7 us
  other arithmetic: 10.7 us -> 6.16 us
    all_to_all x1, waiting for transfers between devices: 0.01 us -> 18 us  [on_device(): lax.all_to_all(outgoing, 'table', split_axis=0, concat_axis=0, tiled=True)]
    pallas_call x6 -> x7, Pallas kernels: 37.5 us -> 31.7 us  [call(): pl.pallas_call(kernel, out_shape=out_shape, in_specs=[pl.BlockSpec(memory...]
    ppermute x5, waiting for transfers between devices: 1.37 us -> 5.49 us  [shift(): lax.ppermute(value, axis, [(i, (i + amount) % size) for i in range(size)])]
    ppermute x3, waiting for transfers between devices: 5.73 us -> 2.11 us  [on_device(): lax.ppermute(sends[k - 1], 'table', [(i, (i // plane + k) % outer * plane...]
    concatenate x4 -> x0, other arithmetic: 1.96 us -> none  [the longest x3 1.29 us: on_device(): got = lax.ppermute(jnp.concatenate(send, 1).astype(BF16), 'table', perm)]
    ppermute x4, waiting for transfers between devices: 8.13 us -> 10.1 us  [halve(): got = lax.ppermute(send, 'table', [(i, i ^ bit) for i in range(owners)])]
    another operation x2 -> x0, other arithmetic: 1.94 us -> none
  transfers between devices with their start and end apart: 14 -> 14, of which waited for: 7 -> 8; matrix products, arithmetic and copies ran while one was open for 10% -> 3% of each run, Pallas kernels for 6% -> 2%
where the time goes in v5:
time: 128 us; the launch traced here: 127 us
  waiting for transfers between devices  52.8 us (41%)
  Pallas kernels  31.7 us (25%)
  starting transfers between devices  19.5 us (15%)
  blocking collectives  15.6 us (12%)
  other arithmetic  6.16 us (5%)
    pallas_call x7, Pallas kernels, call(): pl.pallas_call(kernel, out_shape=out_shape, in_specs=[pl.BlockSpec(memory...  31.7 us
    all_to_all x1, waiting for transfers between devices, on_device(): lax.all_to_all(outgoing, 'table', split_axis=0, concat_axis=0, tiled=True)  18 us
    all_to_all x1, waiting for transfers between devices, on_device(): lax.all_to_all(found, 'table', split_axis=0, concat_axis=0, tiled=True)  17 us
    all_to_all x1, blocking collectives, on_device(): lax.all_to_all(requested, 'table', split_axis=0, concat_axis=0, tiled=True)  15.6 us
    ppermute x4, waiting for transfers between devices, halve(): got = lax.ppermute(send, 'table', [(i, i ^ bit) for i in range(owners)])  10.1 us
    ppermute x4, starting transfers between devices, halve(): got = lax.ppermute(send, 'table', [(i, i ^ bit) for i in range(owners)])  5.75 us
    ppermute x5, waiting for transfers between devices, shift(): lax.ppermute(value, axis, [(i, (i + amount) % size) for i in range(size)])  5.49 us
    all_to_all x1, starting transfers between devices, on_device(): lax.all_to_all(outgoing, 'table', split_axis=0, concat_axis=0, tiled=True)  4.78 us
  transfers between devices with their start and end apart: 14, of which 8 were waited for; matrix products, arithmetic and copies ran while one was open for 3% of the time, Pallas kernels for 2%

profile of v5, /device:TPU:0, one launch (start us, length us, event | category | flops | bytes accessed | tf_op | source)
XLA Modules:
  0.0 127.5 jit_solution(6465648761430393459)
XLA Ops:
  0.6 1.7 %shard_map.119 = (s32[16,128]{1,0:T(8,128)}, f32[1,512]{1,0:T(1,128)}) custom-call(s32[1,512]{1,0:T(1,128)} %bitcast.71, s32[1,512]{1,0:T(1,128)} %bitcast.72), custom_call_target="tpu_custom_call" | custom-call | flops 16777216 | bytes 4096 | tf_op jit(solution)/shard_map/pallas_call | solution.py:50
  2.3 15.6 %all_to_all.34 = s32[16,1,128]{2,1,0:T(1,128)} all-to-all(s32[16,1,128]{2,1,0:T(1,128)} %bitcast.70), channel_id=1, replica_groups=mesh['table'=16,'group'=2] {'table'}, dimensions={0} | all-to-all | bytes 16384 | tf_op jit(solution)/shard_map/all_to_all | solution.py:395
  17.9 4.5 %shard_map.120 = (bf16[768,512]{1,0:T(8,128)(2,1)}, f32[1,768]{1,0:T(1,128)}) custom-call(s32[16,128]{1,0:T(8,128)} %bitcast.69, bf16[2048,512]{1,0:T(8,128)(2,1)} %table_ref.1), custom_call_target="tpu_custom_call" | custom-call | flops 1610612736 | bytes 2883584 | tf_op jit(solution)/shard_map/pallas_call | solution.py:50
  22.4 3.6 %all-to-all-start.1 = ((bf16[16,48,512]{2,1,0:T(8,128)(2,1)}), bf16[16,48,512]{2,1,0:T(8,128)(2,1)S(1)}, u32[]{:S(2)}, u32[]{:S(2)}) async-start(bf16[16,48,512]{2,1,0:T(8,128)(2,1)} %bitcast.58), calls=%async_computation.1 | async-start | bytes 1572864 | tf_op jit(solution)/shard_map/all_to_all | solution.py:406
  26.0 0.1 collective-permute-start
  26.1 1.4 %collective-permute-done.refs_1_ = f32[1,768]{1,0:T(1,128)S(1)} collective-permute-done((f32[1,768]{1,0:T(1,128)}, f32[1,768]{1,0:T(1,128)S(1)}, u32[]{:S(2)}, u32[]{:S(2)}) %collective-permute-start) | collective-permute-done | bytes 3104 | tf_op jit(solution)/shard_map/ppermute | solution.py:372
  27.4 17.0 %all-to-all-done.1 = bf16[16,48,512]{2,1,0:T(8,128)(2,1)S(1)} async-done(((bf16[16,48,512]{2,1,0:T(8,128)(2,1)}), bf16[16,48,512]{2,1,0:T(8,128)(2,1)S(1)}, u32[]{:S(2)}, u32[]{:S(2)}) %all-to-all-start.1) | async-done | bytes 786464 | tf_op jit(solution)/shard_map/all_to_all | solution.py:406
  44.5 0.0 copy-start.1
  44.5 0.9 copy-done.1
  45.4 19.6 %shard_map.121 = (bf16[512,512]{1,0:T(8,128)(2,1)}, bf16[512,512]{1,0:T(8,128)(2,1)}, bf16[512,640]{1,0:T(8,128)(2,1)}, bf16[512,768]{1,0:T(8,128)(2,1)}, bf16[5...) custom-call(s32[1,8]{1,0:T(1,128)} %len_ref.1, f32[1,512]{1,0:T(1,128)} %get-tuple-element.31.slot_ref, ...), custom_call_target="tpu_custom_call" | custom-call | flops 6174015488 | bytes 6291456 | tf_op jit(solution)/shard_map/pallas_call | solution.py:50
  65.0 0.1 collective-permute-start.4
  65.1 0.5 collective-permute-start.1
  65.6 2.9 %collective-permute-done.1 = bf16[512,640]{1,0:T(8,128)(2,1)S(1)} collective-permute-done((bf16[512,640]{1,0:T(8,128)(2,1)}, bf16[512,640]{1,0:T(8,128)(2,1)S(1)}, u32[]{:S(2)}, u32[]{:S(2)}) %collective-permute-start.1) | collective-permute-done | bytes 655392 | tf_op jit(solution)/shard_map/ppermute | solution.py:372
  68.5 0.0 copy-start.3
  68.5 2.0 %fusion.3 = bf16[4,2,32,640]{3,2,0,1:T(8,128)(2,1)} fusion(bf16[4,2,2,32,640]{4,3,2,1,0:T(8,128)(2,1)} %bitcast.64, s32[]{:T(128)S(6)} %select_n.65, bf16[4,2,2,32,640]{4,3,2,1,0:T(8,128)(2,1)S(1)} %bitcast.66), kind=kLoop, calls=%fused_computation.9 | loop fusion | flops 655360 | bytes 984064 | tf_op jit(solution)/shard_map/convert_element_type | solution.py:475
  70.5 0.0 collective-permute-done.4
  70.5 1.1 fusion
  71.7 0.0 copy-start.2
  71.7 2.4 %shard_map.123 = bf16[768,512]{1,0:T(8,128)(2,1)} custom-call(f32[1,512]{1,0:T(1,128)} %get-tuple-element.31.slot_ref, bf16[512,512]{1,0:T(8,128)(2,1)} %get-tuple-element.48.grad_ref), custom_call_target="tpu_custom_call" | custom-call | flops 402653184 | bytes 1048576 | tf_op jit(solution)/shard_map/pallas_call | solution.py:50
  74.1 0.0 copy-done.3
  74.1 4.8 %all-to-all-start.2 = ((bf16[16,48,512]{2,1,0:T(8,128)(2,1)}), bf16[16,48,512]{2,1,0:T(8,128)(2,1)S(1)}, u32[]{:S(2)}, u32[]{:S(2)}) async-start(bf16[16,48,512]{2,1,0:T(8,128)(2,1)} %bitcast.59), calls=%async_computation.2 | async-start | bytes 1572864 | tf_op jit(solution)/shard_map/all_to_all | solution.py:521
  78.9 2.0 %collective-permute-start.5 = (bf16[4,2,32,768]{3,2,0,1:T(8,128)(2,1)S(1)}, bf16[4,2,32,768]{3,2,0,1:T(8,128)(2,1)}, u32[]{:S(2)}, u32[]{:S(2)}) collective-permute-start(bf16[4,2,32,768]{3,2,0,1:T(8,128)(2,1)S(1)} %fusion), channel_id=1, source_target_pairs={{0,4},{2,6},{4,0},{6,2},{8,12},{10,14},{12,8},{14,10},{16,20},{18,... | collective-permute-start | bytes 1179656 | tf_op jit(solution)/shard_map/ppermute | solution.py:478
  80.9 18.0 %all-to-all-done.2 = bf16[16,48,512]{2,1,0:T(8,128)(2,1)S(1)} async-done(((bf16[16,48,512]{2,1,0:T(8,128)(2,1)}), bf16[16,48,512]{2,1,0:T(8,128)(2,1)S(1)}, u32[]{:S(2)}, u32[]{:S(2)}) %all-to-all-start.2) | async-done | bytes 786464 | tf_op jit(solution)/shard_map/all_to_all | solution.py:521
  98.9 0.0 collective-permute-start.7
  98.9 0.6 collective-permute-start.2
  99.5 1.1 convert_add_fusion.1
  100.6 0.0 copy-done.2
  100.6 0.1 convert_add_fusion
  100.7 0.0 copy-start
  100.7 0.0 collective-permute-done.5
  100.7 1.1 fusion.6
  101.8 1.5 %collective-permute-start.6 = (bf16[4,32,768]{2,1,0:T(8,128)(2,1)S(1)}, bf16[4,32,768]{2,1,0:T(8,128)(2,1)S(1)}, u32[]{:S(2)}, u32[]{:S(2)}) collective-permute-start(bf16[4,32,768]{2,1,0:T(8,128)(2,1)S(1)} %get-tuple-element.57), channel_id=1, source_target_pairs={{0,2},{2,0},{4,6},{6,4},{8,10},{10,8},{12,14},{14,12},{16,18},{18,... | collective-permute-start | bytes 589832 | tf_op jit(solution)/shard_map/ppermute | solution.py:478
  103.4 6.2 %collective-permute-done.2 = bf16[4,2,32,640]{3,2,0,1:T(8,128)(2,1)S(1)} collective-permute-done((bf16[4,2,32,640]{3,2,0,1:T(8,128)(2,1)}, bf16[4,2,32,640]{3,2,0,1:T(8,128)(2,1)S(1)}, u32[]{:S(2)}, u32[]{:S(2)}) %collective-permute-start.2) | collective-permute-done | bytes 327712 | tf_op jit(solution)/shard_map/ppermute | solution.py:478
  109.6 0.1 fusion.7
  109.7 1.7 %collective-permute-start.3 = (bf16[4,32,640]{2,1,0:T(8,128)(2,1)S(1)}, bf16[4,32,640]{2,1,0:T(8,128)(2,1)S(1)}, u32[]{:S(2)}, u32[]{:S(2)}) collective-permute-start(bf16[4,32,640]{2,1,0:T(8,128)(2,1)S(1)} %get-tuple-element.59), channel_id=1, source_target_pairs={{0,4},{2,6},{4,0},{6,2},{8,12},{10,14},{12,8},{14,10},{16,20},{18,... | collective-permute-start | bytes 491528 | tf_op jit(solution)/shard_map/ppermute | solution.py:478
  111.4 3.8 %collective-permute-done.3.refs_1_ = bf16[4,32,640]{2,1,0:T(8,128)(2,1)S(1)} collective-permute-done((bf16[4,32,640]{2,1,0:T(8,128)(2,1)S(1)}, bf16[4,32,640]{2,1,0:T(8,128)(2,1)S(1)}, u32[]{:S(2)}, u32[]{:S(2)}) %collective-permute-start.3) | collective-permute-done | bytes 163872 | tf_op jit(solution)/shard_map/ppermute | solution.py:478
  115.2 0.0 collective-permute-done.6.refs_3_
  115.2 0.1 shard_map.122
  115.3 2.2 %collective-permute-start.8 = (bf16[32,1408]{1,0:T(8,128)(2,1)S(1)}, bf16[32,1408]{1,0:T(8,128)(2,1)S(1)}, u32[]{:S(2)}, u32[]{:S(2)}) collective-permute-start(bf16[32,1408]{1,0:T(8,128)(2,1)S(1)} %get-tuple-element.51), channel_id=1, source_target_pairs={{0,8},{2,10},{4,12},{6,14},{8,16},{10,18},{12,20},{14,22},{16,24},... | collective-permute-start | bytes 270344 | tf_op jit(solution)/shard_map/ppermute | solution.py:501
  117.5 0.8 collective-permute-start.9
  118.3 1.7 %collective-permute-start.10 = (bf16[32,1408]{1,0:T(8,128)(2,1)S(1)}, bf16[32,1408]{1,0:T(8,128)(2,1)S(1)}, u32[]{:S(2)}, u32[]{:S(2)}) collective-permute-start(bf16[32,1408]{1,0:T(8,128)(2,1)S(1)} %get-tuple-element.53), channel_id=1, source_target_pairs={{0,24},{2,26},{4,28},{6,30},{8,0},{10,2},{12,4},{14,6},{16,8},{18,... | collective-permute-start | bytes 270344 | tf_op jit(solution)/shard_map/ppermute | solution.py:501
  120.0 0.0 collective-permute-done.7.refs_3_
  120.0 0.0 copy-done
  120.0 2.7 %shard_map.124 = f32[1024,512]{1,0:T(8,128)} custom-call(f32[1,768]{1,0:T(1,128)S(1)} %copy-done, f32[1,768]{1,0:T(1,128)S(1)} %collective-permute-done.refs_1_, bf16[768,512]{1,0:T(8,128)(2,1)S(1)} %bitcast.55, bf16[768,512]{1,0:T(8,128)(2,1)S(1)} %collective-permute-done.7.refs_3_), custom_call_target="tpu_custom_call" | custom-call | flops 1610612736 | bytes 3670016 | tf_op jit(solution)/shard_map/pallas_call | solution.py:50
  122.8 0.0 collective-permute-done.8.refs_0_
  122.8 2.1 %collective-permute-done.9.refs_1_ = bf16[32,1408]{1,0:T(8,128)(2,1)S(1)} collective-permute-done((bf16[32,1408]{1,0:T(8,128)(2,1)S(1)}, bf16[32,1408]{1,0:T(8,128)(2,1)S(1)}, u32[]{:S(2)}, u32[]{:S(2)}) %collective-permute-start.9) | collective-permute-done | bytes 90144 | tf_op jit(solution)/shard_map/ppermute | solution.py:501
  124.9 0.0 collective-permute-done.10.refs_2_
  124.9 0.7 shard_map.125
  125.6 0.0 collective-permute-start.11
  125.6 1.2 collective-permute-done.11
  126.8 0.6 pad_maximum_fusion
  (1 shorter events, 0.0 us)
Async XLA Ops:
  22.4 22.1 %all-to-all-start.1 = ((bf16[16,48,512]{2,1,0:T(8,128)(2,1)}), bf16[16,48,512]{2,1,0:T(8,128)(2,1)S(1)}, u32[]{:S(2)}, u32[]{:S(2)}) async-start(bf16[16,48,512]{2,1,0:T(8,128)(2,1)} %bitcast.58), calls=%async_computation.1 | async-start | bytes 1572864 | tf_op jit(solution)/shard_map/all_to_all | solution.py:406
  26.0 1.4 %collective-permute-start = (f32[1,768]{1,0:T(1,128)}, f32[1,768]{1,0:T(1,128)S(1)}, u32[]{:S(2)}, u32[]{:S(2)}) collective-permute-start(f32[1,768]{1,0:T(1,128)} %get-tuple-element.46.refs_0_), channel_id=1, source_target_pairs={{0,1},{1,0},{2,3},{3,2},{4,5},{5,4},{6,7},{7,6},{8,9},{9,8},{10,11... | collective-permute-start | bytes 9224 | tf_op jit(solution)/shard_map/ppermute | solution.py:372
  44.5 0.9 copy-start.1
  65.0 5.5 %collective-permute-start.4 = (bf16[512,768]{1,0:T(8,128)(2,1)}, bf16[512,768]{1,0:T(8,128)(2,1)S(1)}, u32[]{:S(2)}, u32[]{:S(2)}) collective-permute-start(bf16[512,768]{1,0:T(8,128)(2,1)} %get-tuple-element.42), channel_id=1, source_target_pairs={{0,1},{1,0},{2,3},{3,2},{4,5},{5,4},{6,7},{7,6},{8,9},{9,8},{10,11... | collective-permute-start | bytes 2359304 | tf_op jit(solution)/shard_map/ppermute | solution.py:372
  65.1 3.4 %collective-permute-start.1 = (bf16[512,640]{1,0:T(8,128)(2,1)}, bf16[512,640]{1,0:T(8,128)(2,1)S(1)}, u32[]{:S(2)}, u32[]{:S(2)}) collective-permute-start(bf16[512,640]{1,0:T(8,128)(2,1)} %get-tuple-element.38), channel_id=1, source_target_pairs={{0,1},{1,0},{2,3},{3,2},{4,5},{5,4},{6,7},{7,6},{8,9},{9,8},{10,11... | collective-permute-start | bytes 1966088 | tf_op jit(solution)/shard_map/ppermute | solution.py:372
  68.5 5.6 %copy-start.3 = (bf16[512,640]{1,0:T(8,128)(2,1)}, bf16[512,640]{1,0:T(8,128)(2,1)S(1)}, u32[]{:S(2)}) copy-start(bf16[512,640]{1,0:T(8,128)(2,1)S(1)} %collective-permute-done.1) | copy-start | bytes 1966084
  71.7 29.0 %copy-start.2 = (bf16[512,768]{1,0:T(8,128)(2,1)S(1)}, bf16[512,768]{1,0:T(8,128)(2,1)}, u32[]{:S(2)}) copy-start(bf16[512,768]{1,0:T(8,128)(2,1)} %get-tuple-element.41) | copy-start | bytes 2359300
  74.1 24.8 %all-to-all-start.2 = ((bf16[16,48,512]{2,1,0:T(8,128)(2,1)}), bf16[16,48,512]{2,1,0:T(8,128)(2,1)S(1)}, u32[]{:S(2)}, u32[]{:S(2)}) async-start(bf16[16,48,512]{2,1,0:T(8,128)(2,1)} %bitcast.59), calls=%async_computation.2 | async-start | bytes 1572864 | tf_op jit(solution)/shard_map/all_to_all | solution.py:521
  78.9 21.8 %collective-permute-start.5 = (bf16[4,2,32,768]{3,2,0,1:T(8,128)(2,1)S(1)}, bf16[4,2,32,768]{3,2,0,1:T(8,128)(2,1)}, u32[]{:S(2)}, u32[]{:S(2)}) collective-permute-start(bf16[4,2,32,768]{3,2,0,1:T(8,128)(2,1)S(1)} %fusion), channel_id=1, source_target_pairs={{0,4},{2,6},{4,0},{6,2},{8,12},{10,14},{12,8},{14,10},{16,20},{18,... | collective-permute-start | bytes 1179656 | tf_op jit(solution)/shard_map/ppermute | solution.py:478
  98.9 21.1 %collective-permute-start.7 = (bf16[768,512]{1,0:T(8,128)(2,1)S(1)}, bf16[768,512]{1,0:T(8,128)(2,1)S(1)}, u32[]{:S(2)}, u32[]{:S(2)}) collective-permute-start(bf16[768,512]{1,0:T(8,128)(2,1)S(1)} %bitcast.54), channel_id=1, source_target_pairs={{0,1},{1,0},{2,3},{3,2},{4,5},{5,4},{6,7},{7,6},{8,9},{9,8},{10,11... | collective-permute-start | bytes 2359304 | tf_op jit(solution)/shard_map/ppermute | solution.py:372
  98.9 10.7 %collective-permute-start.2 = (bf16[4,2,32,640]{3,2,0,1:T(8,128)(2,1)}, bf16[4,2,32,640]{3,2,0,1:T(8,128)(2,1)S(1)}, u32[]{:S(2)}, u32[]{:S(2)}) collective-permute-start(bf16[4,2,32,640]{3,2,0,1:T(8,128)(2,1)} %fusion.3), channel_id=1, source_target_pairs={{0,2},{2,0},{4,6},{6,4},{8,10},{10,8},{12,14},{14,12},{16,18},{18,... | collective-permute-start | bytes 983048 | tf_op jit(solution)/shard_map/ppermute | solution.py:478
  100.7 19.3 %copy-start = (f32[1,768]{1,0:T(1,128)S(1)}, f32[1,768]{1,0:T(1,128)}, u32[]{:S(2)}) copy-start(f32[1,768]{1,0:T(1,128)} %get-tuple-element.46.refs_0_) | copy-start | bytes 9220
  101.8 13.4 %collective-permute-start.6 = (bf16[4,32,768]{2,1,0:T(8,128)(2,1)S(1)}, bf16[4,32,768]{2,1,0:T(8,128)(2,1)S(1)}, u32[]{:S(2)}, u32[]{:S(2)}) collective-permute-start(bf16[4,32,768]{2,1,0:T(8,128)(2,1)S(1)} %get-tuple-element.57), channel_id=1, source_target_pairs={{0,2},{2,0},{4,6},{6,4},{8,10},{10,8},{12,14},{14,12},{16,18},{18,... | collective-permute-start | bytes 589832 | tf_op jit(solution)/shard_map/ppermute | solution.py:478
  109.7 5.5 %collective-permute-start.3 = (bf16[4,32,640]{2,1,0:T(8,128)(2,1)S(1)}, bf16[4,32,640]{2,1,0:T(8,128)(2,1)S(1)}, u32[]{:S(2)}, u32[]{:S(2)}) collective-permute-start(bf16[4,32,640]{2,1,0:T(8,128)(2,1)S(1)} %get-tuple-element.59), channel_id=1, source_target_pairs={{0,4},{2,6},{4,0},{6,2},{8,12},{10,14},{12,8},{14,10},{16,20},{18,... | collective-permute-start | bytes 491528 | tf_op jit(solution)/shard_map/ppermute | solution.py:478
  115.3 7.5 %collective-permute-start.8 = (bf16[32,1408]{1,0:T(8,128)(2,1)S(1)}, bf16[32,1408]{1,0:T(8,128)(2,1)S(1)}, u32[]{:S(2)}, u32[]{:S(2)}) collective-permute-start(bf16[32,1408]{1,0:T(8,128)(2,1)S(1)} %get-tuple-element.51), channel_id=1, source_target_pairs={{0,8},{2,10},{4,12},{6,14},{8,16},{10,18},{12,20},{14,22},{16,24},... | collective-permute-start | bytes 270344 | tf_op jit(solution)/shard_map/ppermute | solution.py:501
  117.5 7.4 %collective-permute-start.9 = (bf16[32,1408]{1,0:T(8,128)(2,1)S(1)}, bf16[32,1408]{1,0:T(8,128)(2,1)S(1)}, u32[]{:S(2)}, u32[]{:S(2)}) collective-permute-start(bf16[32,1408]{1,0:T(8,128)(2,1)S(1)} %get-tuple-element.52), channel_id=1, source_target_pairs={{0,16},{2,18},{4,20},{6,22},{8,24},{10,26},{12,28},{14,30},{16,0},... | collective-permute-start | bytes 270344 | tf_op jit(solution)/shard_map/ppermute | solution.py:501
  118.3 6.6 %collective-permute-start.10 = (bf16[32,1408]{1,0:T(8,128)(2,1)S(1)}, bf16[32,1408]{1,0:T(8,128)(2,1)S(1)}, u32[]{:S(2)}, u32[]{:S(2)}) collective-permute-start(bf16[32,1408]{1,0:T(8,128)(2,1)S(1)} %get-tuple-element.53), channel_id=1, source_target_pairs={{0,24},{2,26},{4,28},{6,30},{8,0},{10,2},{12,4},{14,6},{16,8},{18,... | collective-permute-start | bytes 270344 | tf_op jit(solution)/shard_map/ppermute | solution.py:501
  125.6 1.2 collective-permute-start.11

commit v6 on v5

--- a/solution.py
+++ b/solution.py
@@ -8,7 +8,6 @@
 from jax.experimental.pallas import tpu as pltpu
 from jax.sharding import PartitionSpec as P
 
-HEADS = 8
 HEAD_DIM = 64
 LANES = 128
 QUERY_ROWS = 256
@@ -138,7 +137,7 @@
     wparts,
     len_ref,
     slot_ref,
-    ret_ref,
+    ret_hbm,
     w_in_hbm,
     w_out_hbm,
     gain_ref,
@@ -148,6 +147,7 @@
     result_hbm, row_hbm = rest[:2]
     grads_hbms = rest[2 : 2 + 2 * groups]
     (
+    ret_ref,
     w_in_ref,
     w_out_ref,
     cot_ref,
@@ -171,12 +171,14 @@
     sems,
     ) = rest[2 + 2 * groups :]
     count, width = cot_ref.shape
-    slots = ret_ref.shape[0]
+    slots = ret_hbm.shape[0]
     per = LANES // HEAD_DIM
     slabs = width // LANES
     qrows = QUERY_ROWS if count % QUERY_ROWS == 0 else count
     half_scale = 0.5 / math.sqrt(HEAD_DIM)
 
+    get_ret = pltpu.make_async_copy(ret_hbm, ret_ref, sems.at[8 + 2 * groups])
+    get_ret.start()
     parts = [pl.ds(i * width, width) for i in range(4)]
     get_ins = [
         pltpu.make_async_copy(w_in_hbm.at[:, part], w_in_ref.at[:, part], sems.at[i])
@@ -192,15 +194,17 @@
         pick_ref[:, start : start + LANES] = hot(
             slot == (iota((count, LANES), 1) + start).astype(F32)
         )
+    get_ret.wait()
     emb_ref[...] = dot_nn(pick_ref[...], ret_ref[...]).astype(BF16)
 
     for i in range(4):
         get_ins[i].wait()
         pre = dot_nn(emb_ref[...], w_in_ref[:, parts[i]])
-        sig = 0.5 * jnp.tanh(0.5 * pre) + 0.5
-        act = pre * sig
+        half = 0.5 * pre
+        th = jnp.tanh(half)
+        act = half + half * th
         proj_ref[i] = act.astype(BF16)
-        slope_ref[i] = sig + act * (1.0 - sig)
+        slope_ref[i] = 0.5 * ((1.0 + th) + act * (1.0 - th))
 
     pos = iota((count, 1), 0)
     begin = jnp.zeros((count, 1), jnp.int32)
@@ -212,30 +216,38 @@
     allowed = (key >= begin) & (key <= iota((count, count), 0))
     bias_ref[...] = jnp.where(allowed, 3.0e38, -30.0)
 
+    lane = iota((qrows, LANES), 1)
+    inside = [(lane >= a * HEAD_DIM) & (lane < (a + 1) * HEAD_DIM) for a in range(per)]
     lane = iota((count, LANES), 1)
-
-    def only(value, head, factor=1.0):
-        inside = (lane >= head * HEAD_DIM) & (lane < (head + 1) * HEAD_DIM)
-        return jnp.where(inside, value.astype(F32) * factor, 0.0).astype(BF16)
+    inside_all = [(lane >= a * HEAD_DIM) & (lane < (a + 1) * HEAD_DIM) for a in range(per)]
+
+    def stacked(value, factor=1.0):
+        value = value.astype(F32) * factor
+        return jnp.concatenate([jnp.where(m, value, 0.0) for m in inside], 0).astype(BF16)
+
+    def apart(value):
+        value = value.astype(F32)
+        return [jnp.where(m, value, 0.0).astype(BF16) for m in inside_all]
 
     def forward(p, _):
         cols = pl.ds(pl.multiple_of(p * LANES, LANES), LANES)
-        val, qry, key_all = proj_ref[1, :, cols], proj_ref[2, :, cols], proj_ref[3, :, cols]
-        qrys = [only(qry, a, half_scale) for a in range(per)]
-        vals = [only(val, a) for a in range(per)]
+        key_all = proj_ref[3, :, cols]
+        vals = apart(proj_ref[1, :, cols])
         for r0 in range(0, count, qrows):
             r1 = r0 + qrows
-            total = None
-            for a in range(per):
-                half = dot_nt(qrys[a][r0:r1], key_all[:r1])
-                half = jnp.minimum(half, bias_ref[r0:r1, :r1])
-                th = jnp.tanh(half)
-                weight = half + half * th
-                weight_b = weight.astype(BF16)
-                weight_ref[p * per + a, r0:r1, :r1] = weight_b
-                wslope_ref[p * per + a, r0:r1, :r1] = (1.0 + th) + weight * (1.0 - th)
-                part = dot_nn(weight_b, vals[a][:r1])
-                total = part if total is None else total + part
+            half = dot_nt(stacked(proj_ref[2, r0:r1, cols], half_scale), key_all[:r1])
+            half = jnp.minimum(half.reshape(per, qrows, r1), bias_ref[r0:r1, :r1][None])
+            th = jnp.tanh(half)
+            weight = half + half * th
+            weight_b = weight.astype(BF16)
+            base = per * r0
+            weight_ref[p, base : base + per * qrows, :r1] = weight_b.reshape(per * qrows, r1)
+            wslope_ref[p, base : base + per * qrows, :r1] = (
+                (1.0 + th) + weight * (1.0 - th)
+            ).reshape(per * qrows, r1)
+            total = dot_nn(weight_b[0], vals[0][:r1])
+            for a in range(1, per):
+                total = total + dot_nn(weight_b[a], vals[a][:r1])
             att_ref[r0:r1, cols] = total
         return 0
 
@@ -272,23 +284,26 @@
     def backward(p, _):
         start = pl.multiple_of(p * LANES, LANES)
         cols = pl.ds(start, LANES)
-        val, qry, key_all = proj_ref[1, :, cols], proj_ref[2, :, cols], proj_ref[3, :, cols]
-        gatt = gatt_ref[:, cols]
-        qrys = [only(qry, a, half_scale) for a in range(per)]
-        keys = [only(key_all, a) for a in range(per)]
-        gatts = [only(gatt, a) for a in range(per)]
-        gval_ref[...] = jnp.zeros_like(gval_ref)
-        gkey_ref[...] = jnp.zeros_like(gkey_ref)
-        for r0 in range(0, count, qrows):
+        val = proj_ref[1, :, cols]
+        keys = apart(proj_ref[3, :, cols])
+        for r0 in reversed(range(0, count, qrows)):
             r1 = r0 + qrows
-            gqry = None
-            for a in range(per):
-                gweight = dot_nt(gatts[a][r0:r1], val[:r1])
-                gscore = (gweight * wslope_ref[p * per + a, r0:r1, :r1]).astype(BF16)
-                part = dot_nn(gscore, keys[a][:r1])
-                gqry = part if gqry is None else gqry + part
-                gval_ref[:r1, :] += dot_tn(weight_ref[p * per + a, r0:r1, :r1], gatts[a][r0:r1])
-                gkey_ref[:r1, :] += dot_tn(gscore, qrys[a][r0:r1])
+            base = per * r0
+            rows = slice(base, base + per * qrows)
+            gatt = stacked(gatt_ref[r0:r1, cols])
+            gweight = dot_nt(gatt, val[:r1])
+            gscore = (gweight * wslope_ref[p, rows, :r1]).astype(BF16)
+            gqry = dot_nn(gscore[:qrows], keys[0][:r1])
+            for a in range(1, per):
+                gqry = gqry + dot_nn(gscore[a * qrows : (a + 1) * qrows], keys[a][:r1])
+            gval = dot_tn(weight_ref[p, rows, :r1], gatt)
+            gkey = dot_tn(gscore, stacked(proj_ref[2, r0:r1, cols], half_scale))
+            if r1 == count:
+                gval_ref[...] = gval
+                gkey_ref[...] = gkey
+            else:
+                gval_ref[:r1, :] += gval
+                gkey_ref[:r1, :] += gkey
             gpre_ref[r0:r1, pl.ds(2 * width + start, LANES)] = (
                 gqry * half_scale * slope_ref[2, r0:r1, cols]
             ).astype(BF16)
@@ -320,11 +335,14 @@
             )
             put.start()
             puts.append(put)
-    row_ref[...] = (
-        cot_ref[...].astype(F32) + dot_nt(gpre_ref[...], w_in_ref[...])
-    ).astype(BF16)
-    puts.append(pltpu.make_async_copy(row_ref, row_hbm, sems.at[7]))
-    puts[-1].start()
+    for i, r0 in enumerate((0, count // 2)):
+        rows = pl.ds(r0, count // 2)
+        row_ref[rows, :] = (
+            cot_ref[rows, :].astype(F32) + dot_nt(gpre_ref[rows, :], w_in_ref[...])
+        ).astype(BF16)
+        sem = sems.at[7 + i * (2 + 2 * groups)]
+        puts.append(pltpu.make_async_copy(row_ref.at[rows], row_hbm.at[rows], sem))
+        puts[-1].start()
     for put in puts:
         put.wait()
 
@@ -408,6 +426,7 @@
     returned, *all_ids = lax.optimization_barrier((returned, *all_ids))
 
     wparts = min(groups, width // LANES)
+    heads_per = LANES // HEAD_DIM
     cols_in = 4 * width // groups
     cols_out = width // wparts
     cols_all = cols_in + cols_out + LANES
@@ -428,9 +447,10 @@
         24 * count * width,
         (lengths, slot, returned, w_in, w_out, gain.reshape(1, width), cotangent),
         smem=(0,),
-        far=(3, 4, 6),
+        far=(2, 3, 4, 6),
         far_out=range(2 + 2 * groups),
         scratch=[
+            pltpu.VMEM((slots, width), BF16),
             pltpu.VMEM(w_in.shape, BF16),
             pltpu.VMEM(w_out.shape, BF16),
             square,
@@ -442,8 +462,8 @@
             pltpu.VMEM((4, count, width), BF16),
             pltpu.VMEM((4, count, width), F32),
             pltpu.VMEM((count, count), F32),
-            pltpu.VMEM((HEADS, count, count), BF16),
-            pltpu.VMEM((HEADS, count, count), F32),
+            pltpu.VMEM((width // LANES, heads_per * count, count), BF16),
+            pltpu.VMEM((width // LANES, heads_per * count, count), F32),
             pltpu.VMEM((count, width), F32),
             square,
             square,
@@ -451,7 +471,19 @@
             pltpu.VMEM((count, LANES), F32),
             pltpu.VMEM((count, LANES), F32),
             pltpu.VMEM((width, width), BF16),
-            pltpu.SemaphoreType.DMA((8 + 2 * groups,)),
+            pltpu.SemaphoreType.DMA((10 + 2 * groups,)),
+        ],
+    )
+    (outgoing,) = call(
+        slots_kernel,
+        [jax.ShapeDtypeStruct((slots, width), BF16)],
+        2 * slots * count * width,
+        4 * count * width,
+        (slot, row_grad),
+        far_out=(0,),
+        scratch=[
+            pltpu.VMEM((slots, width), BF16),
+            pltpu.SemaphoreType.DMA((slots // row_step(slots),)),
         ],
     )
     rows = width // owners
@@ -471,18 +503,18 @@
     def add(terms):
         return sum(term.astype(F32) for term in terms)
 
-    def halve(terms, index, axis, bit, tie=None):
+    def halve(terms, index, axis, bit):
         send = add([entry(term, 1 - index, axis) for term in terms]).astype(BF16)
-        if tie is not None:
-            tie, send = lax.optimization_barrier((tie, send))
+        *terms, send = lax.optimization_barrier((*terms, send))
         got = lax.ppermute(send, "table", [(i, i ^ bit) for i in range(owners)])
-        return [add([entry(term, index, axis) for term in terms]), got], tie
+        return [add([entry(term, index, axis) for term in terms]), got]
 
     if side == 2:
-        left, row_grad = halve(sides[0], low, 2, 1, row_grad)
-        right, row_grad = halve(sides[1], middle, 1, 2, row_grad)
-        left, _ = halve(left, middle, 1, 2)
-        right, _ = halve(right, low, 1, 1)
+        left = halve(sides[0], low, 2, 1)
+        right = halve(sides[1], middle, 1, 2)
+        outgoing, left[0], right[0] = lax.optimization_barrier((outgoing, left[0], right[0]))
+        left = halve(left, middle, 1, 2)
+        right = halve(right, low, 1, 1)
     else:
         left, right = [[term[:, 0, 0] for term in terms] for terms in sides]
     cols = cols_all
@@ -506,18 +538,6 @@
         for k in range(1, outer)
     ]
 
-    (outgoing,) = call(
-        slots_kernel,
-        [jax.ShapeDtypeStruct((slots, width), BF16)],
-        2 * slots * count * width,
-        4 * count * width,
-        (slot, row_grad),
-        far_out=(0,),
-        scratch=[
-            pltpu.VMEM((slots, width), BF16),
-            pltpu.SemaphoreType.DMA((slots // row_step(slots),)),
-        ],
-    )
     incoming = lax.all_to_all(outgoing, "table", split_axis=0, concat_axis=0, tiled=True)
     all_incoming = [incoming] + [shift(incoming, "group", groups, k) for k in range(1, groups)]
     grad_rows = table.shape[0] // groups
@@ -537,7 +557,6 @@
         ],
     )
 
-    kept, table_grad = lax.optimization_barrier((kept, table_grad))
     w_in_grad, mine, gain_grad = call(
         finish_kernel,
         [

time: 128 us -> 121 us (0.945)
  waiting for transfers between devices: 52.8 us -> 47.5 us
    ppermute x4, waiting for transfers between devices: 10.1 us -> 5.47 us  [halve(): got = lax.ppermute(send, 'table', [(i, i ^ bit) for i in range(owners)])]
    ppermute x3, waiting for transfers between devices: 2.11 us -> 5.6 us  [on_device(): lax.ppermute(sends[k - 1], 'table', [(i, (i // plane + k) % outer * plane...]
    ppermute x5, waiting for transfers between devices: 5.49 us -> 2.57 us  [shift(): lax.ppermute(value, axis, [(i, (i + amount) % size) for i in range(size)])]
    all_to_all x1, waiting for transfers between devices: 18 us -> 16.6 us  [on_device(): lax.all_to_all(outgoing, 'table', split_axis=0, concat_axis=0, tiled=True)]
  transfers between devices with their start and end apart: 14 -> 14, of which waited for: 8 -> 8; matrix products, arithmetic and copies ran while one was open for 3% -> 4% of each run, Pallas kernels for 2% -> 3%
where the time goes in v6:
time: 121 us; the launch traced here: 120 us
  waiting for transfers between devices  47.5 us (39%)
  Pallas kernels  31.3 us (26%)
  starting transfers between devices  18.9 us (16%)
  blocking collectives  15.5 us (13%)
  other arithmetic  5.44 us (4%)
    pallas_call x7, Pallas kernels, call(): pl.pallas_call(kernel, out_shape=out_shape, in_specs=[pl.BlockSpec(memory...  31.3 us
    all_to_all x1, waiting for transfers between devices, on_device(): lax.all_to_all(found, 'table', split_axis=0, concat_axis=0, tiled=True)  17.3 us
    all_to_all x1, waiting for transfers between devices, on_device(): lax.all_to_all(outgoing, 'table', split_axis=0, concat_axis=0, tiled=True)  16.6 us
    all_to_all x1, blocking collectives, on_device(): lax.all_to_all(requested, 'table', split_axis=0, concat_axis=0, tiled=True)  15.5 us
    ppermute x4, starting transfers between devices, halve(): got = lax.ppermute(send, 'table', [(i, i ^ bit) for i in range(owners)])  5.7 us
    ppermute x3, waiting for transfers between devices, on_device(): lax.ppermute(sends[k - 1], 'table', [(i, (i // plane + k) % outer * plane...  5.6 us
    ppermute x4, waiting for transfers between devices, halve(): got = lax.ppermute(send, 'table', [(i, i ^ bit) for i in range(owners)])  5.47 us
    all_to_all x1, starting transfers between devices, on_device(): lax.all_to_all(outgoing, 'table', split_axis=0, concat_axis=0, tiled=True)  4.85 us
  transfers between devices with their start and end apart: 14, of which 8 were waited for; matrix products, arithmetic and copies ran while one was open for 4% of the time, Pallas kernels for 3%

profile of v6, /device:TPU:0, one launch (start us, length us, event | category | flops | bytes accessed | tf_op | source)
XLA Modules:
  0.0 120.5 jit_solution(6787101420946810940)
XLA Ops:
  0.6 1.7 %shard_map.119 = (s32[16,128]{1,0:T(8,128)}, f32[1,512]{1,0:T(1,128)}) custom-call(s32[1,512]{1,0:T(1,128)} %bitcast.54, s32[1,512]{1,0:T(1,128)} %bitcast.55), custom_call_target="tpu_custom_call" | custom-call | flops 16777216 | bytes 4096 | tf_op jit(solution)/shard_map/pallas_call | solution.py:49
  2.3 15.5 %all_to_all.34 = s32[16,1,128]{2,1,0:T(1,128)} all-to-all(s32[16,1,128]{2,1,0:T(1,128)} %bitcast.53), channel_id=1, replica_groups=mesh['table'=16,'group'=2] {'table'}, dimensions={0} | all-to-all | bytes 16384 | tf_op jit(solution)/shard_map/all_to_all | solution.py:413
  17.7 4.5 %shard_map.120 = (bf16[768,512]{1,0:T(8,128)(2,1)}, f32[1,768]{1,0:T(1,128)}) custom-call(s32[16,128]{1,0:T(8,128)} %bitcast.52, bf16[2048,512]{1,0:T(8,128)(2,1)} %table_ref.1), custom_call_target="tpu_custom_call" | custom-call | flops 1610612736 | bytes 2883584 | tf_op jit(solution)/shard_map/pallas_call | solution.py:49
  22.2 3.6 %all-to-all-start.1 = ((bf16[16,48,512]{2,1,0:T(8,128)(2,1)}), bf16[16,48,512]{2,1,0:T(8,128)(2,1)S(1)}, u32[]{:S(2)}, u32[]{:S(2)}) async-start(bf16[16,48,512]{2,1,0:T(8,128)(2,1)} %bitcast.42), calls=%async_computation.1 | async-start | bytes 1572864 | tf_op jit(solution)/shard_map/all_to_all | solution.py:424
  25.9 0.1 collective-permute-start
  25.9 1.4 %collective-permute-done.refs_1_ = f32[1,768]{1,0:T(1,128)S(1)} collective-permute-done((f32[1,768]{1,0:T(1,128)}, f32[1,768]{1,0:T(1,128)S(1)}, u32[]{:S(2)}, u32[]{:S(2)}) %collective-permute-start) | collective-permute-done | bytes 3104 | tf_op jit(solution)/shard_map/ppermute | solution.py:390
  27.3 17.3 %all-to-all-done.1 = bf16[16,48,512]{2,1,0:T(8,128)(2,1)S(1)} async-done(((bf16[16,48,512]{2,1,0:T(8,128)(2,1)}), bf16[16,48,512]{2,1,0:T(8,128)(2,1)S(1)}, u32[]{:S(2)}, u32[]{:S(2)}) %all-to-all-start.1) | async-done | bytes 786464 | tf_op jit(solution)/shard_map/all_to_all | solution.py:424
  44.6 0.0 copy-start.1
  44.6 0.9 copy-done.1
  45.5 19.3 %shard_map.121 = (bf16[512,512]{1,0:T(8,128)(2,1)}, bf16[512,512]{1,0:T(8,128)(2,1)}, bf16[512,640]{1,0:T(8,128)(2,1)}, bf16[512,768]{1,0:T(8,128)(2,1)}, bf16[5...) custom-call(s32[1,8]{1,0:T(1,128)} %len_ref.1, f32[1,512]{1,0:T(1,128)} %get-tuple-element.40.slot_ref, ...), custom_call_target="tpu_custom_call" | custom-call | flops 6174015488 | bytes 6291456 | tf_op jit(solution)/shard_map/pallas_call | solution.py:49
  64.8 0.0 copy-start.3
  64.8 0.0 copy-start.2
  64.8 0.1 collective-permute-start.1
  64.9 0.5 collective-permute-start.2
  65.4 2.4 %shard_map.122 = bf16[768,512]{1,0:T(8,128)(2,1)} custom-call(f32[1,512]{1,0:T(1,128)} %get-tuple-element.40.slot_ref, bf16[512,512]{1,0:T(8,128)(2,1)} %get-tuple-element.48.grad_ref), custom_call_target="tpu_custom_call" | custom-call | flops 402653184 | bytes 1048576 | tf_op jit(solution)/shard_map/pallas_call | solution.py:49
  67.7 0.0 collective-permute-done.1
  67.7 1.8 %fusion.1 = bf16[4,2,32,640]{3,2,0,1:T(8,128)(2,1)} fusion(bf16[4,2,2,32,640]{4,3,2,1,0:T(8,128)(2,1)} %bitcast.47, s32[]{:T(128)S(6)} %select_n.61, bf16[4,2,2,32,640]{4,3,2,1,0:T(8,128)(2,1)S(1)} %bitcast.49), kind=kLoop, calls=%fused_computation.7 | loop fusion | flops 655360 | bytes 984064 | tf_op jit(solution)/shard_map/convert_element_type | solution.py:507
  69.5 0.0 copy-done.3
  69.6 0.1 add_bitcast_fusion.1
  69.6 0.0 collective-permute-done.2
  69.6 0.0 copy-done.2
  69.6 0.8 fusion
  70.5 0.1 add_bitcast_fusion
  70.6 4.8 %all-to-all-start.2 = ((bf16[16,48,512]{2,1,0:T(8,128)(2,1)}), bf16[16,48,512]{2,1,0:T(8,128)(2,1)S(1)}, u32[]{:S(2)}, u32[]{:S(2)}) async-start(bf16[16,48,512]{2,1,0:T(8,128)(2,1)} %bitcast.16), calls=%async_computation.2 | async-start | bytes 1572864 | tf_op jit(solution)/shard_map/all_to_all | solution.py:541
  75.4 1.9 %collective-permute-start.4 = (bf16[4,2,32,640]{3,2,0,1:T(8,128)(2,1)}, bf16[4,2,32,640]{3,2,0,1:T(8,128)(2,1)}, u32[]{:S(2)}, u32[]{:S(2)}) collective-permute-start(bf16[4,2,32,640]{3,2,0,1:T(8,128)(2,1)} %fusion.1), channel_id=1, source_target_pairs={{0,2},{2,0},{4,6},{6,4},{8,10},{10,8},{12,14},{14,12},{16,18},{18,... | collective-permute-start | bytes 983048 | tf_op jit(solution)/shard_map/ppermute | solution.py:509
  77.4 1.5 %collective-permute-start.6 = (bf16[4,2,32,768]{3,2,0,1:T(8,128)(2,1)}, bf16[4,2,32,768]{3,2,0,1:T(8,128)(2,1)S(1)}, u32[]{:S(2)}, u32[]{:S(2)}) collective-permute-start(bf16[4,2,32,768]{3,2,0,1:T(8,128)(2,1)} %fusion), channel_id=1, source_target_pairs={{0,4},{2,6},{4,0},{6,2},{8,12},{10,14},{12,8},{14,10},{16,20},{18,... | collective-permute-start | bytes 1179656 | tf_op jit(solution)/shard_map/ppermute | solution.py:509
  78.8 16.6 %all-to-all-done.2 = bf16[16,48,512]{2,1,0:T(8,128)(2,1)S(1)} async-done(((bf16[16,48,512]{2,1,0:T(8,128)(2,1)}), bf16[16,48,512]{2,1,0:T(8,128)(2,1)S(1)}, u32[]{:S(2)}, u32[]{:S(2)}) %all-to-all-start.2) | async-done | bytes 786464 | tf_op jit(solution)/shard_map/all_to_all | solution.py:541
  95.4 0.0 collective-permute-start.3
  95.4 0.0 collective-permute-done.4
  95.4 1.0 fusion.3
  96.4 0.0 copy-start
  96.4 1.7 %collective-permute-start.5 = (bf16[4,32,640]{2,1,0:T(8,128)(2,1)S(1)}, bf16[4,32,640]{2,1,0:T(8,128)(2,1)S(1)}, u32[]{:S(2)}, u32[]{:S(2)}) collective-permute-start(bf16[4,32,640]{2,1,0:T(8,128)(2,1)S(1)} %fusion.3), channel_id=1, source_target_pairs={{0,4},{2,6},{4,0},{6,2},{8,12},{10,14},{12,8},{14,10},{16,20},{18,... | collective-permute-start | bytes 491528 | tf_op jit(solution)/shard_map/ppermute | solution.py:509
  98.1 0.0 collective-permute-done.6
  98.1 0.6 collective-permute-start.7
  98.7 1.0 add_bitcast_fusion.3.refs_0_
  99.7 3.3 %collective-permute-done.5.refs_1_ = bf16[4,32,640]{2,1,0:T(8,128)(2,1)S(1)} collective-permute-done((bf16[4,32,640]{2,1,0:T(8,128)(2,1)S(1)}, bf16[4,32,640]{2,1,0:T(8,128)(2,1)S(1)}, u32[]{:S(2)}, u32[]{:S(2)}) %collective-permute-start.5) | collective-permute-done | bytes 163872 | tf_op jit(solution)/shard_map/ppermute | solution.py:509
  103.0 2.1 %collective-permute-done.7.refs_3_ = bf16[4,32,768]{2,1,0:T(8,128)(2,1)S(1)} collective-permute-done((bf16[4,32,768]{2,1,0:T(8,128)(2,1)S(1)}, bf16[4,32,768]{2,1,0:T(8,128)(2,1)S(1)}, u32[]{:S(2)}, u32[]{:S(2)}) %collective-permute-start.7) | collective-permute-done | bytes 196640 | tf_op jit(solution)/shard_map/ppermute | solution.py:509
  105.2 0.1 shard_map.124
  105.3 1.7 %collective-permute-start.8 = (bf16[32,1408]{1,0:T(8,128)(2,1)S(1)}, bf16[32,1408]{1,0:T(8,128)(2,1)S(1)}, u32[]{:S(2)}, u32[]{:S(2)}) collective-permute-start(bf16[32,1408]{1,0:T(8,128)(2,1)S(1)} %get-tuple-element.69), channel_id=1, source_target_pairs={{0,8},{2,10},{4,12},{6,14},{8,16},{10,18},{12,20},{14,22},{16,24},... | collective-permute-start | bytes 270344 | tf_op jit(solution)/shard_map/ppermute | solution.py:533
  107.0 1.4 %collective-permute-start.9 = (bf16[32,1408]{1,0:T(8,128)(2,1)S(1)}, bf16[32,1408]{1,0:T(8,128)(2,1)S(1)}, u32[]{:S(2)}, u32[]{:S(2)}) collective-permute-start(bf16[32,1408]{1,0:T(8,128)(2,1)S(1)} %get-tuple-element.70), channel_id=1, source_target_pairs={{0,16},{2,18},{4,20},{6,22},{8,24},{10,26},{12,28},{14,30},{16,0},... | collective-permute-start | bytes 270344 | tf_op jit(solution)/shard_map/ppermute | solution.py:533
  108.4 1.0 collective-permute-start.10
  109.4 3.4 %collective-permute-done.8.refs_0_ = bf16[32,1408]{1,0:T(8,128)(2,1)S(1)} collective-permute-done((bf16[32,1408]{1,0:T(8,128)(2,1)S(1)}, bf16[32,1408]{1,0:T(8,128)(2,1)S(1)}, u32[]{:S(2)}, u32[]{:S(2)}) %collective-permute-start.8) | collective-permute-done | bytes 90144 | tf_op jit(solution)/shard_map/ppermute | solution.py:533
  112.8 2.2 %collective-permute-done.9.refs_1_ = bf16[32,1408]{1,0:T(8,128)(2,1)S(1)} collective-permute-done((bf16[32,1408]{1,0:T(8,128)(2,1)S(1)}, bf16[32,1408]{1,0:T(8,128)(2,1)S(1)}, u32[]{:S(2)}, u32[]{:S(2)}) %collective-permute-start.9) | collective-permute-done | bytes 90144 | tf_op jit(solution)/shard_map/ppermute | solution.py:533
  115.0 0.0 collective-permute-done.10.refs_2_
  115.0 0.7 shard_map.125
  115.7 0.0 collective-permute-start.11
  115.7 1.2 collective-permute-done.11
  116.9 0.6 pad_maximum_fusion
  117.6 0.0 collective-permute-done.3.refs_3_
  117.6 0.0 copy-done
  117.6 2.7 %shard_map.123 = f32[1024,512]{1,0:T(8,128)} custom-call(f32[1,768]{1,0:T(1,128)S(1)} %copy-done, f32[1,768]{1,0:T(1,128)S(1)} %collective-permute-done.refs_1_, bf16[768,512]{1,0:T(8,128)(2,1)S(1)} %bitcast.39, bf16[768,512]{1,0:T(8,128)(2,1)S(1)} %collective-permute-done.3.refs_3_), custom_call_target="tpu_custom_call" | custom-call | flops 1610612736 | bytes 3670016 | tf_op jit(solution)/shard_map/pallas_call | solution.py:49
  (3 shorter events, 0.1 us)
Async XLA Ops:
  22.2 22.3 %all-to-all-start.1 = ((bf16[16,48,512]{2,1,0:T(8,128)(2,1)}), bf16[16,48,512]{2,1,0:T(8,128)(2,1)S(1)}, u32[]{:S(2)}, u32[]{:S(2)}) async-start(bf16[16,48,512]{2,1,0:T(8,128)(2,1)} %bitcast.42), calls=%async_computation.1 | async-start | bytes 1572864 | tf_op jit(solution)/shard_map/all_to_all | solution.py:424
  25.9 1.4 %collective-permute-start = (f32[1,768]{1,0:T(1,128)}, f32[1,768]{1,0:T(1,128)S(1)}, u32[]{:S(2)}, u32[]{:S(2)}) collective-permute-start(f32[1,768]{1,0:T(1,128)} %get-tuple-element.46.refs_0_), channel_id=1, source_target_pairs={{0,1},{1,0},{2,3},{3,2},{4,5},{5,4},{6,7},{7,6},{8,9},{9,8},{10,11... | collective-permute-start | bytes 9224 | tf_op jit(solution)/shard_map/ppermute | solution.py:390
  44.6 0.9 copy-start.1
  64.8 4.8 %copy-start.3 = (bf16[512,640]{1,0:T(8,128)(2,1)S(1)}, bf16[512,640]{1,0:T(8,128)(2,1)}, u32[]{:S(2)}) copy-start(bf16[512,640]{1,0:T(8,128)(2,1)} %get-tuple-element.49) | copy-start | bytes 1966084
  64.8 4.9 %copy-start.2 = (bf16[512,768]{1,0:T(8,128)(2,1)S(1)}, bf16[512,768]{1,0:T(8,128)(2,1)}, u32[]{:S(2)}) copy-start(bf16[512,768]{1,0:T(8,128)(2,1)} %get-tuple-element.53) | copy-start | bytes 2359300
  64.8 2.9 %collective-permute-start.1 = (bf16[512,640]{1,0:T(8,128)(2,1)}, bf16[512,640]{1,0:T(8,128)(2,1)S(1)}, u32[]{:S(2)}, u32[]{:S(2)}) collective-permute-start(bf16[512,640]{1,0:T(8,128)(2,1)} %get-tuple-element.50), channel_id=1, source_target_pairs={{0,1},{1,0},{2,3},{3,2},{4,5},{5,4},{6,7},{7,6},{8,9},{9,8},{10,11... | collective-permute-start | bytes 1966088 | tf_op jit(solution)/shard_map/ppermute | solution.py:390
  64.9 4.8 %collective-permute-start.2 = (bf16[512,768]{1,0:T(8,128)(2,1)}, bf16[512,768]{1,0:T(8,128)(2,1)S(1)}, u32[]{:S(2)}, u32[]{:S(2)}) collective-permute-start(bf16[512,768]{1,0:T(8,128)(2,1)} %get-tuple-element.54), channel_id=1, source_target_pairs={{0,1},{1,0},{2,3},{3,2},{4,5},{5,4},{6,7},{7,6},{8,9},{9,8},{10,11... | collective-permute-start | bytes 2359304 | tf_op jit(solution)/shard_map/ppermute | solution.py:390
  70.6 24.8 %all-to-all-start.2 = ((bf16[16,48,512]{2,1,0:T(8,128)(2,1)}), bf16[16,48,512]{2,1,0:T(8,128)(2,1)S(1)}, u32[]{:S(2)}, u32[]{:S(2)}) async-start(bf16[16,48,512]{2,1,0:T(8,128)(2,1)} %bitcast.16), calls=%async_computation.2 | async-start | bytes 1572864 | tf_op jit(solution)/shard_map/all_to_all | solution.py:541
  75.4 20.0 %collective-permute-start.4 = (bf16[4,2,32,640]{3,2,0,1:T(8,128)(2,1)}, bf16[4,2,32,640]{3,2,0,1:T(8,128)(2,1)}, u32[]{:S(2)}, u32[]{:S(2)}) collective-permute-start(bf16[4,2,32,640]{3,2,0,1:T(8,128)(2,1)} %fusion.1), channel_id=1, source_target_pairs={{0,2},{2,0},{4,6},{6,4},{8,10},{10,8},{12,14},{14,12},{16,18},{18,... | collective-permute-start | bytes 983048 | tf_op jit(solution)/shard_map/ppermute | solution.py:509
  77.4 20.7 %collective-permute-start.6 = (bf16[4,2,32,768]{3,2,0,1:T(8,128)(2,1)}, bf16[4,2,32,768]{3,2,0,1:T(8,128)(2,1)S(1)}, u32[]{:S(2)}, u32[]{:S(2)}) collective-permute-start(bf16[4,2,32,768]{3,2,0,1:T(8,128)(2,1)} %fusion), channel_id=1, source_target_pairs={{0,4},{2,6},{4,0},{6,2},{8,12},{10,14},{12,8},{14,10},{16,20},{18,... | collective-permute-start | bytes 1179656 | tf_op jit(solution)/shard_map/ppermute | solution.py:509
  95.4 22.2 %collective-permute-start.3 = (bf16[768,512]{1,0:T(8,128)(2,1)S(1)}, bf16[768,512]{1,0:T(8,128)(2,1)S(1)}, u32[]{:S(2)}, u32[]{:S(2)}) collective-permute-start(bf16[768,512]{1,0:T(8,128)(2,1)S(1)} %bitcast.38), channel_id=1, source_target_pairs={{0,1},{1,0},{2,3},{3,2},{4,5},{5,4},{6,7},{7,6},{8,9},{9,8},{10,11... | collective-permute-start | bytes 2359304 | tf_op jit(solution)/shard_map/ppermute | solution.py:390
  96.4 21.2 %copy-start = (f32[1,768]{1,0:T(1,128)S(1)}, f32[1,768]{1,0:T(1,128)}, u32[]{:S(2)}) copy-start(f32[1,768]{1,0:T(1,128)} %get-tuple-element.46.refs_0_) | copy-start | bytes 9220
  96.4 6.7 %collective-permute-start.5 = (bf16[4,32,640]{2,1,0:T(8,128)(2,1)S(1)}, bf16[4,32,640]{2,1,0:T(8,128)(2,1)S(1)}, u32[]{:S(2)}, u32[]{:S(2)}) collective-permute-start(bf16[4,32,640]{2,1,0:T(8,128)(2,1)S(1)} %fusion.3), channel_id=1, source_target_pairs={{0,4},{2,6},{4,0},{6,2},{8,12},{10,14},{12,8},{14,10},{16,20},{18,... | collective-permute-start | bytes 491528 | tf_op jit(solution)/shard_map/ppermute | solution.py:509
  98.1 7.1 %collective-permute-start.7 = (bf16[4,32,768]{2,1,0:T(8,128)(2,1)S(1)}, bf16[4,32,768]{2,1,0:T(8,128)(2,1)S(1)}, u32[]{:S(2)}, u32[]{:S(2)}) collective-permute-start(bf16[4,32,768]{2,1,0:T(8,128)(2,1)S(1)} %fusion.2), channel_id=1, source_target_pairs={{0,2},{2,0},{4,6},{6,4},{8,10},{10,8},{12,14},{14,12},{16,18},{18,... | collective-permute-start | bytes 589832 | tf_op jit(solution)/shard_map/ppermute | solution.py:509
  105.3 7.5 %collective-permute-start.8 = (bf16[32,1408]{1,0:T(8,128)(2,1)S(1)}, bf16[32,1408]{1,0:T(8,128)(2,1)S(1)}, u32[]{:S(2)}, u32[]{:S(2)}) collective-permute-start(bf16[32,1408]{1,0:T(8,128)(2,1)S(1)} %get-tuple-element.69), channel_id=1, source_target_pairs={{0,8},{2,10},{4,12},{6,14},{8,16},{10,18},{12,20},{14,22},{16,24},... | collective-permute-start | bytes 270344 | tf_op jit(solution)/shard_map/ppermute | solution.py:533
  107.0 8.0 %collective-permute-start.9 = (bf16[32,1408]{1,0:T(8,128)(2,1)S(1)}, bf16[32,1408]{1,0:T(8,128)(2,1)S(1)}, u32[]{:S(2)}, u32[]{:S(2)}) collective-permute-start(bf16[32,1408]{1,0:T(8,128)(2,1)S(1)} %get-tuple-element.70), channel_id=1, source_target_pairs={{0,16},{2,18},{4,20},{6,22},{8,24},{10,26},{12,28},{14,30},{16,0},... | collective-permute-start | bytes 270344 | tf_op jit(solution)/shard_map/ppermute | solution.py:533
  108.4 6.6 %collective-permute-start.10 = (bf16[32,1408]{1,0:T(8,128)(2,1)S(1)}, bf16[32,1408]{1,0:T(8,128)(2,1)S(1)}, u32[]{:S(2)}, u32[]{:S(2)}) collective-permute-start(bf16[32,1408]{1,0:T(8,128)(2,1)S(1)} %get-tuple-element.71), channel_id=1, source_target_pairs={{0,24},{2,26},{4,28},{6,30},{8,0},{10,2},{12,4},{14,6},{16,8},{18,... | collective-permute-start | bytes 270344 | tf_op jit(solution)/shard_map/ppermute | solution.py:533
  115.7 1.2 %collective-permute-start.11 = (f32[32,256]{1,0:T(8,128)S(1)}, f32[32,256]{1,0:T(8,128)S(1)}, u32[]{:S(2)}, u32[]{:S(2)}) collective-permute-start(f32[32,256]{1,0:T(8,128)S(1)} %get-tuple-element.73), channel_id=1, source_target_pairs={{0,1},{1,0},{2,3},{3,2},{4,5},{5,4},{6,7},{7,6},{8,9},{9,8},{10,11... | collective-permute-start | bytes 98312 | tf_op jit(solution)/shard_map/ppermute | solution.py:390

commit v7 on v6

--- a/solution.py
+++ b/solution.py
@@ -225,6 +225,13 @@
         value = value.astype(F32) * factor
         return jnp.concatenate([jnp.where(m, value, 0.0) for m in inside], 0).astype(BF16)
 
+    row = iota((LANES, qrows), 0)
+    inside_rows = [(row >= a * HEAD_DIM) & (row < (a + 1) * HEAD_DIM) for a in range(per)]
+
+    def stacked_t(value, factor=1.0):
+        value = (value.astype(F32) * factor).T
+        return jnp.concatenate([jnp.where(m, value, 0.0) for m in inside_rows], 1).astype(BF16)
+
     def apart(value):
         value = value.astype(F32)
         return [jnp.where(m, value, 0.0).astype(BF16) for m in inside_all]
@@ -296,19 +303,19 @@
             gqry = dot_nn(gscore[:qrows], keys[0][:r1])
             for a in range(1, per):
                 gqry = gqry + dot_nn(gscore[a * qrows : (a + 1) * qrows], keys[a][:r1])
-            gval = dot_tn(weight_ref[p, rows, :r1], gatt)
-            gkey = dot_tn(gscore, stacked(proj_ref[2, r0:r1, cols], half_scale))
+            gval = dot_nn(stacked_t(gatt_ref[r0:r1, cols]), weight_ref[p, rows, :r1])
+            gkey = dot_nn(stacked_t(proj_ref[2, r0:r1, cols], half_scale), gscore)
             if r1 == count:
                 gval_ref[...] = gval
                 gkey_ref[...] = gkey
             else:
-                gval_ref[:r1, :] += gval
-                gkey_ref[:r1, :] += gkey
+                gval_ref[:, :r1] += gval
+                gkey_ref[:, :r1] += gkey
             gpre_ref[r0:r1, pl.ds(2 * width + start, LANES)] = (
                 gqry * half_scale * slope_ref[2, r0:r1, cols]
             ).astype(BF16)
-        gpre_ref[:, pl.ds(width + start, LANES)] = (gval_ref[...] * slope_ref[1, :, cols]).astype(BF16)
-        gpre_ref[:, pl.ds(3 * width + start, LANES)] = (gkey_ref[...] * slope_ref[3, :, cols]).astype(BF16)
+        gpre_ref[:, pl.ds(width + start, LANES)] = (gval_ref[...].T * slope_ref[1, :, cols]).astype(BF16)
+        gpre_ref[:, pl.ds(3 * width + start, LANES)] = (gkey_ref[...].T * slope_ref[3, :, cols]).astype(BF16)
         return 0
 
     lax.fori_loop(0, slabs, backward, 0)
@@ -468,12 +475,64 @@
             square,
             square,
             pltpu.VMEM((count, 4 * width), BF16),
-            pltpu.VMEM((count, LANES), F32),
-            pltpu.VMEM((count, LANES), F32),
+            pltpu.VMEM((LANES, count), F32),
+            pltpu.VMEM((LANES, count), F32),
             pltpu.VMEM((width, width), BF16),
             pltpu.SemaphoreType.DMA((10 + 2 * groups,)),
         ],
     )
+    rows = width // owners
+    side = 2 if owners % 4 == 0 else 1
+    plane = side * side
+    outer = owners // plane
+    here = lax.axis_index("table")
+    high, middle, low = here // plane, here // side % side, here % side
+    sides = []
+    for i in range(2):
+        terms = [grads[i]] + [shift(grads[2 * k + i], "group", groups, k) for k in range(1, groups)]
+        sides.append([term.reshape(outer, side, side, rows, term.shape[1]) for term in terms])
+
+    def entry(value, index, axis):
+        return lax.dynamic_index_in_dim(value, index, axis, keepdims=False)
+
+    def add(terms):
+        return sum(term.astype(F32) for term in terms)
+
+    def halve(terms, index, axis, bit, tie=None):
+        send = add([entry(term, 1 - index, axis) for term in terms]).astype(BF16)
+        if tie is not None:
+            tie, send = lax.optimization_barrier((tie, send))
+        got = lax.ppermute(send, "table", [(i, i ^ bit) for i in range(owners)])
+        return [add([entry(term, index, axis) for term in terms]), got], tie
+
+    if side == 2:
+        left, row_grad = halve(sides[0], low, 2, 1, row_grad)
+        right, row_grad = halve(sides[1], middle, 1, 2, row_grad)
+        left, _ = halve(left, middle, 1, 2)
+        right, _ = halve(right, low, 1, 1)
+    else:
+        left, right = [[term[:, 0, 0] for term in terms] for terms in sides]
+    cols = cols_all
+    kept, *sends = call(
+        functools.partial(plane_kernel, outer, len(left)),
+        [
+            jax.ShapeDtypeStruct((rows, cols), F32),
+            *[jax.ShapeDtypeStruct((rows, cols), BF16) for _ in range(1, outer)],
+        ],
+        12 * outer * rows * cols,
+        8 * outer * rows * cols,
+        (*left, *right),
+        limit=24,
+    )
+    got = [
+        lax.ppermute(
+            sends[k - 1],
+            "table",
+            [(i, ((i // plane + k) % outer) * plane + i % plane) for i in range(owners)],
+        )
+        for k in range(1, outer)
+    ]
+
     (outgoing,) = call(
         slots_kernel,
         [jax.ShapeDtypeStruct((slots, width), BF16)],
@@ -486,59 +545,8 @@
             pltpu.SemaphoreType.DMA((slots // row_step(slots),)),
         ],
     )
-    rows = width // owners
-    side = 2 if owners % 4 == 0 else 1
-    plane = side * side
-    outer = owners // plane
-    here = lax.axis_index("table")
-    high, middle, low = here // plane, here // side % side, here % side
-    sides = []
-    for i in range(2):
-        terms = [grads[i]] + [shift(grads[2 * k + i], "group", groups, k) for k in range(1, groups)]
-        sides.append([term.reshape(outer, side, side, rows, term.shape[1]) for term in terms])
-
-    def entry(value, index, axis):
-        return lax.dynamic_index_in_dim(value, index, axis, keepdims=False)
-
-    def add(terms):
-        return sum(term.astype(F32) for term in terms)
-
-    def halve(terms, index, axis, bit):
-        send = add([entry(term, 1 - index, axis) for term in terms]).astype(BF16)
-        *terms, send = lax.optimization_barrier((*terms, send))
-        got = lax.ppermute(send, "table", [(i, i ^ bit) for i in range(owners)])
-        return [add([entry(term, index, axis) for term in terms]), got]
-
-    if side == 2:
-        left = halve(sides[0], low, 2, 1)
-        right = halve(sides[1], middle, 1, 2)
-        outgoing, left[0], right[0] = lax.optimization_barrier((outgoing, left[0], right[0]))
-        left = halve(left, middle, 1, 2)
-        right = halve(right, low, 1, 1)
-    else:
-        left, right = [[term[:, 0, 0] for term in terms] for terms in sides]
-    cols = cols_all
-    kept, *sends = call(
-        functools.partial(plane_kernel, outer, len(left)),
-        [
-            jax.ShapeDtypeStruct((rows, cols), F32),
-            *[jax.ShapeDtypeStruct((rows, cols), BF16) for _ in range(1, outer)],
-        ],
-        12 * outer * rows * cols,
-        8 * outer * rows * cols,
-        (*left, *right),
-        limit=24,
-    )
-    got = [
-        lax.ppermute(
-            sends[k - 1],
-            "table",
-            [(i, ((i // plane + k) % outer) * plane + i % plane) for i in range(owners)],
-        )
-        for k in range(1, outer)
-    ]
-
     incoming = lax.all_to_all(outgoing, "table", split_axis=0, concat_axis=0, tiled=True)
+    incoming, *got = lax.optimization_barrier((incoming, *got))
     all_incoming = [incoming] + [shift(incoming, "group", groups, k) for k in range(1, groups)]
     grad_rows = table.shape[0] // groups
     (table_grad,) = call(

time: 121 us -> 121 us (level)
    all_to_all x1, waiting for transfers between devices: 16.6 us -> 0.01 us  [on_device(): lax.all_to_all(outgoing, 'table', split_axis=0, concat_axis=0, tiled=True)]
    ppermute x4, waiting for transfers between devices: 5.47 us -> 19.7 us  [halve(): got = lax.ppermute(send, 'table', [(i, i ^ bit) for i in range(owners)])]
    ppermute x5, waiting for transfers between devices: 2.57 us -> 5.4 us  [shift(): lax.ppermute(value, axis, [(i, (i + amount) % size) for i in range(size)])]
  transfers between devices with their start and end apart: 14 -> 14, of which waited for: 8 -> 8; matrix products, arithmetic and copies ran while one was open for 4% -> 4% of each run, Pallas kernels for 3% -> 1%
where the time goes in v7:
time: 121 us
  waiting for transfers between devices  46.9 us (39%)
  Pallas kernels  30.3 us (25%)
  starting transfers between devices  20 us (17%)
  blocking collectives  15.5 us (13%)
  other arithmetic  6.17 us (5%)
    pallas_call x7, Pallas kernels, call(): pl.pallas_call(kernel, out_shape=out_shape, in_specs=[pl.BlockSpec(memory...  30.3 us
    ppermute x4, waiting for transfers between devices, halve(): got = lax.ppermute(send, 'table', [(i, i ^ bit) for i in range(owners)])  19.7 us
    all_to_all x1, waiting for transfers between devices, on_device(): lax.all_to_all(found, 'table', split_axis=0, concat_axis=0, tiled=True)  17.3 us
    all_to_all x1, blocking collectives, on_device(): lax.all_to_all(requested, 'table', split_axis=0, concat_axis=0, tiled=True)  15.5 us
    ppermute x4, starting transfers between devices, halve(): got = lax.ppermute(send, 'table', [(i, i ^ bit) for i in range(owners)])  5.59 us
    ppermute x5, waiting for transfers between devices, shift(): lax.ppermute(value, axis, [(i, (i + amount) % size) for i in range(size)])  5.4 us
    all_to_all x1, starting transfers between devices, on_device(): lax.all_to_all(outgoing, 'table', split_axis=0, concat_axis=0, tiled=True)  4.86 us
    ppermute x3, starting transfers between devices, on_device(): lax.ppermute(sends[k - 1], 'table', [(i, (i // plane + k) % outer * plane...  4.82 us
  transfers between devices with their start and end apart: 14, of which 8 were waited for; matrix products, arithmetic and copies ran while one was open for 4% of the time, Pallas kernels for 1%

profile of v7, /device:TPU:0, one launch (start us, length us, event | category | flops | bytes accessed | tf_op | source)
XLA Modules:
  0.0 120.7 jit_solution(15043668335911517002)
XLA Ops:
  0.6 1.7 %shard_map.119 = (s32[16,128]{1,0:T(8,128)}, f32[1,512]{1,0:T(1,128)}) custom-call(s32[1,512]{1,0:T(1,128)} %bitcast.71, s32[1,512]{1,0:T(1,128)} %bitcast.72), custom_call_target="tpu_custom_call" | custom-call | flops 16777216 | bytes 4096 | tf_op jit(solution)/shard_map/pallas_call | solution.py:49
  2.3 15.5 %all_to_all.35 = s32[16,1,128]{2,1,0:T(1,128)} all-to-all(s32[16,1,128]{2,1,0:T(1,128)} %bitcast.70), channel_id=1, replica_groups=mesh['table'=16,'group'=2] {'table'}, dimensions={0} | all-to-all | bytes 16384 | tf_op jit(solution)/shard_map/all_to_all | solution.py:420
  17.7 4.5 %shard_map.120 = (bf16[768,512]{1,0:T(8,128)(2,1)}, f32[1,768]{1,0:T(1,128)}) custom-call(s32[16,128]{1,0:T(8,128)} %bitcast.69, bf16[2048,512]{1,0:T(8,128)(2,1)} %table_ref.1), custom_call_target="tpu_custom_call" | custom-call | flops 1610612736 | bytes 2883584 | tf_op jit(solution)/shard_map/pallas_call | solution.py:49
  22.2 3.6 %all-to-all-start.1 = ((bf16[16,48,512]{2,1,0:T(8,128)(2,1)}), bf16[16,48,512]{2,1,0:T(8,128)(2,1)S(1)}, u32[]{:S(2)}, u32[]{:S(2)}) async-start(bf16[16,48,512]{2,1,0:T(8,128)(2,1)} %bitcast.59), calls=%async_computation.1 | async-start | bytes 1572864 | tf_op jit(solution)/shard_map/all_to_all | solution.py:431
  25.9 0.1 collective-permute-start
  25.9 1.4 %collective-permute-done.refs_1_ = f32[1,768]{1,0:T(1,128)S(1)} collective-permute-done((f32[1,768]{1,0:T(1,128)}, f32[1,768]{1,0:T(1,128)S(1)}, u32[]{:S(2)}, u32[]{:S(2)}) %collective-permute-start) | collective-permute-done | bytes 3104 | tf_op jit(solution)/shard_map/ppermute | solution.py:397
  27.3 17.3 %all-to-all-done.1 = bf16[16,48,512]{2,1,0:T(8,128)(2,1)S(1)} async-done(((bf16[16,48,512]{2,1,0:T(8,128)(2,1)}), bf16[16,48,512]{2,1,0:T(8,128)(2,1)S(1)}, u32[]{:S(2)}, u32[]{:S(2)}) %all-to-all-start.1) | async-done | bytes 786464 | tf_op jit(solution)/shard_map/all_to_all | solution.py:431
  44.6 0.0 copy-start.1
  44.6 0.9 copy-done.1
  45.5 18.2 %shard_map.121 = (bf16[512,512]{1,0:T(8,128)(2,1)}, bf16[512,512]{1,0:T(8,128)(2,1)}, bf16[512,640]{1,0:T(8,128)(2,1)}, bf16[512,768]{1,0:T(8,128)(2,1)}, bf16[5...) custom-call(s32[1,8]{1,0:T(1,128)} %len_ref.1, f32[1,512]{1,0:T(1,128)} %get-tuple-element.33.slot_ref, ...), custom_call_target="tpu_custom_call" | custom-call | flops 6174015488 | bytes 6291456 | tf_op jit(solution)/shard_map/pallas_call | solution.py:49
  63.7 0.1 collective-permute-start.2
  63.8 0.5 collective-permute-start.1
  64.3 2.9 %collective-permute-done.1 = bf16[512,640]{1,0:T(8,128)(2,1)S(1)} collective-permute-done((bf16[512,640]{1,0:T(8,128)(2,1)}, bf16[512,640]{1,0:T(8,128)(2,1)S(1)}, u32[]{:S(2)}, u32[]{:S(2)}) %collective-permute-start.1) | collective-permute-done | bytes 655392 | tf_op jit(solution)/shard_map/ppermute | solution.py:397
  67.2 0.0 copy-start.4
  67.2 2.0 %fusion.3 = bf16[4,2,32,640]{3,2,0,1:T(8,128)(2,1)} fusion(bf16[4,2,2,32,640]{4,3,2,1,0:T(8,128)(2,1)} %bitcast.64, s32[]{:T(128)S(6)} %select_n.61, bf16[4,2,2,32,640]{4,3,2,1,0:T(8,128)(2,1)S(1)} %bitcast.66), kind=kLoop, calls=%fused_computation.9 | loop fusion | flops 655360 | bytes 984064 | tf_op jit(solution)/shard_map/convert_element_type | solution.py:502
  69.2 0.0 collective-permute-done.2
  69.2 0.0 copy-start.3
  69.2 1.2 fusion
  70.4 0.0 copy-start.2
  70.4 2.4 %shard_map.122 = bf16[768,512]{1,0:T(8,128)(2,1)} custom-call(f32[1,512]{1,0:T(1,128)} %get-tuple-element.33.slot_ref, bf16[512,512]{1,0:T(8,128)(2,1)} %get-tuple-element.47.grad_ref), custom_call_target="tpu_custom_call" | custom-call | flops 402653184 | bytes 1048576 | tf_op jit(solution)/shard_map/pallas_call | solution.py:49
  72.9 0.0 copy-done.4
  72.9 4.9 %all-to-all-start.2 = ((bf16[16,48,512]{2,1,0:T(8,128)(2,1)}), bf16[16,48,512]{2,1,0:T(8,128)(2,1)S(1)}, u32[]{:S(2)}, u32[]{:S(2)}) async-start(bf16[16,48,512]{2,1,0:T(8,128)(2,1)} %bitcast.57), calls=%async_computation.2 | async-start | bytes 1572864 | tf_op jit(solution)/shard_map/all_to_all | solution.py:548
  77.7 2.0 %collective-permute-start.5 = (bf16[4,2,32,768]{3,2,0,1:T(8,128)(2,1)S(1)}, bf16[4,2,32,768]{3,2,0,1:T(8,128)(2,1)}, u32[]{:S(2)}, u32[]{:S(2)}) collective-permute-start(bf16[4,2,32,768]{3,2,0,1:T(8,128)(2,1)S(1)} %fusion), channel_id=1, source_target_pairs={{0,4},{2,6},{4,0},{6,2},{8,12},{10,14},{12,8},{14,10},{16,20},{18,... | collective-permute-start | bytes 1179656 | tf_op jit(solution)/shard_map/ppermute | solution.py:505
  79.7 1.5 %collective-permute-start.3 = (bf16[4,2,32,640]{3,2,0,1:T(8,128)(2,1)}, bf16[4,2,32,640]{3,2,0,1:T(8,128)(2,1)S(1)}, u32[]{:S(2)}, u32[]{:S(2)}) collective-permute-start(bf16[4,2,32,640]{3,2,0,1:T(8,128)(2,1)} %fusion.3), channel_id=1, source_target_pairs={{0,2},{2,0},{4,6},{6,4},{8,10},{10,8},{12,14},{14,12},{16,18},{18,... | collective-permute-start | bytes 983048 | tf_op jit(solution)/shard_map/ppermute | solution.py:505
  81.2 0.0 copy-done.3
  81.2 1.1 convert_add_fusion.1
  82.3 0.0 copy-done.2
  82.3 0.1 convert_add_fusion
  82.4 14.4 %collective-permute-done.5 = bf16[4,2,32,768]{3,2,0,1:T(8,128)(2,1)} collective-permute-done((bf16[4,2,32,768]{3,2,0,1:T(8,128)(2,1)S(1)}, bf16[4,2,32,768]{3,2,0,1:T(8,128)(2,1)}, u32[]{:S(2)}, u32[]{:S(2)}) %collective-permute-start.5) | collective-permute-done | bytes 393248 | tf_op jit(solution)/shard_map/ppermute | solution.py:505
  96.7 1.1 fusion.6
  97.8 0.0 copy-start
  97.9 2.0 %collective-permute-start.6 = (bf16[4,32,768]{2,1,0:T(8,128)(2,1)S(1)}, bf16[4,32,768]{2,1,0:T(8,128)(2,1)S(1)}, u32[]{:S(2)}, u32[]{:S(2)}) collective-permute-start(bf16[4,32,768]{2,1,0:T(8,128)(2,1)S(1)} %get-tuple-element.61), channel_id=1, source_target_pairs={{0,2},{2,0},{4,6},{6,4},{8,10},{10,8},{12,14},{14,12},{16,18},{18,... | collective-permute-start | bytes 589832 | tf_op jit(solution)/shard_map/ppermute | solution.py:505
  99.9 0.0 collective-permute-done.3
  99.9 0.1 fusion.7
  100.0 0.1 collective-permute-start.4
  100.1 5.3 %collective-permute-done.4.refs_1_ = bf16[4,32,640]{2,1,0:T(8,128)(2,1)S(1)} collective-permute-done((bf16[4,32,640]{2,1,0:T(8,128)(2,1)S(1)}, bf16[4,32,640]{2,1,0:T(8,128)(2,1)S(1)}, u32[]{:S(2)}, u32[]{:S(2)}) %collective-permute-start.4) | collective-permute-done | bytes 163872 | tf_op jit(solution)/shard_map/ppermute | solution.py:505
  105.3 0.0 collective-permute-done.6.refs_3_
  105.3 0.1 shard_map.123
  105.4 1.0 collective-permute-start.7
  106.4 2.9 %collective-permute-start.8 = (bf16[32,1408]{1,0:T(8,128)(2,1)S(1)}, bf16[32,1408]{1,0:T(8,128)(2,1)S(1)}, u32[]{:S(2)}, u32[]{:S(2)}) collective-permute-start(bf16[32,1408]{1,0:T(8,128)(2,1)S(1)} %get-tuple-element.51), channel_id=1, source_target_pairs={{0,16},{2,18},{4,20},{6,22},{8,24},{10,26},{12,28},{14,30},{16,0},... | collective-permute-start | bytes 270344 | tf_op jit(solution)/shard_map/ppermute | solution.py:528
  109.3 0.9 collective-permute-start.9
  110.2 1.7 %collective-permute-done.7.refs_0_ = bf16[32,1408]{1,0:T(8,128)(2,1)S(1)} collective-permute-done((bf16[32,1408]{1,0:T(8,128)(2,1)S(1)}, bf16[32,1408]{1,0:T(8,128)(2,1)S(1)}, u32[]{:S(2)}, u32[]{:S(2)}) %collective-permute-start.7) | collective-permute-done | bytes 90144 | tf_op jit(solution)/shard_map/ppermute | solution.py:528
  112.0 2.8 %collective-permute-done.8.refs_1_ = bf16[32,1408]{1,0:T(8,128)(2,1)S(1)} collective-permute-done((bf16[32,1408]{1,0:T(8,128)(2,1)S(1)}, bf16[32,1408]{1,0:T(8,128)(2,1)S(1)}, u32[]{:S(2)}, u32[]{:S(2)}) %collective-permute-start.8) | collective-permute-done | bytes 90144 | tf_op jit(solution)/shard_map/ppermute | solution.py:528
  114.8 0.0 collective-permute-done.9.refs_2_
  114.8 0.0 all-to-all-done.2
  114.8 0.0 collective-permute-start.10
  114.8 0.7 shard_map.125
  115.5 0.5 collective-permute-start.11
  116.0 1.1 collective-permute-done.11
  117.2 0.6 pad_maximum_fusion
  117.8 0.0 collective-permute-done.10.refs_3_
  117.8 0.0 copy-done
  117.8 2.7 %shard_map.124 = f32[1024,512]{1,0:T(8,128)} custom-call(f32[1,768]{1,0:T(1,128)S(1)} %copy-done, f32[1,768]{1,0:T(1,128)S(1)} %collective-permute-done.refs_1_, bf16[768,512]{1,0:T(8,128)(2,1)S(1)} %bitcast.55, bf16[768,512]{1,0:T(8,128)(2,1)S(1)} %collective-permute-done.10.refs_3_), custom_call_target="tpu_custom_call" | custom-call | flops 1610612736 | bytes 3670016 | tf_op jit(solution)/shard_map/pallas_call | solution.py:49
  (1 shorter events, 0.0 us)
Async XLA Ops:
  22.2 22.3 %all-to-all-start.1 = ((bf16[16,48,512]{2,1,0:T(8,128)(2,1)}), bf16[16,48,512]{2,1,0:T(8,128)(2,1)S(1)}, u32[]{:S(2)}, u32[]{:S(2)}) async-start(bf16[16,48,512]{2,1,0:T(8,128)(2,1)} %bitcast.59), calls=%async_computation.1 | async-start | bytes 1572864 | tf_op jit(solution)/shard_map/all_to_all | solution.py:431
  25.9 1.4 %collective-permute-start = (f32[1,768]{1,0:T(1,128)}, f32[1,768]{1,0:T(1,128)S(1)}, u32[]{:S(2)}, u32[]{:S(2)}) collective-permute-start(f32[1,768]{1,0:T(1,128)} %get-tuple-element.39.refs_0_), channel_id=1, source_target_pairs={{0,1},{1,0},{2,3},{3,2},{4,5},{5,4},{6,7},{7,6},{8,9},{9,8},{10,11... | collective-permute-start | bytes 9224 | tf_op jit(solution)/shard_map/ppermute | solution.py:397
  44.6 0.9 copy-start.1
  63.7 5.5 %collective-permute-start.2 = (bf16[512,768]{1,0:T(8,128)(2,1)}, bf16[512,768]{1,0:T(8,128)(2,1)S(1)}, u32[]{:S(2)}, u32[]{:S(2)}) collective-permute-start(bf16[512,768]{1,0:T(8,128)(2,1)} %get-tuple-element.46), channel_id=1, source_target_pairs={{0,1},{1,0},{2,3},{3,2},{4,5},{5,4},{6,7},{7,6},{8,9},{9,8},{10,11... | collective-permute-start | bytes 2359304 | tf_op jit(solution)/shard_map/ppermute | solution.py:397
  63.8 3.4 %collective-permute-start.1 = (bf16[512,640]{1,0:T(8,128)(2,1)}, bf16[512,640]{1,0:T(8,128)(2,1)S(1)}, u32[]{:S(2)}, u32[]{:S(2)}) collective-permute-start(bf16[512,640]{1,0:T(8,128)(2,1)} %get-tuple-element.43), channel_id=1, source_target_pairs={{0,1},{1,0},{2,3},{3,2},{4,5},{5,4},{6,7},{7,6},{8,9},{9,8},{10,11... | collective-permute-start | bytes 1966088 | tf_op jit(solution)/shard_map/ppermute | solution.py:397
  67.2 5.7 %copy-start.4 = (bf16[512,640]{1,0:T(8,128)(2,1)}, bf16[512,640]{1,0:T(8,128)(2,1)S(1)}, u32[]{:S(2)}) copy-start(bf16[512,640]{1,0:T(8,128)(2,1)S(1)} %collective-permute-done.1) | copy-start | bytes 1966084
  69.2 12.0 %copy-start.3 = (bf16[512,640]{1,0:T(8,128)(2,1)S(1)}, bf16[512,640]{1,0:T(8,128)(2,1)}, u32[]{:S(2)}) copy-start(bf16[512,640]{1,0:T(8,128)(2,1)} %get-tuple-element.42) | copy-start | bytes 1966084
  70.4 11.8 %copy-start.2 = (bf16[512,768]{1,0:T(8,128)(2,1)S(1)}, bf16[512,768]{1,0:T(8,128)(2,1)}, u32[]{:S(2)}) copy-start(bf16[512,768]{1,0:T(8,128)(2,1)} %get-tuple-element.45) | copy-start | bytes 2359300
  72.9 41.9 %all-to-all-start.2 = ((bf16[16,48,512]{2,1,0:T(8,128)(2,1)}), bf16[16,48,512]{2,1,0:T(8,128)(2,1)S(1)}, u32[]{:S(2)}, u32[]{:S(2)}) async-start(bf16[16,48,512]{2,1,0:T(8,128)(2,1)} %bitcast.57), calls=%async_computation.2 | async-start | bytes 1572864 | tf_op jit(solution)/shard_map/all_to_all | solution.py:548
  77.7 19.0 %collective-permute-start.5 = (bf16[4,2,32,768]{3,2,0,1:T(8,128)(2,1)S(1)}, bf16[4,2,32,768]{3,2,0,1:T(8,128)(2,1)}, u32[]{:S(2)}, u32[]{:S(2)}) collective-permute-start(bf16[4,2,32,768]{3,2,0,1:T(8,128)(2,1)S(1)} %fusion), channel_id=1, source_target_pairs={{0,4},{2,6},{4,0},{6,2},{8,12},{10,14},{12,8},{14,10},{16,20},{18,... | collective-permute-start | bytes 1179656 | tf_op jit(solution)/shard_map/ppermute | solution.py:505
  79.7 20.2 %collective-permute-start.3 = (bf16[4,2,32,640]{3,2,0,1:T(8,128)(2,1)}, bf16[4,2,32,640]{3,2,0,1:T(8,128)(2,1)S(1)}, u32[]{:S(2)}, u32[]{:S(2)}) collective-permute-start(bf16[4,2,32,640]{3,2,0,1:T(8,128)(2,1)} %fusion.3), channel_id=1, source_target_pairs={{0,2},{2,0},{4,6},{6,4},{8,10},{10,8},{12,14},{14,12},{16,18},{18,... | collective-permute-start | bytes 983048 | tf_op jit(solution)/shard_map/ppermute | solution.py:505
  97.8 19.9 %copy-start = (f32[1,768]{1,0:T(1,128)S(1)}, f32[1,768]{1,0:T(1,128)}, u32[]{:S(2)}) copy-start(f32[1,768]{1,0:T(1,128)} %get-tuple-element.39.refs_0_) | copy-start | bytes 9220
  97.9 7.5 %collective-permute-start.6 = (bf16[4,32,768]{2,1,0:T(8,128)(2,1)S(1)}, bf16[4,32,768]{2,1,0:T(8,128)(2,1)S(1)}, u32[]{:S(2)}, u32[]{:S(2)}) collective-permute-start(bf16[4,32,768]{2,1,0:T(8,128)(2,1)S(1)} %get-tuple-element.61), channel_id=1, source_target_pairs={{0,2},{2,0},{4,6},{6,4},{8,10},{10,8},{12,14},{14,12},{16,18},{18,... | collective-permute-start | bytes 589832 | tf_op jit(solution)/shard_map/ppermute | solution.py:505
  100.0 5.4 %collective-permute-start.4 = (bf16[4,32,640]{2,1,0:T(8,128)(2,1)S(1)}, bf16[4,32,640]{2,1,0:T(8,128)(2,1)S(1)}, u32[]{:S(2)}, u32[]{:S(2)}) collective-permute-start(bf16[4,32,640]{2,1,0:T(8,128)(2,1)S(1)} %get-tuple-element.63), channel_id=1, source_target_pairs={{0,4},{2,6},{4,0},{6,2},{8,12},{10,14},{12,8},{14,10},{16,20},{18,... | collective-permute-start | bytes 491528 | tf_op jit(solution)/shard_map/ppermute | solution.py:505
  105.4 6.6 %collective-permute-start.7 = (bf16[32,1408]{1,0:T(8,128)(2,1)S(1)}, bf16[32,1408]{1,0:T(8,128)(2,1)S(1)}, u32[]{:S(2)}, u32[]{:S(2)}) collective-permute-start(bf16[32,1408]{1,0:T(8,128)(2,1)S(1)} %get-tuple-element.50), channel_id=1, source_target_pairs={{0,8},{2,10},{4,12},{6,14},{8,16},{10,18},{12,20},{14,22},{16,24},... | collective-permute-start | bytes 270344 | tf_op jit(solution)/shard_map/ppermute | solution.py:528
  106.4 8.4 %collective-permute-start.8 = (bf16[32,1408]{1,0:T(8,128)(2,1)S(1)}, bf16[32,1408]{1,0:T(8,128)(2,1)S(1)}, u32[]{:S(2)}, u32[]{:S(2)}) collective-permute-start(bf16[32,1408]{1,0:T(8,128)(2,1)S(1)} %get-tuple-element.51), channel_id=1, source_target_pairs={{0,16},{2,18},{4,20},{6,22},{8,24},{10,26},{12,28},{14,30},{16,0},... | collective-permute-start | bytes 270344 | tf_op jit(solution)/shard_map/ppermute | solution.py:528
  109.3 5.5 %collective-permute-start.9 = (bf16[32,1408]{1,0:T(8,128)(2,1)S(1)}, bf16[32,1408]{1,0:T(8,128)(2,1)S(1)}, u32[]{:S(2)}, u32[]{:S(2)}) collective-permute-start(bf16[32,1408]{1,0:T(8,128)(2,1)S(1)} %get-tuple-element.52), channel_id=1, source_target_pairs={{0,24},{2,26},{4,28},{6,30},{8,0},{10,2},{12,4},{14,6},{16,8},{18,... | collective-permute-start | bytes 270344 | tf_op jit(solution)/shard_map/ppermute | solution.py:528
  114.8 3.0 %collective-permute-start.10 = (bf16[768,512]{1,0:T(8,128)(2,1)S(1)}, bf16[768,512]{1,0:T(8,128)(2,1)S(1)}, u32[]{:S(2)}, u32[]{:S(2)}) collective-permute-start(bf16[768,512]{1,0:T(8,128)(2,1)S(1)} %bitcast.54), channel_id=1, source_target_pairs={{0,1},{1,0},{2,3},{3,2},{4,5},{5,4},{6,7},{7,6},{8,9},{9,8},{10,11... | collective-permute-start | bytes 2359304 | tf_op jit(solution)/shard_map/ppermute | solution.py:397
  115.5 1.6 %collective-permute-start.11 = (f32[32,256]{1,0:T(8,128)S(1)}, f32[32,256]{1,0:T(8,128)S(1)}, u32[]{:S(2)}, u32[]{:S(2)}) collective-permute-start(f32[32,256]{1,0:T(8,128)S(1)} %get-tuple-element.59), channel_id=1, source_target_pairs={{0,1},{1,0},{2,3},{3,2},{4,5},{5,4},{6,7},{7,6},{8,9},{9,8},{10,11... | collective-permute-start | bytes 98312 | tf_op jit(solution)/shard_map/ppermute | solution.py:397

commit v8 on v7

--- a/solution.py
+++ b/solution.py
@@ -10,7 +10,7 @@
 
 HEAD_DIM = 64
 LANES = 128
-QUERY_ROWS = 256
+QUERY_ROWS = 128
 
 F32 = jnp.float32
 BF16 = jnp.bfloat16
@@ -503,7 +503,8 @@
         if tie is not None:
             tie, send = lax.optimization_barrier((tie, send))
         got = lax.ppermute(send, "table", [(i, i ^ bit) for i in range(owners)])
-        return [add([entry(term, index, axis) for term in terms]), got], tie
+        kept = [entry(term, index, axis) for term in terms]
+        return (kept if tie is not None else [add(kept)]) + [got], tie
 
     if side == 2:
         left, row_grad = halve(sides[0], low, 2, 1, row_grad)

time: 121 us -> 124 us (1.025)
  Pallas kernels: 30.3 us -> 31.6 us
    convert_element_type x4, other arithmetic: 4.37 us -> 5.68 us  [halve(): send = add([entry(term, 1 - index, axis) for term in terms]).astype(BF16)]
    pallas_call x7, Pallas kernels: 30.3 us -> 31.6 us  [call(): pl.pallas_call(kernel, out_shape=out_shape, in_specs=[pl.BlockSpec(memory...]
  transfers between devices with their start and end apart: 14 -> 14, of which waited for: 8 -> 9; matrix products, arithmetic and copies ran while one was open for 4% -> 4% of each run, Pallas kernels for 1% -> 1%
where the time goes in v8:
time: 124 us; the launch traced here: 123 us
  waiting for transfers between devices  48.1 us (39%)
  Pallas kernels  31.6 us (25%)
  starting transfers between devices  20 us (16%)
  blocking collectives  15.5 us (12%)
  other arithmetic  6.33 us (5%)
    pallas_call x7, Pallas kernels, call(): pl.pallas_call(kernel, out_shape=out_shape, in_specs=[pl.BlockSpec(memory...  31.6 us
    ppermute x4, waiting for transfers between devices, halve(): got = lax.ppermute(send, 'table', [(i, i ^ bit) for i in range(owners)])  20.8 us
    all_to_all x1, waiting for transfers between devices, on_device(): lax.all_to_all(found, 'table', split_axis=0, concat_axis=0, tiled=True)  17.3 us
    all_to_all x1, blocking collectives, on_device(): lax.all_to_all(requested, 'table', split_axis=0, concat_axis=0, tiled=True)  15.5 us
    convert_element_type x4, other arithmetic, halve(): send = add([entry(term, 1 - index, axis) for term in terms]).astype(BF16)  5.68 us
    ppermute x4, starting transfers between devices, halve(): got = lax.ppermute(send, 'table', [(i, i ^ bit) for i in range(owners)])  5.59 us
    ppermute x5, waiting for transfers between devices, shift(): lax.ppermute(value, axis, [(i, (i + amount) % size) for i in range(size)])  5.4 us
    all_to_all x1, starting transfers between devices, on_device(): lax.all_to_all(outgoing, 'table', split_axis=0, concat_axis=0, tiled=True)  4.87 us
  transfers between devices with their start and end apart: 14, of which 9 were waited for; matrix products, arithmetic and copies ran while one was open for 4% of the time, Pallas kernels for 1%

profile of v8, /device:TPU:0, one launch (start us, length us, event | category | flops | bytes accessed | tf_op | source)
XLA Modules:
  0.0 123.3 jit_solution(10305893494158910447)
XLA Ops:
  0.6 1.7 %shard_map.119 = (s32[16,128]{1,0:T(8,128)}, f32[1,512]{1,0:T(1,128)}) custom-call(s32[1,512]{1,0:T(1,128)} %bitcast.79, s32[1,512]{1,0:T(1,128)} %bitcast.80), custom_call_target="tpu_custom_call" | custom-call | flops 16777216 | bytes 4096 | tf_op jit(solution)/shard_map/pallas_call | solution.py:49
  2.3 15.5 %all_to_all.35 = s32[16,1,128]{2,1,0:T(1,128)} all-to-all(s32[16,1,128]{2,1,0:T(1,128)} %bitcast.78), channel_id=1, replica_groups=mesh['table'=16,'group'=2] {'table'}, dimensions={0} | all-to-all | bytes 16384 | tf_op jit(solution)/shard_map/all_to_all | solution.py:420
  17.7 4.5 %shard_map.120 = (bf16[768,512]{1,0:T(8,128)(2,1)}, f32[1,768]{1,0:T(1,128)}) custom-call(s32[16,128]{1,0:T(8,128)} %bitcast.77, bf16[2048,512]{1,0:T(8,128)(2,1)} %table_ref.1), custom_call_target="tpu_custom_call" | custom-call | flops 1610612736 | bytes 2883584 | tf_op jit(solution)/shard_map/pallas_call | solution.py:49
  22.2 3.6 %all-to-all-start.1 = ((bf16[16,48,512]{2,1,0:T(8,128)(2,1)}), bf16[16,48,512]{2,1,0:T(8,128)(2,1)S(1)}, u32[]{:S(2)}, u32[]{:S(2)}) async-start(bf16[16,48,512]{2,1,0:T(8,128)(2,1)} %bitcast.67), calls=%async_computation.1 | async-start | bytes 1572864 | tf_op jit(solution)/shard_map/all_to_all | solution.py:431
  25.9 0.1 collective-permute-start
  25.9 1.4 %collective-permute-done.refs_1_ = f32[1,768]{1,0:T(1,128)S(1)} collective-permute-done((f32[1,768]{1,0:T(1,128)}, f32[1,768]{1,0:T(1,128)S(1)}, u32[]{:S(2)}, u32[]{:S(2)}) %collective-permute-start) | collective-permute-done | bytes 3104 | tf_op jit(solution)/shard_map/ppermute | solution.py:397
  27.3 17.3 %all-to-all-done.1 = bf16[16,48,512]{2,1,0:T(8,128)(2,1)S(1)} async-done(((bf16[16,48,512]{2,1,0:T(8,128)(2,1)}), bf16[16,48,512]{2,1,0:T(8,128)(2,1)S(1)}, u32[]{:S(2)}, u32[]{:S(2)}) %all-to-all-start.1) | async-done | bytes 786464 | tf_op jit(solution)/shard_map/all_to_all | solution.py:431
  44.6 0.0 copy-start.1
  44.6 0.9 copy-done.1
  45.5 19.5 %shard_map.121 = (bf16[512,512]{1,0:T(8,128)(2,1)}, bf16[512,512]{1,0:T(8,128)(2,1)}, bf16[512,640]{1,0:T(8,128)(2,1)}, bf16[512,768]{1,0:T(8,128)(2,1)}, bf16[5...) custom-call(s32[1,8]{1,0:T(1,128)} %len_ref.1, f32[1,512]{1,0:T(1,128)} %get-tuple-element.33.slot_ref, ...), custom_call_target="tpu_custom_call" | custom-call | flops 6174015488 | bytes 6291456 | tf_op jit(solution)/shard_map/pallas_call | solution.py:49
  65.0 0.1 collective-permute-start.2
  65.1 0.5 collective-permute-start.1
  65.6 2.9 %collective-permute-done.1 = bf16[512,640]{1,0:T(8,128)(2,1)S(1)} collective-permute-done((bf16[512,640]{1,0:T(8,128)(2,1)}, bf16[512,640]{1,0:T(8,128)(2,1)S(1)}, u32[]{:S(2)}, u32[]{:S(2)}) %collective-permute-start.1) | collective-permute-done | bytes 655392 | tf_op jit(solution)/shard_map/ppermute | solution.py:397
  68.5 0.0 copy-start.4
  68.5 2.0 %fusion.2 = bf16[4,2,32,640]{3,2,0,1:T(8,128)(2,1)} fusion(bf16[4,2,2,32,640]{4,3,2,1,0:T(8,128)(2,1)} %bitcast.72, s32[]{:T(128)S(6)} %select_n.71, bf16[4,2,2,32,640]{4,3,2,1,0:T(8,128)(2,1)S(1)} %bitcast.74), kind=kLoop, calls=%fused_computation.6 | loop fusion | flops 655360 | bytes 984064 | tf_op jit(solution)/shard_map/convert_element_type | solution.py:502
  70.5 0.0 collective-permute-done.2
  70.5 0.0 copy-start.2
  70.5 1.2 fusion
  71.7 0.0 copy-start.3
  71.7 2.4 %shard_map.122 = bf16[768,512]{1,0:T(8,128)(2,1)} custom-call(f32[1,512]{1,0:T(1,128)} %get-tuple-element.33.slot_ref, bf16[512,512]{1,0:T(8,128)(2,1)} %get-tuple-element.47.grad_ref), custom_call_target="tpu_custom_call" | custom-call | flops 402653184 | bytes 1048576 | tf_op jit(solution)/shard_map/pallas_call | solution.py:49
  74.2 0.0 copy-done.4
  74.2 4.9 %all-to-all-start.2 = ((bf16[16,48,512]{2,1,0:T(8,128)(2,1)}), bf16[16,48,512]{2,1,0:T(8,128)(2,1)S(1)}, u32[]{:S(2)}, u32[]{:S(2)}) async-start(bf16[16,48,512]{2,1,0:T(8,128)(2,1)} %bitcast.65), calls=%async_computation.2 | async-start | bytes 1572864 | tf_op jit(solution)/shard_map/all_to_all | solution.py:549
  79.1 2.0 %collective-permute-start.5 = (bf16[4,2,32,768]{3,2,0,1:T(8,128)(2,1)S(1)}, bf16[4,2,32,768]{3,2,0,1:T(8,128)(2,1)}, u32[]{:S(2)}, u32[]{:S(2)}) collective-permute-start(bf16[4,2,32,768]{3,2,0,1:T(8,128)(2,1)S(1)} %fusion), channel_id=1, source_target_pairs={{0,4},{2,6},{4,0},{6,2},{8,12},{10,14},{12,8},{14,10},{16,20},{18,... | collective-permute-start | bytes 1179656 | tf_op jit(solution)/shard_map/ppermute | solution.py:505
  81.0 1.5 %collective-permute-start.3 = (bf16[4,2,32,640]{3,2,0,1:T(8,128)(2,1)}, bf16[4,2,32,640]{3,2,0,1:T(8,128)(2,1)}, u32[]{:S(2)}, u32[]{:S(2)}) collective-permute-start(bf16[4,2,32,640]{3,2,0,1:T(8,128)(2,1)} %fusion.2), channel_id=1, source_target_pairs={{0,2},{2,0},{4,6},{6,4},{8,10},{10,8},{12,14},{14,12},{16,18},{18,... | collective-permute-start | bytes 983048 | tf_op jit(solution)/shard_map/ppermute | solution.py:505
  82.5 15.6 %collective-permute-done.5 = bf16[4,2,32,768]{3,2,0,1:T(8,128)(2,1)} collective-permute-done((bf16[4,2,32,768]{3,2,0,1:T(8,128)(2,1)S(1)}, bf16[4,2,32,768]{3,2,0,1:T(8,128)(2,1)}, u32[]{:S(2)}, u32[]{:S(2)}) %collective-permute-start.5) | collective-permute-done | bytes 393248 | tf_op jit(solution)/shard_map/ppermute | solution.py:505
  98.1 0.0 copy-done.2
  98.1 1.2 fusion.1
  99.2 0.0 copy-start
  99.2 2.0 %collective-permute-start.6 = (bf16[4,32,768]{2,1,0:T(8,128)(2,1)S(1)}, bf16[4,32,768]{2,1,0:T(8,128)(2,1)S(1)}, u32[]{:S(2)}, u32[]{:S(2)}) collective-permute-start(bf16[4,32,768]{2,1,0:T(8,128)(2,1)S(1)} %get-tuple-element.61), channel_id=1, source_target_pairs={{0,2},{2,0},{4,6},{6,4},{8,10},{10,8},{12,14},{14,12},{16,18},{18,... | collective-permute-start | bytes 589832 | tf_op jit(solution)/shard_map/ppermute | solution.py:505
  101.3 0.0 collective-permute-done.3
  101.3 0.0 copy-done.3
  101.3 1.3 %fusion.3 = (bf16[4,32,640]{2,1,0:T(8,128)(2,1)S(1)}, f32[4,32,640]{2,1,0:T(8,128)S(1)}) fusion(bf16[4,2,32,640]{3,2,0,1:T(8,128)(2,1)} %collective-permute-done.3, s32[]{:T(128)S(6)} %select_n.74, bf16[4,2,2,32,640]{4,3,2,1,0:T(8,128)(2,1)} %bitcast.75, s32[]{:T(128)S(6)} %select_n.79, s32[]{:T(128)S(6)} %select_n.78, ...), kind=kLoop, calls=%fused_computation.8 | loop fusion | flops 901120 | bytes 1474580 | tf_op jit(solution)/shard_map/convert_element_type | solution.py:502
  102.6 0.1 collective-permute-start.4
  102.7 5.3 %collective-permute-done.4.refs_1_ = bf16[4,32,640]{2,1,0:T(8,128)(2,1)S(1)} collective-permute-done((bf16[4,32,640]{2,1,0:T(8,128)(2,1)S(1)}, bf16[4,32,640]{2,1,0:T(8,128)(2,1)S(1)}, u32[]{:S(2)}, u32[]{:S(2)}) %collective-permute-start.4) | collective-permute-done | bytes 163872 | tf_op jit(solution)/shard_map/ppermute | solution.py:505
  108.0 0.0 collective-permute-done.6.refs_3_
  108.0 0.1 shard_map.123
  108.1 1.0 collective-permute-start.7
  109.0 2.9 %collective-permute-start.8 = (bf16[32,1408]{1,0:T(8,128)(2,1)S(1)}, bf16[32,1408]{1,0:T(8,128)(2,1)S(1)}, u32[]{:S(2)}, u32[]{:S(2)}) collective-permute-start(bf16[32,1408]{1,0:T(8,128)(2,1)S(1)} %get-tuple-element.51), channel_id=1, source_target_pairs={{0,16},{2,18},{4,20},{6,22},{8,24},{10,26},{12,28},{14,30},{16,0},... | collective-permute-start | bytes 270344 | tf_op jit(solution)/shard_map/ppermute | solution.py:529
  111.9 0.9 collective-permute-start.9
  112.9 1.7 %collective-permute-done.7.refs_0_ = bf16[32,1408]{1,0:T(8,128)(2,1)S(1)} collective-permute-done((bf16[32,1408]{1,0:T(8,128)(2,1)S(1)}, bf16[32,1408]{1,0:T(8,128)(2,1)S(1)}, u32[]{:S(2)}, u32[]{:S(2)}) %collective-permute-start.7) | collective-permute-done | bytes 90144 | tf_op jit(solution)/shard_map/ppermute | solution.py:529
  114.6 2.5 %collective-permute-done.8.refs_1_ = bf16[32,1408]{1,0:T(8,128)(2,1)S(1)} collective-permute-done((bf16[32,1408]{1,0:T(8,128)(2,1)S(1)}, bf16[32,1408]{1,0:T(8,128)(2,1)S(1)}, u32[]{:S(2)}, u32[]{:S(2)}) %collective-permute-start.8) | collective-permute-done | bytes 90144 | tf_op jit(solution)/shard_map/ppermute | solution.py:529
  117.1 0.3 collective-permute-done.9.refs_2_
  117.4 0.0 all-to-all-done.2
  117.4 0.0 collective-permute-start.10
  117.4 0.7 shard_map.125
  118.1 0.5 collective-permute-start.11
  118.7 1.1 collective-permute-done.11
  119.8 0.6 pad_maximum_fusion
  120.4 0.0 collective-permute-done.10.refs_3_
  120.4 0.0 copy-done
  120.4 2.7 %shard_map.124 = f32[1024,512]{1,0:T(8,128)} custom-call(f32[1,768]{1,0:T(1,128)S(1)} %copy-done, f32[1,768]{1,0:T(1,128)S(1)} %collective-permute-done.refs_1_, bf16[768,512]{1,0:T(8,128)(2,1)S(1)} %bitcast.63, bf16[768,512]{1,0:T(8,128)(2,1)S(1)} %collective-permute-done.10.refs_3_), custom_call_target="tpu_custom_call" | custom-call | flops 1610612736 | bytes 3670016 | tf_op jit(solution)/shard_map/pallas_call | solution.py:49
  (1 shorter events, 0.0 us)
Async XLA Ops:
  22.2 22.3 %all-to-all-start.1 = ((bf16[16,48,512]{2,1,0:T(8,128)(2,1)}), bf16[16,48,512]{2,1,0:T(8,128)(2,1)S(1)}, u32[]{:S(2)}, u32[]{:S(2)}) async-start(bf16[16,48,512]{2,1,0:T(8,128)(2,1)} %bitcast.67), calls=%async_computation.1 | async-start | bytes 1572864 | tf_op jit(solution)/shard_map/all_to_all | solution.py:431
  25.9 1.4 %collective-permute-start = (f32[1,768]{1,0:T(1,128)}, f32[1,768]{1,0:T(1,128)S(1)}, u32[]{:S(2)}, u32[]{:S(2)}) collective-permute-start(f32[1,768]{1,0:T(1,128)} %get-tuple-element.39.refs_0_), channel_id=1, source_target_pairs={{0,1},{1,0},{2,3},{3,2},{4,5},{5,4},{6,7},{7,6},{8,9},{9,8},{10,11... | collective-permute-start | bytes 9224 | tf_op jit(solution)/shard_map/ppermute | solution.py:397
  44.6 0.9 copy-start.1
  65.0 5.5 %collective-permute-start.2 = (bf16[512,768]{1,0:T(8,128)(2,1)}, bf16[512,768]{1,0:T(8,128)(2,1)S(1)}, u32[]{:S(2)}, u32[]{:S(2)}) collective-permute-start(bf16[512,768]{1,0:T(8,128)(2,1)} %get-tuple-element.46), channel_id=1, source_target_pairs={{0,1},{1,0},{2,3},{3,2},{4,5},{5,4},{6,7},{7,6},{8,9},{9,8},{10,11... | collective-permute-start | bytes 2359304 | tf_op jit(solution)/shard_map/ppermute | solution.py:397
  65.1 3.4 %collective-permute-start.1 = (bf16[512,640]{1,0:T(8,128)(2,1)}, bf16[512,640]{1,0:T(8,128)(2,1)S(1)}, u32[]{:S(2)}, u32[]{:S(2)}) collective-permute-start(bf16[512,640]{1,0:T(8,128)(2,1)} %get-tuple-element.43), channel_id=1, source_target_pairs={{0,1},{1,0},{2,3},{3,2},{4,5},{5,4},{6,7},{7,6},{8,9},{9,8},{10,11... | collective-permute-start | bytes 1966088 | tf_op jit(solution)/shard_map/ppermute | solution.py:397
  68.5 5.7 %copy-start.4 = (bf16[512,640]{1,0:T(8,128)(2,1)}, bf16[512,640]{1,0:T(8,128)(2,1)S(1)}, u32[]{:S(2)}) copy-start(bf16[512,640]{1,0:T(8,128)(2,1)S(1)} %collective-permute-done.1) | copy-start | bytes 1966084
  70.5 27.5 %copy-start.2 = (bf16[512,768]{1,0:T(8,128)(2,1)S(1)}, bf16[512,768]{1,0:T(8,128)(2,1)}, u32[]{:S(2)}) copy-start(bf16[512,768]{1,0:T(8,128)(2,1)} %get-tuple-element.45) | copy-start | bytes 2359300
  71.7 29.5 %copy-start.3 = (bf16[512,640]{1,0:T(8,128)(2,1)S(1)}, bf16[512,640]{1,0:T(8,128)(2,1)}, u32[]{:S(2)}) copy-start(bf16[512,640]{1,0:T(8,128)(2,1)} %get-tuple-element.42) | copy-start | bytes 1966084
  74.2 43.3 %all-to-all-start.2 = ((bf16[16,48,512]{2,1,0:T(8,128)(2,1)}), bf16[16,48,512]{2,1,0:T(8,128)(2,1)S(1)}, u32[]{:S(2)}, u32[]{:S(2)}) async-start(bf16[16,48,512]{2,1,0:T(8,128)(2,1)} %bitcast.65), calls=%async_computation.2 | async-start | bytes 1572864 | tf_op jit(solution)/shard_map/all_to_all | solution.py:549
  79.1 19.0 %collective-permute-start.5 = (bf16[4,2,32,768]{3,2,0,1:T(8,128)(2,1)S(1)}, bf16[4,2,32,768]{3,2,0,1:T(8,128)(2,1)}, u32[]{:S(2)}, u32[]{:S(2)}) collective-permute-start(bf16[4,2,32,768]{3,2,0,1:T(8,128)(2,1)S(1)} %fusion), channel_id=1, source_target_pairs={{0,4},{2,6},{4,0},{6,2},{8,12},{10,14},{12,8},{14,10},{16,20},{18,... | collective-permute-start | bytes 1179656 | tf_op jit(solution)/shard_map/ppermute | solution.py:505
  81.0 20.2 %collective-permute-start.3 = (bf16[4,2,32,640]{3,2,0,1:T(8,128)(2,1)}, bf16[4,2,32,640]{3,2,0,1:T(8,128)(2,1)}, u32[]{:S(2)}, u32[]{:S(2)}) collective-permute-start(bf16[4,2,32,640]{3,2,0,1:T(8,128)(2,1)} %fusion.2), channel_id=1, source_target_pairs={{0,2},{2,0},{4,6},{6,4},{8,10},{10,8},{12,14},{14,12},{16,18},{18,... | collective-permute-start | bytes 983048 | tf_op jit(solution)/shard_map/ppermute | solution.py:505
  99.2 21.2 %copy-start = (f32[1,768]{1,0:T(1,128)S(1)}, f32[1,768]{1,0:T(1,128)}, u32[]{:S(2)}) copy-start(f32[1,768]{1,0:T(1,128)} %get-tuple-element.39.refs_0_) | copy-start | bytes 9220
  99.2 8.7 %collective-permute-start.6 = (bf16[4,32,768]{2,1,0:T(8,128)(2,1)S(1)}, bf16[4,32,768]{2,1,0:T(8,128)(2,1)S(1)}, u32[]{:S(2)}, u32[]{:S(2)}) collective-permute-start(bf16[4,32,768]{2,1,0:T(8,128)(2,1)S(1)} %get-tuple-element.61), channel_id=1, source_target_pairs={{0,2},{2,0},{4,6},{6,4},{8,10},{10,8},{12,14},{14,12},{16,18},{18,... | collective-permute-start | bytes 589832 | tf_op jit(solution)/shard_map/ppermute | solution.py:505
  102.6 5.4 %collective-permute-start.4 = (bf16[4,32,640]{2,1,0:T(8,128)(2,1)S(1)}, bf16[4,32,640]{2,1,0:T(8,128)(2,1)S(1)}, u32[]{:S(2)}, u32[]{:S(2)}) collective-permute-start(bf16[4,32,640]{2,1,0:T(8,128)(2,1)S(1)} %get-tuple-element.63), channel_id=1, source_target_pairs={{0,4},{2,6},{4,0},{6,2},{8,12},{10,14},{12,8},{14,10},{16,20},{18,... | collective-permute-start | bytes 491528 | tf_op jit(solution)/shard_map/ppermute | solution.py:505
  108.1 6.5 %collective-permute-start.7 = (bf16[32,1408]{1,0:T(8,128)(2,1)S(1)}, bf16[32,1408]{1,0:T(8,128)(2,1)S(1)}, u32[]{:S(2)}, u32[]{:S(2)}) collective-permute-start(bf16[32,1408]{1,0:T(8,128)(2,1)S(1)} %get-tuple-element.50), channel_id=1, source_target_pairs={{0,8},{2,10},{4,12},{6,14},{8,16},{10,18},{12,20},{14,22},{16,24},... | collective-permute-start | bytes 270344 | tf_op jit(solution)/shard_map/ppermute | solution.py:529
  109.0 8.1 %collective-permute-start.8 = (bf16[32,1408]{1,0:T(8,128)(2,1)S(1)}, bf16[32,1408]{1,0:T(8,128)(2,1)S(1)}, u32[]{:S(2)}, u32[]{:S(2)}) collective-permute-start(bf16[32,1408]{1,0:T(8,128)(2,1)S(1)} %get-tuple-element.51), channel_id=1, source_target_pairs={{0,16},{2,18},{4,20},{6,22},{8,24},{10,26},{12,28},{14,30},{16,0},... | collective-permute-start | bytes 270344 | tf_op jit(solution)/shard_map/ppermute | solution.py:529
  111.9 5.5 %collective-permute-start.9 = (bf16[32,1408]{1,0:T(8,128)(2,1)S(1)}, bf16[32,1408]{1,0:T(8,128)(2,1)S(1)}, u32[]{:S(2)}, u32[]{:S(2)}) collective-permute-start(bf16[32,1408]{1,0:T(8,128)(2,1)S(1)} %get-tuple-element.52), channel_id=1, source_target_pairs={{0,24},{2,26},{4,28},{6,30},{8,0},{10,2},{12,4},{14,6},{16,8},{18,... | collective-permute-start | bytes 270344 | tf_op jit(solution)/shard_map/ppermute | solution.py:529
  117.4 3.0 %collective-permute-start.10 = (bf16[768,512]{1,0:T(8,128)(2,1)S(1)}, bf16[768,512]{1,0:T(8,128)(2,1)S(1)}, u32[]{:S(2)}, u32[]{:S(2)}) collective-permute-start(bf16[768,512]{1,0:T(8,128)(2,1)S(1)} %bitcast.62), channel_id=1, source_target_pairs={{0,1},{1,0},{2,3},{3,2},{4,5},{5,4},{6,7},{7,6},{8,9},{9,8},{10,11... | collective-permute-start | bytes 2359304 | tf_op jit(solution)/shard_map/ppermute | solution.py:397
  118.1 1.6 %collective-permute-start.11 = (f32[32,256]{1,0:T(8,128)S(1)}, f32[32,256]{1,0:T(8,128)S(1)}, u32[]{:S(2)}, u32[]{:S(2)}) collective-permute-start(f32[32,256]{1,0:T(8,128)S(1)} %get-tuple-element.59), channel_id=1, source_target_pairs={{0,1},{1,0},{2,3},{3,2},{4,5},{5,4},{6,7},{7,6},{8,9},{9,8},{10,11... | collective-permute-start | bytes 98312 | tf_op jit(solution)/shard_map/ppermute | solution.py:397

commit v9 on v8

--- a/solution.py
+++ b/solution.py
@@ -10,7 +10,7 @@
 
 HEAD_DIM = 64
 LANES = 128
-QUERY_ROWS = 128
+QUERY_ROWS = 256
 
 F32 = jnp.float32
 BF16 = jnp.bfloat16
@@ -481,6 +481,20 @@
             pltpu.SemaphoreType.DMA((10 + 2 * groups,)),
         ],
     )
+    def fill_slots(row_grad):
+        return call(
+            slots_kernel,
+            [jax.ShapeDtypeStruct((slots, width), BF16)],
+            2 * slots * count * width,
+            4 * count * width,
+            (slot, row_grad),
+            far_out=(0,),
+            scratch=[
+                pltpu.VMEM((slots, width), BF16),
+                pltpu.SemaphoreType.DMA((slots // row_step(slots),)),
+            ],
+        )[0]
+
     rows = width // owners
     side = 2 if owners % 4 == 0 else 1
     plane = side * side
@@ -509,9 +523,12 @@
     if side == 2:
         left, row_grad = halve(sides[0], low, 2, 1, row_grad)
         right, row_grad = halve(sides[1], middle, 1, 2, row_grad)
+        outgoing = fill_slots(row_grad)
+        outgoing, left[-1], right[-1] = lax.optimization_barrier((outgoing, left[-1], right[-1]))
         left, _ = halve(left, middle, 1, 2)
         right, _ = halve(right, low, 1, 1)
     else:
+        outgoing = fill_slots(row_grad)
         left, right = [[term[:, 0, 0] for term in terms] for terms in sides]
     cols = cols_all
     kept, *sends = call(
@@ -534,18 +551,6 @@
         for k in range(1, outer)
     ]
 
-    (outgoing,) = call(
-        slots_kernel,
-        [jax.ShapeDtypeStruct((slots, width), BF16)],
-        2 * slots * count * width,
-        4 * count * width,
-        (slot, row_grad),
-        far_out=(0,),
-        scratch=[
-            pltpu.VMEM((slots, width), BF16),
-            pltpu.SemaphoreType.DMA((slots // row_step(slots),)),
-        ],
-    )
     incoming = lax.all_to_all(outgoing, "table", split_axis=0, concat_axis=0, tiled=True)
     incoming, *got = lax.optimization_barrier((incoming, *got))
     all_incoming = [incoming] + [shift(incoming, "group", groups, k) for k in range(1, groups)]

time: 124 us -> 118 us (0.952)
  waiting for transfers between devices: 48.1 us -> 45.4 us
  other arithmetic: 6.33 us -> 4.58 us
  Pallas kernels: 31.6 us -> 30.3 us
    ppermute x4, waiting for transfers between devices: 20.8 us -> 13.1 us  [halve(): got = lax.ppermute(send, 'table', [(i, i ^ bit) for i in range(owners)])]
    ppermute x3, waiting for transfers between devices: 4.56 us -> 9.85 us  [on_device(): lax.ppermute(sends[k - 1], 'table', [(i, (i // plane + k) % outer * plane...]
    convert_element_type x4, other arithmetic: 5.68 us -> 3.93 us  [halve(): send = add([entry(term, 1 - index, axis) for term in terms]).astype(BF16)]
    pallas_call x7, Pallas kernels: 31.6 us -> 30.3 us  [call(): pl.pallas_call(kernel, out_shape=out_shape, in_specs=[pl.BlockSpec(memory...]
  transfers between devices with their start and end apart: 14 -> 14, of which waited for: 9 -> 9; matrix products, arithmetic and copies ran while one was open for 4% -> 3% of each run, Pallas kernels for 1% -> 3%
where the time goes in v9:
time: 118 us
  waiting for transfers between devices  45.4 us (38%)
  Pallas kernels  30.3 us (26%)
  starting transfers between devices  19.5 us (17%)
  blocking collectives  15.6 us (13%)
  other arithmetic  4.58 us (4%)
  local copies, waits for them, and re-layouts  1.46 us (1%)
    pallas_call x7, Pallas kernels, call(): pl.pallas_call(kernel, out_shape=out_shape, in_specs=[pl.BlockSpec(memory...  30.3 us
    all_to_all x1, waiting for transfers between devices, on_device(): lax.all_to_all(found, 'table', split_axis=0, concat_axis=0, tiled=True)  17 us
    all_to_all x1, blocking collectives, on_device(): lax.all_to_all(requested, 'table', split_axis=0, concat_axis=0, tiled=True)  15.6 us
    ppermute x4, waiting for transfers between devices, halve(): got = lax.ppermute(send, 'table', [(i, i ^ bit) for i in range(owners)])  13.1 us
    ppermute x3, waiting for transfers between devices, on_device(): lax.ppermute(sends[k - 1], 'table', [(i, (i // plane + k) % outer * plane...  9.85 us
    ppermute x4, starting transfers between devices, halve(): got = lax.ppermute(send, 'table', [(i, i ^ bit) for i in range(owners)])  5.61 us
    ppermute x5, waiting for transfers between devices, shift(): lax.ppermute(value, axis, [(i, (i + amount) % size) for i in range(size)])  5.4 us
    ppermute x3, starting transfers between devices, on_device(): lax.ppermute(sends[k - 1], 'table', [(i, (i // plane + k) % outer * plane...  4.94 us
  transfers between devices with their start and end apart: 14, of which 9 were waited for; matrix products, arithmetic and copies ran while one was open for 3% of the time, Pallas kernels for 3%

profile of v9, /device:TPU:0, one launch (start us, length us, event | category | flops | bytes accessed | tf_op | source)
XLA Modules:
  0.0 117.8 jit_solution(12898567799447848469)
XLA Ops:
  0.6 1.7 %shard_map.119 = (s32[16,128]{1,0:T(8,128)}, f32[1,512]{1,0:T(1,128)}) custom-call(s32[1,512]{1,0:T(1,128)} %bitcast.79, s32[1,512]{1,0:T(1,128)} %bitcast.80), custom_call_target="tpu_custom_call" | custom-call | flops 16777216 | bytes 4096 | tf_op jit(solution)/shard_map/pallas_call | solution.py:49
  2.3 15.6 %all_to_all.35 = s32[16,1,128]{2,1,0:T(1,128)} all-to-all(s32[16,1,128]{2,1,0:T(1,128)} %bitcast.78), channel_id=1, replica_groups=mesh['table'=16,'group'=2] {'table'}, dimensions={0} | all-to-all | bytes 16384 | tf_op jit(solution)/shard_map/all_to_all | solution.py:420
  17.9 4.5 %shard_map.120 = (bf16[768,512]{1,0:T(8,128)(2,1)}, f32[1,768]{1,0:T(1,128)}) custom-call(s32[16,128]{1,0:T(8,128)} %bitcast.77, bf16[2048,512]{1,0:T(8,128)(2,1)} %table_ref.1), custom_call_target="tpu_custom_call" | custom-call | flops 1610612736 | bytes 2883584 | tf_op jit(solution)/shard_map/pallas_call | solution.py:49
  22.4 3.6 %all-to-all-start.1 = ((bf16[16,48,512]{2,1,0:T(8,128)(2,1)}), bf16[16,48,512]{2,1,0:T(8,128)(2,1)S(1)}, u32[]{:S(2)}, u32[]{:S(2)}) async-start(bf16[16,48,512]{2,1,0:T(8,128)(2,1)} %bitcast.67), calls=%async_computation.1 | async-start | bytes 1572864 | tf_op jit(solution)/shard_map/all_to_all | solution.py:431
  26.0 0.1 collective-permute-start
  26.1 1.4 %collective-permute-done.refs_1_ = f32[1,768]{1,0:T(1,128)S(1)} collective-permute-done((f32[1,768]{1,0:T(1,128)}, f32[1,768]{1,0:T(1,128)S(1)}, u32[]{:S(2)}, u32[]{:S(2)}) %collective-permute-start) | collective-permute-done | bytes 3104 | tf_op jit(solution)/shard_map/ppermute | solution.py:397
  27.4 17.0 %all-to-all-done.1 = bf16[16,48,512]{2,1,0:T(8,128)(2,1)S(1)} async-done(((bf16[16,48,512]{2,1,0:T(8,128)(2,1)}), bf16[16,48,512]{2,1,0:T(8,128)(2,1)S(1)}, u32[]{:S(2)}, u32[]{:S(2)}) %all-to-all-start.1) | async-done | bytes 786464 | tf_op jit(solution)/shard_map/all_to_all | solution.py:431
  44.5 0.0 copy-start.1
  44.5 0.9 copy-done.1
  45.4 18.2 %shard_map.121 = (bf16[512,512]{1,0:T(8,128)(2,1)}, bf16[512,512]{1,0:T(8,128)(2,1)}, bf16[512,640]{1,0:T(8,128)(2,1)}, bf16[512,768]{1,0:T(8,128)(2,1)}, bf16[5...) custom-call(s32[1,8]{1,0:T(1,128)} %len_ref.1, f32[1,512]{1,0:T(1,128)} %get-tuple-element.36.slot_ref, ...), custom_call_target="tpu_custom_call" | custom-call | flops 6174015488 | bytes 6291456 | tf_op jit(solution)/shard_map/pallas_call | solution.py:49
  63.6 0.1 collective-permute-start.2
  63.7 0.5 collective-permute-start.1
  64.2 2.9 %collective-permute-done.1 = bf16[512,640]{1,0:T(8,128)(2,1)S(1)} collective-permute-done((bf16[512,640]{1,0:T(8,128)(2,1)}, bf16[512,640]{1,0:T(8,128)(2,1)S(1)}, u32[]{:S(2)}, u32[]{:S(2)}) %collective-permute-start.1) | collective-permute-done | bytes 655392 | tf_op jit(solution)/shard_map/ppermute | solution.py:397
  67.1 0.0 copy-start.4
  67.1 1.3 %fusion.2 = bf16[4,2,32,640]{3,2,0,1:T(8,128)(2,1)S(1)} fusion(bf16[4,2,2,32,640]{4,3,2,1,0:T(8,128)(2,1)} %bitcast.72, s32[]{:T(128)S(6)} %select_n.71, bf16[4,2,2,32,640]{4,3,2,1,0:T(8,128)(2,1)S(1)} %bitcast.74), kind=kLoop, calls=%fused_computation.6 | loop fusion | flops 655360 | bytes 984064 | tf_op jit(solution)/shard_map/convert_element_type | solution.py:516
  68.4 0.0 collective-permute-done.2
  68.4 0.0 copy-start.2
  68.4 1.2 %fusion = bf16[4,2,32,768]{3,2,0,1:T(8,128)(2,1)S(1)} fusion(bf16[4,2,2,32,768]{4,3,2,1,0:T(8,128)(2,1)} %bitcast.68, s32[]{:T(128)S(6)} %select_n.74, bf16[4,2,2,32,768]{4,3,2,1,0:T(8,128)(2,1)S(1)} %bitcast.70), kind=kLoop, calls=%fused_computation.2 | loop fusion | flops 786432 | bytes 1180672 | tf_op jit(solution)/shard_map/convert_element_type | solution.py:516
  69.6 0.0 copy-start.3
  69.6 1.6 %collective-permute-start.4 = (bf16[4,2,32,768]{3,2,0,1:T(8,128)(2,1)S(1)}, bf16[4,2,32,768]{3,2,0,1:T(8,128)(2,1)S(1)}, u32[]{:S(2)}, u32[]{:S(2)}) collective-permute-start(bf16[4,2,32,768]{3,2,0,1:T(8,128)(2,1)S(1)} %fusion), channel_id=1, source_target_pairs={{0,4},{2,6},{4,0},{6,2},{8,12},{10,14},{12,8},{14,10},{16,20},{18,... | collective-permute-start | bytes 1179656 | tf_op jit(solution)/shard_map/ppermute | solution.py:519
  71.2 0.6 collective-permute-start.3
  71.8 2.4 %shard_map.122 = bf16[768,512]{1,0:T(8,128)(2,1)} custom-call(f32[1,512]{1,0:T(1,128)} %get-tuple-element.36.slot_ref, bf16[512,512]{1,0:T(8,128)(2,1)} %get-tuple-element.50.grad_ref), custom_call_target="tpu_custom_call" | custom-call | flops 402653184 | bytes 1048576 | tf_op jit(solution)/shard_map/pallas_call | solution.py:49
  74.1 6.5 %collective-permute-done.3 = bf16[4,2,32,640]{3,2,0,1:T(8,128)(2,1)S(1)} collective-permute-done((bf16[4,2,32,640]{3,2,0,1:T(8,128)(2,1)S(1)}, bf16[4,2,32,640]{3,2,0,1:T(8,128)(2,1)S(1)}, u32[]{:S(2)}, u32[]{:S(2)}) %collective-permute-start.3) | collective-permute-done | bytes 327712 | tf_op jit(solution)/shard_map/ppermute | solution.py:519
  80.7 0.0 copy-start.5
  80.7 0.2 collective-permute-done.4
  80.9 0.6 copy-done.5
  81.4 0.0 copy-done.4
  81.4 4.2 %all-to-all-start.2 = ((bf16[16,48,512]{2,1,0:T(8,128)(2,1)}), bf16[16,48,512]{2,1,0:T(8,128)(2,1)S(1)}, u32[]{:S(2)}, u32[]{:S(2)}) async-start(bf16[16,48,512]{2,1,0:T(8,128)(2,1)} %bitcast.65), calls=%async_computation.2 | async-start | bytes 1572864 | tf_op jit(solution)/shard_map/all_to_all | solution.py:554
  85.7 0.0 copy-done.2
  85.7 0.2 fusion.1
  85.8 0.0 copy-start
  85.8 1.9 %collective-permute-start.6 = (bf16[4,32,768]{2,1,0:T(8,128)(2,1)S(1)}, bf16[4,32,768]{2,1,0:T(8,128)(2,1)S(1)}, u32[]{:S(2)}, u32[]{:S(2)}) collective-permute-start(bf16[4,32,768]{2,1,0:T(8,128)(2,1)S(1)} %get-tuple-element.67), channel_id=1, source_target_pairs={{0,2},{2,0},{4,6},{6,4},{8,10},{10,8},{12,14},{14,12},{16,18},{18,... | collective-permute-start | bytes 589832 | tf_op jit(solution)/shard_map/ppermute | solution.py:519
  87.8 0.0 copy-done.3
  87.8 1.3 %fusion.3 = (bf16[4,32,640]{2,1,0:T(8,128)(2,1)S(1)}, f32[4,32,640]{2,1,0:T(8,128)S(1)}) fusion(bf16[4,2,32,640]{3,2,0,1:T(8,128)(2,1)} %copy-done.5, s32[]{:T(128)S(6)} %select_n.74, bf16[4,2,2,32,640]{4,3,2,1,0:T(8,128)(2,1)} %bitcast.75, s32[]{:T(128)S(6)} %select_n.79, s32[]{:T(128)S(6)} %select_n.78, bf16[4,2,2,32,640]{4,3,2,1,0:T(8,128)(2,1)S(1)} %bitcast.73, ...), kind=kLoop, calls=%fused_computation.8 | loop fusion | flops 901120 | bytes 1474580 | tf_op jit(solution)/shard_map/convert_element_type | solution.py:516
  89.1 1.5 %collective-permute-start.5 = (bf16[4,32,640]{2,1,0:T(8,128)(2,1)S(1)}, bf16[4,32,640]{2,1,0:T(8,128)(2,1)S(1)}, u32[]{:S(2)}, u32[]{:S(2)}) collective-permute-start(bf16[4,32,640]{2,1,0:T(8,128)(2,1)S(1)} %get-tuple-element.69), channel_id=1, source_target_pairs={{0,4},{2,6},{4,0},{6,2},{8,12},{10,14},{12,8},{14,10},{16,20},{18,... | collective-permute-start | bytes 491528 | tf_op jit(solution)/shard_map/ppermute | solution.py:519
  90.6 6.4 %collective-permute-done.5.refs_1_ = bf16[4,32,640]{2,1,0:T(8,128)(2,1)S(1)} collective-permute-done((bf16[4,32,640]{2,1,0:T(8,128)(2,1)S(1)}, bf16[4,32,640]{2,1,0:T(8,128)(2,1)S(1)}, u32[]{:S(2)}, u32[]{:S(2)}) %collective-permute-start.5) | collective-permute-done | bytes 163872 | tf_op jit(solution)/shard_map/ppermute | solution.py:519
  97.0 0.0 collective-permute-done.6.refs_3_
  97.0 0.1 shard_map.123
  97.1 1.5 %collective-permute-start.7 = (bf16[32,1408]{1,0:T(8,128)(2,1)S(1)}, bf16[32,1408]{1,0:T(8,128)(2,1)S(1)}, u32[]{:S(2)}, u32[]{:S(2)}) collective-permute-start(bf16[32,1408]{1,0:T(8,128)(2,1)S(1)} %get-tuple-element.56), channel_id=1, source_target_pairs={{0,8},{2,10},{4,12},{6,14},{8,16},{10,18},{12,20},{14,22},{16,24},... | collective-permute-start | bytes 270344 | tf_op jit(solution)/shard_map/ppermute | solution.py:546
  98.6 3.4 %collective-permute-start.8 = (bf16[32,1408]{1,0:T(8,128)(2,1)S(1)}, bf16[32,1408]{1,0:T(8,128)(2,1)S(1)}, u32[]{:S(2)}, u32[]{:S(2)}) collective-permute-start(bf16[32,1408]{1,0:T(8,128)(2,1)S(1)} %get-tuple-element.57), channel_id=1, source_target_pairs={{0,16},{2,18},{4,20},{6,22},{8,24},{10,26},{12,28},{14,30},{16,0},... | collective-permute-start | bytes 270344 | tf_op jit(solution)/shard_map/ppermute | solution.py:546
  102.1 0.0 collective-permute-start.9
  102.1 3.0 %collective-permute-done.7.refs_0_ = bf16[32,1408]{1,0:T(8,128)(2,1)S(1)} collective-permute-done((bf16[32,1408]{1,0:T(8,128)(2,1)S(1)}, bf16[32,1408]{1,0:T(8,128)(2,1)S(1)}, u32[]{:S(2)}, u32[]{:S(2)}) %collective-permute-start.7) | collective-permute-done | bytes 90144 | tf_op jit(solution)/shard_map/ppermute | solution.py:546
  105.0 6.9 %collective-permute-done.8.refs_1_ = bf16[32,1408]{1,0:T(8,128)(2,1)S(1)} collective-permute-done((bf16[32,1408]{1,0:T(8,128)(2,1)S(1)}, bf16[32,1408]{1,0:T(8,128)(2,1)S(1)}, u32[]{:S(2)}, u32[]{:S(2)}) %collective-permute-start.8) | collective-permute-done | bytes 90144 | tf_op jit(solution)/shard_map/ppermute | solution.py:546
  111.9 0.0 collective-permute-done.9.refs_2_
  111.9 0.0 all-to-all-done.2
  111.9 0.0 collective-permute-start.10
  111.9 0.7 shard_map.125
  112.6 0.5 collective-permute-start.11
  113.1 1.1 collective-permute-done.11
  114.3 0.6 pad_maximum_fusion
  114.9 0.0 collective-permute-done.10.refs_3_
  114.9 0.0 copy-done
  114.9 2.7 %shard_map.124 = f32[1024,512]{1,0:T(8,128)} custom-call(f32[1,768]{1,0:T(1,128)S(1)} %copy-done, f32[1,768]{1,0:T(1,128)S(1)} %collective-permute-done.refs_1_, bf16[768,512]{1,0:T(8,128)(2,1)S(1)} %bitcast.63, bf16[768,512]{1,0:T(8,128)(2,1)S(1)} %collective-permute-done.10.refs_3_), custom_call_target="tpu_custom_call" | custom-call | flops 1610612736 | bytes 3670016 | tf_op jit(solution)/shard_map/pallas_call | solution.py:49
  (1 shorter events, 0.0 us)
Async XLA Ops:
  22.4 22.1 %all-to-all-start.1 = ((bf16[16,48,512]{2,1,0:T(8,128)(2,1)}), bf16[16,48,512]{2,1,0:T(8,128)(2,1)S(1)}, u32[]{:S(2)}, u32[]{:S(2)}) async-start(bf16[16,48,512]{2,1,0:T(8,128)(2,1)} %bitcast.67), calls=%async_computation.1 | async-start | bytes 1572864 | tf_op jit(solution)/shard_map/all_to_all | solution.py:431
  26.0 1.4 %collective-permute-start = (f32[1,768]{1,0:T(1,128)}, f32[1,768]{1,0:T(1,128)S(1)}, u32[]{:S(2)}, u32[]{:S(2)}) collective-permute-start(f32[1,768]{1,0:T(1,128)} %get-tuple-element.42.refs_0_), channel_id=1, source_target_pairs={{0,1},{1,0},{2,3},{3,2},{4,5},{5,4},{6,7},{7,6},{8,9},{9,8},{10,11... | collective-permute-start | bytes 9224 | tf_op jit(solution)/shard_map/ppermute | solution.py:397
  44.5 0.9 copy-start.1
  63.6 4.8 %collective-permute-start.2 = (bf16[512,768]{1,0:T(8,128)(2,1)}, bf16[512,768]{1,0:T(8,128)(2,1)S(1)}, u32[]{:S(2)}, u32[]{:S(2)}) collective-permute-start(bf16[512,768]{1,0:T(8,128)(2,1)} %get-tuple-element.49), channel_id=1, source_target_pairs={{0,1},{1,0},{2,3},{3,2},{4,5},{5,4},{6,7},{7,6},{8,9},{9,8},{10,11... | collective-permute-start | bytes 2359304 | tf_op jit(solution)/shard_map/ppermute | solution.py:397
  63.7 3.4 %collective-permute-start.1 = (bf16[512,640]{1,0:T(8,128)(2,1)}, bf16[512,640]{1,0:T(8,128)(2,1)S(1)}, u32[]{:S(2)}, u32[]{:S(2)}) collective-permute-start(bf16[512,640]{1,0:T(8,128)(2,1)} %get-tuple-element.46), channel_id=1, source_target_pairs={{0,1},{1,0},{2,3},{3,2},{4,5},{5,4},{6,7},{7,6},{8,9},{9,8},{10,11... | collective-permute-start | bytes 1966088 | tf_op jit(solution)/shard_map/ppermute | solution.py:397
  67.1 14.3 %copy-start.4 = (bf16[512,640]{1,0:T(8,128)(2,1)}, bf16[512,640]{1,0:T(8,128)(2,1)S(1)}, u32[]{:S(2)}) copy-start(bf16[512,640]{1,0:T(8,128)(2,1)S(1)} %collective-permute-done.1) | copy-start | bytes 1966084
  68.4 17.3 %copy-start.2 = (bf16[512,768]{1,0:T(8,128)(2,1)S(1)}, bf16[512,768]{1,0:T(8,128)(2,1)}, u32[]{:S(2)}) copy-start(bf16[512,768]{1,0:T(8,128)(2,1)} %get-tuple-element.48) | copy-start | bytes 2359300
  69.6 18.2 %copy-start.3 = (bf16[512,640]{1,0:T(8,128)(2,1)S(1)}, bf16[512,640]{1,0:T(8,128)(2,1)}, u32[]{:S(2)}) copy-start(bf16[512,640]{1,0:T(8,128)(2,1)} %get-tuple-element.45) | copy-start | bytes 1966084
  69.6 11.2 %collective-permute-start.4 = (bf16[4,2,32,768]{3,2,0,1:T(8,128)(2,1)S(1)}, bf16[4,2,32,768]{3,2,0,1:T(8,128)(2,1)S(1)}, u32[]{:S(2)}, u32[]{:S(2)}) collective-permute-start(bf16[4,2,32,768]{3,2,0,1:T(8,128)(2,1)S(1)} %fusion), channel_id=1, source_target_pairs={{0,4},{2,6},{4,0},{6,2},{8,12},{10,14},{12,8},{14,10},{16,20},{18,... | collective-permute-start | bytes 1179656 | tf_op jit(solution)/shard_map/ppermute | solution.py:519
  71.2 9.5 %collective-permute-start.3 = (bf16[4,2,32,640]{3,2,0,1:T(8,128)(2,1)S(1)}, bf16[4,2,32,640]{3,2,0,1:T(8,128)(2,1)S(1)}, u32[]{:S(2)}, u32[]{:S(2)}) collective-permute-start(bf16[4,2,32,640]{3,2,0,1:T(8,128)(2,1)S(1)} %fusion.2), channel_id=1, source_target_pairs={{0,2},{2,0},{4,6},{6,4},{8,10},{10,8},{12,14},{14,12},{16,18},{18,... | collective-permute-start | bytes 983048 | tf_op jit(solution)/shard_map/ppermute | solution.py:519
  80.7 0.7 copy-start.5
  81.4 30.5 %all-to-all-start.2 = ((bf16[16,48,512]{2,1,0:T(8,128)(2,1)}), bf16[16,48,512]{2,1,0:T(8,128)(2,1)S(1)}, u32[]{:S(2)}, u32[]{:S(2)}) async-start(bf16[16,48,512]{2,1,0:T(8,128)(2,1)} %bitcast.65), calls=%async_computation.2 | async-start | bytes 1572864 | tf_op jit(solution)/shard_map/all_to_all | solution.py:554
  85.8 29.1 %copy-start = (f32[1,768]{1,0:T(1,128)S(1)}, f32[1,768]{1,0:T(1,128)}, u32[]{:S(2)}) copy-start(f32[1,768]{1,0:T(1,128)} %get-tuple-element.42.refs_0_) | copy-start | bytes 9220
  85.8 11.2 %collective-permute-start.6 = (bf16[4,32,768]{2,1,0:T(8,128)(2,1)S(1)}, bf16[4,32,768]{2,1,0:T(8,128)(2,1)S(1)}, u32[]{:S(2)}, u32[]{:S(2)}) collective-permute-start(bf16[4,32,768]{2,1,0:T(8,128)(2,1)S(1)} %get-tuple-element.67), channel_id=1, source_target_pairs={{0,2},{2,0},{4,6},{6,4},{8,10},{10,8},{12,14},{14,12},{16,18},{18,... | collective-permute-start | bytes 589832 | tf_op jit(solution)/shard_map/ppermute | solution.py:519
  89.1 7.9 %collective-permute-start.5 = (bf16[4,32,640]{2,1,0:T(8,128)(2,1)S(1)}, bf16[4,32,640]{2,1,0:T(8,128)(2,1)S(1)}, u32[]{:S(2)}, u32[]{:S(2)}) collective-permute-start(bf16[4,32,640]{2,1,0:T(8,128)(2,1)S(1)} %get-tuple-element.69), channel_id=1, source_target_pairs={{0,4},{2,6},{4,0},{6,2},{8,12},{10,14},{12,8},{14,10},{16,20},{18,... | collective-permute-start | bytes 491528 | tf_op jit(solution)/shard_map/ppermute | solution.py:519
  97.1 7.9 %collective-permute-start.7 = (bf16[32,1408]{1,0:T(8,128)(2,1)S(1)}, bf16[32,1408]{1,0:T(8,128)(2,1)S(1)}, u32[]{:S(2)}, u32[]{:S(2)}) collective-permute-start(bf16[32,1408]{1,0:T(8,128)(2,1)S(1)} %get-tuple-element.56), channel_id=1, source_target_pairs={{0,8},{2,10},{4,12},{6,14},{8,16},{10,18},{12,20},{14,22},{16,24},... | collective-permute-start | bytes 270344 | tf_op jit(solution)/shard_map/ppermute | solution.py:546
  98.6 13.3 %collective-permute-start.8 = (bf16[32,1408]{1,0:T(8,128)(2,1)S(1)}, bf16[32,1408]{1,0:T(8,128)(2,1)S(1)}, u32[]{:S(2)}, u32[]{:S(2)}) collective-permute-start(bf16[32,1408]{1,0:T(8,128)(2,1)S(1)} %get-tuple-element.57), channel_id=1, source_target_pairs={{0,16},{2,18},{4,20},{6,22},{8,24},{10,26},{12,28},{14,30},{16,0},... | collective-permute-start | bytes 270344 | tf_op jit(solution)/shard_map/ppermute | solution.py:546
  102.1 9.9 %collective-permute-start.9 = (bf16[32,1408]{1,0:T(8,128)(2,1)S(1)}, bf16[32,1408]{1,0:T(8,128)(2,1)S(1)}, u32[]{:S(2)}, u32[]{:S(2)}) collective-permute-start(bf16[32,1408]{1,0:T(8,128)(2,1)S(1)} %get-tuple-element.58), channel_id=1, source_target_pairs={{0,24},{2,26},{4,28},{6,30},{8,0},{10,2},{12,4},{14,6},{16,8},{18,... | collective-permute-start | bytes 270344 | tf_op jit(solution)/shard_map/ppermute | solution.py:546
  111.9 3.0 %collective-permute-start.10 = (bf16[768,512]{1,0:T(8,128)(2,1)S(1)}, bf16[768,512]{1,0:T(8,128)(2,1)S(1)}, u32[]{:S(2)}, u32[]{:S(2)}) collective-permute-start(bf16[768,512]{1,0:T(8,128)(2,1)S(1)} %bitcast.62), channel_id=1, source_target_pairs={{0,1},{1,0},{2,3},{3,2},{4,5},{5,4},{6,7},{7,6},{8,9},{9,8},{10,11... | collective-permute-start | bytes 2359304 | tf_op jit(solution)/shard_map/ppermute | solution.py:397
  112.6 1.6 %collective-permute-start.11 = (f32[32,256]{1,0:T(8,128)S(1)}, f32[32,256]{1,0:T(8,128)S(1)}, u32[]{:S(2)}, u32[]{:S(2)}) collective-permute-start(f32[32,256]{1,0:T(8,128)S(1)} %get-tuple-element.65), channel_id=1, source_target_pairs={{0,1},{1,0},{2,3},{3,2},{4,5},{5,4},{6,7},{7,6},{8,9},{9,8},{10,11... | collective-permute-start | bytes 98312 | tf_op jit(solution)/shard_map/ppermute | solution.py:397

commit v10 on v9

--- a/solution.py
+++ b/solution.py
@@ -197,8 +197,9 @@
     get_ret.wait()
     emb_ref[...] = dot_nn(pick_ref[...], ret_ref[...]).astype(BF16)
 
+    for fetch in get_ins:
+        fetch.wait()
     for i in range(4):
-        get_ins[i].wait()
         pre = dot_nn(emb_ref[...], w_in_ref[:, parts[i]])
         half = 0.5 * pre
         th = jnp.tanh(half)
@@ -258,7 +259,7 @@
             att_ref[r0:r1, cols] = total
         return 0
 
-    lax.fori_loop(0, slabs, forward, 0)
+    lax.fori_loop(0, slabs, forward, 0, unroll=2)
 
     get_cot.wait()
     get_out.wait()
@@ -318,7 +319,7 @@
         gpre_ref[:, pl.ds(3 * width + start, LANES)] = (gkey_ref[...].T * slope_ref[3, :, cols]).astype(BF16)
         return 0
 
-    lax.fori_loop(0, slabs, backward, 0)
+    lax.fori_loop(0, slabs, backward, 0, unroll=2)
 
     puts = [put_result]
     me = lax.axis_index("group")
@@ -524,7 +525,6 @@
         left, row_grad = halve(sides[0], low, 2, 1, row_grad)
         right, row_grad = halve(sides[1], middle, 1, 2, row_grad)
         outgoing = fill_slots(row_grad)
-        outgoing, left[-1], right[-1] = lax.optimization_barrier((outgoing, left[-1], right[-1]))
         left, _ = halve(left, middle, 1, 2)
         right, _ = halve(right, low, 1, 1)
     else:
@@ -538,7 +538,7 @@
             *[jax.ShapeDtypeStruct((rows, cols), BF16) for _ in range(1, outer)],
         ],
         12 * outer * rows * cols,
-        8 * outer * rows * cols,
+        160 * outer * rows * cols,
         (*left, *right),
         limit=24,
     )
@@ -552,7 +552,7 @@
     ]
 
     incoming = lax.all_to_all(outgoing, "table", split_axis=0, concat_axis=0, tiled=True)
-    incoming, *got = lax.optimization_barrier((incoming, *got))
+    incoming, kept = lax.optimization_barrier((incoming, kept))
     all_incoming = [incoming] + [shift(incoming, "group", groups, k) for k in range(1, groups)]
     grad_rows = table.shape[0] // groups
     (table_grad,) = call(

time: 118 us -> 122 us (1.034)
  waiting for transfers between devices: 45.4 us -> 49.6 us
  other arithmetic: 4.58 us -> 6.33 us
    ppermute x4, waiting for transfers between devices: 13.1 us -> 20.9 us  [halve(): got = lax.ppermute(send, 'table', [(i, i ^ bit) for i in range(owners)])]
    ppermute x3, waiting for transfers between devices: 9.85 us -> 5.91 us  [on_device(): lax.ppermute(sends[k - 1], 'table', [(i, (i // plane + k) % outer * plane...]
    convert_element_type x4, other arithmetic: 3.93 us -> 5.68 us  [halve(): send = add([entry(term, 1 - index, axis) for term in terms]).astype(BF16)]
  transfers between devices with their start and end apart: 14 -> 14, of which waited for: 9 -> 8; matrix products, arithmetic and copies ran while one was open for 3% -> 4% of each run, Pallas kernels for 3% -> 1%
where the time goes in v10:
time: 122 us
  waiting for transfers between devices  49.6 us (41%)
  Pallas kernels  29.1 us (24%)
  starting transfers between devices  19.5 us (16%)
  blocking collectives  15.5 us (13%)
  other arithmetic  6.33 us (5%)
    pallas_call x7, Pallas kernels, call(): pl.pallas_call(kernel, out_shape=out_shape, in_specs=[pl.BlockSpec(memory...  29.1 us
    ppermute x4, waiting for transfers between devices, halve(): got = lax.ppermute(send, 'table', [(i, i ^ bit) for i in range(owners)])  20.9 us
    all_to_all x1, waiting for transfers between devices, on_device(): lax.all_to_all(found, 'table', split_axis=0, concat_axis=0, tiled=True)  17.3 us
    all_to_all x1, blocking collectives, on_device(): lax.all_to_all(requested, 'table', split_axis=0, concat_axis=0, tiled=True)  15.5 us
    ppermute x3, waiting for transfers between devices, on_device(): lax.ppermute(sends[k - 1], 'table', [(i, (i // plane + k) % outer * plane...  5.91 us
    convert_element_type x4, other arithmetic, halve(): send = add([entry(term, 1 - index, axis) for term in terms]).astype(BF16)  5.68 us
    ppermute x4, starting transfers between devices, halve(): got = lax.ppermute(send, 'table', [(i, i ^ bit) for i in range(owners)])  5.53 us
    ppermute x5, waiting for transfers between devices, shift(): lax.ppermute(value, axis, [(i, (i + amount) % size) for i in range(size)])  5.48 us
  transfers between devices with their start and end apart: 14, of which 8 were waited for; matrix products, arithmetic and copies ran while one was open for 4% of the time, Pallas kernels for 1%

profile of v10, /device:TPU:0, one launch (start us, length us, event | category | flops | bytes accessed | tf_op | source)
XLA Modules:
  0.0 121.6 jit_solution(12637395336522462107)
XLA Ops:
  0.6 1.7 %shard_map.119 = (s32[16,128]{1,0:T(8,128)}, f32[1,512]{1,0:T(1,128)}) custom-call(s32[1,512]{1,0:T(1,128)} %bitcast.79, s32[1,512]{1,0:T(1,128)} %bitcast.80), custom_call_target="tpu_custom_call" | custom-call | flops 16777216 | bytes 4096 | tf_op jit(solution)/shard_map/pallas_call | solution.py:49
  2.3 15.5 %all_to_all.35 = s32[16,1,128]{2,1,0:T(1,128)} all-to-all(s32[16,1,128]{2,1,0:T(1,128)} %bitcast.78), channel_id=1, replica_groups=mesh['table'=16,'group'=2] {'table'}, dimensions={0} | all-to-all | bytes 16384 | tf_op jit(solution)/shard_map/all_to_all | solution.py:421
  17.7 4.5 %shard_map.120 = (bf16[768,512]{1,0:T(8,128)(2,1)}, f32[1,768]{1,0:T(1,128)}) custom-call(s32[16,128]{1,0:T(8,128)} %bitcast.77, bf16[2048,512]{1,0:T(8,128)(2,1)} %table_ref.1), custom_call_target="tpu_custom_call" | custom-call | flops 1610612736 | bytes 2883584 | tf_op jit(solution)/shard_map/pallas_call | solution.py:49
  22.2 3.6 %all-to-all-start.1 = ((bf16[16,48,512]{2,1,0:T(8,128)(2,1)}), bf16[16,48,512]{2,1,0:T(8,128)(2,1)S(1)}, u32[]{:S(2)}, u32[]{:S(2)}) async-start(bf16[16,48,512]{2,1,0:T(8,128)(2,1)} %bitcast.67), calls=%async_computation.1 | async-start | bytes 1572864 | tf_op jit(solution)/shard_map/all_to_all | solution.py:432
  25.9 0.1 collective-permute-start
  25.9 1.4 %collective-permute-done.refs_1_ = f32[1,768]{1,0:T(1,128)S(1)} collective-permute-done((f32[1,768]{1,0:T(1,128)}, f32[1,768]{1,0:T(1,128)S(1)}, u32[]{:S(2)}, u32[]{:S(2)}) %collective-permute-start) | collective-permute-done | bytes 3104 | tf_op jit(solution)/shard_map/ppermute | solution.py:398
  27.3 17.3 %all-to-all-done.1 = bf16[16,48,512]{2,1,0:T(8,128)(2,1)S(1)} async-done(((bf16[16,48,512]{2,1,0:T(8,128)(2,1)}), bf16[16,48,512]{2,1,0:T(8,128)(2,1)S(1)}, u32[]{:S(2)}, u32[]{:S(2)}) %all-to-all-start.1) | async-done | bytes 786464 | tf_op jit(solution)/shard_map/all_to_all | solution.py:432
  44.6 0.0 copy-start.1
  44.6 0.9 copy-done.1
  45.5 17.0 %shard_map.121 = (bf16[512,512]{1,0:T(8,128)(2,1)}, bf16[512,512]{1,0:T(8,128)(2,1)}, bf16[512,640]{1,0:T(8,128)(2,1)}, bf16[512,768]{1,0:T(8,128)(2,1)}, bf16[5...) custom-call(s32[1,8]{1,0:T(1,128)} %len_ref.1, f32[1,512]{1,0:T(1,128)} %get-tuple-element.31.slot_ref, ...), custom_call_target="tpu_custom_call" | custom-call | flops 6174015488 | bytes 6291456 | tf_op jit(solution)/shard_map/pallas_call | solution.py:49
  62.5 0.1 collective-permute-start.2
  62.5 0.5 collective-permute-start.1
  63.0 2.9 %collective-permute-done.1 = bf16[512,640]{1,0:T(8,128)(2,1)S(1)} collective-permute-done((bf16[512,640]{1,0:T(8,128)(2,1)}, bf16[512,640]{1,0:T(8,128)(2,1)S(1)}, u32[]{:S(2)}, u32[]{:S(2)}) %collective-permute-start.1) | collective-permute-done | bytes 655392 | tf_op jit(solution)/shard_map/ppermute | solution.py:398
  66.0 0.0 copy-start.4
  66.0 2.0 %fusion.2 = bf16[4,2,32,640]{3,2,0,1:T(8,128)(2,1)} fusion(bf16[4,2,2,32,640]{4,3,2,1,0:T(8,128)(2,1)} %bitcast.72, s32[]{:T(128)S(6)} %select_n.71, bf16[4,2,2,32,640]{4,3,2,1,0:T(8,128)(2,1)S(1)} %bitcast.74), kind=kLoop, calls=%fused_computation.6 | loop fusion | flops 655360 | bytes 984064 | tf_op jit(solution)/shard_map/convert_element_type | solution.py:517
  68.0 0.0 collective-permute-done.2
  68.0 0.0 copy-start.2
  68.0 1.2 fusion
  69.2 0.0 copy-start.3
  69.2 2.4 %shard_map.122 = bf16[768,512]{1,0:T(8,128)(2,1)} custom-call(f32[1,512]{1,0:T(1,128)} %get-tuple-element.31.slot_ref, bf16[512,512]{1,0:T(8,128)(2,1)} %get-tuple-element.45.grad_ref), custom_call_target="tpu_custom_call" | custom-call | flops 402653184 | bytes 1048576 | tf_op jit(solution)/shard_map/pallas_call | solution.py:49
  71.6 0.0 copy-done.4
  71.6 4.8 %all-to-all-start.2 = ((bf16[16,48,512]{2,1,0:T(8,128)(2,1)}), bf16[16,48,512]{2,1,0:T(8,128)(2,1)S(1)}, u32[]{:S(2)}, u32[]{:S(2)}) async-start(bf16[16,48,512]{2,1,0:T(8,128)(2,1)} %bitcast.65), calls=%async_computation.2 | async-start | bytes 1572864 | tf_op jit(solution)/shard_map/all_to_all | solution.py:554
  76.5 1.9 %collective-permute-start.5 = (bf16[4,2,32,768]{3,2,0,1:T(8,128)(2,1)S(1)}, bf16[4,2,32,768]{3,2,0,1:T(8,128)(2,1)}, u32[]{:S(2)}, u32[]{:S(2)}) collective-permute-start(bf16[4,2,32,768]{3,2,0,1:T(8,128)(2,1)S(1)} %fusion), channel_id=1, source_target_pairs={{0,4},{2,6},{4,0},{6,2},{8,12},{10,14},{12,8},{14,10},{16,20},{18,... | collective-permute-start | bytes 1179656 | tf_op jit(solution)/shard_map/ppermute | solution.py:520
  78.4 1.5 %collective-permute-start.3 = (bf16[4,2,32,640]{3,2,0,1:T(8,128)(2,1)}, bf16[4,2,32,640]{3,2,0,1:T(8,128)(2,1)}, u32[]{:S(2)}, u32[]{:S(2)}) collective-permute-start(bf16[4,2,32,640]{3,2,0,1:T(8,128)(2,1)} %fusion.2), channel_id=1, source_target_pairs={{0,2},{2,0},{4,6},{6,4},{8,10},{10,8},{12,14},{14,12},{16,18},{18,... | collective-permute-start | bytes 983048 | tf_op jit(solution)/shard_map/ppermute | solution.py:520
  79.9 15.6 %collective-permute-done.5 = bf16[4,2,32,768]{3,2,0,1:T(8,128)(2,1)} collective-permute-done((bf16[4,2,32,768]{3,2,0,1:T(8,128)(2,1)S(1)}, bf16[4,2,32,768]{3,2,0,1:T(8,128)(2,1)}, u32[]{:S(2)}, u32[]{:S(2)}) %collective-permute-start.5) | collective-permute-done | bytes 393248 | tf_op jit(solution)/shard_map/ppermute | solution.py:520
  95.5 0.0 copy-done.2
  95.5 1.2 fusion.1
  96.7 0.0 copy-start
  96.7 2.0 %collective-permute-start.6 = (bf16[4,32,768]{2,1,0:T(8,128)(2,1)S(1)}, bf16[4,32,768]{2,1,0:T(8,128)(2,1)S(1)}, u32[]{:S(2)}, u32[]{:S(2)}) collective-permute-start(bf16[4,32,768]{2,1,0:T(8,128)(2,1)S(1)} %get-tuple-element.57), channel_id=1, source_target_pairs={{0,2},{2,0},{4,6},{6,4},{8,10},{10,8},{12,14},{14,12},{16,18},{18,... | collective-permute-start | bytes 589832 | tf_op jit(solution)/shard_map/ppermute | solution.py:520
  98.7 0.0 collective-permute-done.3
  98.7 0.0 copy-done.3
  98.7 1.3 %fusion.3 = (bf16[4,32,640]{2,1,0:T(8,128)(2,1)S(1)}, f32[4,32,640]{2,1,0:T(8,128)S(1)}) fusion(bf16[4,2,32,640]{3,2,0,1:T(8,128)(2,1)} %collective-permute-done.3, s32[]{:T(128)S(6)} %select_n.74, bf16[4,2,2,32,640]{4,3,2,1,0:T(8,128)(2,1)} %bitcast.75, s32[]{:T(128)S(6)} %select_n.79, s32[]{:T(128)S(6)} %select_n.78, ...), kind=kLoop, calls=%fused_computation.8 | loop fusion | flops 901120 | bytes 1474580 | tf_op jit(solution)/shard_map/convert_element_type | solution.py:517
  100.0 0.1 collective-permute-start.4
  100.1 5.3 %collective-permute-done.4.refs_1_ = bf16[4,32,640]{2,1,0:T(8,128)(2,1)S(1)} collective-permute-done((bf16[4,32,640]{2,1,0:T(8,128)(2,1)S(1)}, bf16[4,32,640]{2,1,0:T(8,128)(2,1)S(1)}, u32[]{:S(2)}, u32[]{:S(2)}) %collective-permute-start.4) | collective-permute-done | bytes 163872 | tf_op jit(solution)/shard_map/ppermute | solution.py:520
  105.4 0.0 collective-permute-done.6.refs_3_
  105.4 0.1 shard_map.123
  105.5 0.0 all-to-all-done.2
  105.5 0.1 collective-permute-start.7
  105.6 1.0 collective-permute-start.8
  106.6 2.9 %collective-permute-start.9 = (bf16[32,1408]{1,0:T(8,128)(2,1)S(1)}, bf16[32,1408]{1,0:T(8,128)(2,1)S(1)}, u32[]{:S(2)}, u32[]{:S(2)}) collective-permute-start(bf16[32,1408]{1,0:T(8,128)(2,1)S(1)} %get-tuple-element.52), channel_id=1, source_target_pairs={{0,16},{2,18},{4,20},{6,22},{8,24},{10,26},{12,28},{14,30},{16,0},... | collective-permute-start | bytes 270344 | tf_op jit(solution)/shard_map/ppermute | solution.py:546
  109.5 0.9 collective-permute-start.10
  110.4 2.5 %collective-permute-done.8.refs_0_ = bf16[32,1408]{1,0:T(8,128)(2,1)S(1)} collective-permute-done((bf16[32,1408]{1,0:T(8,128)(2,1)S(1)}, bf16[32,1408]{1,0:T(8,128)(2,1)S(1)}, u32[]{:S(2)}, u32[]{:S(2)}) %collective-permute-start.8) | collective-permute-done | bytes 90144 | tf_op jit(solution)/shard_map/ppermute | solution.py:546
  112.9 3.4 %collective-permute-done.9.refs_1_ = bf16[32,1408]{1,0:T(8,128)(2,1)S(1)} collective-permute-done((bf16[32,1408]{1,0:T(8,128)(2,1)S(1)}, bf16[32,1408]{1,0:T(8,128)(2,1)S(1)}, u32[]{:S(2)}, u32[]{:S(2)}) %collective-permute-start.9) | collective-permute-done | bytes 90144 | tf_op jit(solution)/shard_map/ppermute | solution.py:546
  116.3 0.0 collective-permute-done.10.refs_2_
  116.3 0.7 shard_map.125
  117.0 0.0 collective-permute-start.11
  117.0 1.2 collective-permute-done.11
  118.2 0.6 pad_maximum_fusion
  118.9 0.0 collective-permute-done.7.refs_3_
  118.9 0.0 copy-done
  118.9 2.8 %shard_map.124 = f32[1024,512]{1,0:T(8,128)} custom-call(f32[1,768]{1,0:T(1,128)S(1)} %copy-done, f32[1,768]{1,0:T(1,128)S(1)} %collective-permute-done.refs_1_, bf16[768,512]{1,0:T(8,128)(2,1)S(1)} %bitcast.63, bf16[768,512]{1,0:T(8,128)(2,1)S(1)} %collective-permute-done.7.refs_3_), custom_call_target="tpu_custom_call" | custom-call | flops 1610612736 | bytes 3670016 | tf_op jit(solution)/shard_map/pallas_call | solution.py:49
  (1 shorter events, 0.0 us)
Async XLA Ops:
  22.2 22.3 %all-to-all-start.1 = ((bf16[16,48,512]{2,1,0:T(8,128)(2,1)}), bf16[16,48,512]{2,1,0:T(8,128)(2,1)S(1)}, u32[]{:S(2)}, u32[]{:S(2)}) async-start(bf16[16,48,512]{2,1,0:T(8,128)(2,1)} %bitcast.67), calls=%async_computation.1 | async-start | bytes 1572864 | tf_op jit(solution)/shard_map/all_to_all | solution.py:432
  25.9 1.4 %collective-permute-start = (f32[1,768]{1,0:T(1,128)}, f32[1,768]{1,0:T(1,128)S(1)}, u32[]{:S(2)}, u32[]{:S(2)}) collective-permute-start(f32[1,768]{1,0:T(1,128)} %get-tuple-element.37.refs_0_), channel_id=1, source_target_pairs={{0,1},{1,0},{2,3},{3,2},{4,5},{5,4},{6,7},{7,6},{8,9},{9,8},{10,11... | collective-permute-start | bytes 9224 | tf_op jit(solution)/shard_map/ppermute | solution.py:398
  44.6 0.9 copy-start.1
  62.5 5.5 %collective-permute-start.2 = (bf16[512,768]{1,0:T(8,128)(2,1)}, bf16[512,768]{1,0:T(8,128)(2,1)S(1)}, u32[]{:S(2)}, u32[]{:S(2)}) collective-permute-start(bf16[512,768]{1,0:T(8,128)(2,1)} %get-tuple-element.44), channel_id=1, source_target_pairs={{0,1},{1,0},{2,3},{3,2},{4,5},{5,4},{6,7},{7,6},{8,9},{9,8},{10,11... | collective-permute-start | bytes 2359304 | tf_op jit(solution)/shard_map/ppermute | solution.py:398
  62.5 3.4 %collective-permute-start.1 = (bf16[512,640]{1,0:T(8,128)(2,1)}, bf16[512,640]{1,0:T(8,128)(2,1)S(1)}, u32[]{:S(2)}, u32[]{:S(2)}) collective-permute-start(bf16[512,640]{1,0:T(8,128)(2,1)} %get-tuple-element.41), channel_id=1, source_target_pairs={{0,1},{1,0},{2,3},{3,2},{4,5},{5,4},{6,7},{7,6},{8,9},{9,8},{10,11... | collective-permute-start | bytes 1966088 | tf_op jit(solution)/shard_map/ppermute | solution.py:398
  66.0 5.7 %copy-start.4 = (bf16[512,640]{1,0:T(8,128)(2,1)}, bf16[512,640]{1,0:T(8,128)(2,1)S(1)}, u32[]{:S(2)}) copy-start(bf16[512,640]{1,0:T(8,128)(2,1)S(1)} %collective-permute-done.1) | copy-start | bytes 1966084
  68.0 27.5 %copy-start.2 = (bf16[512,768]{1,0:T(8,128)(2,1)S(1)}, bf16[512,768]{1,0:T(8,128)(2,1)}, u32[]{:S(2)}) copy-start(bf16[512,768]{1,0:T(8,128)(2,1)} %get-tuple-element.43) | copy-start | bytes 2359300
  69.2 29.5 %copy-start.3 = (bf16[512,640]{1,0:T(8,128)(2,1)S(1)}, bf16[512,640]{1,0:T(8,128)(2,1)}, u32[]{:S(2)}) copy-start(bf16[512,640]{1,0:T(8,128)(2,1)} %get-tuple-element.40) | copy-start | bytes 1966084
  71.6 33.8 %all-to-all-start.2 = ((bf16[16,48,512]{2,1,0:T(8,128)(2,1)}), bf16[16,48,512]{2,1,0:T(8,128)(2,1)S(1)}, u32[]{:S(2)}, u32[]{:S(2)}) async-start(bf16[16,48,512]{2,1,0:T(8,128)(2,1)} %bitcast.65), calls=%async_computation.2 | async-start | bytes 1572864 | tf_op jit(solution)/shard_map/all_to_all | solution.py:554
  76.5 19.0 %collective-permute-start.5 = (bf16[4,2,32,768]{3,2,0,1:T(8,128)(2,1)S(1)}, bf16[4,2,32,768]{3,2,0,1:T(8,128)(2,1)}, u32[]{:S(2)}, u32[]{:S(2)}) collective-permute-start(bf16[4,2,32,768]{3,2,0,1:T(8,128)(2,1)S(1)} %fusion), channel_id=1, source_target_pairs={{0,4},{2,6},{4,0},{6,2},{8,12},{10,14},{12,8},{14,10},{16,20},{18,... | collective-permute-start | bytes 1179656 | tf_op jit(solution)/shard_map/ppermute | solution.py:520
  78.4 20.3 %collective-permute-start.3 = (bf16[4,2,32,640]{3,2,0,1:T(8,128)(2,1)}, bf16[4,2,32,640]{3,2,0,1:T(8,128)(2,1)}, u32[]{:S(2)}, u32[]{:S(2)}) collective-permute-start(bf16[4,2,32,640]{3,2,0,1:T(8,128)(2,1)} %fusion.2), channel_id=1, source_target_pairs={{0,2},{2,0},{4,6},{6,4},{8,10},{10,8},{12,14},{14,12},{16,18},{18,... | collective-permute-start | bytes 983048 | tf_op jit(solution)/shard_map/ppermute | solution.py:520
  96.7 22.2 %copy-start = (f32[1,768]{1,0:T(1,128)S(1)}, f32[1,768]{1,0:T(1,128)}, u32[]{:S(2)}) copy-start(f32[1,768]{1,0:T(1,128)} %get-tuple-element.37.refs_0_) | copy-start | bytes 9220
  96.7 8.7 %collective-permute-start.6 = (bf16[4,32,768]{2,1,0:T(8,128)(2,1)S(1)}, bf16[4,32,768]{2,1,0:T(8,128)(2,1)S(1)}, u32[]{:S(2)}, u32[]{:S(2)}) collective-permute-start(bf16[4,32,768]{2,1,0:T(8,128)(2,1)S(1)} %get-tuple-element.57), channel_id=1, source_target_pairs={{0,2},{2,0},{4,6},{6,4},{8,10},{10,8},{12,14},{14,12},{16,18},{18,... | collective-permute-start | bytes 589832 | tf_op jit(solution)/shard_map/ppermute | solution.py:520
  100.0 5.4 %collective-permute-start.4 = (bf16[4,32,640]{2,1,0:T(8,128)(2,1)S(1)}, bf16[4,32,640]{2,1,0:T(8,128)(2,1)S(1)}, u32[]{:S(2)}, u32[]{:S(2)}) collective-permute-start(bf16[4,32,640]{2,1,0:T(8,128)(2,1)S(1)} %get-tuple-element.59), channel_id=1, source_target_pairs={{0,4},{2,6},{4,0},{6,2},{8,12},{10,14},{12,8},{14,10},{16,20},{18,... | collective-permute-start | bytes 491528 | tf_op jit(solution)/shard_map/ppermute | solution.py:520
  105.5 13.4 %collective-permute-start.7 = (bf16[768,512]{1,0:T(8,128)(2,1)S(1)}, bf16[768,512]{1,0:T(8,128)(2,1)S(1)}, u32[]{:S(2)}, u32[]{:S(2)}) collective-permute-start(bf16[768,512]{1,0:T(8,128)(2,1)S(1)} %bitcast.62), channel_id=1, source_target_pairs={{0,1},{1,0},{2,3},{3,2},{4,5},{5,4},{6,7},{7,6},{8,9},{9,8},{10,11... | collective-permute-start | bytes 2359304 | tf_op jit(solution)/shard_map/ppermute | solution.py:398
  105.6 7.4 %collective-permute-start.8 = (bf16[32,1408]{1,0:T(8,128)(2,1)S(1)}, bf16[32,1408]{1,0:T(8,128)(2,1)S(1)}, u32[]{:S(2)}, u32[]{:S(2)}) collective-permute-start(bf16[32,1408]{1,0:T(8,128)(2,1)S(1)} %get-tuple-element.51), channel_id=1, source_target_pairs={{0,8},{2,10},{4,12},{6,14},{8,16},{10,18},{12,20},{14,22},{16,24},... | collective-permute-start | bytes 270344 | tf_op jit(solution)/shard_map/ppermute | solution.py:546
  106.6 9.7 %collective-permute-start.9 = (bf16[32,1408]{1,0:T(8,128)(2,1)S(1)}, bf16[32,1408]{1,0:T(8,128)(2,1)S(1)}, u32[]{:S(2)}, u32[]{:S(2)}) collective-permute-start(bf16[32,1408]{1,0:T(8,128)(2,1)S(1)} %get-tuple-element.52), channel_id=1, source_target_pairs={{0,16},{2,18},{4,20},{6,22},{8,24},{10,26},{12,28},{14,30},{16,0},... | collective-permute-start | bytes 270344 | tf_op jit(solution)/shard_map/ppermute | solution.py:546
  109.5 6.8 %collective-permute-start.10 = (bf16[32,1408]{1,0:T(8,128)(2,1)S(1)}, bf16[32,1408]{1,0:T(8,128)(2,1)S(1)}, u32[]{:S(2)}, u32[]{:S(2)}) collective-permute-start(bf16[32,1408]{1,0:T(8,128)(2,1)S(1)} %get-tuple-element.53), channel_id=1, source_target_pairs={{0,24},{2,26},{4,28},{6,30},{8,0},{10,2},{12,4},{14,6},{16,8},{18,... | collective-permute-start | bytes 270344 | tf_op jit(solution)/shard_map/ppermute | solution.py:546
  117.0 1.2 collective-permute-start.11

commit v11 on v10

--- a/solution.py
+++ b/solution.py
@@ -259,7 +259,7 @@
             att_ref[r0:r1, cols] = total
         return 0
 
-    lax.fori_loop(0, slabs, forward, 0, unroll=2)
+    lax.fori_loop(0, slabs, forward, 0, unroll=4)
 
     get_cot.wait()
     get_out.wait()
@@ -319,7 +319,7 @@
         gpre_ref[:, pl.ds(3 * width + start, LANES)] = (gkey_ref[...].T * slope_ref[3, :, cols]).astype(BF16)
         return 0
 
-    lax.fori_loop(0, slabs, backward, 0, unroll=2)
+    lax.fori_loop(0, slabs, backward, 0, unroll=4)
 
     puts = [put_result]
     me = lax.axis_index("group")
@@ -552,7 +552,7 @@
     ]
 
     incoming = lax.all_to_all(outgoing, "table", split_axis=0, concat_axis=0, tiled=True)
-    incoming, kept = lax.optimization_barrier((incoming, kept))
+    incoming, *got = lax.optimization_barrier((incoming, *got))
     all_incoming = [incoming] + [shift(incoming, "group", groups, k) for k in range(1, groups)]
     grad_rows = table.shape[0] // groups
     (table_grad,) = call(
@@ -583,7 +583,9 @@
         (kept, *got),
         limit=24,
     )
-    pieces = jnp.stack([mine] + [shift(mine, "group", groups, k) for k in range(1, groups)])
+    others = [shift(mine, "group", groups, k) for k in range(1, groups)]
+    table_grad, *others = lax.optimization_barrier((table_grad, *others))
+    pieces = jnp.stack([mine, *others])
     w_out_grad = jnp.concatenate(
         [
             lax.dynamic_index_in_dim(pieces, (me - p) % groups, 0, keepdims=False)

time: 122 us -> 119 us (0.975)
  Pallas kernels: 29.1 us -> 26.9 us
  waiting for transfers between devices: 49.6 us -> 48.1 us
    pallas_call x7, Pallas kernels: 29.1 us -> 26.9 us  [call(): pl.pallas_call(kernel, out_shape=out_shape, in_specs=[pl.BlockSpec(memory...]
    ppermute x3, waiting for transfers between devices: 5.91 us -> 4.56 us  [on_device(): lax.ppermute(sends[k - 1], 'table', [(i, (i // plane + k) % outer * plane...]
  transfers between devices with their start and end apart: 14 -> 14, of which waited for: 8 -> 9; matrix products, arithmetic and copies ran while one was open for 4% -> 4% of each run, Pallas kernels for 1% -> 3%
where the time goes in v11:
time: 119 us; the launch traced here: 118 us
  waiting for transfers between devices  48.1 us (40%)
  Pallas kernels  26.9 us (23%)
  starting transfers between devices  20 us (17%)
  blocking collectives  15.5 us (13%)
  other arithmetic  6.31 us (5%)
    pallas_call x7, Pallas kernels, call(): pl.pallas_call(kernel, out_shape=out_shape, in_specs=[pl.BlockSpec(memory...  26.9 us
    ppermute x4, waiting for transfers between devices, halve(): got = lax.ppermute(send, 'table', [(i, i ^ bit) for i in range(owners)])  20.9 us
    all_to_all x1, waiting for transfers between devices, on_device(): lax.all_to_all(found, 'table', split_axis=0, concat_axis=0, tiled=True)  17.3 us
    all_to_all x1, blocking collectives, on_device(): lax.all_to_all(requested, 'table', split_axis=0, concat_axis=0, tiled=True)  15.5 us
    convert_element_type x4, other arithmetic, halve(): send = add([entry(term, 1 - index, axis) for term in terms]).astype(BF16)  5.65 us
    ppermute x4, starting transfers between devices, halve(): got = lax.ppermute(send, 'table', [(i, i ^ bit) for i in range(owners)])  5.53 us
    ppermute x5, waiting for transfers between devices, shift(): lax.ppermute(value, axis, [(i, (i + amount) % size) for i in range(size)])  5.36 us
    all_to_all x1, starting transfers between devices, on_device(): lax.all_to_all(outgoing, 'table', split_axis=0, concat_axis=0, tiled=True)  4.85 us
  transfers between devices with their start and end apart: 14, of which 9 were waited for; matrix products, arithmetic and copies ran while one was open for 4% of the time, Pallas kernels for 3%

profile of v11, /device:TPU:0, one launch (start us, length us, event | category | flops | bytes accessed | tf_op | source)
XLA Modules:
  0.0 118.4 jit_solution(12495808340121035669)
XLA Ops:
  0.6 1.7 %shard_map.119 = (s32[16,128]{1,0:T(8,128)}, f32[1,512]{1,0:T(1,128)}) custom-call(s32[1,512]{1,0:T(1,128)} %bitcast.79, s32[1,512]{1,0:T(1,128)} %bitcast.80), custom_call_target="tpu_custom_call" | custom-call | flops 16777216 | bytes 4096 | tf_op jit(solution)/shard_map/pallas_call | solution.py:49
  2.3 15.5 %all_to_all.35 = s32[16,1,128]{2,1,0:T(1,128)} all-to-all(s32[16,1,128]{2,1,0:T(1,128)} %bitcast.78), channel_id=1, replica_groups=mesh['table'=16,'group'=2] {'table'}, dimensions={0} | all-to-all | bytes 16384 | tf_op jit(solution)/shard_map/all_to_all | solution.py:421
  17.7 4.5 %shard_map.120 = (bf16[768,512]{1,0:T(8,128)(2,1)}, f32[1,768]{1,0:T(1,128)}) custom-call(s32[16,128]{1,0:T(8,128)} %bitcast.77, bf16[2048,512]{1,0:T(8,128)(2,1)} %table_ref.1), custom_call_target="tpu_custom_call" | custom-call | flops 1610612736 | bytes 2883584 | tf_op jit(solution)/shard_map/pallas_call | solution.py:49
  22.2 3.6 %all-to-all-start.1 = ((bf16[16,48,512]{2,1,0:T(8,128)(2,1)}), bf16[16,48,512]{2,1,0:T(8,128)(2,1)S(1)}, u32[]{:S(2)}, u32[]{:S(2)}) async-start(bf16[16,48,512]{2,1,0:T(8,128)(2,1)} %bitcast.67), calls=%async_computation.1 | async-start | bytes 1572864 | tf_op jit(solution)/shard_map/all_to_all | solution.py:432
  25.9 0.1 collective-permute-start
  25.9 1.4 %collective-permute-done.refs_1_ = f32[1,768]{1,0:T(1,128)S(1)} collective-permute-done((f32[1,768]{1,0:T(1,128)}, f32[1,768]{1,0:T(1,128)S(1)}, u32[]{:S(2)}, u32[]{:S(2)}) %collective-permute-start) | collective-permute-done | bytes 3104 | tf_op jit(solution)/shard_map/ppermute | solution.py:398
  27.3 17.3 %all-to-all-done.1 = bf16[16,48,512]{2,1,0:T(8,128)(2,1)S(1)} async-done(((bf16[16,48,512]{2,1,0:T(8,128)(2,1)}), bf16[16,48,512]{2,1,0:T(8,128)(2,1)S(1)}, u32[]{:S(2)}, u32[]{:S(2)}) %all-to-all-start.1) | async-done | bytes 786464 | tf_op jit(solution)/shard_map/all_to_all | solution.py:432
  44.6 0.0 copy-start.1
  44.6 0.9 copy-done.1
  45.5 14.8 %shard_map.121 = (bf16[512,512]{1,0:T(8,128)(2,1)}, bf16[512,512]{1,0:T(8,128)(2,1)}, bf16[512,640]{1,0:T(8,128)(2,1)}, bf16[512,768]{1,0:T(8,128)(2,1)}, bf16[5...) custom-call(s32[1,8]{1,0:T(1,128)} %len_ref.1, f32[1,512]{1,0:T(1,128)} %get-tuple-element.35.slot_ref, ...), custom_call_target="tpu_custom_call" | custom-call | flops 6174015488 | bytes 6291456 | tf_op jit(solution)/shard_map/pallas_call | solution.py:49
  60.3 0.1 collective-permute-start.2
  60.4 0.5 collective-permute-start.1
  60.9 2.9 %collective-permute-done.1 = bf16[512,640]{1,0:T(8,128)(2,1)S(1)} collective-permute-done((bf16[512,640]{1,0:T(8,128)(2,1)}, bf16[512,640]{1,0:T(8,128)(2,1)S(1)}, u32[]{:S(2)}, u32[]{:S(2)}) %collective-permute-start.1) | collective-permute-done | bytes 655392 | tf_op jit(solution)/shard_map/ppermute | solution.py:398
  63.8 0.0 copy-start.4
  63.8 2.0 %fusion.2 = bf16[4,2,32,640]{3,2,0,1:T(8,128)(2,1)} fusion(bf16[4,2,2,32,640]{4,3,2,1,0:T(8,128)(2,1)} %bitcast.72, s32[]{:T(128)S(6)} %select_n.71, bf16[4,2,2,32,640]{4,3,2,1,0:T(8,128)(2,1)S(1)} %bitcast.74), kind=kLoop, calls=%fused_computation.6 | loop fusion | flops 655360 | bytes 984064 | tf_op jit(solution)/shard_map/convert_element_type | solution.py:517
  65.8 0.0 collective-permute-done.2
  65.8 0.0 copy-start.2
  65.8 1.2 %fusion = bf16[4,2,32,768]{3,2,0,1:T(8,128)(2,1)S(1)} fusion(bf16[4,2,2,32,768]{4,3,2,1,0:T(8,128)(2,1)} %bitcast.68, s32[]{:T(128)S(6)} %select_n.74, bf16[4,2,2,32,768]{4,3,2,1,0:T(8,128)(2,1)S(1)} %bitcast.70), kind=kLoop, calls=%fused_computation.2 | loop fusion | flops 786432 | bytes 1180672 | tf_op jit(solution)/shard_map/convert_element_type | solution.py:517
  67.0 0.0 copy-start.3
  67.0 2.4 %shard_map.122 = bf16[768,512]{1,0:T(8,128)(2,1)} custom-call(f32[1,512]{1,0:T(1,128)} %get-tuple-element.35.slot_ref, bf16[512,512]{1,0:T(8,128)(2,1)} %get-tuple-element.49.grad_ref), custom_call_target="tpu_custom_call" | custom-call | flops 402653184 | bytes 1048576 | tf_op jit(solution)/shard_map/pallas_call | solution.py:49
  69.5 0.0 copy-done.4
  69.5 4.8 %all-to-all-start.2 = ((bf16[16,48,512]{2,1,0:T(8,128)(2,1)}), bf16[16,48,512]{2,1,0:T(8,128)(2,1)S(1)}, u32[]{:S(2)}, u32[]{:S(2)}) async-start(bf16[16,48,512]{2,1,0:T(8,128)(2,1)} %bitcast.65), calls=%async_computation.2 | async-start | bytes 1572864 | tf_op jit(solution)/shard_map/all_to_all | solution.py:554
  74.3 1.9 %collective-permute-start.5 = (bf16[4,2,32,768]{3,2,0,1:T(8,128)(2,1)S(1)}, bf16[4,2,32,768]{3,2,0,1:T(8,128)(2,1)}, u32[]{:S(2)}, u32[]{:S(2)}) collective-permute-start(bf16[4,2,32,768]{3,2,0,1:T(8,128)(2,1)S(1)} %fusion), channel_id=1, source_target_pairs={{0,4},{2,6},{4,0},{6,2},{8,12},{10,14},{12,8},{14,10},{16,20},{18,... | collective-permute-start | bytes 1179656 | tf_op jit(solution)/shard_map/ppermute | solution.py:520
  76.3 1.5 %collective-permute-start.3 = (bf16[4,2,32,640]{3,2,0,1:T(8,128)(2,1)}, bf16[4,2,32,640]{3,2,0,1:T(8,128)(2,1)}, u32[]{:S(2)}, u32[]{:S(2)}) collective-permute-start(bf16[4,2,32,640]{3,2,0,1:T(8,128)(2,1)} %fusion.2), channel_id=1, source_target_pairs={{0,2},{2,0},{4,6},{6,4},{8,10},{10,8},{12,14},{14,12},{16,18},{18,... | collective-permute-start | bytes 983048 | tf_op jit(solution)/shard_map/ppermute | solution.py:520
  77.7 0.0 copy-start
  77.7 15.6 %collective-permute-done.5 = bf16[4,2,32,768]{3,2,0,1:T(8,128)(2,1)} collective-permute-done((bf16[4,2,32,768]{3,2,0,1:T(8,128)(2,1)S(1)}, bf16[4,2,32,768]{3,2,0,1:T(8,128)(2,1)}, u32[]{:S(2)}, u32[]{:S(2)}) %collective-permute-start.5) | collective-permute-done | bytes 393248 | tf_op jit(solution)/shard_map/ppermute | solution.py:520
  93.3 0.0 copy-done.2
  93.3 1.2 fusion.1
  94.5 2.0 %collective-permute-start.6 = (bf16[4,32,768]{2,1,0:T(8,128)(2,1)S(1)}, bf16[4,32,768]{2,1,0:T(8,128)(2,1)S(1)}, u32[]{:S(2)}, u32[]{:S(2)}) collective-permute-start(bf16[4,32,768]{2,1,0:T(8,128)(2,1)S(1)} %get-tuple-element.65), channel_id=1, source_target_pairs={{0,2},{2,0},{4,6},{6,4},{8,10},{10,8},{12,14},{14,12},{16,18},{18,... | collective-permute-start | bytes 589832 | tf_op jit(solution)/shard_map/ppermute | solution.py:520
  96.6 0.0 collective-permute-done.3
  96.6 0.0 copy-done.3
  96.6 1.3 %fusion.3 = (bf16[4,32,640]{2,1,0:T(8,128)(2,1)S(1)}, f32[4,32,640]{2,1,0:T(8,128)S(1)}) fusion(bf16[4,2,32,640]{3,2,0,1:T(8,128)(2,1)} %collective-permute-done.3, s32[]{:T(128)S(6)} %select_n.74, bf16[4,2,2,32,640]{4,3,2,1,0:T(8,128)(2,1)} %bitcast.75, s32[]{:T(128)S(6)} %select_n.79, s32[]{:T(128)S(6)} %select_n.78, ...), kind=kLoop, calls=%fused_computation.8 | loop fusion | flops 901120 | bytes 1474580 | tf_op jit(solution)/shard_map/convert_element_type | solution.py:517
  97.8 0.1 collective-permute-start.4
  97.9 5.3 %collective-permute-done.4.refs_1_ = bf16[4,32,640]{2,1,0:T(8,128)(2,1)S(1)} collective-permute-done((bf16[4,32,640]{2,1,0:T(8,128)(2,1)S(1)}, bf16[4,32,640]{2,1,0:T(8,128)(2,1)S(1)}, u32[]{:S(2)}, u32[]{:S(2)}) %collective-permute-start.4) | collective-permute-done | bytes 163872 | tf_op jit(solution)/shard_map/ppermute | solution.py:520
  103.2 0.0 collective-permute-done.6.refs_3_
  103.2 0.1 shard_map.123
  103.3 1.0 collective-permute-start.7
  104.3 2.9 %collective-permute-start.8 = (bf16[32,1408]{1,0:T(8,128)(2,1)S(1)}, bf16[32,1408]{1,0:T(8,128)(2,1)S(1)}, u32[]{:S(2)}, u32[]{:S(2)}) collective-permute-start(bf16[32,1408]{1,0:T(8,128)(2,1)S(1)} %get-tuple-element.53), channel_id=1, source_target_pairs={{0,16},{2,18},{4,20},{6,22},{8,24},{10,26},{12,28},{14,30},{16,0},... | collective-permute-start | bytes 270344 | tf_op jit(solution)/shard_map/ppermute | solution.py:546
  107.2 0.9 collective-permute-start.9
  108.1 1.7 %collective-permute-done.7.refs_0_ = bf16[32,1408]{1,0:T(8,128)(2,1)S(1)} collective-permute-done((bf16[32,1408]{1,0:T(8,128)(2,1)S(1)}, bf16[32,1408]{1,0:T(8,128)(2,1)S(1)}, u32[]{:S(2)}, u32[]{:S(2)}) %collective-permute-start.7) | collective-permute-done | bytes 90144 | tf_op jit(solution)/shard_map/ppermute | solution.py:546
  109.8 2.5 %collective-permute-done.8.refs_1_ = bf16[32,1408]{1,0:T(8,128)(2,1)S(1)} collective-permute-done((bf16[32,1408]{1,0:T(8,128)(2,1)S(1)}, bf16[32,1408]{1,0:T(8,128)(2,1)S(1)}, u32[]{:S(2)}, u32[]{:S(2)}) %collective-permute-start.8) | collective-permute-done | bytes 90144 | tf_op jit(solution)/shard_map/ppermute | solution.py:546
  112.4 0.3 collective-permute-done.9.refs_2_
  112.7 0.0 all-to-all-done.2
  112.7 0.0 collective-permute-start.10
  112.7 0.7 shard_map.125
  113.4 0.5 collective-permute-start.11
  113.9 1.1 collective-permute-done.10.refs_3_
  115.0 0.0 copy-done
  115.0 2.7 %shard_map.124 = f32[1024,512]{1,0:T(8,128)} custom-call(f32[1,768]{1,0:T(1,128)S(1)} %copy-done, f32[1,768]{1,0:T(1,128)S(1)} %collective-permute-done.refs_1_, bf16[768,512]{1,0:T(8,128)(2,1)S(1)} %bitcast.63, bf16[768,512]{1,0:T(8,128)(2,1)S(1)} %collective-permute-done.10.refs_3_), custom_call_target="tpu_custom_call" | custom-call | flops 1610612736 | bytes 3670016 | tf_op jit(solution)/shard_map/pallas_call | solution.py:49
  117.7 0.0 collective-permute-done.11
  117.8 0.6 pad_maximum_fusion
  (1 shorter events, 0.0 us)
Async XLA Ops:
  22.2 22.3 %all-to-all-start.1 = ((bf16[16,48,512]{2,1,0:T(8,128)(2,1)}), bf16[16,48,512]{2,1,0:T(8,128)(2,1)S(1)}, u32[]{:S(2)}, u32[]{:S(2)}) async-start(bf16[16,48,512]{2,1,0:T(8,128)(2,1)} %bitcast.67), calls=%async_computation.1 | async-start | bytes 1572864 | tf_op jit(solution)/shard_map/all_to_all | solution.py:432
  25.9 1.4 %collective-permute-start = (f32[1,768]{1,0:T(1,128)}, f32[1,768]{1,0:T(1,128)S(1)}, u32[]{:S(2)}, u32[]{:S(2)}) collective-permute-start(f32[1,768]{1,0:T(1,128)} %get-tuple-element.41.refs_0_), channel_id=1, source_target_pairs={{0,1},{1,0},{2,3},{3,2},{4,5},{5,4},{6,7},{7,6},{8,9},{9,8},{10,11... | collective-permute-start | bytes 9224 | tf_op jit(solution)/shard_map/ppermute | solution.py:398
  44.6 0.9 copy-start.1
  60.3 5.5 %collective-permute-start.2 = (bf16[512,768]{1,0:T(8,128)(2,1)}, bf16[512,768]{1,0:T(8,128)(2,1)S(1)}, u32[]{:S(2)}, u32[]{:S(2)}) collective-permute-start(bf16[512,768]{1,0:T(8,128)(2,1)} %get-tuple-element.48), channel_id=1, source_target_pairs={{0,1},{1,0},{2,3},{3,2},{4,5},{5,4},{6,7},{7,6},{8,9},{9,8},{10,11... | collective-permute-start | bytes 2359304 | tf_op jit(solution)/shard_map/ppermute | solution.py:398
  60.4 3.4 %collective-permute-start.1 = (bf16[512,640]{1,0:T(8,128)(2,1)}, bf16[512,640]{1,0:T(8,128)(2,1)S(1)}, u32[]{:S(2)}, u32[]{:S(2)}) collective-permute-start(bf16[512,640]{1,0:T(8,128)(2,1)} %get-tuple-element.45), channel_id=1, source_target_pairs={{0,1},{1,0},{2,3},{3,2},{4,5},{5,4},{6,7},{7,6},{8,9},{9,8},{10,11... | collective-permute-start | bytes 1966088 | tf_op jit(solution)/shard_map/ppermute | solution.py:398
  63.8 5.7 %copy-start.4 = (bf16[512,640]{1,0:T(8,128)(2,1)}, bf16[512,640]{1,0:T(8,128)(2,1)S(1)}, u32[]{:S(2)}) copy-start(bf16[512,640]{1,0:T(8,128)(2,1)S(1)} %collective-permute-done.1) | copy-start | bytes 1966084
  65.8 27.5 %copy-start.2 = (bf16[512,768]{1,0:T(8,128)(2,1)S(1)}, bf16[512,768]{1,0:T(8,128)(2,1)}, u32[]{:S(2)}) copy-start(bf16[512,768]{1,0:T(8,128)(2,1)} %get-tuple-element.47) | copy-start | bytes 2359300
  67.0 29.5 %copy-start.3 = (bf16[512,640]{1,0:T(8,128)(2,1)S(1)}, bf16[512,640]{1,0:T(8,128)(2,1)}, u32[]{:S(2)}) copy-start(bf16[512,640]{1,0:T(8,128)(2,1)} %get-tuple-element.44) | copy-start | bytes 1966084
  69.5 43.2 %all-to-all-start.2 = ((bf16[16,48,512]{2,1,0:T(8,128)(2,1)}), bf16[16,48,512]{2,1,0:T(8,128)(2,1)S(1)}, u32[]{:S(2)}, u32[]{:S(2)}) async-start(bf16[16,48,512]{2,1,0:T(8,128)(2,1)} %bitcast.65), calls=%async_computation.2 | async-start | bytes 1572864 | tf_op jit(solution)/shard_map/all_to_all | solution.py:554
  74.3 19.0 %collective-permute-start.5 = (bf16[4,2,32,768]{3,2,0,1:T(8,128)(2,1)S(1)}, bf16[4,2,32,768]{3,2,0,1:T(8,128)(2,1)}, u32[]{:S(2)}, u32[]{:S(2)}) collective-permute-start(bf16[4,2,32,768]{3,2,0,1:T(8,128)(2,1)S(1)} %fusion), channel_id=1, source_target_pairs={{0,4},{2,6},{4,0},{6,2},{8,12},{10,14},{12,8},{14,10},{16,20},{18,... | collective-permute-start | bytes 1179656 | tf_op jit(solution)/shard_map/ppermute | solution.py:520
  76.3 20.3 %collective-permute-start.3 = (bf16[4,2,32,640]{3,2,0,1:T(8,128)(2,1)}, bf16[4,2,32,640]{3,2,0,1:T(8,128)(2,1)}, u32[]{:S(2)}, u32[]{:S(2)}) collective-permute-start(bf16[4,2,32,640]{3,2,0,1:T(8,128)(2,1)} %fusion.2), channel_id=1, source_target_pairs={{0,2},{2,0},{4,6},{6,4},{8,10},{10,8},{12,14},{14,12},{16,18},{18,... | collective-permute-start | bytes 983048 | tf_op jit(solution)/shard_map/ppermute | solution.py:520
  77.7 37.2 %copy-start = (f32[1,768]{1,0:T(1,128)S(1)}, f32[1,768]{1,0:T(1,128)}, u32[]{:S(2)}) copy-start(f32[1,768]{1,0:T(1,128)} %get-tuple-element.41.refs_0_) | copy-start | bytes 9220
  94.5 8.7 %collective-permute-start.6 = (bf16[4,32,768]{2,1,0:T(8,128)(2,1)S(1)}, bf16[4,32,768]{2,1,0:T(8,128)(2,1)S(1)}, u32[]{:S(2)}, u32[]{:S(2)}) collective-permute-start(bf16[4,32,768]{2,1,0:T(8,128)(2,1)S(1)} %get-tuple-element.65), channel_id=1, source_target_pairs={{0,2},{2,0},{4,6},{6,4},{8,10},{10,8},{12,14},{14,12},{16,18},{18,... | collective-permute-start | bytes 589832 | tf_op jit(solution)/shard_map/ppermute | solution.py:520
  97.8 5.4 %collective-permute-start.4 = (bf16[4,32,640]{2,1,0:T(8,128)(2,1)S(1)}, bf16[4,32,640]{2,1,0:T(8,128)(2,1)S(1)}, u32[]{:S(2)}, u32[]{:S(2)}) collective-permute-start(bf16[4,32,640]{2,1,0:T(8,128)(2,1)S(1)} %get-tuple-element.67), channel_id=1, source_target_pairs={{0,4},{2,6},{4,0},{6,2},{8,12},{10,14},{12,8},{14,10},{16,20},{18,... | collective-permute-start | bytes 491528 | tf_op jit(solution)/shard_map/ppermute | solution.py:520
  103.3 6.5 %collective-permute-start.7 = (bf16[32,1408]{1,0:T(8,128)(2,1)S(1)}, bf16[32,1408]{1,0:T(8,128)(2,1)S(1)}, u32[]{:S(2)}, u32[]{:S(2)}) collective-permute-start(bf16[32,1408]{1,0:T(8,128)(2,1)S(1)} %get-tuple-element.52), channel_id=1, source_target_pairs={{0,8},{2,10},{4,12},{6,14},{8,16},{10,18},{12,20},{14,22},{16,24},... | collective-permute-start | bytes 270344 | tf_op jit(solution)/shard_map/ppermute | solution.py:546
  104.3 8.1 %collective-permute-start.8 = (bf16[32,1408]{1,0:T(8,128)(2,1)S(1)}, bf16[32,1408]{1,0:T(8,128)(2,1)S(1)}, u32[]{:S(2)}, u32[]{:S(2)}) collective-permute-start(bf16[32,1408]{1,0:T(8,128)(2,1)S(1)} %get-tuple-element.53), channel_id=1, source_target_pairs={{0,16},{2,18},{4,20},{6,22},{8,24},{10,26},{12,28},{14,30},{16,0},... | collective-permute-start | bytes 270344 | tf_op jit(solution)/shard_map/ppermute | solution.py:546
  107.2 5.5 %collective-permute-start.9 = (bf16[32,1408]{1,0:T(8,128)(2,1)S(1)}, bf16[32,1408]{1,0:T(8,128)(2,1)S(1)}, u32[]{:S(2)}, u32[]{:S(2)}) collective-permute-start(bf16[32,1408]{1,0:T(8,128)(2,1)S(1)} %get-tuple-element.54), channel_id=1, source_target_pairs={{0,24},{2,26},{4,28},{6,30},{8,0},{10,2},{12,4},{14,6},{16,8},{18,... | collective-permute-start | bytes 270344 | tf_op jit(solution)/shard_map/ppermute | solution.py:546
  112.7 2.3 %collective-permute-start.10 = (bf16[768,512]{1,0:T(8,128)(2,1)S(1)}, bf16[768,512]{1,0:T(8,128)(2,1)S(1)}, u32[]{:S(2)}, u32[]{:S(2)}) collective-permute-start(bf16[768,512]{1,0:T(8,128)(2,1)S(1)} %bitcast.62), channel_id=1, source_target_pairs={{0,1},{1,0},{2,3},{3,2},{4,5},{5,4},{6,7},{7,6},{8,9},{9,8},{10,11... | collective-permute-start | bytes 2359304 | tf_op jit(solution)/shard_map/ppermute | solution.py:398
  113.4 4.3 %collective-permute-start.11 = (f32[32,256]{1,0:T(8,128)S(1)}, f32[32,256]{1,0:T(8,128)S(1)}, u32[]{:S(2)}, u32[]{:S(2)}) collective-permute-start(f32[32,256]{1,0:T(8,128)S(1)} %get-tuple-element.60), channel_id=1, source_target_pairs={{0,1},{1,0},{2,3},{3,2},{4,5},{5,4},{6,7},{7,6},{8,9},{9,8},{10,11... | collective-permute-start | bytes 98312 | tf_op jit(solution)/shard_map/ppermute | solution.py:398

commit v12 on v11

--- a/solution.py
+++ b/solution.py
@@ -197,7 +197,7 @@
     get_ret.wait()
     emb_ref[...] = dot_nn(pick_ref[...], ret_ref[...]).astype(BF16)
 
-    for fetch in get_ins:
+    for fetch in (*get_ins, get_cot, get_out):
         fetch.wait()
     for i in range(4):
         pre = dot_nn(emb_ref[...], w_in_ref[:, parts[i]])
@@ -261,8 +261,6 @@
 
     lax.fori_loop(0, slabs, forward, 0, unroll=4)
 
-    get_cot.wait()
-    get_out.wait()
     gain = gain_ref[...]
     gain_sum = jnp.zeros((1, width), F32)
     for r0 in range(0, count, qrows):
@@ -285,8 +283,6 @@
         mean1 = jnp.mean(gnorm, 1, keepdims=True)
         mean2 = jnp.mean(gnorm * normed, 1, keepdims=True)
         gatt_ref[rows, :] = ((gnorm - mean1 - normed * mean2) * inv).astype(BF16)
-    put_result = pltpu.make_async_copy(result_ref, result_hbm, sems.at[6])
-    put_result.start()
     gwo_ref[...] = dot_tn(mixed_ref[...], cot_ref[...]).astype(BF16)
 
     def backward(p, _):
@@ -321,6 +317,8 @@
 
     lax.fori_loop(0, slabs, backward, 0, unroll=4)
 
+    put_result = pltpu.make_async_copy(result_ref, result_hbm, sems.at[6])
+    put_result.start()
     puts = [put_result]
     me = lax.axis_index("group")
     emb_t = emb_ref[...].T
@@ -525,6 +523,7 @@
         left, row_grad = halve(sides[0], low, 2, 1, row_grad)
         right, row_grad = halve(sides[1], middle, 1, 2, row_grad)
         outgoing = fill_slots(row_grad)
+        outgoing, left[-1], right[-1] = lax.optimization_barrier((outgoing, left[-1], right[-1]))
         left, _ = halve(left, middle, 1, 2)
         right, _ = halve(right, low, 1, 1)
     else:

time: 119 us -> 114 us (0.958)
  waiting for transfers between devices: 48.1 us -> 45.2 us
  other arithmetic: 6.31 us -> 4.57 us
    ppermute x4, waiting for transfers between devices: 20.9 us -> 12.9 us  [halve(): got = lax.ppermute(send, 'table', [(i, i ^ bit) for i in range(owners)])]
    ppermute x3, waiting for transfers between devices: 4.56 us -> 9.87 us  [on_device(): lax.ppermute(sends[k - 1], 'table', [(i, (i // plane + k) % outer * plane...]
    convert_element_type x4, other arithmetic: 5.65 us -> 3.9 us  [halve(): send = add([entry(term, 1 - index, axis) for term in terms]).astype(BF16)]
  transfers between devices with their start and end apart: 14 -> 14, of which waited for: 9 -> 9; matrix products, arithmetic and copies ran while one was open for 4% -> 2% of each run, Pallas kernels for 3% -> 5%
where the time goes in v12:
time: 114 us
  waiting for transfers between devices  45.2 us (40%)
  Pallas kernels  26.6 us (23%)
  starting transfers between devices  19.5 us (17%)
  blocking collectives  15.6 us (14%)
  other arithmetic  4.57 us (4%)
  local copies, waits for them, and re-layouts  1.47 us (1%)
    pallas_call x7, Pallas kernels, call(): pl.pallas_call(kernel, out_shape=out_shape, in_specs=[pl.BlockSpec(memory...  26.6 us
    all_to_all x1, waiting for transfers between devices, on_device(): lax.all_to_all(found, 'table', split_axis=0, concat_axis=0, tiled=True)  17 us
    all_to_all x1, blocking collectives, on_device(): lax.all_to_all(requested, 'table', split_axis=0, concat_axis=0, tiled=True)  15.6 us
    ppermute x4, waiting for transfers between devices, halve(): got = lax.ppermute(send, 'table', [(i, i ^ bit) for i in range(owners)])  12.9 us
    ppermute x3, waiting for transfers between devices, on_device(): lax.ppermute(sends[k - 1], 'table', [(i, (i // plane + k) % outer * plane...  9.87 us
    ppermute x4, starting transfers between devices, halve(): got = lax.ppermute(send, 'table', [(i, i ^ bit) for i in range(owners)])  5.61 us
    ppermute x5, waiting for transfers between devices, shift(): lax.ppermute(value, axis, [(i, (i + amount) % size) for i in range(size)])  5.36 us
    ppermute x3, starting transfers between devices, on_device(): lax.ppermute(sends[k - 1], 'table', [(i, (i // plane + k) % outer * plane...  4.94 us
  transfers between devices with their start and end apart: 14, of which 9 were waited for; matrix products, arithmetic and copies ran while one was open for 2% of the time, Pallas kernels for 5%

profile of v12, /device:TPU:0, one launch (start us, length us, event | category | flops | bytes accessed | tf_op | source)
XLA Modules:
  0.0 113.8 jit_solution(13400673235767110436)
XLA Ops:
  0.6 1.7 %shard_map.119 = (s32[16,128]{1,0:T(8,128)}, f32[1,512]{1,0:T(1,128)}) custom-call(s32[1,512]{1,0:T(1,128)} %bitcast.79, s32[1,512]{1,0:T(1,128)} %bitcast.80), custom_call_target="tpu_custom_call" | custom-call | flops 16777216 | bytes 4096 | tf_op jit(solution)/shard_map/pallas_call | solution.py:49
  2.3 15.6 %all_to_all.35 = s32[16,1,128]{2,1,0:T(1,128)} all-to-all(s32[16,1,128]{2,1,0:T(1,128)} %bitcast.78), channel_id=1, replica_groups=mesh['table'=16,'group'=2] {'table'}, dimensions={0} | all-to-all | bytes 16384 | tf_op jit(solution)/shard_map/all_to_all | solution.py:419
  17.9 4.5 %shard_map.120 = (bf16[768,512]{1,0:T(8,128)(2,1)}, f32[1,768]{1,0:T(1,128)}) custom-call(s32[16,128]{1,0:T(8,128)} %bitcast.77, bf16[2048,512]{1,0:T(8,128)(2,1)} %table_ref.1), custom_call_target="tpu_custom_call" | custom-call | flops 1610612736 | bytes 2883584 | tf_op jit(solution)/shard_map/pallas_call | solution.py:49
  22.4 3.6 %all-to-all-start.1 = ((bf16[16,48,512]{2,1,0:T(8,128)(2,1)}), bf16[16,48,512]{2,1,0:T(8,128)(2,1)S(1)}, u32[]{:S(2)}, u32[]{:S(2)}) async-start(bf16[16,48,512]{2,1,0:T(8,128)(2,1)} %bitcast.67), calls=%async_computation.1 | async-start | bytes 1572864 | tf_op jit(solution)/shard_map/all_to_all | solution.py:430
  26.0 0.1 collective-permute-start
  26.1 1.4 %collective-permute-done.refs_1_ = f32[1,768]{1,0:T(1,128)S(1)} collective-permute-done((f32[1,768]{1,0:T(1,128)}, f32[1,768]{1,0:T(1,128)S(1)}, u32[]{:S(2)}, u32[]{:S(2)}) %collective-permute-start) | collective-permute-done | bytes 3104 | tf_op jit(solution)/shard_map/ppermute | solution.py:396
  27.4 17.0 %all-to-all-done.1 = bf16[16,48,512]{2,1,0:T(8,128)(2,1)S(1)} async-done(((bf16[16,48,512]{2,1,0:T(8,128)(2,1)}), bf16[16,48,512]{2,1,0:T(8,128)(2,1)S(1)}, u32[]{:S(2)}, u32[]{:S(2)}) %all-to-all-start.1) | async-done | bytes 786464 | tf_op jit(solution)/shard_map/all_to_all | solution.py:430
  44.5 0.0 copy-start.1
  44.5 0.9 copy-done.1
  45.4 14.4 %shard_map.121 = (bf16[512,512]{1,0:T(8,128)(2,1)}, bf16[512,512]{1,0:T(8,128)(2,1)}, bf16[512,640]{1,0:T(8,128)(2,1)}, bf16[512,768]{1,0:T(8,128)(2,1)}, bf16[5...) custom-call(s32[1,8]{1,0:T(1,128)} %len_ref.1, f32[1,512]{1,0:T(1,128)} %get-tuple-element.38.slot_ref, ...), custom_call_target="tpu_custom_call" | custom-call | flops 6174015488 | bytes 6291456 | tf_op jit(solution)/shard_map/pallas_call | solution.py:49
  59.8 0.1 collective-permute-start.2
  59.8 0.5 collective-permute-start.1
  60.3 2.9 %collective-permute-done.1 = bf16[512,640]{1,0:T(8,128)(2,1)S(1)} collective-permute-done((bf16[512,640]{1,0:T(8,128)(2,1)}, bf16[512,640]{1,0:T(8,128)(2,1)S(1)}, u32[]{:S(2)}, u32[]{:S(2)}) %collective-permute-start.1) | collective-permute-done | bytes 655392 | tf_op jit(solution)/shard_map/ppermute | solution.py:396
  63.3 0.0 copy-start.4
  63.3 1.3 %fusion.2 = bf16[4,2,32,640]{3,2,0,1:T(8,128)(2,1)S(1)} fusion(bf16[4,2,2,32,640]{4,3,2,1,0:T(8,128)(2,1)} %bitcast.72, s32[]{:T(128)S(6)} %select_n.71, bf16[4,2,2,32,640]{4,3,2,1,0:T(8,128)(2,1)S(1)} %bitcast.74), kind=kLoop, calls=%fused_computation.6 | loop fusion | flops 655360 | bytes 984064 | tf_op jit(solution)/shard_map/convert_element_type | solution.py:515
  64.5 0.0 collective-permute-done.2
  64.6 0.0 copy-start.2
  64.6 1.2 %fusion = bf16[4,2,32,768]{3,2,0,1:T(8,128)(2,1)S(1)} fusion(bf16[4,2,2,32,768]{4,3,2,1,0:T(8,128)(2,1)} %bitcast.68, s32[]{:T(128)S(6)} %select_n.74, bf16[4,2,2,32,768]{4,3,2,1,0:T(8,128)(2,1)S(1)} %bitcast.70), kind=kLoop, calls=%fused_computation.2 | loop fusion | flops 786432 | bytes 1180672 | tf_op jit(solution)/shard_map/convert_element_type | solution.py:515
  65.8 0.0 copy-start.3
  65.8 1.6 %collective-permute-start.4 = (bf16[4,2,32,768]{3,2,0,1:T(8,128)(2,1)S(1)}, bf16[4,2,32,768]{3,2,0,1:T(8,128)(2,1)S(1)}, u32[]{:S(2)}, u32[]{:S(2)}) collective-permute-start(bf16[4,2,32,768]{3,2,0,1:T(8,128)(2,1)S(1)} %fusion), channel_id=1, source_target_pairs={{0,4},{2,6},{4,0},{6,2},{8,12},{10,14},{12,8},{14,10},{16,20},{18,... | collective-permute-start | bytes 1179656 | tf_op jit(solution)/shard_map/ppermute | solution.py:518
  67.3 0.6 collective-permute-start.3
  67.9 2.6 %shard_map.122 = bf16[768,512]{1,0:T(8,128)(2,1)} custom-call(f32[1,512]{1,0:T(1,128)} %get-tuple-element.38.slot_ref, bf16[512,512]{1,0:T(8,128)(2,1)} %get-tuple-element.52.grad_ref), custom_call_target="tpu_custom_call" | custom-call | flops 402653184 | bytes 1048576 | tf_op jit(solution)/shard_map/pallas_call | solution.py:49
  70.5 6.3 %collective-permute-done.3 = bf16[4,2,32,640]{3,2,0,1:T(8,128)(2,1)S(1)} collective-permute-done((bf16[4,2,32,640]{3,2,0,1:T(8,128)(2,1)S(1)}, bf16[4,2,32,640]{3,2,0,1:T(8,128)(2,1)S(1)}, u32[]{:S(2)}, u32[]{:S(2)}) %collective-permute-start.3) | collective-permute-done | bytes 327712 | tf_op jit(solution)/shard_map/ppermute | solution.py:518
  76.8 0.0 copy-start.5
  76.8 0.2 collective-permute-done.4
  77.0 0.6 copy-done.5
  77.6 0.0 copy-done.4
  77.6 4.2 %all-to-all-start.2 = ((bf16[16,48,512]{2,1,0:T(8,128)(2,1)}), bf16[16,48,512]{2,1,0:T(8,128)(2,1)S(1)}, u32[]{:S(2)}, u32[]{:S(2)}) async-start(bf16[16,48,512]{2,1,0:T(8,128)(2,1)} %bitcast.65), calls=%async_computation.2 | async-start | bytes 1572864 | tf_op jit(solution)/shard_map/all_to_all | solution.py:553
  81.8 0.0 copy-done.2
  81.8 0.0 copy-start
  81.8 0.2 fusion.1
  82.0 2.0 %collective-permute-start.6 = (bf16[4,32,768]{2,1,0:T(8,128)(2,1)S(1)}, bf16[4,32,768]{2,1,0:T(8,128)(2,1)S(1)}, u32[]{:S(2)}, u32[]{:S(2)}) collective-permute-start(bf16[4,32,768]{2,1,0:T(8,128)(2,1)S(1)} %get-tuple-element.71), channel_id=1, source_target_pairs={{0,2},{2,0},{4,6},{6,4},{8,10},{10,8},{12,14},{14,12},{16,18},{18,... | collective-permute-start | bytes 589832 | tf_op jit(solution)/shard_map/ppermute | solution.py:518
  83.9 0.0 copy-done.3
  83.9 1.3 %fusion.3 = (bf16[4,32,640]{2,1,0:T(8,128)(2,1)S(1)}, f32[4,32,640]{2,1,0:T(8,128)S(1)}) fusion(bf16[4,2,32,640]{3,2,0,1:T(8,128)(2,1)} %copy-done.5, s32[]{:T(128)S(6)} %select_n.74, bf16[4,2,2,32,640]{4,3,2,1,0:T(8,128)(2,1)} %bitcast.75, s32[]{:T(128)S(6)} %select_n.79, s32[]{:T(128)S(6)} %select_n.78, bf16[4,2,2,32,640]{4,3,2,1,0:T(8,128)(2,1)S(1)} %bitcast.73, ...), kind=kLoop, calls=%fused_computation.8 | loop fusion | flops 901120 | bytes 1474580 | tf_op jit(solution)/shard_map/convert_element_type | solution.py:515
  85.2 1.5 %collective-permute-start.5 = (bf16[4,32,640]{2,1,0:T(8,128)(2,1)S(1)}, bf16[4,32,640]{2,1,0:T(8,128)(2,1)S(1)}, u32[]{:S(2)}, u32[]{:S(2)}) collective-permute-start(bf16[4,32,640]{2,1,0:T(8,128)(2,1)S(1)} %get-tuple-element.73), channel_id=1, source_target_pairs={{0,4},{2,6},{4,0},{6,2},{8,12},{10,14},{12,8},{14,10},{16,20},{18,... | collective-permute-start | bytes 491528 | tf_op jit(solution)/shard_map/ppermute | solution.py:518
  86.7 6.4 %collective-permute-done.5.refs_1_ = bf16[4,32,640]{2,1,0:T(8,128)(2,1)S(1)} collective-permute-done((bf16[4,32,640]{2,1,0:T(8,128)(2,1)S(1)}, bf16[4,32,640]{2,1,0:T(8,128)(2,1)S(1)}, u32[]{:S(2)}, u32[]{:S(2)}) %collective-permute-start.5) | collective-permute-done | bytes 163872 | tf_op jit(solution)/shard_map/ppermute | solution.py:518
  93.2 0.0 collective-permute-done.6.refs_3_
  93.2 0.1 shard_map.123
  93.2 1.5 %collective-permute-start.7 = (bf16[32,1408]{1,0:T(8,128)(2,1)S(1)}, bf16[32,1408]{1,0:T(8,128)(2,1)S(1)}, u32[]{:S(2)}, u32[]{:S(2)}) collective-permute-start(bf16[32,1408]{1,0:T(8,128)(2,1)S(1)} %get-tuple-element.58), channel_id=1, source_target_pairs={{0,8},{2,10},{4,12},{6,14},{8,16},{10,18},{12,20},{14,22},{16,24},... | collective-permute-start | bytes 270344 | tf_op jit(solution)/shard_map/ppermute | solution.py:545
  94.8 3.4 %collective-permute-start.8 = (bf16[32,1408]{1,0:T(8,128)(2,1)S(1)}, bf16[32,1408]{1,0:T(8,128)(2,1)S(1)}, u32[]{:S(2)}, u32[]{:S(2)}) collective-permute-start(bf16[32,1408]{1,0:T(8,128)(2,1)S(1)} %get-tuple-element.59), channel_id=1, source_target_pairs={{0,16},{2,18},{4,20},{6,22},{8,24},{10,26},{12,28},{14,30},{16,0},... | collective-permute-start | bytes 270344 | tf_op jit(solution)/shard_map/ppermute | solution.py:545
  98.2 0.0 collective-permute-start.9
  98.2 3.0 %collective-permute-done.7.refs_0_ = bf16[32,1408]{1,0:T(8,128)(2,1)S(1)} collective-permute-done((bf16[32,1408]{1,0:T(8,128)(2,1)S(1)}, bf16[32,1408]{1,0:T(8,128)(2,1)S(1)}, u32[]{:S(2)}, u32[]{:S(2)}) %collective-permute-start.7) | collective-permute-done | bytes 90144 | tf_op jit(solution)/shard_map/ppermute | solution.py:545
  101.2 6.9 %collective-permute-done.8.refs_1_ = bf16[32,1408]{1,0:T(8,128)(2,1)S(1)} collective-permute-done((bf16[32,1408]{1,0:T(8,128)(2,1)S(1)}, bf16[32,1408]{1,0:T(8,128)(2,1)S(1)}, u32[]{:S(2)}, u32[]{:S(2)}) %collective-permute-start.8) | collective-permute-done | bytes 90144 | tf_op jit(solution)/shard_map/ppermute | solution.py:545
  108.1 0.0 collective-permute-done.9.refs_2_
  108.1 0.0 all-to-all-done.2
  108.1 0.0 collective-permute-start.10
  108.1 0.7 shard_map.125
  108.8 0.5 collective-permute-start.11
  109.3 1.1 collective-permute-done.10.refs_3_
  110.3 0.0 copy-done
  110.4 2.7 %shard_map.124 = f32[1024,512]{1,0:T(8,128)} custom-call(f32[1,768]{1,0:T(1,128)S(1)} %copy-done, f32[1,768]{1,0:T(1,128)S(1)} %collective-permute-done.refs_1_, bf16[768,512]{1,0:T(8,128)(2,1)S(1)} %bitcast.63, bf16[768,512]{1,0:T(8,128)(2,1)S(1)} %collective-permute-done.10.refs_3_), custom_call_target="tpu_custom_call" | custom-call | flops 1610612736 | bytes 3670016 | tf_op jit(solution)/shard_map/pallas_call | solution.py:49
  113.1 0.0 collective-permute-done.11
  113.2 0.6 pad_maximum_fusion
  (1 shorter events, 0.0 us)
Async XLA Ops:
  22.4 22.1 %all-to-all-start.1 = ((bf16[16,48,512]{2,1,0:T(8,128)(2,1)}), bf16[16,48,512]{2,1,0:T(8,128)(2,1)S(1)}, u32[]{:S(2)}, u32[]{:S(2)}) async-start(bf16[16,48,512]{2,1,0:T(8,128)(2,1)} %bitcast.67), calls=%async_computation.1 | async-start | bytes 1572864 | tf_op jit(solution)/shard_map/all_to_all | solution.py:430
  26.0 1.4 %collective-permute-start = (f32[1,768]{1,0:T(1,128)}, f32[1,768]{1,0:T(1,128)S(1)}, u32[]{:S(2)}, u32[]{:S(2)}) collective-permute-start(f32[1,768]{1,0:T(1,128)} %get-tuple-element.44.refs_0_), channel_id=1, source_target_pairs={{0,1},{1,0},{2,3},{3,2},{4,5},{5,4},{6,7},{7,6},{8,9},{9,8},{10,11... | collective-permute-start | bytes 9224 | tf_op jit(solution)/shard_map/ppermute | solution.py:396
  44.5 0.9 copy-start.1
  59.8 4.8 %collective-permute-start.2 = (bf16[512,768]{1,0:T(8,128)(2,1)}, bf16[512,768]{1,0:T(8,128)(2,1)S(1)}, u32[]{:S(2)}, u32[]{:S(2)}) collective-permute-start(bf16[512,768]{1,0:T(8,128)(2,1)} %get-tuple-element.51), channel_id=1, source_target_pairs={{0,1},{1,0},{2,3},{3,2},{4,5},{5,4},{6,7},{7,6},{8,9},{9,8},{10,11... | collective-permute-start | bytes 2359304 | tf_op jit(solution)/shard_map/ppermute | solution.py:396
  59.8 3.4 %collective-permute-start.1 = (bf16[512,640]{1,0:T(8,128)(2,1)}, bf16[512,640]{1,0:T(8,128)(2,1)S(1)}, u32[]{:S(2)}, u32[]{:S(2)}) collective-permute-start(bf16[512,640]{1,0:T(8,128)(2,1)} %get-tuple-element.48), channel_id=1, source_target_pairs={{0,1},{1,0},{2,3},{3,2},{4,5},{5,4},{6,7},{7,6},{8,9},{9,8},{10,11... | collective-permute-start | bytes 1966088 | tf_op jit(solution)/shard_map/ppermute | solution.py:396
  63.3 14.3 %copy-start.4 = (bf16[512,640]{1,0:T(8,128)(2,1)}, bf16[512,640]{1,0:T(8,128)(2,1)S(1)}, u32[]{:S(2)}) copy-start(bf16[512,640]{1,0:T(8,128)(2,1)S(1)} %collective-permute-done.1) | copy-start | bytes 1966084
  64.6 17.2 %copy-start.2 = (bf16[512,768]{1,0:T(8,128)(2,1)S(1)}, bf16[512,768]{1,0:T(8,128)(2,1)}, u32[]{:S(2)}) copy-start(bf16[512,768]{1,0:T(8,128)(2,1)} %get-tuple-element.50) | copy-start | bytes 2359300
  65.8 18.2 %copy-start.3 = (bf16[512,640]{1,0:T(8,128)(2,1)S(1)}, bf16[512,640]{1,0:T(8,128)(2,1)}, u32[]{:S(2)}) copy-start(bf16[512,640]{1,0:T(8,128)(2,1)} %get-tuple-element.47) | copy-start | bytes 1966084
  65.8 11.2 %collective-permute-start.4 = (bf16[4,2,32,768]{3,2,0,1:T(8,128)(2,1)S(1)}, bf16[4,2,32,768]{3,2,0,1:T(8,128)(2,1)S(1)}, u32[]{:S(2)}, u32[]{:S(2)}) collective-permute-start(bf16[4,2,32,768]{3,2,0,1:T(8,128)(2,1)S(1)} %fusion), channel_id=1, source_target_pairs={{0,4},{2,6},{4,0},{6,2},{8,12},{10,14},{12,8},{14,10},{16,20},{18,... | collective-permute-start | bytes 1179656 | tf_op jit(solution)/shard_map/ppermute | solution.py:518
  67.3 9.5 %collective-permute-start.3 = (bf16[4,2,32,640]{3,2,0,1:T(8,128)(2,1)S(1)}, bf16[4,2,32,640]{3,2,0,1:T(8,128)(2,1)S(1)}, u32[]{:S(2)}, u32[]{:S(2)}) collective-permute-start(bf16[4,2,32,640]{3,2,0,1:T(8,128)(2,1)S(1)} %fusion.2), channel_id=1, source_target_pairs={{0,2},{2,0},{4,6},{6,4},{8,10},{10,8},{12,14},{14,12},{16,18},{18,... | collective-permute-start | bytes 983048 | tf_op jit(solution)/shard_map/ppermute | solution.py:518
  76.8 0.7 copy-start.5
  77.6 30.5 %all-to-all-start.2 = ((bf16[16,48,512]{2,1,0:T(8,128)(2,1)}), bf16[16,48,512]{2,1,0:T(8,128)(2,1)S(1)}, u32[]{:S(2)}, u32[]{:S(2)}) async-start(bf16[16,48,512]{2,1,0:T(8,128)(2,1)} %bitcast.65), calls=%async_computation.2 | async-start | bytes 1572864 | tf_op jit(solution)/shard_map/all_to_all | solution.py:553
  81.8 28.5 %copy-start = (f32[1,768]{1,0:T(1,128)S(1)}, f32[1,768]{1,0:T(1,128)}, u32[]{:S(2)}) copy-start(f32[1,768]{1,0:T(1,128)} %get-tuple-element.44.refs_0_) | copy-start | bytes 9220
  82.0 11.2 %collective-permute-start.6 = (bf16[4,32,768]{2,1,0:T(8,128)(2,1)S(1)}, bf16[4,32,768]{2,1,0:T(8,128)(2,1)S(1)}, u32[]{:S(2)}, u32[]{:S(2)}) collective-permute-start(bf16[4,32,768]{2,1,0:T(8,128)(2,1)S(1)} %get-tuple-element.71), channel_id=1, source_target_pairs={{0,2},{2,0},{4,6},{6,4},{8,10},{10,8},{12,14},{14,12},{16,18},{18,... | collective-permute-start | bytes 589832 | tf_op jit(solution)/shard_map/ppermute | solution.py:518
  85.2 8.0 %collective-permute-start.5 = (bf16[4,32,640]{2,1,0:T(8,128)(2,1)S(1)}, bf16[4,32,640]{2,1,0:T(8,128)(2,1)S(1)}, u32[]{:S(2)}, u32[]{:S(2)}) collective-permute-start(bf16[4,32,640]{2,1,0:T(8,128)(2,1)S(1)} %get-tuple-element.73), channel_id=1, source_target_pairs={{0,4},{2,6},{4,0},{6,2},{8,12},{10,14},{12,8},{14,10},{16,20},{18,... | collective-permute-start | bytes 491528 | tf_op jit(solution)/shard_map/ppermute | solution.py:518
  93.2 7.9 %collective-permute-start.7 = (bf16[32,1408]{1,0:T(8,128)(2,1)S(1)}, bf16[32,1408]{1,0:T(8,128)(2,1)S(1)}, u32[]{:S(2)}, u32[]{:S(2)}) collective-permute-start(bf16[32,1408]{1,0:T(8,128)(2,1)S(1)} %get-tuple-element.58), channel_id=1, source_target_pairs={{0,8},{2,10},{4,12},{6,14},{8,16},{10,18},{12,20},{14,22},{16,24},... | collective-permute-start | bytes 270344 | tf_op jit(solution)/shard_map/ppermute | solution.py:545
  94.8 13.3 %collective-permute-start.8 = (bf16[32,1408]{1,0:T(8,128)(2,1)S(1)}, bf16[32,1408]{1,0:T(8,128)(2,1)S(1)}, u32[]{:S(2)}, u32[]{:S(2)}) collective-permute-start(bf16[32,1408]{1,0:T(8,128)(2,1)S(1)} %get-tuple-element.59), channel_id=1, source_target_pairs={{0,16},{2,18},{4,20},{6,22},{8,24},{10,26},{12,28},{14,30},{16,0},... | collective-permute-start | bytes 270344 | tf_op jit(solution)/shard_map/ppermute | solution.py:545
  98.2 9.9 %collective-permute-start.9 = (bf16[32,1408]{1,0:T(8,128)(2,1)S(1)}, bf16[32,1408]{1,0:T(8,128)(2,1)S(1)}, u32[]{:S(2)}, u32[]{:S(2)}) collective-permute-start(bf16[32,1408]{1,0:T(8,128)(2,1)S(1)} %get-tuple-element.60), channel_id=1, source_target_pairs={{0,24},{2,26},{4,28},{6,30},{8,0},{10,2},{12,4},{14,6},{16,8},{18,... | collective-permute-start | bytes 270344 | tf_op jit(solution)/shard_map/ppermute | solution.py:545
  108.1 2.3 %collective-permute-start.10 = (bf16[768,512]{1,0:T(8,128)(2,1)S(1)}, bf16[768,512]{1,0:T(8,128)(2,1)S(1)}, u32[]{:S(2)}, u32[]{:S(2)}) collective-permute-start(bf16[768,512]{1,0:T(8,128)(2,1)S(1)} %bitcast.62), channel_id=1, source_target_pairs={{0,1},{1,0},{2,3},{3,2},{4,5},{5,4},{6,7},{7,6},{8,9},{9,8},{10,11... | collective-permute-start | bytes 2359304 | tf_op jit(solution)/shard_map/ppermute | solution.py:396
  108.8 4.3 %collective-permute-start.11 = (f32[32,256]{1,0:T(8,128)S(1)}, f32[32,256]{1,0:T(8,128)S(1)}, u32[]{:S(2)}, u32[]{:S(2)}) collective-permute-start(f32[32,256]{1,0:T(8,128)S(1)} %get-tuple-element.66), channel_id=1, source_target_pairs={{0,1},{1,0},{2,3},{3,2},{4,5},{5,4},{6,7},{7,6},{8,9},{9,8},{10,11... | collective-permute-start | bytes 98312 | tf_op jit(solution)/shard_map/ppermute | solution.py:396

commit v13 on v12

--- a/solution.py
+++ b/solution.py
@@ -75,10 +75,12 @@
     req_ref[...] = found.astype(jnp.int32)
 
 
-def lookup_kernel(cap, wanted_ref, table_ref, found_ref, ids_ref):
+def lookup_kernel(cap, wanted_ref, table_hbm, found_ref, ids_ref, table_ref, pick_ref, sem):
     owners, width = wanted_ref.shape
     slots = found_ref.shape[0]
     rows = table_ref.shape[0]
+    fetch = pltpu.make_async_copy(table_hbm, table_ref, sem)
+    fetch.start()
     wanted = wanted_ref[...]
     high = (wanted >> 8).astype(F32).astype(BF16)
     low = (wanted & 255).astype(F32).astype(BF16)
@@ -93,11 +95,15 @@
     )
     wide = jnp.broadcast_to(ids, (slots, LANES))
     ids_ref[...] = wide.T[0:1, :]
-    step = 256 if slots % 256 == 0 else slots
+    step = row_step(slots)
     for start in range(0, slots, step):
         part = ids[start : start + step]
-        pick = hot(iota((step, rows), 1).astype(F32) == part)
-        found_ref[start : start + step, :] = dot_nn(pick, table_ref[...]).astype(BF16)
+        pick_ref[start : start + step, :] = hot(iota((step, rows), 1).astype(F32) == part)
+    fetch.wait()
+    for start in range(0, slots, step):
+        found_ref[start : start + step, :] = dot_nn(
+            pick_ref[start : start + step, :], table_ref[...]
+        ).astype(BF16)
 
 
 def collect_kernel(groups, *refs):
@@ -334,7 +340,8 @@
         cols = pl.ds(pl.multiple_of(lax.rem(part, wparts) * cols_out, LANES), cols_out)
         grads_ref[k, :, cols_in : cols_in + cols_out] = gwo_ref[:, cols]
         grads_ref[k, :, cols_in + cols_out :] = gain_col
-        cut = grads_hbms[2 * k].shape[1]
+    cut = grads_hbms[0].shape[1]
+    for k in range(groups):
         for i, cols in enumerate((pl.ds(0, cut), pl.ds(cut, grads_ref.shape[2] - cut))):
             put = pltpu.make_async_copy(
                 grads_ref.at[k, :, cols], grads_hbms[2 * k + i], sems.at[8 + 2 * k + i]
@@ -426,6 +433,12 @@
         2 * slots * table.shape[0] * width,
         2 * (slots + table.shape[0]) * width,
         (wanted, table),
+        far=(1,),
+        scratch=[
+            pltpu.VMEM(table.shape, BF16),
+            pltpu.VMEM((slots, table.shape[0]), BF16),
+            pltpu.SemaphoreType.DMA,
+        ],
     )
     returned = lax.all_to_all(found, "table", split_axis=0, concat_axis=0, tiled=True)
     all_ids = [ids] + [shift(ids, "group", groups, k) for k in range(1, groups)]
@@ -480,19 +493,18 @@
             pltpu.SemaphoreType.DMA((10 + 2 * groups,)),
         ],
     )
-    def fill_slots(row_grad):
-        return call(
-            slots_kernel,
-            [jax.ShapeDtypeStruct((slots, width), BF16)],
-            2 * slots * count * width,
-            4 * count * width,
-            (slot, row_grad),
-            far_out=(0,),
-            scratch=[
-                pltpu.VMEM((slots, width), BF16),
-                pltpu.SemaphoreType.DMA((slots // row_step(slots),)),
-            ],
-        )[0]
+    (outgoing,) = call(
+        slots_kernel,
+        [jax.ShapeDtypeStruct((slots, width), BF16)],
+        2 * slots * count * width,
+        4 * count * width,
+        (slot, row_grad),
+        far_out=(0,),
+        scratch=[
+            pltpu.VMEM((slots, width), BF16),
+            pltpu.SemaphoreType.DMA((slots // row_step(slots),)),
+        ],
+    )
 
     rows = width // owners
     side = 2 if owners % 4 == 0 else 1
@@ -511,23 +523,18 @@
     def add(terms):
         return sum(term.astype(F32) for term in terms)
 
-    def halve(terms, index, axis, bit, tie=None):
+    def halve(terms, index, axis, bit, last):
         send = add([entry(term, 1 - index, axis) for term in terms]).astype(BF16)
-        if tie is not None:
-            tie, send = lax.optimization_barrier((tie, send))
         got = lax.ppermute(send, "table", [(i, i ^ bit) for i in range(owners)])
         kept = [entry(term, index, axis) for term in terms]
-        return (kept if tie is not None else [add(kept)]) + [got], tie
+        return ([add(kept)] if last else kept) + [got]
 
     if side == 2:
-        left, row_grad = halve(sides[0], low, 2, 1, row_grad)
-        right, row_grad = halve(sides[1], middle, 1, 2, row_grad)
-        outgoing = fill_slots(row_grad)
-        outgoing, left[-1], right[-1] = lax.optimization_barrier((outgoing, left[-1], right[-1]))
-        left, _ = halve(left, middle, 1, 2)
-        right, _ = halve(right, low, 1, 1)
+        left = halve(sides[0], low, 2, 1, False)
+        right = halve(sides[1], middle, 1, 2, False)
+        left = halve(left, middle, 1, 2, True)
+        right = halve(right, low, 1, 1, True)
     else:
-        outgoing = fill_slots(row_grad)
         left, right = [[term[:, 0, 0] for term in terms] for terms in sides]
     cols = cols_all
     kept, *sends = call(
@@ -537,7 +544,7 @@
             *[jax.ShapeDtypeStruct((rows, cols), BF16) for _ in range(1, outer)],
         ],
         12 * outer * rows * cols,
-        160 * outer * rows * cols,
+        8 * outer * rows * cols,
         (*left, *right),
         limit=24,
     )
@@ -551,7 +558,7 @@
     ]
 
     incoming = lax.all_to_all(outgoing, "table", split_axis=0, concat_axis=0, tiled=True)
-    incoming, *got = lax.optimization_barrier((incoming, *got))
+    incoming, kept = lax.optimization_barrier((incoming, kept))
     all_incoming = [incoming] + [shift(incoming, "group", groups, k) for k in range(1, groups)]
     grad_rows = table.shape[0] // groups
     (table_grad,) = call(
@@ -570,6 +577,7 @@
         ],
     )
 
+    kept, table_grad = lax.optimization_barrier((kept, table_grad))
     w_in_grad, mine, gain_grad = call(
         finish_kernel,
         [
@@ -583,7 +591,6 @@
         limit=24,
     )
     others = [shift(mine, "group", groups, k) for k in range(1, groups)]
-    table_grad, *others = lax.optimization_barrier((table_grad, *others))
     pieces = jnp.stack([mine, *others])
     w_out_grad = jnp.concatenate(
         [

time: 114 us -> 111 us (0.974)
  waiting for transfers between devices: 45.2 us -> 41.2 us
    ppermute x3, waiting for transfers between devices: 9.87 us -> 3.18 us  [on_device(): lax.ppermute(sends[k - 1], 'table', [(i, (i // plane + k) % outer * plane...]
    ppermute x4, waiting for transfers between devices: 12.9 us -> 18.4 us  [halve(): got = lax.ppermute(send, 'table', [(i, i ^ bit) for i in range(owners)])]
    ppermute x5, waiting for transfers between devices: 5.36 us -> 2.57 us  [shift(): lax.ppermute(value, axis, [(i, (i + amount) % size) for i in range(size)])]
  transfers between devices with their start and end apart: 14 -> 14, of which waited for: 9 -> 6; matrix products, arithmetic and copies ran while one was open for 2% -> 4% of each run, Pallas kernels for 5% -> 5%
where the time goes in v13:
time: 111 us; the launch traced here: 110 us
  waiting for transfers between devices  41.2 us (37%)
  Pallas kernels  27.7 us (25%)
  starting transfers between devices  19.4 us (17%)
  blocking collectives  15.6 us (14%)
  other arithmetic  4.74 us (4%)
    pallas_call x7, Pallas kernels, call(): pl.pallas_call(kernel, out_shape=out_shape, in_specs=[pl.BlockSpec(memory...  27.7 us
    ppermute x4, waiting for transfers between devices, halve(): got = lax.ppermute(send, 'table', [(i, i ^ bit) for i in range(owners)])  18.4 us
    all_to_all x1, waiting for transfers between devices, on_device(): lax.all_to_all(found, 'table', split_axis=0, concat_axis=0, tiled=True)  17.1 us
    all_to_all x1, blocking collectives, on_device(): lax.all_to_all(requested, 'table', split_axis=0, concat_axis=0, tiled=True)  15.6 us
    ppermute x4, starting transfers between devices, halve(): got = lax.ppermute(send, 'table', [(i, i ^ bit) for i in range(owners)])  5.69 us
    ppermute x3, starting transfers between devices, on_device(): lax.ppermute(sends[k - 1], 'table', [(i, (i // plane + k) % outer * plane...  4.83 us
    all_to_all x1, starting transfers between devices, on_device(): lax.all_to_all(outgoing, 'table', split_axis=0, concat_axis=0, tiled=True)  4.79 us
    convert_element_type x4, other arithmetic, halve(): send = add([entry(term, 1 - index, axis) for term in terms]).astype(BF16)  4.09 us
  transfers between devices with their start and end apart: 14, of which 6 were waited for; matrix products, arithmetic and copies ran while one was open for 4% of the time, Pallas kernels for 5%

profile of v13, /device:TPU:0, one launch (start us, length us, event | category | flops | bytes accessed | tf_op | source)
XLA Modules:
  0.0 110.3 jit_solution(16171055352931410283)
XLA Ops:
  0.6 1.7 %shard_map.119 = (s32[16,128]{1,0:T(8,128)}, f32[1,512]{1,0:T(1,128)}) custom-call(s32[1,512]{1,0:T(1,128)} %bitcast.77, s32[1,512]{1,0:T(1,128)} %bitcast.78), custom_call_target="tpu_custom_call" | custom-call | flops 16777216 | bytes 4096 | tf_op jit(solution)/shard_map/pallas_call | solution.py:49
  2.3 15.6 %all_to_all.35 = s32[16,1,128]{2,1,0:T(1,128)} all-to-all(s32[16,1,128]{2,1,0:T(1,128)} %bitcast.76), channel_id=1, replica_groups=mesh['table'=16,'group'=2] {'table'}, dimensions={0} | all-to-all | bytes 16384 | tf_op jit(solution)/shard_map/all_to_all | solution.py:426
  17.9 5.0 %shard_map.120 = (bf16[768,512]{1,0:T(8,128)(2,1)}, f32[1,768]{1,0:T(1,128)}) custom-call(s32[16,128]{1,0:T(8,128)} %bitcast.75, bf16[2048,512]{1,0:T(8,128)(2,1)} %table_hbm.1), custom_call_target="tpu_custom_call" | custom-call | flops 1610612736 | bytes 2883584 | tf_op jit(solution)/shard_map/pallas_call | solution.py:49
  22.9 3.6 %all-to-all-start.1 = ((bf16[16,48,512]{2,1,0:T(8,128)(2,1)}), bf16[16,48,512]{2,1,0:T(8,128)(2,1)S(1)}, u32[]{:S(2)}, u32[]{:S(2)}) async-start(bf16[16,48,512]{2,1,0:T(8,128)(2,1)} %bitcast.67), calls=%async_computation.1 | async-start | bytes 1572864 | tf_op jit(solution)/shard_map/all_to_all | solution.py:443
  26.5 0.1 collective-permute-start
  26.6 1.4 %collective-permute-done.refs_1_ = f32[1,768]{1,0:T(1,128)S(1)} collective-permute-done((f32[1,768]{1,0:T(1,128)}, f32[1,768]{1,0:T(1,128)S(1)}, u32[]{:S(2)}, u32[]{:S(2)}) %collective-permute-start) | collective-permute-done | bytes 3104 | tf_op jit(solution)/shard_map/ppermute | solution.py:403
  27.9 17.1 %all-to-all-done.1 = bf16[16,48,512]{2,1,0:T(8,128)(2,1)S(1)} async-done(((bf16[16,48,512]{2,1,0:T(8,128)(2,1)}), bf16[16,48,512]{2,1,0:T(8,128)(2,1)S(1)}, u32[]{:S(2)}, u32[]{:S(2)}) %all-to-all-start.1) | async-done | bytes 786464 | tf_op jit(solution)/shard_map/all_to_all | solution.py:443
  45.0 0.0 copy-start.1
  45.0 0.9 copy-done.1
  45.9 15.1 %shard_map.121 = (bf16[512,512]{1,0:T(8,128)(2,1)}, bf16[512,512]{1,0:T(8,128)(2,1)}, bf16[512,640]{1,0:T(8,128)(2,1)}, bf16[512,768]{1,0:T(8,128)(2,1)}, bf16[5...) custom-call(s32[1,8]{1,0:T(1,128)} %len_ref.1, f32[1,512]{1,0:T(1,128)} %get-tuple-element.29.slot_ref, ...), custom_call_target="tpu_custom_call" | custom-call | flops 6174015488 | bytes 6291456 | tf_op jit(solution)/shard_map/pallas_call | solution.py:49
  61.0 0.0 copy-start.2
  61.0 0.1 collective-permute-start.4
  61.1 0.0 copy-start.3
  61.1 2.5 %shard_map.122 = bf16[768,512]{1,0:T(8,128)(2,1)} custom-call(f32[1,512]{1,0:T(1,128)} %get-tuple-element.29.slot_ref, bf16[512,512]{1,0:T(8,128)(2,1)} %get-tuple-element.35.grad_ref), custom_call_target="tpu_custom_call" | custom-call | flops 402653184 | bytes 1048576 | tf_op jit(solution)/shard_map/pallas_call | solution.py:49
  63.6 4.8 %all-to-all-start.2 = ((bf16[16,48,512]{2,1,0:T(8,128)(2,1)}), bf16[16,48,512]{2,1,0:T(8,128)(2,1)S(1)}, u32[]{:S(2)}, u32[]{:S(2)}) async-start(bf16[16,48,512]{2,1,0:T(8,128)(2,1)} %bitcast.65), calls=%async_computation.2 | async-start | bytes 1572864 | tf_op jit(solution)/shard_map/all_to_all | solution.py:560
  68.4 0.2 collective-permute-start.1
  68.6 0.0 collective-permute-done.4
  68.6 0.0 copy-done.2
  68.6 0.8 fusion
  69.5 1.8 %collective-permute-start.5 = (bf16[4,2,32,768]{3,2,0,1:T(8,128)(2,1)}, bf16[4,2,32,768]{3,2,0,1:T(8,128)(2,1)S(1)}, u32[]{:S(2)}, u32[]{:S(2)}) collective-permute-start(bf16[4,2,32,768]{3,2,0,1:T(8,128)(2,1)} %fusion), channel_id=1, source_target_pairs={{0,4},{2,6},{4,0},{6,2},{8,12},{10,14},{12,8},{14,10},{16,20},{18,... | collective-permute-start | bytes 1179656 | tf_op jit(solution)/shard_map/ppermute | solution.py:528
  71.3 0.0 collective-permute-done.1
  71.3 0.0 copy-done.3
  71.3 1.8 %fusion.2 = bf16[4,2,32,640]{3,2,0,1:T(8,128)(2,1)} fusion(bf16[4,2,2,32,640]{4,3,2,1,0:T(8,128)(2,1)S(1)} %bitcast.72, s32[]{:T(128)S(6)} %select_n.77, bf16[4,2,2,32,640]{4,3,2,1,0:T(8,128)(2,1)} %bitcast.11), kind=kLoop, calls=%fused_computation.6 | loop fusion | flops 655360 | bytes 984064 | tf_op jit(solution)/shard_map/convert_element_type | solution.py:527
  73.1 1.5 %collective-permute-start.2 = (bf16[4,2,32,640]{3,2,0,1:T(8,128)(2,1)}, bf16[4,2,32,640]{3,2,0,1:T(8,128)(2,1)}, u32[]{:S(2)}, u32[]{:S(2)}) collective-permute-start(bf16[4,2,32,640]{3,2,0,1:T(8,128)(2,1)} %fusion.2), channel_id=1, source_target_pairs={{0,2},{2,0},{4,6},{6,4},{8,10},{10,8},{12,14},{14,12},{16,18},{18,... | collective-permute-start | bytes 983048 | tf_op jit(solution)/shard_map/ppermute | solution.py:528
  74.6 0.0 copy-start
  74.6 13.7 %collective-permute-done.5 = bf16[4,2,32,768]{3,2,0,1:T(8,128)(2,1)S(1)} collective-permute-done((bf16[4,2,32,768]{3,2,0,1:T(8,128)(2,1)}, bf16[4,2,32,768]{3,2,0,1:T(8,128)(2,1)S(1)}, u32[]{:S(2)}, u32[]{:S(2)}) %collective-permute-start.5) | collective-permute-done | bytes 393248 | tf_op jit(solution)/shard_map/ppermute | solution.py:528
  88.3 0.1 fusion.1
  88.4 1.4 %collective-permute-start.6 = (bf16[4,32,768]{2,1,0:T(8,128)(2,1)S(1)}, bf16[4,32,768]{2,1,0:T(8,128)(2,1)S(1)}, u32[]{:S(2)}, u32[]{:S(2)}) collective-permute-start(bf16[4,32,768]{2,1,0:T(8,128)(2,1)S(1)} %get-tuple-element.53), channel_id=1, source_target_pairs={{0,2},{2,0},{4,6},{6,4},{8,10},{10,8},{12,14},{14,12},{16,18},{18,... | collective-permute-start | bytes 589832 | tf_op jit(solution)/shard_map/ppermute | solution.py:528
  89.8 0.0 collective-permute-done.2
  89.8 1.3 %fusion.3 = (bf16[4,32,640]{2,1,0:T(8,128)(2,1)S(1)}, f32[4,32,640]{2,1,0:T(8,128)S(1)}) fusion(bf16[4,2,32,640]{3,2,0,1:T(8,128)(2,1)} %collective-permute-done.2, s32[]{:T(128)S(6)} %select_n.78, bf16[4,2,2,32,640]{4,3,2,1,0:T(8,128)(2,1)} %bitcast.11, s32[]{:T(128)S(6)} %select_n.79, s32[]{:T(128)S(6)} %select_n.76, ...), kind=kLoop, calls=%fused_computation.8 | loop fusion | flops 901120 | bytes 1474580 | tf_op jit(solution)/shard_map/convert_element_type | solution.py:527
  91.1 1.0 collective-permute-start.3
  92.1 4.7 %collective-permute-done.3.refs_1_ = bf16[4,32,640]{2,1,0:T(8,128)(2,1)S(1)} collective-permute-done((bf16[4,32,640]{2,1,0:T(8,128)(2,1)S(1)}, bf16[4,32,640]{2,1,0:T(8,128)(2,1)S(1)}, u32[]{:S(2)}, u32[]{:S(2)}) %collective-permute-start.3) | collective-permute-done | bytes 163872 | tf_op jit(solution)/shard_map/ppermute | solution.py:528
  96.8 0.0 collective-permute-done.6.refs_3_
  96.8 0.1 shard_map.123
  96.9 0.0 all-to-all-done.2
  96.9 0.1 collective-permute-start.7
  97.0 1.1 %collective-permute-start.8 = (bf16[32,1408]{1,0:T(8,128)(2,1)S(1)}, bf16[32,1408]{1,0:T(8,128)(2,1)S(1)}, u32[]{:S(2)}, u32[]{:S(2)}) collective-permute-start(bf16[32,1408]{1,0:T(8,128)(2,1)S(1)} %get-tuple-element.47), channel_id=1, source_target_pairs={{0,8},{2,10},{4,12},{6,14},{8,16},{10,18},{12,20},{14,22},{16,24},... | collective-permute-start | bytes 270344 | tf_op jit(solution)/shard_map/ppermute | solution.py:552
  98.1 2.7 %collective-permute-start.9 = (bf16[32,1408]{1,0:T(8,128)(2,1)S(1)}, bf16[32,1408]{1,0:T(8,128)(2,1)S(1)}, u32[]{:S(2)}, u32[]{:S(2)}) collective-permute-start(bf16[32,1408]{1,0:T(8,128)(2,1)S(1)} %get-tuple-element.48), channel_id=1, source_target_pairs={{0,16},{2,18},{4,20},{6,22},{8,24},{10,26},{12,28},{14,30},{16,0},... | collective-permute-start | bytes 270344 | tf_op jit(solution)/shard_map/ppermute | solution.py:552
  100.8 1.0 collective-permute-start.10
  101.8 0.0 collective-permute-done.7.refs_3_
  101.8 0.0 copy-done
  101.8 2.7 %shard_map.124 = f32[1024,512]{1,0:T(8,128)} custom-call(f32[1,768]{1,0:T(1,128)S(1)} %copy-done, f32[1,768]{1,0:T(1,128)S(1)} %collective-permute-done.refs_1_, bf16[768,512]{1,0:T(8,128)(2,1)S(1)} %bitcast.63, bf16[768,512]{1,0:T(8,128)(2,1)S(1)} %collective-permute-done.7.refs_3_), custom_call_target="tpu_custom_call" | custom-call | flops 1610612736 | bytes 3670016 | tf_op jit(solution)/shard_map/pallas_call | solution.py:49
  104.6 0.0 collective-permute-done.8.refs_0_
  104.6 3.2 %collective-permute-done.9.refs_1_ = bf16[32,1408]{1,0:T(8,128)(2,1)S(1)} collective-permute-done((bf16[32,1408]{1,0:T(8,128)(2,1)S(1)}, bf16[32,1408]{1,0:T(8,128)(2,1)S(1)}, u32[]{:S(2)}, u32[]{:S(2)}) %collective-permute-start.9) | collective-permute-done | bytes 90144 | tf_op jit(solution)/shard_map/ppermute | solution.py:552
  107.8 0.0 collective-permute-done.10.refs_2_
  107.8 0.7 shard_map.125
  108.5 0.0 collective-permute-start.11
  108.5 1.2 %collective-permute-done.11 = f32[32,256]{1,0:T(8,128)S(1)} collective-permute-done((f32[32,256]{1,0:T(8,128)S(1)}, f32[32,256]{1,0:T(8,128)S(1)}, u32[]{:S(2)}, u32[]{:S(2)}) %collective-permute-start.11) | collective-permute-done | bytes 32800 | tf_op jit(solution)/shard_map/ppermute | solution.py:403
  109.7 0.6 pad_maximum_fusion
  (1 shorter events, 0.0 us)
Async XLA Ops:
  22.9 22.1 %all-to-all-start.1 = ((bf16[16,48,512]{2,1,0:T(8,128)(2,1)}), bf16[16,48,512]{2,1,0:T(8,128)(2,1)S(1)}, u32[]{:S(2)}, u32[]{:S(2)}) async-start(bf16[16,48,512]{2,1,0:T(8,128)(2,1)} %bitcast.67), calls=%async_computation.1 | async-start | bytes 1572864 | tf_op jit(solution)/shard_map/all_to_all | solution.py:443
  26.5 1.4 %collective-permute-start = (f32[1,768]{1,0:T(1,128)}, f32[1,768]{1,0:T(1,128)S(1)}, u32[]{:S(2)}, u32[]{:S(2)}) collective-permute-start(f32[1,768]{1,0:T(1,128)} %get-tuple-element.42.refs_0_), channel_id=1, source_target_pairs={{0,1},{1,0},{2,3},{3,2},{4,5},{5,4},{6,7},{7,6},{8,9},{9,8},{10,11... | collective-permute-start | bytes 9224 | tf_op jit(solution)/shard_map/ppermute | solution.py:403
  45.0 0.9 copy-start.1
  61.0 7.6 %copy-start.2 = (bf16[512,768]{1,0:T(8,128)(2,1)S(1)}, bf16[512,768]{1,0:T(8,128)(2,1)}, u32[]{:S(2)}) copy-start(bf16[512,768]{1,0:T(8,128)(2,1)} %get-tuple-element.38) | copy-start | bytes 2359300
  61.0 7.6 %collective-permute-start.4 = (bf16[512,768]{1,0:T(8,128)(2,1)}, bf16[512,768]{1,0:T(8,128)(2,1)S(1)}, u32[]{:S(2)}, u32[]{:S(2)}) collective-permute-start(bf16[512,768]{1,0:T(8,128)(2,1)} %get-tuple-element.39), channel_id=1, source_target_pairs={{0,1},{1,0},{2,3},{3,2},{4,5},{5,4},{6,7},{7,6},{8,9},{9,8},{10,11... | collective-permute-start | bytes 2359304 | tf_op jit(solution)/shard_map/ppermute | solution.py:403
  61.1 10.2 %copy-start.3 = (bf16[512,640]{1,0:T(8,128)(2,1)S(1)}, bf16[512,640]{1,0:T(8,128)(2,1)}, u32[]{:S(2)}) copy-start(bf16[512,640]{1,0:T(8,128)(2,1)} %get-tuple-element.36) | copy-start | bytes 1966084
  63.6 33.3 %all-to-all-start.2 = ((bf16[16,48,512]{2,1,0:T(8,128)(2,1)}), bf16[16,48,512]{2,1,0:T(8,128)(2,1)S(1)}, u32[]{:S(2)}, u32[]{:S(2)}) async-start(bf16[16,48,512]{2,1,0:T(8,128)(2,1)} %bitcast.65), calls=%async_computation.2 | async-start | bytes 1572864 | tf_op jit(solution)/shard_map/all_to_all | solution.py:560
  68.4 2.9 %collective-permute-start.1 = (bf16[512,640]{1,0:T(8,128)(2,1)}, bf16[512,640]{1,0:T(8,128)(2,1)}, u32[]{:S(2)}, u32[]{:S(2)}) collective-permute-start(bf16[512,640]{1,0:T(8,128)(2,1)} %get-tuple-element.37), channel_id=1, source_target_pairs={{0,1},{1,0},{2,3},{3,2},{4,5},{5,4},{6,7},{7,6},{8,9},{9,8},{10,11... | collective-permute-start | bytes 1966088 | tf_op jit(solution)/shard_map/ppermute | solution.py:403
  69.5 18.8 %collective-permute-start.5 = (bf16[4,2,32,768]{3,2,0,1:T(8,128)(2,1)}, bf16[4,2,32,768]{3,2,0,1:T(8,128)(2,1)S(1)}, u32[]{:S(2)}, u32[]{:S(2)}) collective-permute-start(bf16[4,2,32,768]{3,2,0,1:T(8,128)(2,1)} %fusion), channel_id=1, source_target_pairs={{0,4},{2,6},{4,0},{6,2},{8,12},{10,14},{12,8},{14,10},{16,20},{18,... | collective-permute-start | bytes 1179656 | tf_op jit(solution)/shard_map/ppermute | solution.py:528
  73.1 16.7 %collective-permute-start.2 = (bf16[4,2,32,640]{3,2,0,1:T(8,128)(2,1)}, bf16[4,2,32,640]{3,2,0,1:T(8,128)(2,1)}, u32[]{:S(2)}, u32[]{:S(2)}) collective-permute-start(bf16[4,2,32,640]{3,2,0,1:T(8,128)(2,1)} %fusion.2), channel_id=1, source_target_pairs={{0,2},{2,0},{4,6},{6,4},{8,10},{10,8},{12,14},{14,12},{16,18},{18,... | collective-permute-start | bytes 983048 | tf_op jit(solution)/shard_map/ppermute | solution.py:528
  74.6 27.2 %copy-start = (f32[1,768]{1,0:T(1,128)S(1)}, f32[1,768]{1,0:T(1,128)}, u32[]{:S(2)}) copy-start(f32[1,768]{1,0:T(1,128)} %get-tuple-element.42.refs_0_) | copy-start | bytes 9220
  88.4 8.4 %collective-permute-start.6 = (bf16[4,32,768]{2,1,0:T(8,128)(2,1)S(1)}, bf16[4,32,768]{2,1,0:T(8,128)(2,1)S(1)}, u32[]{:S(2)}, u32[]{:S(2)}) collective-permute-start(bf16[4,32,768]{2,1,0:T(8,128)(2,1)S(1)} %get-tuple-element.53), channel_id=1, source_target_pairs={{0,2},{2,0},{4,6},{6,4},{8,10},{10,8},{12,14},{14,12},{16,18},{18,... | collective-permute-start | bytes 589832 | tf_op jit(solution)/shard_map/ppermute | solution.py:528
  91.1 5.7 %collective-permute-start.3 = (bf16[4,32,640]{2,1,0:T(8,128)(2,1)S(1)}, bf16[4,32,640]{2,1,0:T(8,128)(2,1)S(1)}, u32[]{:S(2)}, u32[]{:S(2)}) collective-permute-start(bf16[4,32,640]{2,1,0:T(8,128)(2,1)S(1)} %get-tuple-element.55), channel_id=1, source_target_pairs={{0,4},{2,6},{4,0},{6,2},{8,12},{10,14},{12,8},{14,10},{16,20},{18,... | collective-permute-start | bytes 491528 | tf_op jit(solution)/shard_map/ppermute | solution.py:528
  96.9 4.9 %collective-permute-start.7 = (bf16[768,512]{1,0:T(8,128)(2,1)S(1)}, bf16[768,512]{1,0:T(8,128)(2,1)S(1)}, u32[]{:S(2)}, u32[]{:S(2)}) collective-permute-start(bf16[768,512]{1,0:T(8,128)(2,1)S(1)} %bitcast.62), channel_id=1, source_target_pairs={{0,1},{1,0},{2,3},{3,2},{4,5},{5,4},{6,7},{7,6},{8,9},{9,8},{10,11... | collective-permute-start | bytes 2359304 | tf_op jit(solution)/shard_map/ppermute | solution.py:403
  97.0 7.6 %collective-permute-start.8 = (bf16[32,1408]{1,0:T(8,128)(2,1)S(1)}, bf16[32,1408]{1,0:T(8,128)(2,1)S(1)}, u32[]{:S(2)}, u32[]{:S(2)}) collective-permute-start(bf16[32,1408]{1,0:T(8,128)(2,1)S(1)} %get-tuple-element.47), channel_id=1, source_target_pairs={{0,8},{2,10},{4,12},{6,14},{8,16},{10,18},{12,20},{14,22},{16,24},... | collective-permute-start | bytes 270344 | tf_op jit(solution)/shard_map/ppermute | solution.py:552
  98.1 9.7 %collective-permute-start.9 = (bf16[32,1408]{1,0:T(8,128)(2,1)S(1)}, bf16[32,1408]{1,0:T(8,128)(2,1)S(1)}, u32[]{:S(2)}, u32[]{:S(2)}) collective-permute-start(bf16[32,1408]{1,0:T(8,128)(2,1)S(1)} %get-tuple-element.48), channel_id=1, source_target_pairs={{0,16},{2,18},{4,20},{6,22},{8,24},{10,26},{12,28},{14,30},{16,0},... | collective-permute-start | bytes 270344 | tf_op jit(solution)/shard_map/ppermute | solution.py:552
  100.8 7.0 %collective-permute-start.10 = (bf16[32,1408]{1,0:T(8,128)(2,1)S(1)}, bf16[32,1408]{1,0:T(8,128)(2,1)S(1)}, u32[]{:S(2)}, u32[]{:S(2)}) collective-permute-start(bf16[32,1408]{1,0:T(8,128)(2,1)S(1)} %get-tuple-element.49), channel_id=1, source_target_pairs={{0,24},{2,26},{4,28},{6,30},{8,0},{10,2},{12,4},{14,6},{16,8},{18,... | collective-permute-start | bytes 270344 | tf_op jit(solution)/shard_map/ppermute | solution.py:552
  108.5 1.2 %collective-permute-start.11 = (f32[32,256]{1,0:T(8,128)S(1)}, f32[32,256]{1,0:T(8,128)S(1)}, u32[]{:S(2)}, u32[]{:S(2)}) collective-permute-start(f32[32,256]{1,0:T(8,128)S(1)} %get-tuple-element.51), channel_id=1, source_target_pairs={{0,1},{1,0},{2,3},{3,2},{4,5},{5,4},{6,7},{7,6},{8,9},{9,8},{10,11... | collective-permute-start | bytes 98312 | tf_op jit(solution)/shard_map/ppermute | solution.py:403

commit v14 on v13

--- a/solution.py
+++ b/solution.py
@@ -10,7 +10,7 @@
 
 HEAD_DIM = 64
 LANES = 128
-QUERY_ROWS = 256
+QUERY_ROWS = 128
 
 F32 = jnp.float32
 BF16 = jnp.bfloat16
@@ -75,12 +75,10 @@
     req_ref[...] = found.astype(jnp.int32)
 
 
-def lookup_kernel(cap, wanted_ref, table_hbm, found_ref, ids_ref, table_ref, pick_ref, sem):
+def lookup_kernel(cap, wanted_ref, table_ref, found_ref, ids_ref):
     owners, width = wanted_ref.shape
     slots = found_ref.shape[0]
     rows = table_ref.shape[0]
-    fetch = pltpu.make_async_copy(table_hbm, table_ref, sem)
-    fetch.start()
     wanted = wanted_ref[...]
     high = (wanted >> 8).astype(F32).astype(BF16)
     low = (wanted & 255).astype(F32).astype(BF16)
@@ -95,15 +93,11 @@
     )
     wide = jnp.broadcast_to(ids, (slots, LANES))
     ids_ref[...] = wide.T[0:1, :]
-    step = row_step(slots)
+    step = 256 if slots % 256 == 0 else slots
     for start in range(0, slots, step):
         part = ids[start : start + step]
-        pick_ref[start : start + step, :] = hot(iota((step, rows), 1).astype(F32) == part)
-    fetch.wait()
-    for start in range(0, slots, step):
-        found_ref[start : start + step, :] = dot_nn(
-            pick_ref[start : start + step, :], table_ref[...]
-        ).astype(BF16)
+        pick = hot(iota((step, rows), 1).astype(F32) == part)
+        found_ref[start : start + step, :] = dot_nn(pick, table_ref[...]).astype(BF16)
 
 
 def collect_kernel(groups, *refs):
@@ -340,8 +334,7 @@
         cols = pl.ds(pl.multiple_of(lax.rem(part, wparts) * cols_out, LANES), cols_out)
         grads_ref[k, :, cols_in : cols_in + cols_out] = gwo_ref[:, cols]
         grads_ref[k, :, cols_in + cols_out :] = gain_col
-    cut = grads_hbms[0].shape[1]
-    for k in range(groups):
+        cut = grads_hbms[2 * k].shape[1]
         for i, cols in enumerate((pl.ds(0, cut), pl.ds(cut, grads_ref.shape[2] - cut))):
             put = pltpu.make_async_copy(
                 grads_ref.at[k, :, cols], grads_hbms[2 * k + i], sems.at[8 + 2 * k + i]
@@ -433,12 +426,6 @@
         2 * slots * table.shape[0] * width,
         2 * (slots + table.shape[0]) * width,
         (wanted, table),
-        far=(1,),
-        scratch=[
-            pltpu.VMEM(table.shape, BF16),
-            pltpu.VMEM((slots, table.shape[0]), BF16),
-            pltpu.SemaphoreType.DMA,
-        ],
     )
     returned = lax.all_to_all(found, "table", split_axis=0, concat_axis=0, tiled=True)
     all_ids = [ids] + [shift(ids, "group", groups, k) for k in range(1, groups)]

time: 111 us -> 111 us (level)
  no operation moved by 1% of the time
where the time goes in v14:
time: 111 us; the launch traced here: 110 us
  waiting for transfers between devices  41.4 us (37%)
  Pallas kernels  27.7 us (25%)
  starting transfers between devices  19.2 us (17%)
  blocking collectives  15.6 us (14%)
  other arithmetic  4.74 us (4%)
    pallas_call x7, Pallas kernels, call(): pl.pallas_call(kernel, out_shape=out_shape, in_specs=[pl.BlockSpec(memory...  27.7 us
    ppermute x4, waiting for transfers between devices, halve(): got = lax.ppermute(send, 'table', [(i, i ^ bit) for i in range(owners)])  18.5 us
    all_to_all x1, waiting for transfers between devices, on_device(): lax.all_to_all(found, 'table', split_axis=0, concat_axis=0, tiled=True)  17 us
    all_to_all x1, blocking collectives, on_device(): lax.all_to_all(requested, 'table', split_axis=0, concat_axis=0, tiled=True)  15.6 us
    ppermute x4, starting transfers between devices, halve(): got = lax.ppermute(send, 'table', [(i, i ^ bit) for i in range(owners)])  5.61 us
    all_to_all x1, starting transfers between devices, on_device(): lax.all_to_all(outgoing, 'table', split_axis=0, concat_axis=0, tiled=True)  4.77 us
    ppermute x3, starting transfers between devices, on_device(): lax.ppermute(sends[k - 1], 'table', [(i, (i // plane + k) % outer * plane...  4.76 us
    convert_element_type x4, other arithmetic, halve(): send = add([entry(term, 1 - index, axis) for term in terms]).astype(BF16)  4.09 us
  transfers between devices with their start and end apart: 14, of which 6 were waited for; matrix products, arithmetic and copies ran while one was open for 4% of the time, Pallas kernels for 5%

profile of v14, /device:TPU:0, one launch (start us, length us, event | category | flops | bytes accessed | tf_op | source)
XLA Modules:
  0.0 110.3 jit_solution(9826284863104901248)
XLA Ops:
  0.6 1.7 %shard_map.119 = (s32[16,128]{1,0:T(8,128)}, f32[1,512]{1,0:T(1,128)}) custom-call(s32[1,512]{1,0:T(1,128)} %bitcast.77, s32[1,512]{1,0:T(1,128)} %bitcast.78), custom_call_target="tpu_custom_call" | custom-call | flops 16777216 | bytes 4096 | tf_op jit(solution)/shard_map/pallas_call | solution.py:49
  2.3 15.6 %all_to_all.35 = s32[16,1,128]{2,1,0:T(1,128)} all-to-all(s32[16,1,128]{2,1,0:T(1,128)} %bitcast.76), channel_id=1, replica_groups=mesh['table'=16,'group'=2] {'table'}, dimensions={0} | all-to-all | bytes 16384 | tf_op jit(solution)/shard_map/all_to_all | solution.py:419
  17.9 4.5 %shard_map.120 = (bf16[768,512]{1,0:T(8,128)(2,1)}, f32[1,768]{1,0:T(1,128)}) custom-call(s32[16,128]{1,0:T(8,128)} %bitcast.75, bf16[2048,512]{1,0:T(8,128)(2,1)} %table_ref.1), custom_call_target="tpu_custom_call" | custom-call | flops 1610612736 | bytes 2883584 | tf_op jit(solution)/shard_map/pallas_call | solution.py:49
  22.4 3.6 %all-to-all-start.1 = ((bf16[16,48,512]{2,1,0:T(8,128)(2,1)}), bf16[16,48,512]{2,1,0:T(8,128)(2,1)S(1)}, u32[]{:S(2)}, u32[]{:S(2)}) async-start(bf16[16,48,512]{2,1,0:T(8,128)(2,1)} %bitcast.67), calls=%async_computation.1 | async-start | bytes 1572864 | tf_op jit(solution)/shard_map/all_to_all | solution.py:430
  26.0 0.1 collective-permute-start
  26.1 1.4 %collective-permute-done.refs_1_ = f32[1,768]{1,0:T(1,128)S(1)} collective-permute-done((f32[1,768]{1,0:T(1,128)}, f32[1,768]{1,0:T(1,128)S(1)}, u32[]{:S(2)}, u32[]{:S(2)}) %collective-permute-start) | collective-permute-done | bytes 3104 | tf_op jit(solution)/shard_map/ppermute | solution.py:396
  27.4 17.0 %all-to-all-done.1 = bf16[16,48,512]{2,1,0:T(8,128)(2,1)S(1)} async-done(((bf16[16,48,512]{2,1,0:T(8,128)(2,1)}), bf16[16,48,512]{2,1,0:T(8,128)(2,1)S(1)}, u32[]{:S(2)}, u32[]{:S(2)}) %all-to-all-start.1) | async-done | bytes 786464 | tf_op jit(solution)/shard_map/all_to_all | solution.py:430
  44.5 0.0 copy-start.1
  44.5 0.9 copy-done.1
  45.4 15.4 %shard_map.121 = (bf16[512,512]{1,0:T(8,128)(2,1)}, bf16[512,512]{1,0:T(8,128)(2,1)}, bf16[512,640]{1,0:T(8,128)(2,1)}, bf16[512,768]{1,0:T(8,128)(2,1)}, bf16[5...) custom-call(s32[1,8]{1,0:T(1,128)} %len_ref.1, f32[1,512]{1,0:T(1,128)} %get-tuple-element.29.slot_ref, ...), custom_call_target="tpu_custom_call" | custom-call | flops 6174015488 | bytes 6291456 | tf_op jit(solution)/shard_map/pallas_call | solution.py:49
  60.8 0.0 copy-start.2
  60.8 0.1 collective-permute-start.4
  60.9 0.0 copy-start.3
  60.9 2.7 %shard_map.122 = bf16[768,512]{1,0:T(8,128)(2,1)} custom-call(f32[1,512]{1,0:T(1,128)} %get-tuple-element.29.slot_ref, bf16[512,512]{1,0:T(8,128)(2,1)} %get-tuple-element.35.grad_ref), custom_call_target="tpu_custom_call" | custom-call | flops 402653184 | bytes 1048576 | tf_op jit(solution)/shard_map/pallas_call | solution.py:49
  63.6 4.8 %all-to-all-start.2 = ((bf16[16,48,512]{2,1,0:T(8,128)(2,1)}), bf16[16,48,512]{2,1,0:T(8,128)(2,1)S(1)}, u32[]{:S(2)}, u32[]{:S(2)}) async-start(bf16[16,48,512]{2,1,0:T(8,128)(2,1)} %bitcast.65), calls=%async_computation.2 | async-start | bytes 1572864 | tf_op jit(solution)/shard_map/all_to_all | solution.py:547
  68.4 0.2 collective-permute-start.1
  68.6 0.0 collective-permute-done.4
  68.6 0.0 copy-done.2
  68.6 0.8 fusion
  69.5 1.7 %collective-permute-start.5 = (bf16[4,2,32,768]{3,2,0,1:T(8,128)(2,1)}, bf16[4,2,32,768]{3,2,0,1:T(8,128)(2,1)S(1)}, u32[]{:S(2)}, u32[]{:S(2)}) collective-permute-start(bf16[4,2,32,768]{3,2,0,1:T(8,128)(2,1)} %fusion), channel_id=1, source_target_pairs={{0,4},{2,6},{4,0},{6,2},{8,12},{10,14},{12,8},{14,10},{16,20},{18,... | collective-permute-start | bytes 1179656 | tf_op jit(solution)/shard_map/ppermute | solution.py:515
  71.2 0.0 collective-permute-done.1
  71.2 0.0 copy-done.3
  71.2 1.8 %fusion.2 = bf16[4,2,32,640]{3,2,0,1:T(8,128)(2,1)} fusion(bf16[4,2,2,32,640]{4,3,2,1,0:T(8,128)(2,1)S(1)} %bitcast.72, s32[]{:T(128)S(6)} %select_n.77, bf16[4,2,2,32,640]{4,3,2,1,0:T(8,128)(2,1)} %bitcast.11), kind=kLoop, calls=%fused_computation.6 | loop fusion | flops 655360 | bytes 984064 | tf_op jit(solution)/shard_map/convert_element_type | solution.py:514
  73.0 1.5 %collective-permute-start.2 = (bf16[4,2,32,640]{3,2,0,1:T(8,128)(2,1)}, bf16[4,2,32,640]{3,2,0,1:T(8,128)(2,1)}, u32[]{:S(2)}, u32[]{:S(2)}) collective-permute-start(bf16[4,2,32,640]{3,2,0,1:T(8,128)(2,1)} %fusion.2), channel_id=1, source_target_pairs={{0,2},{2,0},{4,6},{6,4},{8,10},{10,8},{12,14},{14,12},{16,18},{18,... | collective-permute-start | bytes 983048 | tf_op jit(solution)/shard_map/ppermute | solution.py:515
  74.5 0.0 copy-start
  74.5 13.7 %collective-permute-done.5 = bf16[4,2,32,768]{3,2,0,1:T(8,128)(2,1)S(1)} collective-permute-done((bf16[4,2,32,768]{3,2,0,1:T(8,128)(2,1)}, bf16[4,2,32,768]{3,2,0,1:T(8,128)(2,1)S(1)}, u32[]{:S(2)}, u32[]{:S(2)}) %collective-permute-start.5) | collective-permute-done | bytes 393248 | tf_op jit(solution)/shard_map/ppermute | solution.py:515
  88.3 0.1 fusion.1
  88.4 1.4 %collective-permute-start.6 = (bf16[4,32,768]{2,1,0:T(8,128)(2,1)S(1)}, bf16[4,32,768]{2,1,0:T(8,128)(2,1)S(1)}, u32[]{:S(2)}, u32[]{:S(2)}) collective-permute-start(bf16[4,32,768]{2,1,0:T(8,128)(2,1)S(1)} %get-tuple-element.53), channel_id=1, source_target_pairs={{0,2},{2,0},{4,6},{6,4},{8,10},{10,8},{12,14},{14,12},{16,18},{18,... | collective-permute-start | bytes 589832 | tf_op jit(solution)/shard_map/ppermute | solution.py:515
  89.8 0.0 collective-permute-done.2
  89.8 1.3 %fusion.3 = (bf16[4,32,640]{2,1,0:T(8,128)(2,1)S(1)}, f32[4,32,640]{2,1,0:T(8,128)S(1)}) fusion(bf16[4,2,32,640]{3,2,0,1:T(8,128)(2,1)} %collective-permute-done.2, s32[]{:T(128)S(6)} %select_n.78, bf16[4,2,2,32,640]{4,3,2,1,0:T(8,128)(2,1)} %bitcast.11, s32[]{:T(128)S(6)} %select_n.79, s32[]{:T(128)S(6)} %select_n.76, ...), kind=kLoop, calls=%fused_computation.8 | loop fusion | flops 901120 | bytes 1474580 | tf_op jit(solution)/shard_map/convert_element_type | solution.py:514
  91.1 1.0 collective-permute-start.3
  92.1 4.8 %collective-permute-done.3.refs_1_ = bf16[4,32,640]{2,1,0:T(8,128)(2,1)S(1)} collective-permute-done((bf16[4,32,640]{2,1,0:T(8,128)(2,1)S(1)}, bf16[4,32,640]{2,1,0:T(8,128)(2,1)S(1)}, u32[]{:S(2)}, u32[]{:S(2)}) %collective-permute-start.3) | collective-permute-done | bytes 163872 | tf_op jit(solution)/shard_map/ppermute | solution.py:515
  96.8 0.0 collective-permute-done.6.refs_3_
  96.8 0.1 shard_map.123
  96.9 0.0 all-to-all-done.2
  96.9 0.1 collective-permute-start.7
  97.0 1.2 %collective-permute-start.8 = (bf16[32,1408]{1,0:T(8,128)(2,1)S(1)}, bf16[32,1408]{1,0:T(8,128)(2,1)S(1)}, u32[]{:S(2)}, u32[]{:S(2)}) collective-permute-start(bf16[32,1408]{1,0:T(8,128)(2,1)S(1)} %get-tuple-element.47), channel_id=1, source_target_pairs={{0,8},{2,10},{4,12},{6,14},{8,16},{10,18},{12,20},{14,22},{16,24},... | collective-permute-start | bytes 270344 | tf_op jit(solution)/shard_map/ppermute | solution.py:539
  98.2 2.6 %collective-permute-start.9 = (bf16[32,1408]{1,0:T(8,128)(2,1)S(1)}, bf16[32,1408]{1,0:T(8,128)(2,1)S(1)}, u32[]{:S(2)}, u32[]{:S(2)}) collective-permute-start(bf16[32,1408]{1,0:T(8,128)(2,1)S(1)} %get-tuple-element.48), channel_id=1, source_target_pairs={{0,16},{2,18},{4,20},{6,22},{8,24},{10,26},{12,28},{14,30},{16,0},... | collective-permute-start | bytes 270344 | tf_op jit(solution)/shard_map/ppermute | solution.py:539
  100.7 1.0 collective-permute-start.10
  101.7 0.0 collective-permute-done.7.refs_3_
  101.7 0.0 copy-done
  101.8 2.7 %shard_map.124 = f32[1024,512]{1,0:T(8,128)} custom-call(f32[1,768]{1,0:T(1,128)S(1)} %copy-done, f32[1,768]{1,0:T(1,128)S(1)} %collective-permute-done.refs_1_, bf16[768,512]{1,0:T(8,128)(2,1)S(1)} %bitcast.63, bf16[768,512]{1,0:T(8,128)(2,1)S(1)} %collective-permute-done.7.refs_3_), custom_call_target="tpu_custom_call" | custom-call | flops 1610612736 | bytes 3670016 | tf_op jit(solution)/shard_map/pallas_call | solution.py:49
  104.5 0.0 collective-permute-done.8.refs_0_
  104.5 3.2 %collective-permute-done.9.refs_1_ = bf16[32,1408]{1,0:T(8,128)(2,1)S(1)} collective-permute-done((bf16[32,1408]{1,0:T(8,128)(2,1)S(1)}, bf16[32,1408]{1,0:T(8,128)(2,1)S(1)}, u32[]{:S(2)}, u32[]{:S(2)}) %collective-permute-start.9) | collective-permute-done | bytes 90144 | tf_op jit(solution)/shard_map/ppermute | solution.py:539
  107.8 0.0 collective-permute-done.10.refs_2_
  107.8 0.7 shard_map.125
  108.5 0.0 collective-permute-start.11
  108.5 1.2 %collective-permute-done.11 = f32[32,256]{1,0:T(8,128)S(1)} collective-permute-done((f32[32,256]{1,0:T(8,128)S(1)}, f32[32,256]{1,0:T(8,128)S(1)}, u32[]{:S(2)}, u32[]{:S(2)}) %collective-permute-start.11) | collective-permute-done | bytes 32800 | tf_op jit(solution)/shard_map/ppermute | solution.py:396
  109.7 0.6 pad_maximum_fusion
  (1 shorter events, 0.0 us)
Async XLA Ops:
  22.4 22.1 %all-to-all-start.1 = ((bf16[16,48,512]{2,1,0:T(8,128)(2,1)}), bf16[16,48,512]{2,1,0:T(8,128)(2,1)S(1)}, u32[]{:S(2)}, u32[]{:S(2)}) async-start(bf16[16,48,512]{2,1,0:T(8,128)(2,1)} %bitcast.67), calls=%async_computation.1 | async-start | bytes 1572864 | tf_op jit(solution)/shard_map/all_to_all | solution.py:430
  26.0 1.4 %collective-permute-start = (f32[1,768]{1,0:T(1,128)}, f32[1,768]{1,0:T(1,128)S(1)}, u32[]{:S(2)}, u32[]{:S(2)}) collective-permute-start(f32[1,768]{1,0:T(1,128)} %get-tuple-element.42.refs_0_), channel_id=1, source_target_pairs={{0,1},{1,0},{2,3},{3,2},{4,5},{5,4},{6,7},{7,6},{8,9},{9,8},{10,11... | collective-permute-start | bytes 9224 | tf_op jit(solution)/shard_map/ppermute | solution.py:396
  44.5 0.9 copy-start.1
  60.8 7.8 %copy-start.2 = (bf16[512,768]{1,0:T(8,128)(2,1)S(1)}, bf16[512,768]{1,0:T(8,128)(2,1)}, u32[]{:S(2)}) copy-start(bf16[512,768]{1,0:T(8,128)(2,1)} %get-tuple-element.38) | copy-start | bytes 2359300
  60.8 7.8 %collective-permute-start.4 = (bf16[512,768]{1,0:T(8,128)(2,1)}, bf16[512,768]{1,0:T(8,128)(2,1)S(1)}, u32[]{:S(2)}, u32[]{:S(2)}) collective-permute-start(bf16[512,768]{1,0:T(8,128)(2,1)} %get-tuple-element.39), channel_id=1, source_target_pairs={{0,1},{1,0},{2,3},{3,2},{4,5},{5,4},{6,7},{7,6},{8,9},{9,8},{10,11... | collective-permute-start | bytes 2359304 | tf_op jit(solution)/shard_map/ppermute | solution.py:396
  60.9 10.3 %copy-start.3 = (bf16[512,640]{1,0:T(8,128)(2,1)S(1)}, bf16[512,640]{1,0:T(8,128)(2,1)}, u32[]{:S(2)}) copy-start(bf16[512,640]{1,0:T(8,128)(2,1)} %get-tuple-element.36) | copy-start | bytes 1966084
  63.6 33.3 %all-to-all-start.2 = ((bf16[16,48,512]{2,1,0:T(8,128)(2,1)}), bf16[16,48,512]{2,1,0:T(8,128)(2,1)S(1)}, u32[]{:S(2)}, u32[]{:S(2)}) async-start(bf16[16,48,512]{2,1,0:T(8,128)(2,1)} %bitcast.65), calls=%async_computation.2 | async-start | bytes 1572864 | tf_op jit(solution)/shard_map/all_to_all | solution.py:547
  68.4 2.8 %collective-permute-start.1 = (bf16[512,640]{1,0:T(8,128)(2,1)}, bf16[512,640]{1,0:T(8,128)(2,1)}, u32[]{:S(2)}, u32[]{:S(2)}) collective-permute-start(bf16[512,640]{1,0:T(8,128)(2,1)} %get-tuple-element.37), channel_id=1, source_target_pairs={{0,1},{1,0},{2,3},{3,2},{4,5},{5,4},{6,7},{7,6},{8,9},{9,8},{10,11... | collective-permute-start | bytes 1966088 | tf_op jit(solution)/shard_map/ppermute | solution.py:396
  69.5 18.8 %collective-permute-start.5 = (bf16[4,2,32,768]{3,2,0,1:T(8,128)(2,1)}, bf16[4,2,32,768]{3,2,0,1:T(8,128)(2,1)S(1)}, u32[]{:S(2)}, u32[]{:S(2)}) collective-permute-start(bf16[4,2,32,768]{3,2,0,1:T(8,128)(2,1)} %fusion), channel_id=1, source_target_pairs={{0,4},{2,6},{4,0},{6,2},{8,12},{10,14},{12,8},{14,10},{16,20},{18,... | collective-permute-start | bytes 1179656 | tf_op jit(solution)/shard_map/ppermute | solution.py:515
  73.0 16.8 %collective-permute-start.2 = (bf16[4,2,32,640]{3,2,0,1:T(8,128)(2,1)}, bf16[4,2,32,640]{3,2,0,1:T(8,128)(2,1)}, u32[]{:S(2)}, u32[]{:S(2)}) collective-permute-start(bf16[4,2,32,640]{3,2,0,1:T(8,128)(2,1)} %fusion.2), channel_id=1, source_target_pairs={{0,2},{2,0},{4,6},{6,4},{8,10},{10,8},{12,14},{14,12},{16,18},{18,... | collective-permute-start | bytes 983048 | tf_op jit(solution)/shard_map/ppermute | solution.py:515
  74.5 27.2 %copy-start = (f32[1,768]{1,0:T(1,128)S(1)}, f32[1,768]{1,0:T(1,128)}, u32[]{:S(2)}) copy-start(f32[1,768]{1,0:T(1,128)} %get-tuple-element.42.refs_0_) | copy-start | bytes 9220
  88.4 8.4 %collective-permute-start.6 = (bf16[4,32,768]{2,1,0:T(8,128)(2,1)S(1)}, bf16[4,32,768]{2,1,0:T(8,128)(2,1)S(1)}, u32[]{:S(2)}, u32[]{:S(2)}) collective-permute-start(bf16[4,32,768]{2,1,0:T(8,128)(2,1)S(1)} %get-tuple-element.53), channel_id=1, source_target_pairs={{0,2},{2,0},{4,6},{6,4},{8,10},{10,8},{12,14},{14,12},{16,18},{18,... | collective-permute-start | bytes 589832 | tf_op jit(solution)/shard_map/ppermute | solution.py:515
  91.1 5.8 %collective-permute-start.3 = (bf16[4,32,640]{2,1,0:T(8,128)(2,1)S(1)}, bf16[4,32,640]{2,1,0:T(8,128)(2,1)S(1)}, u32[]{:S(2)}, u32[]{:S(2)}) collective-permute-start(bf16[4,32,640]{2,1,0:T(8,128)(2,1)S(1)} %get-tuple-element.55), channel_id=1, source_target_pairs={{0,4},{2,6},{4,0},{6,2},{8,12},{10,14},{12,8},{14,10},{16,20},{18,... | collective-permute-start | bytes 491528 | tf_op jit(solution)/shard_map/ppermute | solution.py:515
  96.9 4.8 %collective-permute-start.7 = (bf16[768,512]{1,0:T(8,128)(2,1)S(1)}, bf16[768,512]{1,0:T(8,128)(2,1)S(1)}, u32[]{:S(2)}, u32[]{:S(2)}) collective-permute-start(bf16[768,512]{1,0:T(8,128)(2,1)S(1)} %bitcast.62), channel_id=1, source_target_pairs={{0,1},{1,0},{2,3},{3,2},{4,5},{5,4},{6,7},{7,6},{8,9},{9,8},{10,11... | collective-permute-start | bytes 2359304 | tf_op jit(solution)/shard_map/ppermute | solution.py:396
  97.0 7.5 %collective-permute-start.8 = (bf16[32,1408]{1,0:T(8,128)(2,1)S(1)}, bf16[32,1408]{1,0:T(8,128)(2,1)S(1)}, u32[]{:S(2)}, u32[]{:S(2)}) collective-permute-start(bf16[32,1408]{1,0:T(8,128)(2,1)S(1)} %get-tuple-element.47), channel_id=1, source_target_pairs={{0,8},{2,10},{4,12},{6,14},{8,16},{10,18},{12,20},{14,22},{16,24},... | collective-permute-start | bytes 270344 | tf_op jit(solution)/shard_map/ppermute | solution.py:539
  98.2 9.6 %collective-permute-start.9 = (bf16[32,1408]{1,0:T(8,128)(2,1)S(1)}, bf16[32,1408]{1,0:T(8,128)(2,1)S(1)}, u32[]{:S(2)}, u32[]{:S(2)}) collective-permute-start(bf16[32,1408]{1,0:T(8,128)(2,1)S(1)} %get-tuple-element.48), channel_id=1, source_target_pairs={{0,16},{2,18},{4,20},{6,22},{8,24},{10,26},{12,28},{14,30},{16,0},... | collective-permute-start | bytes 270344 | tf_op jit(solution)/shard_map/ppermute | solution.py:539
  100.7 7.0 %collective-permute-start.10 = (bf16[32,1408]{1,0:T(8,128)(2,1)S(1)}, bf16[32,1408]{1,0:T(8,128)(2,1)S(1)}, u32[]{:S(2)}, u32[]{:S(2)}) collective-permute-start(bf16[32,1408]{1,0:T(8,128)(2,1)S(1)} %get-tuple-element.49), channel_id=1, source_target_pairs={{0,24},{2,26},{4,28},{6,30},{8,0},{10,2},{12,4},{14,6},{16,8},{18,... | collective-permute-start | bytes 270344 | tf_op jit(solution)/shard_map/ppermute | solution.py:539
  108.5 1.2 %collective-permute-start.11 = (f32[32,256]{1,0:T(8,128)S(1)}, f32[32,256]{1,0:T(8,128)S(1)}, u32[]{:S(2)}, u32[]{:S(2)}) collective-permute-start(f32[32,256]{1,0:T(8,128)S(1)} %get-tuple-element.51), channel_id=1, source_target_pairs={{0,1},{1,0},{2,3},{3,2},{4,5},{5,4},{6,7},{7,6},{8,9},{9,8},{10,11... | collective-permute-start | bytes 98312 | tf_op jit(solution)/shard_map/ppermute | solution.py:396

commit v15 on v14

--- a/solution.py
+++ b/solution.py
@@ -10,7 +10,7 @@
 
 HEAD_DIM = 64
 LANES = 128
-QUERY_ROWS = 128
+QUERY_ROWS = 256
 
 F32 = jnp.float32
 BF16 = jnp.bfloat16
@@ -155,6 +155,7 @@
     row_ref,
     grads_ref,
     pick_ref,
+    put_ref,
     emb_ref,
     proj_ref,
     slope_ref,
@@ -320,6 +321,8 @@
     put_result = pltpu.make_async_copy(result_ref, result_hbm, sems.at[6])
     put_result.start()
     puts = [put_result]
+    put_ref[...] = hot(iota((slots, count), 0).astype(F32) == slot_ref[...])
+
     me = lax.axis_index("group")
     emb_t = emb_ref[...].T
     cols_in = 4 * width // groups
@@ -341,31 +344,16 @@
             )
             put.start()
             puts.append(put)
-    for i, r0 in enumerate((0, count // 2)):
-        rows = pl.ds(r0, count // 2)
-        row_ref[rows, :] = (
-            cot_ref[rows, :].astype(F32) + dot_nt(gpre_ref[rows, :], w_in_ref[...])
-        ).astype(BF16)
+    gemb = (cot_ref[...].astype(F32) + dot_nt(gpre_ref[...], w_in_ref[...])).astype(BF16)
+    step = slots // 2
+    for i, start in enumerate((0, step)):
+        rows = pl.ds(start, step)
+        row_ref[rows, :] = dot_nn(put_ref[rows, :], gemb).astype(BF16)
         sem = sems.at[7 + i * (2 + 2 * groups)]
         puts.append(pltpu.make_async_copy(row_ref.at[rows], row_hbm.at[rows], sem))
         puts[-1].start()
     for put in puts:
         put.wait()
-
-
-def slots_kernel(slot_ref, grad_ref, out_hbm, out_ref, sems):
-    count = grad_ref.shape[0]
-    slots = out_ref.shape[0]
-    step = row_step(slots)
-    stores = []
-    for n, start in enumerate(range(0, slots, step)):
-        put = hot((iota((step, count), 0) + start).astype(F32) == slot_ref[...])
-        out_ref[start : start + step, :] = dot_nn(put, grad_ref[...]).astype(BF16)
-        here = pl.ds(start, step)
-        stores.append(pltpu.make_async_copy(out_ref.at[here], out_hbm.at[here], sems.at[n]))
-        stores[-1].start()
-    for store in stores:
-        store.wait()
 
 
 def plane_kernel(outer, terms, *refs):
@@ -438,11 +426,11 @@
     cols_all = cols_in + cols_out + LANES
     cut = cols_all // LANES // 2 * LANES
     square = pltpu.VMEM((count, width), BF16)
-    result, row_grad, *grads = call(
+    result, outgoing, *grads = call(
         functools.partial(layer_kernel, groups, wparts),
         [
             jax.ShapeDtypeStruct((count, width), BF16),
-            jax.ShapeDtypeStruct((count, width), BF16),
+            jax.ShapeDtypeStruct((slots, width), BF16),
             *[
                 jax.ShapeDtypeStruct((width, cols), BF16)
                 for _ in range(groups)
@@ -461,9 +449,10 @@
             pltpu.VMEM(w_out.shape, BF16),
             square,
             square,
-            square,
+            pltpu.VMEM((slots, width), BF16),
             pltpu.VMEM((groups, width, cols_all), BF16),
             pltpu.VMEM((count, slots), BF16),
+            pltpu.VMEM((slots, count), BF16),
             square,
             pltpu.VMEM((4, count, width), BF16),
             pltpu.VMEM((4, count, width), F32),
@@ -480,19 +469,6 @@
             pltpu.SemaphoreType.DMA((10 + 2 * groups,)),
         ],
     )
-    (outgoing,) = call(
-        slots_kernel,
-        [jax.ShapeDtypeStruct((slots, width), BF16)],
-        2 * slots * count * width,
-        4 * count * width,
-        (slot, row_grad),
-        far_out=(0,),
-        scratch=[
-            pltpu.VMEM((slots, width), BF16),
-            pltpu.SemaphoreType.DMA((slots // row_step(slots),)),
-        ],
-    )
-
     rows = width // owners
     side = 2 if owners % 4 == 0 else 1
     plane = side * side

time: 111 us -> 108 us (0.973)
  Pallas kernels: 27.7 us -> 24.6 us
    pallas_call x7 -> x6, Pallas kernels: 27.7 us -> 24.6 us  [call(): pl.pallas_call(kernel, out_shape=out_shape, in_specs=[pl.BlockSpec(memory...]
  transfers between devices with their start and end apart: 14 -> 14, of which waited for: 6 -> 7; matrix products, arithmetic and copies ran while one was open for 4% -> 5% of each run, Pallas kernels for 5% -> 3%
where the time goes in v15:
time: 108 us
  waiting for transfers between devices  40.6 us (38%)
  Pallas kernels  24.6 us (23%)
  starting transfers between devices  19.5 us (18%)
  blocking collectives  15.6 us (14%)
  other arithmetic  5.74 us (5%)
    pallas_call x6, Pallas kernels, call(): pl.pallas_call(kernel, out_shape=out_shape, in_specs=[pl.BlockSpec(memory...  24.6 us
    ppermute x4, waiting for transfers between devices, halve(): got = lax.ppermute(send, 'table', [(i, i ^ bit) for i in range(owners)])  18.5 us
    all_to_all x1, waiting for transfers between devices, on_device(): lax.all_to_all(found, 'table', split_axis=0, concat_axis=0, tiled=True)  17 us
    all_to_all x1, blocking collectives, on_device(): lax.all_to_all(requested, 'table', split_axis=0, concat_axis=0, tiled=True)  15.6 us
    ppermute x3, starting transfers between devices, on_device(): lax.ppermute(sends[k - 1], 'table', [(i, (i // plane + k) % outer * plane...  5.43 us
    ppermute x4, starting transfers between devices, halve(): got = lax.ppermute(send, 'table', [(i, i ^ bit) for i in range(owners)])  5.17 us
    convert_element_type x4, other arithmetic, halve(): send = add([entry(term, 1 - index, axis) for term in terms]).astype(BF16)  5.09 us
    all_to_all x1, starting transfers between devices, on_device(): lax.all_to_all(outgoing, 'table', split_axis=0, concat_axis=0, tiled=True)  4.91 us
  transfers between devices with their start and end apart: 14, of which 7 were waited for; matrix products, arithmetic and copies ran while one was open for 5% of the time, Pallas kernels for 3%

profile of v15, /device:TPU:0, one launch (start us, length us, event | category | flops | bytes accessed | tf_op | source)
XLA Modules:
  0.0 107.8 jit_solution(2773510130377341282)
XLA Ops:
  0.6 1.7 %shard_map.119 = (s32[16,128]{1,0:T(8,128)}, f32[1,512]{1,0:T(1,128)}) custom-call(s32[1,512]{1,0:T(1,128)} %bitcast.77, s32[1,512]{1,0:T(1,128)} %bitcast.78), custom_call_target="tpu_custom_call" | custom-call | flops 16777216 | bytes 4096 | tf_op jit(solution)/shard_map/pallas_call | solution.py:49
  2.3 15.6 %all_to_all.35 = s32[16,1,128]{2,1,0:T(1,128)} all-to-all(s32[16,1,128]{2,1,0:T(1,128)} %bitcast.76), channel_id=1, replica_groups=mesh['table'=16,'group'=2] {'table'}, dimensions={0} | all-to-all | bytes 16384 | tf_op jit(solution)/shard_map/all_to_all | solution.py:407
  17.9 4.5 %shard_map.120 = (bf16[768,512]{1,0:T(8,128)(2,1)}, f32[1,768]{1,0:T(1,128)}) custom-call(s32[16,128]{1,0:T(8,128)} %bitcast.75, bf16[2048,512]{1,0:T(8,128)(2,1)} %table_ref.1), custom_call_target="tpu_custom_call" | custom-call | flops 1610612736 | bytes 2883584 | tf_op jit(solution)/shard_map/pallas_call | solution.py:49
  22.4 3.6 %all-to-all-start.1 = ((bf16[16,48,512]{2,1,0:T(8,128)(2,1)}), bf16[16,48,512]{2,1,0:T(8,128)(2,1)S(1)}, u32[]{:S(2)}, u32[]{:S(2)}) async-start(bf16[16,48,512]{2,1,0:T(8,128)(2,1)} %bitcast.67), calls=%async_computation.1 | async-start | bytes 1572864 | tf_op jit(solution)/shard_map/all_to_all | solution.py:418
  26.0 0.1 collective-permute-start
  26.1 1.4 %collective-permute-done.refs_1_ = f32[1,768]{1,0:T(1,128)S(1)} collective-permute-done((f32[1,768]{1,0:T(1,128)}, f32[1,768]{1,0:T(1,128)S(1)}, u32[]{:S(2)}, u32[]{:S(2)}) %collective-permute-start) | collective-permute-done | bytes 3104 | tf_op jit(solution)/shard_map/ppermute | solution.py:384
  27.4 17.0 %all-to-all-done.1 = bf16[16,48,512]{2,1,0:T(8,128)(2,1)S(1)} async-done(((bf16[16,48,512]{2,1,0:T(8,128)(2,1)}), bf16[16,48,512]{2,1,0:T(8,128)(2,1)S(1)}, u32[]{:S(2)}, u32[]{:S(2)}) %all-to-all-start.1) | async-done | bytes 786464 | tf_op jit(solution)/shard_map/all_to_all | solution.py:418
  44.5 0.0 copy-start.1
  44.5 0.9 copy-done.1
  45.4 15.0 %shard_map.121 = (bf16[512,512]{1,0:T(8,128)(2,1)}, bf16[768,512]{1,0:T(8,128)(2,1)}, bf16[512,640]{1,0:T(8,128)(2,1)}, bf16[512,768]{1,0:T(8,128)(2,1)}, bf16[5...) custom-call(s32[1,8]{1,0:T(1,128)} %len_ref.1, f32[1,512]{1,0:T(1,128)} %get-tuple-element.29.slot_ref, ...), custom_call_target="tpu_custom_call" | custom-call | flops 6174015488 | bytes 6291456 | tf_op jit(solution)/shard_map/pallas_call | solution.py:49
  60.4 0.0 copy-start.3
  60.4 0.0 copy-start.2
  60.4 0.1 collective-permute-start.4
  60.5 4.9 %all-to-all-start.2 = ((bf16[16,48,512]{2,1,0:T(8,128)(2,1)}), bf16[16,48,512]{2,1,0:T(8,128)(2,1)S(1)}, u32[]{:S(2)}, u32[]{:S(2)}) async-start(bf16[16,48,512]{2,1,0:T(8,128)(2,1)} %bitcast.65), calls=%async_computation.2 | async-start | bytes 1572864 | tf_op jit(solution)/shard_map/all_to_all | solution.py:523
  65.4 0.1 collective-permute-start.1
  65.5 0.0 collective-permute-done.4
  65.5 1.9 %fusion = bf16[4,2,32,768]{3,2,0,1:T(8,128)(2,1)} fusion(bf16[4,2,2,32,768]{4,3,2,1,0:T(8,128)(2,1)} %bitcast.68, s32[]{:T(128)S(6)} %select_n.78, bf16[4,2,2,32,768]{4,3,2,1,0:T(8,128)(2,1)S(1)} %bitcast.70), kind=kLoop, calls=%fused_computation.2 | loop fusion | flops 786432 | bytes 1180672 | tf_op jit(solution)/shard_map/convert_element_type | solution.py:490
  67.4 1.9 %collective-permute-start.5 = (bf16[4,2,32,768]{3,2,0,1:T(8,128)(2,1)}, bf16[4,2,32,768]{3,2,0,1:T(8,128)(2,1)S(1)}, u32[]{:S(2)}, u32[]{:S(2)}) collective-permute-start(bf16[4,2,32,768]{3,2,0,1:T(8,128)(2,1)} %fusion), channel_id=1, source_target_pairs={{0,4},{2,6},{4,0},{6,2},{8,12},{10,14},{12,8},{14,10},{16,20},{18,... | collective-permute-start | bytes 1179656 | tf_op jit(solution)/shard_map/ppermute | solution.py:491
  69.3 0.0 collective-permute-done.1
  69.3 0.0 copy-done.3
  69.3 1.8 %fusion.2 = bf16[4,2,32,640]{3,2,0,1:T(8,128)(2,1)} fusion(bf16[4,2,2,32,640]{4,3,2,1,0:T(8,128)(2,1)S(1)} %bitcast.72, s32[]{:T(128)S(6)} %select_n.77, bf16[4,2,2,32,640]{4,3,2,1,0:T(8,128)(2,1)} %bitcast.11), kind=kLoop, calls=%fused_computation.6 | loop fusion | flops 655360 | bytes 984064 | tf_op jit(solution)/shard_map/convert_element_type | solution.py:490
  71.1 1.5 %collective-permute-start.2 = (bf16[4,2,32,640]{3,2,0,1:T(8,128)(2,1)}, bf16[4,2,32,640]{3,2,0,1:T(8,128)(2,1)}, u32[]{:S(2)}, u32[]{:S(2)}) collective-permute-start(bf16[4,2,32,640]{3,2,0,1:T(8,128)(2,1)} %fusion.2), channel_id=1, source_target_pairs={{0,2},{2,0},{4,6},{6,4},{8,10},{10,8},{12,14},{14,12},{16,18},{18,... | collective-permute-start | bytes 983048 | tf_op jit(solution)/shard_map/ppermute | solution.py:491
  72.5 0.0 copy-start
  72.5 12.7 %collective-permute-done.5 = bf16[4,2,32,768]{3,2,0,1:T(8,128)(2,1)S(1)} collective-permute-done((bf16[4,2,32,768]{3,2,0,1:T(8,128)(2,1)}, bf16[4,2,32,768]{3,2,0,1:T(8,128)(2,1)S(1)}, u32[]{:S(2)}, u32[]{:S(2)}) %collective-permute-start.5) | collective-permute-done | bytes 393248 | tf_op jit(solution)/shard_map/ppermute | solution.py:491
  85.3 0.0 copy-done.2
  85.3 0.1 fusion.1
  85.4 1.3 %collective-permute-start.6 = (bf16[4,32,768]{2,1,0:T(8,128)(2,1)S(1)}, bf16[4,32,768]{2,1,0:T(8,128)(2,1)S(1)}, u32[]{:S(2)}, u32[]{:S(2)}) collective-permute-start(bf16[4,32,768]{2,1,0:T(8,128)(2,1)S(1)} %get-tuple-element.53), channel_id=1, source_target_pairs={{0,2},{2,0},{4,6},{6,4},{8,10},{10,8},{12,14},{14,12},{16,18},{18,... | collective-permute-start | bytes 589832 | tf_op jit(solution)/shard_map/ppermute | solution.py:491
  86.7 0.5 collective-permute-done.2
  87.2 1.3 %fusion.3 = (bf16[4,32,640]{2,1,0:T(8,128)(2,1)S(1)}, f32[4,32,640]{2,1,0:T(8,128)S(1)}) fusion(bf16[4,2,32,640]{3,2,0,1:T(8,128)(2,1)} %collective-permute-done.2, s32[]{:T(128)S(6)} %select_n.78, bf16[4,2,2,32,640]{4,3,2,1,0:T(8,128)(2,1)} %bitcast.11, s32[]{:T(128)S(6)} %select_n.79, s32[]{:T(128)S(6)} %select_n.76, ...), kind=kLoop, calls=%fused_computation.8 | loop fusion | flops 901120 | bytes 1474580 | tf_op jit(solution)/shard_map/convert_element_type | solution.py:490
  88.5 0.5 collective-permute-start.3
  89.0 5.3 %collective-permute-done.3.refs_1_ = bf16[4,32,640]{2,1,0:T(8,128)(2,1)S(1)} collective-permute-done((bf16[4,32,640]{2,1,0:T(8,128)(2,1)S(1)}, bf16[4,32,640]{2,1,0:T(8,128)(2,1)S(1)}, u32[]{:S(2)}, u32[]{:S(2)}) %collective-permute-start.3) | collective-permute-done | bytes 163872 | tf_op jit(solution)/shard_map/ppermute | solution.py:491
  94.3 0.0 collective-permute-done.6.refs_3_
  94.3 0.1 shard_map.122
  94.3 0.0 all-to-all-done.2
  94.3 0.1 collective-permute-start.7
  94.4 1.7 %collective-permute-start.8 = (bf16[32,1408]{1,0:T(8,128)(2,1)S(1)}, bf16[32,1408]{1,0:T(8,128)(2,1)S(1)}, u32[]{:S(2)}, u32[]{:S(2)}) collective-permute-start(bf16[32,1408]{1,0:T(8,128)(2,1)S(1)} %get-tuple-element.47), channel_id=1, source_target_pairs={{0,8},{2,10},{4,12},{6,14},{8,16},{10,18},{12,20},{14,22},{16,24},... | collective-permute-start | bytes 270344 | tf_op jit(solution)/shard_map/ppermute | solution.py:515
  96.2 1.9 %collective-permute-start.9 = (bf16[32,1408]{1,0:T(8,128)(2,1)S(1)}, bf16[32,1408]{1,0:T(8,128)(2,1)S(1)}, u32[]{:S(2)}, u32[]{:S(2)}) collective-permute-start(bf16[32,1408]{1,0:T(8,128)(2,1)S(1)} %get-tuple-element.48), channel_id=1, source_target_pairs={{0,16},{2,18},{4,20},{6,22},{8,24},{10,26},{12,28},{14,30},{16,0},... | collective-permute-start | bytes 270344 | tf_op jit(solution)/shard_map/ppermute | solution.py:515
  98.1 1.7 %collective-permute-start.10 = (bf16[32,1408]{1,0:T(8,128)(2,1)S(1)}, bf16[32,1408]{1,0:T(8,128)(2,1)S(1)}, u32[]{:S(2)}, u32[]{:S(2)}) collective-permute-start(bf16[32,1408]{1,0:T(8,128)(2,1)S(1)} %get-tuple-element.49), channel_id=1, source_target_pairs={{0,24},{2,26},{4,28},{6,30},{8,0},{10,2},{12,4},{14,6},{16,8},{18,... | collective-permute-start | bytes 270344 | tf_op jit(solution)/shard_map/ppermute | solution.py:515
  99.9 0.0 collective-permute-done.7.refs_3_
  99.9 0.0 copy-done
  99.9 2.7 %shard_map.123 = f32[1024,512]{1,0:T(8,128)} custom-call(f32[1,768]{1,0:T(1,128)S(1)} %copy-done, f32[1,768]{1,0:T(1,128)S(1)} %collective-permute-done.refs_1_, bf16[768,512]{1,0:T(8,128)(2,1)S(1)} %bitcast.63, bf16[768,512]{1,0:T(8,128)(2,1)S(1)} %collective-permute-done.7.refs_3_), custom_call_target="tpu_custom_call" | custom-call | flops 1610612736 | bytes 3670016 | tf_op jit(solution)/shard_map/pallas_call | solution.py:49
  102.6 0.0 collective-permute-done.8.refs_0_
  102.6 2.5 %collective-permute-done.9.refs_1_ = bf16[32,1408]{1,0:T(8,128)(2,1)S(1)} collective-permute-done((bf16[32,1408]{1,0:T(8,128)(2,1)S(1)}, bf16[32,1408]{1,0:T(8,128)(2,1)S(1)}, u32[]{:S(2)}, u32[]{:S(2)}) %collective-permute-start.9) | collective-permute-done | bytes 90144 | tf_op jit(solution)/shard_map/ppermute | solution.py:515
  105.2 0.0 collective-permute-done.10.refs_2_
  105.2 0.7 shard_map.124
  105.9 0.0 collective-permute-start.11
  105.9 1.2 %collective-permute-done.11 = f32[32,256]{1,0:T(8,128)S(1)} collective-permute-done((f32[32,256]{1,0:T(8,128)S(1)}, f32[32,256]{1,0:T(8,128)S(1)}, u32[]{:S(2)}, u32[]{:S(2)}) %collective-permute-start.11) | collective-permute-done | bytes 32800 | tf_op jit(solution)/shard_map/ppermute | solution.py:384
  107.1 0.6 pad_maximum_fusion
  (1 shorter events, 0.0 us)
Async XLA Ops:
  22.4 22.1 %all-to-all-start.1 = ((bf16[16,48,512]{2,1,0:T(8,128)(2,1)}), bf16[16,48,512]{2,1,0:T(8,128)(2,1)S(1)}, u32[]{:S(2)}, u32[]{:S(2)}) async-start(bf16[16,48,512]{2,1,0:T(8,128)(2,1)} %bitcast.67), calls=%async_computation.1 | async-start | bytes 1572864 | tf_op jit(solution)/shard_map/all_to_all | solution.py:418
  26.0 1.4 %collective-permute-start = (f32[1,768]{1,0:T(1,128)}, f32[1,768]{1,0:T(1,128)S(1)}, u32[]{:S(2)}, u32[]{:S(2)}) collective-permute-start(f32[1,768]{1,0:T(1,128)} %get-tuple-element.42.refs_0_), channel_id=1, source_target_pairs={{0,1},{1,0},{2,3},{3,2},{4,5},{5,4},{6,7},{7,6},{8,9},{9,8},{10,11... | collective-permute-start | bytes 9224 | tf_op jit(solution)/shard_map/ppermute | solution.py:384
  44.5 0.9 copy-start.1
  60.4 8.9 %copy-start.3 = (bf16[512,640]{1,0:T(8,128)(2,1)S(1)}, bf16[512,640]{1,0:T(8,128)(2,1)}, u32[]{:S(2)}) copy-start(bf16[512,640]{1,0:T(8,128)(2,1)} %get-tuple-element.36) | copy-start | bytes 1966084
  60.4 24.9 %copy-start.2 = (bf16[512,768]{1,0:T(8,128)(2,1)S(1)}, bf16[512,768]{1,0:T(8,128)(2,1)}, u32[]{:S(2)}) copy-start(bf16[512,768]{1,0:T(8,128)(2,1)} %get-tuple-element.38) | copy-start | bytes 2359300
  60.4 5.1 %collective-permute-start.4 = (bf16[512,768]{1,0:T(8,128)(2,1)}, bf16[512,768]{1,0:T(8,128)(2,1)S(1)}, u32[]{:S(2)}, u32[]{:S(2)}) collective-permute-start(bf16[512,768]{1,0:T(8,128)(2,1)} %get-tuple-element.39), channel_id=1, source_target_pairs={{0,1},{1,0},{2,3},{3,2},{4,5},{5,4},{6,7},{7,6},{8,9},{9,8},{10,11... | collective-permute-start | bytes 2359304 | tf_op jit(solution)/shard_map/ppermute | solution.py:384
  60.5 33.9 %all-to-all-start.2 = ((bf16[16,48,512]{2,1,0:T(8,128)(2,1)}), bf16[16,48,512]{2,1,0:T(8,128)(2,1)S(1)}, u32[]{:S(2)}, u32[]{:S(2)}) async-start(bf16[16,48,512]{2,1,0:T(8,128)(2,1)} %bitcast.65), calls=%async_computation.2 | async-start | bytes 1572864 | tf_op jit(solution)/shard_map/all_to_all | solution.py:523
  65.4 3.9 %collective-permute-start.1 = (bf16[512,640]{1,0:T(8,128)(2,1)}, bf16[512,640]{1,0:T(8,128)(2,1)}, u32[]{:S(2)}, u32[]{:S(2)}) collective-permute-start(bf16[512,640]{1,0:T(8,128)(2,1)} %get-tuple-element.37), channel_id=1, source_target_pairs={{0,1},{1,0},{2,3},{3,2},{4,5},{5,4},{6,7},{7,6},{8,9},{9,8},{10,11... | collective-permute-start | bytes 1966088 | tf_op jit(solution)/shard_map/ppermute | solution.py:384
  67.4 17.9 %collective-permute-start.5 = (bf16[4,2,32,768]{3,2,0,1:T(8,128)(2,1)}, bf16[4,2,32,768]{3,2,0,1:T(8,128)(2,1)S(1)}, u32[]{:S(2)}, u32[]{:S(2)}) collective-permute-start(bf16[4,2,32,768]{3,2,0,1:T(8,128)(2,1)} %fusion), channel_id=1, source_target_pairs={{0,4},{2,6},{4,0},{6,2},{8,12},{10,14},{12,8},{14,10},{16,20},{18,... | collective-permute-start | bytes 1179656 | tf_op jit(solution)/shard_map/ppermute | solution.py:491
  71.1 16.1 %collective-permute-start.2 = (bf16[4,2,32,640]{3,2,0,1:T(8,128)(2,1)}, bf16[4,2,32,640]{3,2,0,1:T(8,128)(2,1)}, u32[]{:S(2)}, u32[]{:S(2)}) collective-permute-start(bf16[4,2,32,640]{3,2,0,1:T(8,128)(2,1)} %fusion.2), channel_id=1, source_target_pairs={{0,2},{2,0},{4,6},{6,4},{8,10},{10,8},{12,14},{14,12},{16,18},{18,... | collective-permute-start | bytes 983048 | tf_op jit(solution)/shard_map/ppermute | solution.py:491
  72.5 27.3 %copy-start = (f32[1,768]{1,0:T(1,128)S(1)}, f32[1,768]{1,0:T(1,128)}, u32[]{:S(2)}) copy-start(f32[1,768]{1,0:T(1,128)} %get-tuple-element.42.refs_0_) | copy-start | bytes 9220
  85.4 8.9 %collective-permute-start.6 = (bf16[4,32,768]{2,1,0:T(8,128)(2,1)S(1)}, bf16[4,32,768]{2,1,0:T(8,128)(2,1)S(1)}, u32[]{:S(2)}, u32[]{:S(2)}) collective-permute-start(bf16[4,32,768]{2,1,0:T(8,128)(2,1)S(1)} %get-tuple-element.53), channel_id=1, source_target_pairs={{0,2},{2,0},{4,6},{6,4},{8,10},{10,8},{12,14},{14,12},{16,18},{18,... | collective-permute-start | bytes 589832 | tf_op jit(solution)/shard_map/ppermute | solution.py:491
  88.5 5.8 %collective-permute-start.3 = (bf16[4,32,640]{2,1,0:T(8,128)(2,1)S(1)}, bf16[4,32,640]{2,1,0:T(8,128)(2,1)S(1)}, u32[]{:S(2)}, u32[]{:S(2)}) collective-permute-start(bf16[4,32,640]{2,1,0:T(8,128)(2,1)S(1)} %get-tuple-element.55), channel_id=1, source_target_pairs={{0,4},{2,6},{4,0},{6,2},{8,12},{10,14},{12,8},{14,10},{16,20},{18,... | collective-permute-start | bytes 491528 | tf_op jit(solution)/shard_map/ppermute | solution.py:491
  94.3 5.5 %collective-permute-start.7 = (bf16[768,512]{1,0:T(8,128)(2,1)S(1)}, bf16[768,512]{1,0:T(8,128)(2,1)S(1)}, u32[]{:S(2)}, u32[]{:S(2)}) collective-permute-start(bf16[768,512]{1,0:T(8,128)(2,1)S(1)} %bitcast.62), channel_id=1, source_target_pairs={{0,1},{1,0},{2,3},{3,2},{4,5},{5,4},{6,7},{7,6},{8,9},{9,8},{10,11... | collective-permute-start | bytes 2359304 | tf_op jit(solution)/shard_map/ppermute | solution.py:384
  94.4 8.2 %collective-permute-start.8 = (bf16[32,1408]{1,0:T(8,128)(2,1)S(1)}, bf16[32,1408]{1,0:T(8,128)(2,1)S(1)}, u32[]{:S(2)}, u32[]{:S(2)}) collective-permute-start(bf16[32,1408]{1,0:T(8,128)(2,1)S(1)} %get-tuple-element.47), channel_id=1, source_target_pairs={{0,8},{2,10},{4,12},{6,14},{8,16},{10,18},{12,20},{14,22},{16,24},... | collective-permute-start | bytes 270344 | tf_op jit(solution)/shard_map/ppermute | solution.py:515
  96.2 9.0 %collective-permute-start.9 = (bf16[32,1408]{1,0:T(8,128)(2,1)S(1)}, bf16[32,1408]{1,0:T(8,128)(2,1)S(1)}, u32[]{:S(2)}, u32[]{:S(2)}) collective-permute-start(bf16[32,1408]{1,0:T(8,128)(2,1)S(1)} %get-tuple-element.48), channel_id=1, source_target_pairs={{0,16},{2,18},{4,20},{6,22},{8,24},{10,26},{12,28},{14,30},{16,0},... | collective-permute-start | bytes 270344 | tf_op jit(solution)/shard_map/ppermute | solution.py:515
  98.1 7.1 %collective-permute-start.10 = (bf16[32,1408]{1,0:T(8,128)(2,1)S(1)}, bf16[32,1408]{1,0:T(8,128)(2,1)S(1)}, u32[]{:S(2)}, u32[]{:S(2)}) collective-permute-start(bf16[32,1408]{1,0:T(8,128)(2,1)S(1)} %get-tuple-element.49), channel_id=1, source_target_pairs={{0,24},{2,26},{4,28},{6,30},{8,0},{10,2},{12,4},{14,6},{16,8},{18,... | collective-permute-start | bytes 270344 | tf_op jit(solution)/shard_map/ppermute | solution.py:515
  105.9 1.2 %collective-permute-start.11 = (f32[32,256]{1,0:T(8,128)S(1)}, f32[32,256]{1,0:T(8,128)S(1)}, u32[]{:S(2)}, u32[]{:S(2)}) collective-permute-start(f32[32,256]{1,0:T(8,128)S(1)} %get-tuple-element.51), channel_id=1, source_target_pairs={{0,1},{1,0},{2,3},{3,2},{4,5},{5,4},{6,7},{7,6},{8,9},{9,8},{10,11... | collective-permute-start | bytes 98312 | tf_op jit(solution)/shard_map/ppermute | solution.py:384

commit v16 on v15

--- a/solution.py
+++ b/solution.py
@@ -489,6 +489,8 @@
     def halve(terms, index, axis, bit, last):
         send = add([entry(term, 1 - index, axis) for term in terms]).astype(BF16)
         got = lax.ppermute(send, "table", [(i, i ^ bit) for i in range(owners)])
+        if not last:
+            *terms, got = lax.optimization_barrier((*terms, got))
         kept = [entry(term, index, axis) for term in terms]
         return ([add(kept)] if last else kept) + [got]
 

time: 108 us -> 109 us (level)
  transfers between devices with their start and end apart: 14 -> 14, of which waited for: 7 -> 6; matrix products, arithmetic and copies ran while one was open for 5% -> 5% of each run, Pallas kernels for 3% -> 3%
where the time goes in v16:
time: 109 us; the launch traced here: 108 us
  waiting for transfers between devices  40.4 us (37%)
  Pallas kernels  24.6 us (23%)
  starting transfers between devices  20.1 us (18%)
  blocking collectives  15.6 us (14%)
  other arithmetic  5.69 us (5%)
    pallas_call x6, Pallas kernels, call(): pl.pallas_call(kernel, out_shape=out_shape, in_specs=[pl.BlockSpec(memory...  24.6 us
    ppermute x4, waiting for transfers between devices, halve(): got = lax.ppermute(send, 'table', [(i, i ^ bit) for i in range(owners)])  18.6 us
    all_to_all x1, waiting for transfers between devices, on_device(): lax.all_to_all(found, 'table', split_axis=0, concat_axis=0, tiled=True)  17 us
    all_to_all x1, blocking collectives, on_device(): lax.all_to_all(requested, 'table', split_axis=0, concat_axis=0, tiled=True)  15.6 us
    ppermute x3, starting transfers between devices, on_device(): lax.ppermute(sends[k - 1], 'table', [(i, (i // plane + k) % outer * plane...  5.81 us
    ppermute x4, starting transfers between devices, halve(): got = lax.ppermute(send, 'table', [(i, i ^ bit) for i in range(owners)])  5.23 us
    convert_element_type x4, other arithmetic, halve(): send = add([entry(term, 1 - index, axis) for term in terms]).astype(BF16)  5.04 us
    all_to_all x1, starting transfers between devices, on_device(): lax.all_to_all(outgoing, 'table', split_axis=0, concat_axis=0, tiled=True)  4.77 us
  transfers between devices with their start and end apart: 14, of which 6 were waited for; matrix products, arithmetic and copies ran while one was open for 5% of the time, Pallas kernels for 3%

profile of v16, /device:TPU:0, one launch (start us, length us, event | category | flops | bytes accessed | tf_op | source)
XLA Modules:
  0.0 108.2 jit_solution(4685976989250703517)
XLA Ops:
  0.6 1.7 %shard_map.119 = (s32[16,128]{1,0:T(8,128)}, f32[1,512]{1,0:T(1,128)}) custom-call(s32[1,512]{1,0:T(1,128)} %bitcast.61, s32[1,512]{1,0:T(1,128)} %bitcast.62), custom_call_target="tpu_custom_call" | custom-call | flops 16777216 | bytes 4096 | tf_op jit(solution)/shard_map/pallas_call | solution.py:49
  2.3 15.6 %all_to_all.35 = s32[16,1,128]{2,1,0:T(1,128)} all-to-all(s32[16,1,128]{2,1,0:T(1,128)} %bitcast.60), channel_id=1, replica_groups=mesh['table'=16,'group'=2] {'table'}, dimensions={0} | all-to-all | bytes 16384 | tf_op jit(solution)/shard_map/all_to_all | solution.py:407
  17.9 4.5 %shard_map.120 = (bf16[768,512]{1,0:T(8,128)(2,1)}, f32[1,768]{1,0:T(1,128)}) custom-call(s32[16,128]{1,0:T(8,128)} %bitcast.59, bf16[2048,512]{1,0:T(8,128)(2,1)} %table_ref.1), custom_call_target="tpu_custom_call" | custom-call | flops 1610612736 | bytes 2883584 | tf_op jit(solution)/shard_map/pallas_call | solution.py:49
  22.4 3.6 %all-to-all-start.1 = ((bf16[16,48,512]{2,1,0:T(8,128)(2,1)}), bf16[16,48,512]{2,1,0:T(8,128)(2,1)S(1)}, u32[]{:S(2)}, u32[]{:S(2)}) async-start(bf16[16,48,512]{2,1,0:T(8,128)(2,1)} %bitcast.51), calls=%async_computation.1 | async-start | bytes 1572864 | tf_op jit(solution)/shard_map/all_to_all | solution.py:418
  26.0 0.1 collective-permute-start
  26.1 1.4 %collective-permute-done.refs_1_ = f32[1,768]{1,0:T(1,128)S(1)} collective-permute-done((f32[1,768]{1,0:T(1,128)}, f32[1,768]{1,0:T(1,128)S(1)}, u32[]{:S(2)}, u32[]{:S(2)}) %collective-permute-start) | collective-permute-done | bytes 3104 | tf_op jit(solution)/shard_map/ppermute | solution.py:384
  27.4 17.0 %all-to-all-done.1 = bf16[16,48,512]{2,1,0:T(8,128)(2,1)S(1)} async-done(((bf16[16,48,512]{2,1,0:T(8,128)(2,1)}), bf16[16,48,512]{2,1,0:T(8,128)(2,1)S(1)}, u32[]{:S(2)}, u32[]{:S(2)}) %all-to-all-start.1) | async-done | bytes 786464 | tf_op jit(solution)/shard_map/all_to_all | solution.py:418
  44.5 0.0 copy-start.1
  44.5 0.9 copy-done.1
  45.4 15.0 %shard_map.121 = (bf16[512,512]{1,0:T(8,128)(2,1)}, bf16[768,512]{1,0:T(8,128)(2,1)}, bf16[512,640]{1,0:T(8,128)(2,1)}, bf16[512,768]{1,0:T(8,128)(2,1)}, bf16[5...) custom-call(s32[1,8]{1,0:T(1,128)} %len_ref.1, f32[1,512]{1,0:T(1,128)} %get-tuple-element.35.slot_ref, ...), custom_call_target="tpu_custom_call" | custom-call | flops 6174015488 | bytes 6291456 | tf_op jit(solution)/shard_map/pallas_call | solution.py:49
  60.4 0.0 copy-start.3
  60.4 0.0 copy-start.2
  60.4 0.1 collective-permute-start.4
  60.5 0.5 collective-permute-start.1
  61.0 4.8 %all-to-all-start.2 = ((bf16[16,48,512]{2,1,0:T(8,128)(2,1)}), bf16[16,48,512]{2,1,0:T(8,128)(2,1)S(1)}, u32[]{:S(2)}, u32[]{:S(2)}) async-start(bf16[16,48,512]{2,1,0:T(8,128)(2,1)} %bitcast.49), calls=%async_computation.2 | async-start | bytes 1572864 | tf_op jit(solution)/shard_map/all_to_all | solution.py:525
  65.8 0.0 collective-permute-done.4
  65.8 1.9 %fusion = bf16[4,2,32,768]{3,2,0,1:T(8,128)(2,1)} fusion(bf16[4,2,2,32,768]{4,3,2,1,0:T(8,128)(2,1)} %bitcast.52, s32[]{:T(128)S(6)} %select_n.78, bf16[4,2,2,32,768]{4,3,2,1,0:T(8,128)(2,1)S(1)} %bitcast.54), kind=kLoop, calls=%fused_computation.2 | loop fusion | flops 786432 | bytes 1180672 | tf_op jit(solution)/shard_map/convert_element_type | solution.py:490
  67.6 1.9 %collective-permute-start.5 = (bf16[4,2,32,768]{3,2,0,1:T(8,128)(2,1)}, bf16[4,2,32,768]{3,2,0,1:T(8,128)(2,1)S(1)}, u32[]{:S(2)}, u32[]{:S(2)}) collective-permute-start(bf16[4,2,32,768]{3,2,0,1:T(8,128)(2,1)} %fusion), channel_id=1, source_target_pairs={{0,4},{2,6},{4,0},{6,2},{8,12},{10,14},{12,8},{14,10},{16,20},{18,... | collective-permute-start | bytes 1179656 | tf_op jit(solution)/shard_map/ppermute | solution.py:491
  69.5 0.0 collective-permute-done.1
  69.5 0.0 copy-done.3
  69.5 1.8 %fusion.2 = bf16[4,2,32,640]{3,2,0,1:T(8,128)(2,1)} fusion(bf16[4,2,2,32,640]{4,3,2,1,0:T(8,128)(2,1)S(1)} %bitcast.56, s32[]{:T(128)S(6)} %select_n.71, bf16[4,2,2,32,640]{4,3,2,1,0:T(8,128)(2,1)} %bitcast.11), kind=kLoop, calls=%fused_computation.6 | loop fusion | flops 655360 | bytes 984064 | tf_op jit(solution)/shard_map/convert_element_type | solution.py:490
  71.3 1.5 %collective-permute-start.2 = (bf16[4,2,32,640]{3,2,0,1:T(8,128)(2,1)}, bf16[4,2,32,640]{3,2,0,1:T(8,128)(2,1)}, u32[]{:S(2)}, u32[]{:S(2)}) collective-permute-start(bf16[4,2,32,640]{3,2,0,1:T(8,128)(2,1)} %fusion.2), channel_id=1, source_target_pairs={{0,2},{2,0},{4,6},{6,4},{8,10},{10,8},{12,14},{14,12},{16,18},{18,... | collective-permute-start | bytes 983048 | tf_op jit(solution)/shard_map/ppermute | solution.py:491
  72.8 0.0 copy-start
  72.8 13.8 %collective-permute-done.2 = bf16[4,2,32,640]{3,2,0,1:T(8,128)(2,1)} collective-permute-done((bf16[4,2,32,640]{3,2,0,1:T(8,128)(2,1)}, bf16[4,2,32,640]{3,2,0,1:T(8,128)(2,1)}, u32[]{:S(2)}, u32[]{:S(2)}) %collective-permute-start.2) | collective-permute-done | bytes 327712 | tf_op jit(solution)/shard_map/ppermute | solution.py:491
  86.5 0.0 collective-permute-done.5
  86.5 0.0 copy-done.2
  86.5 0.1 fusion.1
  86.7 1.3 %collective-permute-start.6 = (bf16[4,32,768]{2,1,0:T(8,128)(2,1)S(1)}, bf16[4,32,768]{2,1,0:T(8,128)(2,1)S(1)}, u32[]{:S(2)}, u32[]{:S(2)}) collective-permute-start(bf16[4,32,768]{2,1,0:T(8,128)(2,1)S(1)} %get-tuple-element.65), channel_id=1, source_target_pairs={{0,2},{2,0},{4,6},{6,4},{8,10},{10,8},{12,14},{14,12},{16,18},{18,... | collective-permute-start | bytes 589832 | tf_op jit(solution)/shard_map/ppermute | solution.py:491
  88.0 1.3 %fusion.3 = (bf16[4,32,640]{2,1,0:T(8,128)(2,1)S(1)}, f32[4,32,640]{2,1,0:T(8,128)S(1)}) fusion(bf16[4,2,32,640]{3,2,0,1:T(8,128)(2,1)} %collective-permute-done.2, s32[]{:T(128)S(6)} %select_n.78, s32[]{:T(128)S(6)} %select_n.79, s32[]{:T(128)S(6)} %select_n.77, s32[]{:T(128)S(6)} %select_n.74, s32[]{:T(128)S(6)} %select_n.75, ...), kind=kLoop, calls=%fused_computation.8 | loop fusion | flops 901120 | bytes 1474580 | tf_op jit(solution)/shard_map/convert_element_type | solution.py:490
  89.3 0.6 collective-permute-start.3
  89.9 4.8 %collective-permute-done.3.refs_1_ = bf16[4,32,640]{2,1,0:T(8,128)(2,1)S(1)} collective-permute-done((bf16[4,32,640]{2,1,0:T(8,128)(2,1)S(1)}, bf16[4,32,640]{2,1,0:T(8,128)(2,1)S(1)}, u32[]{:S(2)}, u32[]{:S(2)}) %collective-permute-start.3) | collective-permute-done | bytes 163872 | tf_op jit(solution)/shard_map/ppermute | solution.py:491
  94.7 0.0 collective-permute-done.6.refs_3_
  94.7 0.1 shard_map.122
  94.7 0.0 all-to-all-done.2
  94.7 0.1 collective-permute-start.7
  94.8 1.6 %collective-permute-start.8 = (bf16[32,1408]{1,0:T(8,128)(2,1)S(1)}, bf16[32,1408]{1,0:T(8,128)(2,1)S(1)}, u32[]{:S(2)}, u32[]{:S(2)}) collective-permute-start(bf16[32,1408]{1,0:T(8,128)(2,1)S(1)} %get-tuple-element.59), channel_id=1, source_target_pairs={{0,8},{2,10},{4,12},{6,14},{8,16},{10,18},{12,20},{14,22},{16,24},... | collective-permute-start | bytes 270344 | tf_op jit(solution)/shard_map/ppermute | solution.py:517
  96.4 1.6 %collective-permute-start.9 = (bf16[32,1408]{1,0:T(8,128)(2,1)S(1)}, bf16[32,1408]{1,0:T(8,128)(2,1)S(1)}, u32[]{:S(2)}, u32[]{:S(2)}) collective-permute-start(bf16[32,1408]{1,0:T(8,128)(2,1)S(1)} %get-tuple-element.60), channel_id=1, source_target_pairs={{0,16},{2,18},{4,20},{6,22},{8,24},{10,26},{12,28},{14,30},{16,0},... | collective-permute-start | bytes 270344 | tf_op jit(solution)/shard_map/ppermute | solution.py:517
  98.0 2.6 %collective-permute-start.10 = (bf16[32,1408]{1,0:T(8,128)(2,1)S(1)}, bf16[32,1408]{1,0:T(8,128)(2,1)S(1)}, u32[]{:S(2)}, u32[]{:S(2)}) collective-permute-start(bf16[32,1408]{1,0:T(8,128)(2,1)S(1)} %get-tuple-element.61), channel_id=1, source_target_pairs={{0,24},{2,26},{4,28},{6,30},{8,0},{10,2},{12,4},{14,6},{16,8},{18,... | collective-permute-start | bytes 270344 | tf_op jit(solution)/shard_map/ppermute | solution.py:517
  100.6 0.0 collective-permute-done.7.refs_3_
  100.6 0.0 copy-done
  100.6 2.7 %shard_map.123 = f32[1024,512]{1,0:T(8,128)} custom-call(f32[1,768]{1,0:T(1,128)S(1)} %copy-done, f32[1,768]{1,0:T(1,128)S(1)} %collective-permute-done.refs_1_, bf16[768,512]{1,0:T(8,128)(2,1)S(1)} %bitcast.47, bf16[768,512]{1,0:T(8,128)(2,1)S(1)} %collective-permute-done.7.refs_3_), custom_call_target="tpu_custom_call" | custom-call | flops 1610612736 | bytes 3670016 | tf_op jit(solution)/shard_map/pallas_call | solution.py:49
  103.4 0.0 collective-permute-done.8.refs_0_
  103.4 2.2 %collective-permute-done.9.refs_1_ = bf16[32,1408]{1,0:T(8,128)(2,1)S(1)} collective-permute-done((bf16[32,1408]{1,0:T(8,128)(2,1)S(1)}, bf16[32,1408]{1,0:T(8,128)(2,1)S(1)}, u32[]{:S(2)}, u32[]{:S(2)}) %collective-permute-start.9) | collective-permute-done | bytes 90144 | tf_op jit(solution)/shard_map/ppermute | solution.py:517
  105.6 0.0 collective-permute-done.10.refs_2_
  105.6 0.7 shard_map.124
  106.3 0.0 collective-permute-start.11
  106.3 1.2 %collective-permute-done.11 = f32[32,256]{1,0:T(8,128)S(1)} collective-permute-done((f32[32,256]{1,0:T(8,128)S(1)}, f32[32,256]{1,0:T(8,128)S(1)}, u32[]{:S(2)}, u32[]{:S(2)}) %collective-permute-start.11) | collective-permute-done | bytes 32800 | tf_op jit(solution)/shard_map/ppermute | solution.py:384
  107.5 0.6 pad_maximum_fusion
  (1 shorter events, 0.0 us)
Async XLA Ops:
  22.4 22.1 %all-to-all-start.1 = ((bf16[16,48,512]{2,1,0:T(8,128)(2,1)}), bf16[16,48,512]{2,1,0:T(8,128)(2,1)S(1)}, u32[]{:S(2)}, u32[]{:S(2)}) async-start(bf16[16,48,512]{2,1,0:T(8,128)(2,1)} %bitcast.51), calls=%async_computation.1 | async-start | bytes 1572864 | tf_op jit(solution)/shard_map/all_to_all | solution.py:418
  26.0 1.4 %collective-permute-start = (f32[1,768]{1,0:T(1,128)}, f32[1,768]{1,0:T(1,128)S(1)}, u32[]{:S(2)}, u32[]{:S(2)}) collective-permute-start(f32[1,768]{1,0:T(1,128)} %get-tuple-element.54.refs_0_), channel_id=1, source_target_pairs={{0,1},{1,0},{2,3},{3,2},{4,5},{5,4},{6,7},{7,6},{8,9},{9,8},{10,11... | collective-permute-start | bytes 9224 | tf_op jit(solution)/shard_map/ppermute | solution.py:384
  44.5 0.9 copy-start.1
  60.4 9.2 %copy-start.3 = (bf16[512,640]{1,0:T(8,128)(2,1)S(1)}, bf16[512,640]{1,0:T(8,128)(2,1)}, u32[]{:S(2)}) copy-start(bf16[512,640]{1,0:T(8,128)(2,1)} %get-tuple-element.42) | copy-start | bytes 1966084
  60.4 26.2 %copy-start.2 = (bf16[512,768]{1,0:T(8,128)(2,1)S(1)}, bf16[512,768]{1,0:T(8,128)(2,1)}, u32[]{:S(2)}) copy-start(bf16[512,768]{1,0:T(8,128)(2,1)} %get-tuple-element.47) | copy-start | bytes 2359300
  60.4 5.4 %collective-permute-start.4 = (bf16[512,768]{1,0:T(8,128)(2,1)}, bf16[512,768]{1,0:T(8,128)(2,1)S(1)}, u32[]{:S(2)}, u32[]{:S(2)}) collective-permute-start(bf16[512,768]{1,0:T(8,128)(2,1)} %get-tuple-element.48), channel_id=1, source_target_pairs={{0,1},{1,0},{2,3},{3,2},{4,5},{5,4},{6,7},{7,6},{8,9},{9,8},{10,11... | collective-permute-start | bytes 2359304 | tf_op jit(solution)/shard_map/ppermute | solution.py:384
  60.5 9.1 %collective-permute-start.1 = (bf16[512,640]{1,0:T(8,128)(2,1)}, bf16[512,640]{1,0:T(8,128)(2,1)}, u32[]{:S(2)}, u32[]{:S(2)}) collective-permute-start(bf16[512,640]{1,0:T(8,128)(2,1)} %get-tuple-element.43), channel_id=1, source_target_pairs={{0,1},{1,0},{2,3},{3,2},{4,5},{5,4},{6,7},{7,6},{8,9},{9,8},{10,11... | collective-permute-start | bytes 1966088 | tf_op jit(solution)/shard_map/ppermute | solution.py:384
  61.0 33.8 %all-to-all-start.2 = ((bf16[16,48,512]{2,1,0:T(8,128)(2,1)}), bf16[16,48,512]{2,1,0:T(8,128)(2,1)S(1)}, u32[]{:S(2)}, u32[]{:S(2)}) async-start(bf16[16,48,512]{2,1,0:T(8,128)(2,1)} %bitcast.49), calls=%async_computation.2 | async-start | bytes 1572864 | tf_op jit(solution)/shard_map/all_to_all | solution.py:525
  67.6 18.9 %collective-permute-start.5 = (bf16[4,2,32,768]{3,2,0,1:T(8,128)(2,1)}, bf16[4,2,32,768]{3,2,0,1:T(8,128)(2,1)S(1)}, u32[]{:S(2)}, u32[]{:S(2)}) collective-permute-start(bf16[4,2,32,768]{3,2,0,1:T(8,128)(2,1)} %fusion), channel_id=1, source_target_pairs={{0,4},{2,6},{4,0},{6,2},{8,12},{10,14},{12,8},{14,10},{16,20},{18,... | collective-permute-start | bytes 1179656 | tf_op jit(solution)/shard_map/ppermute | solution.py:491
  71.3 15.2 %collective-permute-start.2 = (bf16[4,2,32,640]{3,2,0,1:T(8,128)(2,1)}, bf16[4,2,32,640]{3,2,0,1:T(8,128)(2,1)}, u32[]{:S(2)}, u32[]{:S(2)}) collective-permute-start(bf16[4,2,32,640]{3,2,0,1:T(8,128)(2,1)} %fusion.2), channel_id=1, source_target_pairs={{0,2},{2,0},{4,6},{6,4},{8,10},{10,8},{12,14},{14,12},{16,18},{18,... | collective-permute-start | bytes 983048 | tf_op jit(solution)/shard_map/ppermute | solution.py:491
  72.8 27.9 %copy-start = (f32[1,768]{1,0:T(1,128)S(1)}, f32[1,768]{1,0:T(1,128)}, u32[]{:S(2)}) copy-start(f32[1,768]{1,0:T(1,128)} %get-tuple-element.54.refs_0_) | copy-start | bytes 9220
  86.7 8.0 %collective-permute-start.6 = (bf16[4,32,768]{2,1,0:T(8,128)(2,1)S(1)}, bf16[4,32,768]{2,1,0:T(8,128)(2,1)S(1)}, u32[]{:S(2)}, u32[]{:S(2)}) collective-permute-start(bf16[4,32,768]{2,1,0:T(8,128)(2,1)S(1)} %get-tuple-element.65), channel_id=1, source_target_pairs={{0,2},{2,0},{4,6},{6,4},{8,10},{10,8},{12,14},{14,12},{16,18},{18,... | collective-permute-start | bytes 589832 | tf_op jit(solution)/shard_map/ppermute | solution.py:491
  89.3 5.4 %collective-permute-start.3 = (bf16[4,32,640]{2,1,0:T(8,128)(2,1)S(1)}, bf16[4,32,640]{2,1,0:T(8,128)(2,1)S(1)}, u32[]{:S(2)}, u32[]{:S(2)}) collective-permute-start(bf16[4,32,640]{2,1,0:T(8,128)(2,1)S(1)} %get-tuple-element.67), channel_id=1, source_target_pairs={{0,4},{2,6},{4,0},{6,2},{8,12},{10,14},{12,8},{14,10},{16,20},{18,... | collective-permute-start | bytes 491528 | tf_op jit(solution)/shard_map/ppermute | solution.py:491
  94.7 5.9 %collective-permute-start.7 = (bf16[768,512]{1,0:T(8,128)(2,1)S(1)}, bf16[768,512]{1,0:T(8,128)(2,1)S(1)}, u32[]{:S(2)}, u32[]{:S(2)}) collective-permute-start(bf16[768,512]{1,0:T(8,128)(2,1)S(1)} %bitcast.46), channel_id=1, source_target_pairs={{0,1},{1,0},{2,3},{3,2},{4,5},{5,4},{6,7},{7,6},{8,9},{9,8},{10,11... | collective-permute-start | bytes 2359304 | tf_op jit(solution)/shard_map/ppermute | solution.py:384
  94.8 8.6 %collective-permute-start.8 = (bf16[32,1408]{1,0:T(8,128)(2,1)S(1)}, bf16[32,1408]{1,0:T(8,128)(2,1)S(1)}, u32[]{:S(2)}, u32[]{:S(2)}) collective-permute-start(bf16[32,1408]{1,0:T(8,128)(2,1)S(1)} %get-tuple-element.59), channel_id=1, source_target_pairs={{0,8},{2,10},{4,12},{6,14},{8,16},{10,18},{12,20},{14,22},{16,24},... | collective-permute-start | bytes 270344 | tf_op jit(solution)/shard_map/ppermute | solution.py:517
  96.4 9.2 %collective-permute-start.9 = (bf16[32,1408]{1,0:T(8,128)(2,1)S(1)}, bf16[32,1408]{1,0:T(8,128)(2,1)S(1)}, u32[]{:S(2)}, u32[]{:S(2)}) collective-permute-start(bf16[32,1408]{1,0:T(8,128)(2,1)S(1)} %get-tuple-element.60), channel_id=1, source_target_pairs={{0,16},{2,18},{4,20},{6,22},{8,24},{10,26},{12,28},{14,30},{16,0},... | collective-permute-start | bytes 270344 | tf_op jit(solution)/shard_map/ppermute | solution.py:517
  98.0 7.5 %collective-permute-start.10 = (bf16[32,1408]{1,0:T(8,128)(2,1)S(1)}, bf16[32,1408]{1,0:T(8,128)(2,1)S(1)}, u32[]{:S(2)}, u32[]{:S(2)}) collective-permute-start(bf16[32,1408]{1,0:T(8,128)(2,1)S(1)} %get-tuple-element.61), channel_id=1, source_target_pairs={{0,24},{2,26},{4,28},{6,30},{8,0},{10,2},{12,4},{14,6},{16,8},{18,... | collective-permute-start | bytes 270344 | tf_op jit(solution)/shard_map/ppermute | solution.py:517
  106.3 1.2 %collective-permute-start.11 = (f32[32,256]{1,0:T(8,128)S(1)}, f32[32,256]{1,0:T(8,128)S(1)}, u32[]{:S(2)}, u32[]{:S(2)}) collective-permute-start(f32[32,256]{1,0:T(8,128)S(1)} %get-tuple-element.63), channel_id=1, source_target_pairs={{0,1},{1,0},{2,3},{3,2},{4,5},{5,4},{6,7},{7,6},{8,9},{9,8},{10,11... | collective-permute-start | bytes 98312 | tf_op jit(solution)/shard_map/ppermute | solution.py:384

commit v17 on v15

--- a/solution.py
+++ b/solution.py
@@ -493,10 +493,10 @@
         return ([add(kept)] if last else kept) + [got]
 
     if side == 2:
-        left = halve(sides[0], low, 2, 1, False)
-        right = halve(sides[1], middle, 1, 2, False)
-        left = halve(left, middle, 1, 2, True)
-        right = halve(right, low, 1, 1, True)
+        left = halve(sides[0], middle, 1, 2, False)
+        right = halve(sides[1], low, 2, 1, False)
+        left = halve(left, low, 1, 1, True)
+        right = halve(right, middle, 1, 2, True)
     else:
         left, right = [[term[:, 0, 0] for term in terms] for terms in sides]
     cols = cols_all

time: 108 us -> 108 us (level)
  waiting for transfers between devices: 40.6 us -> 38.9 us
  starting transfers between devices: 19.5 us -> 21.1 us
    ppermute x4, waiting for transfers between devices: 18.5 us -> 16.8 us  [halve(): got = lax.ppermute(send, 'table', [(i, i ^ bit) for i in range(owners)])]
    ppermute x4, starting transfers between devices: 5.17 us -> 6.72 us  [halve(): got = lax.ppermute(send, 'table', [(i, i ^ bit) for i in range(owners)])]
  transfers between devices with their start and end apart: 14 -> 14, of which waited for: 7 -> 6; matrix products, arithmetic and copies ran while one was open for 5% -> 5% of each run, Pallas kernels for 3% -> 3%
where the time goes in v17:
time: 108 us
  waiting for transfers between devices  38.9 us (36%)
  Pallas kernels  24.6 us (23%)
  starting transfers between devices  21.1 us (20%)
  blocking collectives  15.6 us (14%)
  other arithmetic  5.74 us (5%)
    pallas_call x6, Pallas kernels, call(): pl.pallas_call(kernel, out_shape=out_shape, in_specs=[pl.BlockSpec(memory...  24.6 us
    all_to_all x1, waiting for transfers between devices, on_device(): lax.all_to_all(found, 'table', split_axis=0, concat_axis=0, tiled=True)  17 us
    ppermute x4, waiting for transfers between devices, halve(): got = lax.ppermute(send, 'table', [(i, i ^ bit) for i in range(owners)])  16.8 us
    all_to_all x1, blocking collectives, on_device(): lax.all_to_all(requested, 'table', split_axis=0, concat_axis=0, tiled=True)  15.6 us
    ppermute x4, starting transfers between devices, halve(): got = lax.ppermute(send, 'table', [(i, i ^ bit) for i in range(owners)])  6.72 us
    ppermute x3, starting transfers between devices, on_device(): lax.ppermute(sends[k - 1], 'table', [(i, (i // plane + k) % outer * plane...  5.52 us
    convert_element_type x4, other arithmetic, halve(): send = add([entry(term, 1 - index, axis) for term in terms]).astype(BF16)  5.09 us
    all_to_all x1, starting transfers between devices, on_device(): lax.all_to_all(outgoing, 'table', split_axis=0, concat_axis=0, tiled=True)  4.91 us
  transfers between devices with their start and end apart: 14, of which 6 were waited for; matrix products, arithmetic and copies ran while one was open for 5% of the time, Pallas kernels for 3%

profile of v17, /device:TPU:0, one launch (start us, length us, event | category | flops | bytes accessed | tf_op | source)
XLA Modules:
  0.0 107.7 jit_solution(14988732551648351309)
XLA Ops:
  0.6 1.7 %shard_map.119 = (s32[16,128]{1,0:T(8,128)}, f32[1,512]{1,0:T(1,128)}) custom-call(s32[1,512]{1,0:T(1,128)} %bitcast.77, s32[1,512]{1,0:T(1,128)} %bitcast.78), custom_call_target="tpu_custom_call" | custom-call | flops 16777216 | bytes 4096 | tf_op jit(solution)/shard_map/pallas_call | solution.py:49
  2.3 15.6 %all_to_all.35 = s32[16,1,128]{2,1,0:T(1,128)} all-to-all(s32[16,1,128]{2,1,0:T(1,128)} %bitcast.76), channel_id=1, replica_groups=mesh['table'=16,'group'=2] {'table'}, dimensions={0} | all-to-all | bytes 16384 | tf_op jit(solution)/shard_map/all_to_all | solution.py:407
  17.9 4.5 %shard_map.120 = (bf16[768,512]{1,0:T(8,128)(2,1)}, f32[1,768]{1,0:T(1,128)}) custom-call(s32[16,128]{1,0:T(8,128)} %bitcast.75, bf16[2048,512]{1,0:T(8,128)(2,1)} %table_ref.1), custom_call_target="tpu_custom_call" | custom-call | flops 1610612736 | bytes 2883584 | tf_op jit(solution)/shard_map/pallas_call | solution.py:49
  22.4 3.6 %all-to-all-start.1 = ((bf16[16,48,512]{2,1,0:T(8,128)(2,1)}), bf16[16,48,512]{2,1,0:T(8,128)(2,1)S(1)}, u32[]{:S(2)}, u32[]{:S(2)}) async-start(bf16[16,48,512]{2,1,0:T(8,128)(2,1)} %bitcast.67), calls=%async_computation.1 | async-start | bytes 1572864 | tf_op jit(solution)/shard_map/all_to_all | solution.py:418
  26.0 0.1 collective-permute-start
  26.1 1.4 %collective-permute-done.refs_1_ = f32[1,768]{1,0:T(1,128)S(1)} collective-permute-done((f32[1,768]{1,0:T(1,128)}, f32[1,768]{1,0:T(1,128)S(1)}, u32[]{:S(2)}, u32[]{:S(2)}) %collective-permute-start) | collective-permute-done | bytes 3104 | tf_op jit(solution)/shard_map/ppermute | solution.py:384
  27.4 17.0 %all-to-all-done.1 = bf16[16,48,512]{2,1,0:T(8,128)(2,1)S(1)} async-done(((bf16[16,48,512]{2,1,0:T(8,128)(2,1)}), bf16[16,48,512]{2,1,0:T(8,128)(2,1)S(1)}, u32[]{:S(2)}, u32[]{:S(2)}) %all-to-all-start.1) | async-done | bytes 786464 | tf_op jit(solution)/shard_map/all_to_all | solution.py:418
  44.5 0.0 copy-start.1
  44.5 0.9 copy-done.1
  45.4 15.0 %shard_map.121 = (bf16[512,512]{1,0:T(8,128)(2,1)}, bf16[768,512]{1,0:T(8,128)(2,1)}, bf16[512,640]{1,0:T(8,128)(2,1)}, bf16[512,768]{1,0:T(8,128)(2,1)}, bf16[5...) custom-call(s32[1,8]{1,0:T(1,128)} %len_ref.1, f32[1,512]{1,0:T(1,128)} %get-tuple-element.29.slot_ref, ...), custom_call_target="tpu_custom_call" | custom-call | flops 6174015488 | bytes 6291456 | tf_op jit(solution)/shard_map/pallas_call | solution.py:49
  60.4 0.0 copy-start.3
  60.4 0.0 copy-start.2
  60.4 0.1 collective-permute-start.4
  60.5 4.9 %all-to-all-start.2 = ((bf16[16,48,512]{2,1,0:T(8,128)(2,1)}), bf16[16,48,512]{2,1,0:T(8,128)(2,1)S(1)}, u32[]{:S(2)}, u32[]{:S(2)}) async-start(bf16[16,48,512]{2,1,0:T(8,128)(2,1)} %bitcast.65), calls=%async_computation.2 | async-start | bytes 1572864 | tf_op jit(solution)/shard_map/all_to_all | solution.py:523
  65.4 0.1 collective-permute-start.1
  65.5 0.0 collective-permute-done.4
  65.5 1.9 %fusion = bf16[4,2,32,768]{3,2,0,1:T(8,128)(2,1)} fusion(bf16[4,2,2,32,768]{4,3,2,1,0:T(8,128)(2,1)} %bitcast.68, s32[]{:T(128)S(6)} %select_n.78, bf16[4,2,2,32,768]{4,3,2,1,0:T(8,128)(2,1)S(1)} %bitcast.70), kind=kLoop, calls=%fused_computation.2 | loop fusion | flops 786432 | bytes 1180672 | tf_op jit(solution)/shard_map/convert_element_type | solution.py:490
  67.4 1.9 %collective-permute-start.5 = (bf16[4,2,32,768]{3,2,0,1:T(8,128)(2,1)}, bf16[4,2,32,768]{3,2,0,1:T(8,128)(2,1)S(1)}, u32[]{:S(2)}, u32[]{:S(2)}) collective-permute-start(bf16[4,2,32,768]{3,2,0,1:T(8,128)(2,1)} %fusion), channel_id=1, source_target_pairs={{0,2},{2,0},{4,6},{6,4},{8,10},{10,8},{12,14},{14,12},{16,18},{18,... | collective-permute-start | bytes 1179656 | tf_op jit(solution)/shard_map/ppermute | solution.py:491
  69.3 0.0 collective-permute-done.1
  69.3 0.0 copy-done.3
  69.3 1.8 %fusion.2 = bf16[4,2,32,640]{3,2,0,1:T(8,128)(2,1)} fusion(bf16[4,2,2,32,640]{4,3,2,1,0:T(8,128)(2,1)S(1)} %bitcast.72, s32[]{:T(128)S(6)} %select_n.77, bf16[4,2,2,32,640]{4,3,2,1,0:T(8,128)(2,1)} %bitcast.11), kind=kLoop, calls=%fused_computation.6 | loop fusion | flops 655360 | bytes 984064 | tf_op jit(solution)/shard_map/convert_element_type | solution.py:490
  71.1 1.5 %collective-permute-start.2 = (bf16[4,2,32,640]{3,2,0,1:T(8,128)(2,1)}, bf16[4,2,32,640]{3,2,0,1:T(8,128)(2,1)}, u32[]{:S(2)}, u32[]{:S(2)}) collective-permute-start(bf16[4,2,32,640]{3,2,0,1:T(8,128)(2,1)} %fusion.2), channel_id=1, source_target_pairs={{0,4},{2,6},{4,0},{6,2},{8,12},{10,14},{12,8},{14,10},{16,20},{18,... | collective-permute-start | bytes 983048 | tf_op jit(solution)/shard_map/ppermute | solution.py:491
  72.5 0.0 copy-start
  72.5 12.9 %collective-permute-done.5 = bf16[4,2,32,768]{3,2,0,1:T(8,128)(2,1)S(1)} collective-permute-done((bf16[4,2,32,768]{3,2,0,1:T(8,128)(2,1)}, bf16[4,2,32,768]{3,2,0,1:T(8,128)(2,1)S(1)}, u32[]{:S(2)}, u32[]{:S(2)}) %collective-permute-start.5) | collective-permute-done | bytes 393248 | tf_op jit(solution)/shard_map/ppermute | solution.py:491
  85.5 0.0 copy-done.2
  85.5 0.1 fusion.1
  85.6 1.9 %collective-permute-start.6 = (bf16[4,32,768]{2,1,0:T(8,128)(2,1)S(1)}, bf16[4,32,768]{2,1,0:T(8,128)(2,1)S(1)}, u32[]{:S(2)}, u32[]{:S(2)}) collective-permute-start(bf16[4,32,768]{2,1,0:T(8,128)(2,1)S(1)} %get-tuple-element.53), channel_id=1, source_target_pairs={{0,4},{2,6},{4,0},{6,2},{8,12},{10,14},{12,8},{14,10},{16,20},{18,... | collective-permute-start | bytes 589832 | tf_op jit(solution)/shard_map/ppermute | solution.py:491
  87.5 0.0 collective-permute-done.2
  87.5 1.3 %fusion.3 = (bf16[4,32,640]{2,1,0:T(8,128)(2,1)S(1)}, f32[4,32,640]{2,1,0:T(8,128)S(1)}) fusion(bf16[4,2,32,640]{3,2,0,1:T(8,128)(2,1)} %collective-permute-done.2, s32[]{:T(128)S(6)} %select_n.78, bf16[4,2,2,32,640]{4,3,2,1,0:T(8,128)(2,1)} %bitcast.11, s32[]{:T(128)S(6)} %select_n.73, s32[]{:T(128)S(6)} %select_n.79, ...), kind=kLoop, calls=%fused_computation.8 | loop fusion | flops 901120 | bytes 1474580 | tf_op jit(solution)/shard_map/convert_element_type | solution.py:490
  88.8 1.5 %collective-permute-start.3 = (bf16[4,32,640]{2,1,0:T(8,128)(2,1)S(1)}, bf16[4,32,640]{2,1,0:T(8,128)(2,1)S(1)}, u32[]{:S(2)}, u32[]{:S(2)}) collective-permute-start(bf16[4,32,640]{2,1,0:T(8,128)(2,1)S(1)} %get-tuple-element.55), channel_id=1, source_target_pairs={{0,2},{2,0},{4,6},{6,4},{8,10},{10,8},{12,14},{14,12},{16,18},{18,... | collective-permute-start | bytes 491528 | tf_op jit(solution)/shard_map/ppermute | solution.py:491
  90.3 3.9 %collective-permute-done.3.refs_1_ = bf16[4,32,640]{2,1,0:T(8,128)(2,1)S(1)} collective-permute-done((bf16[4,32,640]{2,1,0:T(8,128)(2,1)S(1)}, bf16[4,32,640]{2,1,0:T(8,128)(2,1)S(1)}, u32[]{:S(2)}, u32[]{:S(2)}) %collective-permute-start.3) | collective-permute-done | bytes 163872 | tf_op jit(solution)/shard_map/ppermute | solution.py:491
  94.2 0.0 collective-permute-done.6.refs_3_
  94.2 0.1 shard_map.122
  94.3 0.0 all-to-all-done.2
  94.3 0.1 collective-permute-start.7
  94.3 1.4 %collective-permute-start.8 = (bf16[32,1408]{1,0:T(8,128)(2,1)S(1)}, bf16[32,1408]{1,0:T(8,128)(2,1)S(1)}, u32[]{:S(2)}, u32[]{:S(2)}) collective-permute-start(bf16[32,1408]{1,0:T(8,128)(2,1)S(1)} %get-tuple-element.47), channel_id=1, source_target_pairs={{0,8},{2,10},{4,12},{6,14},{8,16},{10,18},{12,20},{14,22},{16,24},... | collective-permute-start | bytes 270344 | tf_op jit(solution)/shard_map/ppermute | solution.py:515
  95.8 1.9 %collective-permute-start.9 = (bf16[32,1408]{1,0:T(8,128)(2,1)S(1)}, bf16[32,1408]{1,0:T(8,128)(2,1)S(1)}, u32[]{:S(2)}, u32[]{:S(2)}) collective-permute-start(bf16[32,1408]{1,0:T(8,128)(2,1)S(1)} %get-tuple-element.48), channel_id=1, source_target_pairs={{0,16},{2,18},{4,20},{6,22},{8,24},{10,26},{12,28},{14,30},{16,0},... | collective-permute-start | bytes 270344 | tf_op jit(solution)/shard_map/ppermute | solution.py:515
  97.7 2.2 %collective-permute-start.10 = (bf16[32,1408]{1,0:T(8,128)(2,1)S(1)}, bf16[32,1408]{1,0:T(8,128)(2,1)S(1)}, u32[]{:S(2)}, u32[]{:S(2)}) collective-permute-start(bf16[32,1408]{1,0:T(8,128)(2,1)S(1)} %get-tuple-element.49), channel_id=1, source_target_pairs={{0,24},{2,26},{4,28},{6,30},{8,0},{10,2},{12,4},{14,6},{16,8},{18,... | collective-permute-start | bytes 270344 | tf_op jit(solution)/shard_map/ppermute | solution.py:515
  99.9 0.0 collective-permute-done.7.refs_3_
  99.9 0.0 copy-done
  99.9 2.7 %shard_map.123 = f32[1024,512]{1,0:T(8,128)} custom-call(f32[1,768]{1,0:T(1,128)S(1)} %copy-done, f32[1,768]{1,0:T(1,128)S(1)} %collective-permute-done.refs_1_, bf16[768,512]{1,0:T(8,128)(2,1)S(1)} %bitcast.63, bf16[768,512]{1,0:T(8,128)(2,1)S(1)} %collective-permute-done.7.refs_3_), custom_call_target="tpu_custom_call" | custom-call | flops 1610612736 | bytes 3670016 | tf_op jit(solution)/shard_map/pallas_call | solution.py:49
  102.6 0.0 collective-permute-done.8.refs_0_
  102.6 2.5 %collective-permute-done.9.refs_1_ = bf16[32,1408]{1,0:T(8,128)(2,1)S(1)} collective-permute-done((bf16[32,1408]{1,0:T(8,128)(2,1)S(1)}, bf16[32,1408]{1,0:T(8,128)(2,1)S(1)}, u32[]{:S(2)}, u32[]{:S(2)}) %collective-permute-start.9) | collective-permute-done | bytes 90144 | tf_op jit(solution)/shard_map/ppermute | solution.py:515
  105.1 0.0 collective-permute-done.10.refs_2_
  105.1 0.7 shard_map.124
  105.8 0.0 collective-permute-start.11
  105.8 1.2 %collective-permute-done.11 = f32[32,256]{1,0:T(8,128)S(1)} collective-permute-done((f32[32,256]{1,0:T(8,128)S(1)}, f32[32,256]{1,0:T(8,128)S(1)}, u32[]{:S(2)}, u32[]{:S(2)}) %collective-permute-start.11) | collective-permute-done | bytes 32800 | tf_op jit(solution)/shard_map/ppermute | solution.py:384
  107.0 0.6 pad_maximum_fusion
  (1 shorter events, 0.0 us)
Async XLA Ops:
  22.4 22.1 %all-to-all-start.1 = ((bf16[16,48,512]{2,1,0:T(8,128)(2,1)}), bf16[16,48,512]{2,1,0:T(8,128)(2,1)S(1)}, u32[]{:S(2)}, u32[]{:S(2)}) async-start(bf16[16,48,512]{2,1,0:T(8,128)(2,1)} %bitcast.67), calls=%async_computation.1 | async-start | bytes 1572864 | tf_op jit(solution)/shard_map/all_to_all | solution.py:418
  26.0 1.4 %collective-permute-start = (f32[1,768]{1,0:T(1,128)}, f32[1,768]{1,0:T(1,128)S(1)}, u32[]{:S(2)}, u32[]{:S(2)}) collective-permute-start(f32[1,768]{1,0:T(1,128)} %get-tuple-element.42.refs_0_), channel_id=1, source_target_pairs={{0,1},{1,0},{2,3},{3,2},{4,5},{5,4},{6,7},{7,6},{8,9},{9,8},{10,11... | collective-permute-start | bytes 9224 | tf_op jit(solution)/shard_map/ppermute | solution.py:384
  44.5 0.9 copy-start.1
  60.4 8.9 %copy-start.3 = (bf16[512,640]{1,0:T(8,128)(2,1)S(1)}, bf16[512,640]{1,0:T(8,128)(2,1)}, u32[]{:S(2)}) copy-start(bf16[512,640]{1,0:T(8,128)(2,1)} %get-tuple-element.36) | copy-start | bytes 1966084
  60.4 25.1 %copy-start.2 = (bf16[512,768]{1,0:T(8,128)(2,1)S(1)}, bf16[512,768]{1,0:T(8,128)(2,1)}, u32[]{:S(2)}) copy-start(bf16[512,768]{1,0:T(8,128)(2,1)} %get-tuple-element.38) | copy-start | bytes 2359300
  60.4 5.1 %collective-permute-start.4 = (bf16[512,768]{1,0:T(8,128)(2,1)}, bf16[512,768]{1,0:T(8,128)(2,1)S(1)}, u32[]{:S(2)}, u32[]{:S(2)}) collective-permute-start(bf16[512,768]{1,0:T(8,128)(2,1)} %get-tuple-element.39), channel_id=1, source_target_pairs={{0,1},{1,0},{2,3},{3,2},{4,5},{5,4},{6,7},{7,6},{8,9},{9,8},{10,11... | collective-permute-start | bytes 2359304 | tf_op jit(solution)/shard_map/ppermute | solution.py:384
  60.5 33.8 %all-to-all-start.2 = ((bf16[16,48,512]{2,1,0:T(8,128)(2,1)}), bf16[16,48,512]{2,1,0:T(8,128)(2,1)S(1)}, u32[]{:S(2)}, u32[]{:S(2)}) async-start(bf16[16,48,512]{2,1,0:T(8,128)(2,1)} %bitcast.65), calls=%async_computation.2 | async-start | bytes 1572864 | tf_op jit(solution)/shard_map/all_to_all | solution.py:523
  65.4 3.9 %collective-permute-start.1 = (bf16[512,640]{1,0:T(8,128)(2,1)}, bf16[512,640]{1,0:T(8,128)(2,1)}, u32[]{:S(2)}, u32[]{:S(2)}) collective-permute-start(bf16[512,640]{1,0:T(8,128)(2,1)} %get-tuple-element.37), channel_id=1, source_target_pairs={{0,1},{1,0},{2,3},{3,2},{4,5},{5,4},{6,7},{7,6},{8,9},{9,8},{10,11... | collective-permute-start | bytes 1966088 | tf_op jit(solution)/shard_map/ppermute | solution.py:384
  67.4 18.1 %collective-permute-start.5 = (bf16[4,2,32,768]{3,2,0,1:T(8,128)(2,1)}, bf16[4,2,32,768]{3,2,0,1:T(8,128)(2,1)S(1)}, u32[]{:S(2)}, u32[]{:S(2)}) collective-permute-start(bf16[4,2,32,768]{3,2,0,1:T(8,128)(2,1)} %fusion), channel_id=1, source_target_pairs={{0,2},{2,0},{4,6},{6,4},{8,10},{10,8},{12,14},{14,12},{16,18},{18,... | collective-permute-start | bytes 1179656 | tf_op jit(solution)/shard_map/ppermute | solution.py:491
  71.1 16.4 %collective-permute-start.2 = (bf16[4,2,32,640]{3,2,0,1:T(8,128)(2,1)}, bf16[4,2,32,640]{3,2,0,1:T(8,128)(2,1)}, u32[]{:S(2)}, u32[]{:S(2)}) collective-permute-start(bf16[4,2,32,640]{3,2,0,1:T(8,128)(2,1)} %fusion.2), channel_id=1, source_target_pairs={{0,4},{2,6},{4,0},{6,2},{8,12},{10,14},{12,8},{14,10},{16,20},{18,... | collective-permute-start | bytes 983048 | tf_op jit(solution)/shard_map/ppermute | solution.py:491
  72.5 27.3 %copy-start = (f32[1,768]{1,0:T(1,128)S(1)}, f32[1,768]{1,0:T(1,128)}, u32[]{:S(2)}) copy-start(f32[1,768]{1,0:T(1,128)} %get-tuple-element.42.refs_0_) | copy-start | bytes 9220
  85.6 8.6 %collective-permute-start.6 = (bf16[4,32,768]{2,1,0:T(8,128)(2,1)S(1)}, bf16[4,32,768]{2,1,0:T(8,128)(2,1)S(1)}, u32[]{:S(2)}, u32[]{:S(2)}) collective-permute-start(bf16[4,32,768]{2,1,0:T(8,128)(2,1)S(1)} %get-tuple-element.53), channel_id=1, source_target_pairs={{0,4},{2,6},{4,0},{6,2},{8,12},{10,14},{12,8},{14,10},{16,20},{18,... | collective-permute-start | bytes 589832 | tf_op jit(solution)/shard_map/ppermute | solution.py:491
  88.8 5.4 %collective-permute-start.3 = (bf16[4,32,640]{2,1,0:T(8,128)(2,1)S(1)}, bf16[4,32,640]{2,1,0:T(8,128)(2,1)S(1)}, u32[]{:S(2)}, u32[]{:S(2)}) collective-permute-start(bf16[4,32,640]{2,1,0:T(8,128)(2,1)S(1)} %get-tuple-element.55), channel_id=1, source_target_pairs={{0,2},{2,0},{4,6},{6,4},{8,10},{10,8},{12,14},{14,12},{16,18},{18,... | collective-permute-start | bytes 491528 | tf_op jit(solution)/shard_map/ppermute | solution.py:491
  94.3 5.6 %collective-permute-start.7 = (bf16[768,512]{1,0:T(8,128)(2,1)S(1)}, bf16[768,512]{1,0:T(8,128)(2,1)S(1)}, u32[]{:S(2)}, u32[]{:S(2)}) collective-permute-start(bf16[768,512]{1,0:T(8,128)(2,1)S(1)} %bitcast.62), channel_id=1, source_target_pairs={{0,1},{1,0},{2,3},{3,2},{4,5},{5,4},{6,7},{7,6},{8,9},{9,8},{10,11... | collective-permute-start | bytes 2359304 | tf_op jit(solution)/shard_map/ppermute | solution.py:384
  94.3 8.3 %collective-permute-start.8 = (bf16[32,1408]{1,0:T(8,128)(2,1)S(1)}, bf16[32,1408]{1,0:T(8,128)(2,1)S(1)}, u32[]{:S(2)}, u32[]{:S(2)}) collective-permute-start(bf16[32,1408]{1,0:T(8,128)(2,1)S(1)} %get-tuple-element.47), channel_id=1, source_target_pairs={{0,8},{2,10},{4,12},{6,14},{8,16},{10,18},{12,20},{14,22},{16,24},... | collective-permute-start | bytes 270344 | tf_op jit(solution)/shard_map/ppermute | solution.py:515
  95.8 9.3 %collective-permute-start.9 = (bf16[32,1408]{1,0:T(8,128)(2,1)S(1)}, bf16[32,1408]{1,0:T(8,128)(2,1)S(1)}, u32[]{:S(2)}, u32[]{:S(2)}) collective-permute-start(bf16[32,1408]{1,0:T(8,128)(2,1)S(1)} %get-tuple-element.48), channel_id=1, source_target_pairs={{0,16},{2,18},{4,20},{6,22},{8,24},{10,26},{12,28},{14,30},{16,0},... | collective-permute-start | bytes 270344 | tf_op jit(solution)/shard_map/ppermute | solution.py:515
  97.7 7.4 %collective-permute-start.10 = (bf16[32,1408]{1,0:T(8,128)(2,1)S(1)}, bf16[32,1408]{1,0:T(8,128)(2,1)S(1)}, u32[]{:S(2)}, u32[]{:S(2)}) collective-permute-start(bf16[32,1408]{1,0:T(8,128)(2,1)S(1)} %get-tuple-element.49), channel_id=1, source_target_pairs={{0,24},{2,26},{4,28},{6,30},{8,0},{10,2},{12,4},{14,6},{16,8},{18,... | collective-permute-start | bytes 270344 | tf_op jit(solution)/shard_map/ppermute | solution.py:515
  105.8 1.2 %collective-permute-start.11 = (f32[32,256]{1,0:T(8,128)S(1)}, f32[32,256]{1,0:T(8,128)S(1)}, u32[]{:S(2)}, u32[]{:S(2)}) collective-permute-start(f32[32,256]{1,0:T(8,128)S(1)} %get-tuple-element.51), channel_id=1, source_target_pairs={{0,1},{1,0},{2,3},{3,2},{4,5},{5,4},{6,7},{7,6},{8,9},{9,8},{10,11... | collective-permute-start | bytes 98312 | tf_op jit(solution)/shard_map/ppermute | solution.py:384

commit v18 on v15

--- a/solution.py
+++ b/solution.py
@@ -253,7 +253,7 @@
             weight_ref[p, base : base + per * qrows, :r1] = weight_b.reshape(per * qrows, r1)
             wslope_ref[p, base : base + per * qrows, :r1] = (
                 (1.0 + th) + weight * (1.0 - th)
-            ).reshape(per * qrows, r1)
+            ).astype(BF16).reshape(per * qrows, r1)
             total = dot_nn(weight_b[0], vals[0][:r1])
             for a in range(1, per):
                 total = total + dot_nn(weight_b[a], vals[a][:r1])
@@ -297,7 +297,7 @@
             rows = slice(base, base + per * qrows)
             gatt = stacked(gatt_ref[r0:r1, cols])
             gweight = dot_nt(gatt, val[:r1])
-            gscore = (gweight * wslope_ref[p, rows, :r1]).astype(BF16)
+            gscore = (gweight * wslope_ref[p, rows, :r1].astype(F32)).astype(BF16)
             gqry = dot_nn(gscore[:qrows], keys[0][:r1])
             for a in range(1, per):
                 gqry = gqry + dot_nn(gscore[a * qrows : (a + 1) * qrows], keys[a][:r1])
@@ -458,7 +458,7 @@
             pltpu.VMEM((4, count, width), F32),
             pltpu.VMEM((count, count), F32),
             pltpu.VMEM((width // LANES, heads_per * count, count), BF16),
-            pltpu.VMEM((width // LANES, heads_per * count, count), F32),
+            pltpu.VMEM((width // LANES, heads_per * count, count), BF16),
             pltpu.VMEM((count, width), F32),
             square,
             square,

time: 108 us -> 108 us (level)
  no operation moved by 1% of the time
where the time goes in v18:
time: 108 us
  waiting for transfers between devices  40.7 us (38%)
  Pallas kernels  24.8 us (23%)
  starting transfers between devices  19.4 us (18%)
  blocking collectives  15.6 us (14%)
  other arithmetic  5.74 us (5%)
    pallas_call x6, Pallas kernels, call(): pl.pallas_call(kernel, out_shape=out_shape, in_specs=[pl.BlockSpec(memory...  24.8 us
    ppermute x4, waiting for transfers between devices, halve(): got = lax.ppermute(send, 'table', [(i, i ^ bit) for i in range(owners)])  18.5 us
    all_to_all x1, waiting for transfers between devices, on_device(): lax.all_to_all(found, 'table', split_axis=0, concat_axis=0, tiled=True)  17 us
    all_to_all x1, blocking collectives, on_device(): lax.all_to_all(requested, 'table', split_axis=0, concat_axis=0, tiled=True)  15.6 us
    ppermute x3, starting transfers between devices, on_device(): lax.ppermute(sends[k - 1], 'table', [(i, (i // plane + k) % outer * plane...  5.37 us
    ppermute x4, starting transfers between devices, halve(): got = lax.ppermute(send, 'table', [(i, i ^ bit) for i in range(owners)])  5.11 us
    convert_element_type x4, other arithmetic, halve(): send = add([entry(term, 1 - index, axis) for term in terms]).astype(BF16)  5.09 us
    all_to_all x1, starting transfers between devices, on_device(): lax.all_to_all(outgoing, 'table', split_axis=0, concat_axis=0, tiled=True)  4.9 us
  transfers between devices with their start and end apart: 14, of which 7 were waited for; matrix products, arithmetic and copies ran while one was open for 5% of the time, Pallas kernels for 3%

profile of v18, /device:TPU:0, one launch (start us, length us, event | category | flops | bytes accessed | tf_op | source)
XLA Modules:
  0.0 107.9 jit_solution(17792960402702433307)
XLA Ops:
  0.6 1.7 %shard_map.119 = (s32[16,128]{1,0:T(8,128)}, f32[1,512]{1,0:T(1,128)}) custom-call(s32[1,512]{1,0:T(1,128)} %bitcast.77, s32[1,512]{1,0:T(1,128)} %bitcast.78), custom_call_target="tpu_custom_call" | custom-call | flops 16777216 | bytes 4096 | tf_op jit(solution)/shard_map/pallas_call | solution.py:49
  2.3 15.6 %all_to_all.35 = s32[16,1,128]{2,1,0:T(1,128)} all-to-all(s32[16,1,128]{2,1,0:T(1,128)} %bitcast.76), channel_id=1, replica_groups=mesh['table'=16,'group'=2] {'table'}, dimensions={0} | all-to-all | bytes 16384 | tf_op jit(solution)/shard_map/all_to_all | solution.py:407
  17.9 4.5 %shard_map.120 = (bf16[768,512]{1,0:T(8,128)(2,1)}, f32[1,768]{1,0:T(1,128)}) custom-call(s32[16,128]{1,0:T(8,128)} %bitcast.75, bf16[2048,512]{1,0:T(8,128)(2,1)} %table_ref.1), custom_call_target="tpu_custom_call" | custom-call | flops 1610612736 | bytes 2883584 | tf_op jit(solution)/shard_map/pallas_call | solution.py:49
  22.4 3.6 %all-to-all-start.1 = ((bf16[16,48,512]{2,1,0:T(8,128)(2,1)}), bf16[16,48,512]{2,1,0:T(8,128)(2,1)S(1)}, u32[]{:S(2)}, u32[]{:S(2)}) async-start(bf16[16,48,512]{2,1,0:T(8,128)(2,1)} %bitcast.67), calls=%async_computation.1 | async-start | bytes 1572864 | tf_op jit(solution)/shard_map/all_to_all | solution.py:418
  26.0 0.1 collective-permute-start
  26.1 1.4 %collective-permute-done.refs_1_ = f32[1,768]{1,0:T(1,128)S(1)} collective-permute-done((f32[1,768]{1,0:T(1,128)}, f32[1,768]{1,0:T(1,128)S(1)}, u32[]{:S(2)}, u32[]{:S(2)}) %collective-permute-start) | collective-permute-done | bytes 3104 | tf_op jit(solution)/shard_map/ppermute | solution.py:384
  27.4 17.0 %all-to-all-done.1 = bf16[16,48,512]{2,1,0:T(8,128)(2,1)S(1)} async-done(((bf16[16,48,512]{2,1,0:T(8,128)(2,1)}), bf16[16,48,512]{2,1,0:T(8,128)(2,1)S(1)}, u32[]{:S(2)}, u32[]{:S(2)}) %all-to-all-start.1) | async-done | bytes 786464 | tf_op jit(solution)/shard_map/all_to_all | solution.py:418
  44.5 0.0 copy-start.1
  44.5 0.9 copy-done.1
  45.4 15.1 %shard_map.121 = (bf16[512,512]{1,0:T(8,128)(2,1)}, bf16[768,512]{1,0:T(8,128)(2,1)}, bf16[512,640]{1,0:T(8,128)(2,1)}, bf16[512,768]{1,0:T(8,128)(2,1)}, bf16[5...) custom-call(s32[1,8]{1,0:T(1,128)} %len_ref.1, f32[1,512]{1,0:T(1,128)} %get-tuple-element.29.slot_ref, ...), custom_call_target="tpu_custom_call" | custom-call | flops 6174015488 | bytes 6291456 | tf_op jit(solution)/shard_map/pallas_call | solution.py:49
  60.5 0.0 copy-start.3
  60.5 0.0 copy-start.2
  60.5 0.1 collective-permute-start.4
  60.6 4.9 %all-to-all-start.2 = ((bf16[16,48,512]{2,1,0:T(8,128)(2,1)}), bf16[16,48,512]{2,1,0:T(8,128)(2,1)S(1)}, u32[]{:S(2)}, u32[]{:S(2)}) async-start(bf16[16,48,512]{2,1,0:T(8,128)(2,1)} %bitcast.65), calls=%async_computation.2 | async-start | bytes 1572864 | tf_op jit(solution)/shard_map/all_to_all | solution.py:523
  65.5 0.1 collective-permute-start.1
  65.6 0.0 collective-permute-done.4
  65.6 1.9 %fusion = bf16[4,2,32,768]{3,2,0,1:T(8,128)(2,1)} fusion(bf16[4,2,2,32,768]{4,3,2,1,0:T(8,128)(2,1)} %bitcast.68, s32[]{:T(128)S(6)} %select_n.78, bf16[4,2,2,32,768]{4,3,2,1,0:T(8,128)(2,1)S(1)} %bitcast.70), kind=kLoop, calls=%fused_computation.2 | loop fusion | flops 786432 | bytes 1180672 | tf_op jit(solution)/shard_map/convert_element_type | solution.py:490
  67.5 1.8 %collective-permute-start.5 = (bf16[4,2,32,768]{3,2,0,1:T(8,128)(2,1)}, bf16[4,2,32,768]{3,2,0,1:T(8,128)(2,1)S(1)}, u32[]{:S(2)}, u32[]{:S(2)}) collective-permute-start(bf16[4,2,32,768]{3,2,0,1:T(8,128)(2,1)} %fusion), channel_id=1, source_target_pairs={{0,4},{2,6},{4,0},{6,2},{8,12},{10,14},{12,8},{14,10},{16,20},{18,... | collective-permute-start | bytes 1179656 | tf_op jit(solution)/shard_map/ppermute | solution.py:491
  69.4 0.0 collective-permute-done.1
  69.4 0.0 copy-done.3
  69.4 1.8 %fusion.2 = bf16[4,2,32,640]{3,2,0,1:T(8,128)(2,1)} fusion(bf16[4,2,2,32,640]{4,3,2,1,0:T(8,128)(2,1)S(1)} %bitcast.72, s32[]{:T(128)S(6)} %select_n.77, bf16[4,2,2,32,640]{4,3,2,1,0:T(8,128)(2,1)} %bitcast.11), kind=kLoop, calls=%fused_computation.6 | loop fusion | flops 655360 | bytes 984064 | tf_op jit(solution)/shard_map/convert_element_type | solution.py:490
  71.2 1.5 %collective-permute-start.2 = (bf16[4,2,32,640]{3,2,0,1:T(8,128)(2,1)}, bf16[4,2,32,640]{3,2,0,1:T(8,128)(2,1)}, u32[]{:S(2)}, u32[]{:S(2)}) collective-permute-start(bf16[4,2,32,640]{3,2,0,1:T(8,128)(2,1)} %fusion.2), channel_id=1, source_target_pairs={{0,2},{2,0},{4,6},{6,4},{8,10},{10,8},{12,14},{14,12},{16,18},{18,... | collective-permute-start | bytes 983048 | tf_op jit(solution)/shard_map/ppermute | solution.py:491
  72.6 0.0 copy-start
  72.6 12.8 %collective-permute-done.5 = bf16[4,2,32,768]{3,2,0,1:T(8,128)(2,1)S(1)} collective-permute-done((bf16[4,2,32,768]{3,2,0,1:T(8,128)(2,1)}, bf16[4,2,32,768]{3,2,0,1:T(8,128)(2,1)S(1)}, u32[]{:S(2)}, u32[]{:S(2)}) %collective-permute-start.5) | collective-permute-done | bytes 393248 | tf_op jit(solution)/shard_map/ppermute | solution.py:491
  85.4 0.0 copy-done.2
  85.4 0.1 fusion.1
  85.5 1.3 %collective-permute-start.6 = (bf16[4,32,768]{2,1,0:T(8,128)(2,1)S(1)}, bf16[4,32,768]{2,1,0:T(8,128)(2,1)S(1)}, u32[]{:S(2)}, u32[]{:S(2)}) collective-permute-start(bf16[4,32,768]{2,1,0:T(8,128)(2,1)S(1)} %get-tuple-element.53), channel_id=1, source_target_pairs={{0,2},{2,0},{4,6},{6,4},{8,10},{10,8},{12,14},{14,12},{16,18},{18,... | collective-permute-start | bytes 589832 | tf_op jit(solution)/shard_map/ppermute | solution.py:491
  86.8 0.5 collective-permute-done.2
  87.3 1.3 %fusion.3 = (bf16[4,32,640]{2,1,0:T(8,128)(2,1)S(1)}, f32[4,32,640]{2,1,0:T(8,128)S(1)}) fusion(bf16[4,2,32,640]{3,2,0,1:T(8,128)(2,1)} %collective-permute-done.2, s32[]{:T(128)S(6)} %select_n.78, bf16[4,2,2,32,640]{4,3,2,1,0:T(8,128)(2,1)} %bitcast.11, s32[]{:T(128)S(6)} %select_n.79, s32[]{:T(128)S(6)} %select_n.76, ...), kind=kLoop, calls=%fused_computation.8 | loop fusion | flops 901120 | bytes 1474580 | tf_op jit(solution)/shard_map/convert_element_type | solution.py:490
  88.6 0.5 collective-permute-start.3
  89.1 5.3 %collective-permute-done.3.refs_1_ = bf16[4,32,640]{2,1,0:T(8,128)(2,1)S(1)} collective-permute-done((bf16[4,32,640]{2,1,0:T(8,128)(2,1)S(1)}, bf16[4,32,640]{2,1,0:T(8,128)(2,1)S(1)}, u32[]{:S(2)}, u32[]{:S(2)}) %collective-permute-start.3) | collective-permute-done | bytes 163872 | tf_op jit(solution)/shard_map/ppermute | solution.py:491
  94.4 0.0 collective-permute-done.6.refs_3_
  94.4 0.1 shard_map.122
  94.4 0.0 all-to-all-done.2
  94.5 0.1 collective-permute-start.7
  94.5 1.7 %collective-permute-start.8 = (bf16[32,1408]{1,0:T(8,128)(2,1)S(1)}, bf16[32,1408]{1,0:T(8,128)(2,1)S(1)}, u32[]{:S(2)}, u32[]{:S(2)}) collective-permute-start(bf16[32,1408]{1,0:T(8,128)(2,1)S(1)} %get-tuple-element.47), channel_id=1, source_target_pairs={{0,8},{2,10},{4,12},{6,14},{8,16},{10,18},{12,20},{14,22},{16,24},... | collective-permute-start | bytes 270344 | tf_op jit(solution)/shard_map/ppermute | solution.py:515
  96.3 2.0 %collective-permute-start.9 = (bf16[32,1408]{1,0:T(8,128)(2,1)S(1)}, bf16[32,1408]{1,0:T(8,128)(2,1)S(1)}, u32[]{:S(2)}, u32[]{:S(2)}) collective-permute-start(bf16[32,1408]{1,0:T(8,128)(2,1)S(1)} %get-tuple-element.48), channel_id=1, source_target_pairs={{0,16},{2,18},{4,20},{6,22},{8,24},{10,26},{12,28},{14,30},{16,0},... | collective-permute-start | bytes 270344 | tf_op jit(solution)/shard_map/ppermute | solution.py:515
  98.3 1.6 %collective-permute-start.10 = (bf16[32,1408]{1,0:T(8,128)(2,1)S(1)}, bf16[32,1408]{1,0:T(8,128)(2,1)S(1)}, u32[]{:S(2)}, u32[]{:S(2)}) collective-permute-start(bf16[32,1408]{1,0:T(8,128)(2,1)S(1)} %get-tuple-element.49), channel_id=1, source_target_pairs={{0,24},{2,26},{4,28},{6,30},{8,0},{10,2},{12,4},{14,6},{16,8},{18,... | collective-permute-start | bytes 270344 | tf_op jit(solution)/shard_map/ppermute | solution.py:515
  99.9 0.0 collective-permute-done.7.refs_3_
  99.9 0.0 copy-done
  99.9 2.7 %shard_map.123 = f32[1024,512]{1,0:T(8,128)} custom-call(f32[1,768]{1,0:T(1,128)S(1)} %copy-done, f32[1,768]{1,0:T(1,128)S(1)} %collective-permute-done.refs_1_, bf16[768,512]{1,0:T(8,128)(2,1)S(1)} %bitcast.63, bf16[768,512]{1,0:T(8,128)(2,1)S(1)} %collective-permute-done.7.refs_3_), custom_call_target="tpu_custom_call" | custom-call | flops 1610612736 | bytes 3670016 | tf_op jit(solution)/shard_map/pallas_call | solution.py:49
  102.7 0.0 collective-permute-done.8.refs_0_
  102.7 2.6 %collective-permute-done.9.refs_1_ = bf16[32,1408]{1,0:T(8,128)(2,1)S(1)} collective-permute-done((bf16[32,1408]{1,0:T(8,128)(2,1)S(1)}, bf16[32,1408]{1,0:T(8,128)(2,1)S(1)}, u32[]{:S(2)}, u32[]{:S(2)}) %collective-permute-start.9) | collective-permute-done | bytes 90144 | tf_op jit(solution)/shard_map/ppermute | solution.py:515
  105.3 0.0 collective-permute-done.10.refs_2_
  105.3 0.7 shard_map.124
  106.0 0.0 collective-permute-start.11
  106.0 1.2 %collective-permute-done.11 = f32[32,256]{1,0:T(8,128)S(1)} collective-permute-done((f32[32,256]{1,0:T(8,128)S(1)}, f32[32,256]{1,0:T(8,128)S(1)}, u32[]{:S(2)}, u32[]{:S(2)}) %collective-permute-start.11) | collective-permute-done | bytes 32800 | tf_op jit(solution)/shard_map/ppermute | solution.py:384
  107.2 0.6 pad_maximum_fusion
  (1 shorter events, 0.0 us)
Async XLA Ops:
  22.4 22.1 %all-to-all-start.1 = ((bf16[16,48,512]{2,1,0:T(8,128)(2,1)}), bf16[16,48,512]{2,1,0:T(8,128)(2,1)S(1)}, u32[]{:S(2)}, u32[]{:S(2)}) async-start(bf16[16,48,512]{2,1,0:T(8,128)(2,1)} %bitcast.67), calls=%async_computation.1 | async-start | bytes 1572864 | tf_op jit(solution)/shard_map/all_to_all | solution.py:418
  26.0 1.4 %collective-permute-start = (f32[1,768]{1,0:T(1,128)}, f32[1,768]{1,0:T(1,128)S(1)}, u32[]{:S(2)}, u32[]{:S(2)}) collective-permute-start(f32[1,768]{1,0:T(1,128)} %get-tuple-element.42.refs_0_), channel_id=1, source_target_pairs={{0,1},{1,0},{2,3},{3,2},{4,5},{5,4},{6,7},{7,6},{8,9},{9,8},{10,11... | collective-permute-start | bytes 9224 | tf_op jit(solution)/shard_map/ppermute | solution.py:384
  44.5 0.9 copy-start.1
  60.5 8.9 %copy-start.3 = (bf16[512,640]{1,0:T(8,128)(2,1)S(1)}, bf16[512,640]{1,0:T(8,128)(2,1)}, u32[]{:S(2)}) copy-start(bf16[512,640]{1,0:T(8,128)(2,1)} %get-tuple-element.36) | copy-start | bytes 1966084
  60.5 24.9 %copy-start.2 = (bf16[512,768]{1,0:T(8,128)(2,1)S(1)}, bf16[512,768]{1,0:T(8,128)(2,1)}, u32[]{:S(2)}) copy-start(bf16[512,768]{1,0:T(8,128)(2,1)} %get-tuple-element.38) | copy-start | bytes 2359300
  60.5 5.1 %collective-permute-start.4 = (bf16[512,768]{1,0:T(8,128)(2,1)}, bf16[512,768]{1,0:T(8,128)(2,1)S(1)}, u32[]{:S(2)}, u32[]{:S(2)}) collective-permute-start(bf16[512,768]{1,0:T(8,128)(2,1)} %get-tuple-element.39), channel_id=1, source_target_pairs={{0,1},{1,0},{2,3},{3,2},{4,5},{5,4},{6,7},{7,6},{8,9},{9,8},{10,11... | collective-permute-start | bytes 2359304 | tf_op jit(solution)/shard_map/ppermute | solution.py:384
  60.6 33.9 %all-to-all-start.2 = ((bf16[16,48,512]{2,1,0:T(8,128)(2,1)}), bf16[16,48,512]{2,1,0:T(8,128)(2,1)S(1)}, u32[]{:S(2)}, u32[]{:S(2)}) async-start(bf16[16,48,512]{2,1,0:T(8,128)(2,1)} %bitcast.65), calls=%async_computation.2 | async-start | bytes 1572864 | tf_op jit(solution)/shard_map/all_to_all | solution.py:523
  65.5 3.9 %collective-permute-start.1 = (bf16[512,640]{1,0:T(8,128)(2,1)}, bf16[512,640]{1,0:T(8,128)(2,1)}, u32[]{:S(2)}, u32[]{:S(2)}) collective-permute-start(bf16[512,640]{1,0:T(8,128)(2,1)} %get-tuple-element.37), channel_id=1, source_target_pairs={{0,1},{1,0},{2,3},{3,2},{4,5},{5,4},{6,7},{7,6},{8,9},{9,8},{10,11... | collective-permute-start | bytes 1966088 | tf_op jit(solution)/shard_map/ppermute | solution.py:384
  67.5 17.9 %collective-permute-start.5 = (bf16[4,2,32,768]{3,2,0,1:T(8,128)(2,1)}, bf16[4,2,32,768]{3,2,0,1:T(8,128)(2,1)S(1)}, u32[]{:S(2)}, u32[]{:S(2)}) collective-permute-start(bf16[4,2,32,768]{3,2,0,1:T(8,128)(2,1)} %fusion), channel_id=1, source_target_pairs={{0,4},{2,6},{4,0},{6,2},{8,12},{10,14},{12,8},{14,10},{16,20},{18,... | collective-permute-start | bytes 1179656 | tf_op jit(solution)/shard_map/ppermute | solution.py:491
  71.2 16.1 %collective-permute-start.2 = (bf16[4,2,32,640]{3,2,0,1:T(8,128)(2,1)}, bf16[4,2,32,640]{3,2,0,1:T(8,128)(2,1)}, u32[]{:S(2)}, u32[]{:S(2)}) collective-permute-start(bf16[4,2,32,640]{3,2,0,1:T(8,128)(2,1)} %fusion.2), channel_id=1, source_target_pairs={{0,2},{2,0},{4,6},{6,4},{8,10},{10,8},{12,14},{14,12},{16,18},{18,... | collective-permute-start | bytes 983048 | tf_op jit(solution)/shard_map/ppermute | solution.py:491
  72.6 27.3 %copy-start = (f32[1,768]{1,0:T(1,128)S(1)}, f32[1,768]{1,0:T(1,128)}, u32[]{:S(2)}) copy-start(f32[1,768]{1,0:T(1,128)} %get-tuple-element.42.refs_0_) | copy-start | bytes 9220
  85.5 8.8 %collective-permute-start.6 = (bf16[4,32,768]{2,1,0:T(8,128)(2,1)S(1)}, bf16[4,32,768]{2,1,0:T(8,128)(2,1)S(1)}, u32[]{:S(2)}, u32[]{:S(2)}) collective-permute-start(bf16[4,32,768]{2,1,0:T(8,128)(2,1)S(1)} %get-tuple-element.53), channel_id=1, source_target_pairs={{0,2},{2,0},{4,6},{6,4},{8,10},{10,8},{12,14},{14,12},{16,18},{18,... | collective-permute-start | bytes 589832 | tf_op jit(solution)/shard_map/ppermute | solution.py:491
  88.6 5.8 %collective-permute-start.3 = (bf16[4,32,640]{2,1,0:T(8,128)(2,1)S(1)}, bf16[4,32,640]{2,1,0:T(8,128)(2,1)S(1)}, u32[]{:S(2)}, u32[]{:S(2)}) collective-permute-start(bf16[4,32,640]{2,1,0:T(8,128)(2,1)S(1)} %get-tuple-element.55), channel_id=1, source_target_pairs={{0,4},{2,6},{4,0},{6,2},{8,12},{10,14},{12,8},{14,10},{16,20},{18,... | collective-permute-start | bytes 491528 | tf_op jit(solution)/shard_map/ppermute | solution.py:491
  94.5 5.5 %collective-permute-start.7 = (bf16[768,512]{1,0:T(8,128)(2,1)S(1)}, bf16[768,512]{1,0:T(8,128)(2,1)S(1)}, u32[]{:S(2)}, u32[]{:S(2)}) collective-permute-start(bf16[768,512]{1,0:T(8,128)(2,1)S(1)} %bitcast.62), channel_id=1, source_target_pairs={{0,1},{1,0},{2,3},{3,2},{4,5},{5,4},{6,7},{7,6},{8,9},{9,8},{10,11... | collective-permute-start | bytes 2359304 | tf_op jit(solution)/shard_map/ppermute | solution.py:384
  94.5 8.1 %collective-permute-start.8 = (bf16[32,1408]{1,0:T(8,128)(2,1)S(1)}, bf16[32,1408]{1,0:T(8,128)(2,1)S(1)}, u32[]{:S(2)}, u32[]{:S(2)}) collective-permute-start(bf16[32,1408]{1,0:T(8,128)(2,1)S(1)} %get-tuple-element.47), channel_id=1, source_target_pairs={{0,8},{2,10},{4,12},{6,14},{8,16},{10,18},{12,20},{14,22},{16,24},... | collective-permute-start | bytes 270344 | tf_op jit(solution)/shard_map/ppermute | solution.py:515
  96.3 9.0 %collective-permute-start.9 = (bf16[32,1408]{1,0:T(8,128)(2,1)S(1)}, bf16[32,1408]{1,0:T(8,128)(2,1)S(1)}, u32[]{:S(2)}, u32[]{:S(2)}) collective-permute-start(bf16[32,1408]{1,0:T(8,128)(2,1)S(1)} %get-tuple-element.48), channel_id=1, source_target_pairs={{0,16},{2,18},{4,20},{6,22},{8,24},{10,26},{12,28},{14,30},{16,0},... | collective-permute-start | bytes 270344 | tf_op jit(solution)/shard_map/ppermute | solution.py:515
  98.3 7.0 %collective-permute-start.10 = (bf16[32,1408]{1,0:T(8,128)(2,1)S(1)}, bf16[32,1408]{1,0:T(8,128)(2,1)S(1)}, u32[]{:S(2)}, u32[]{:S(2)}) collective-permute-start(bf16[32,1408]{1,0:T(8,128)(2,1)S(1)} %get-tuple-element.49), channel_id=1, source_target_pairs={{0,24},{2,26},{4,28},{6,30},{8,0},{10,2},{12,4},{14,6},{16,8},{18,... | collective-permute-start | bytes 270344 | tf_op jit(solution)/shard_map/ppermute | solution.py:515
  106.0 1.2 %collective-permute-start.11 = (f32[32,256]{1,0:T(8,128)S(1)}, f32[32,256]{1,0:T(8,128)S(1)}, u32[]{:S(2)}, u32[]{:S(2)}) collective-permute-start(f32[32,256]{1,0:T(8,128)S(1)} %get-tuple-element.51), channel_id=1, source_target_pairs={{0,1},{1,0},{2,3},{3,2},{4,5},{5,4},{6,7},{7,6},{8,9},{9,8},{10,11... | collective-permute-start | bytes 98312 | tf_op jit(solution)/shard_map/ppermute | solution.py:384
